TPU v7x, 512 devices: a whole 4x4x16 slice. The times are simulated.
512 devices in a mesh: tensor: 32 (over y_lo, z), dp: 16 (over x, y_hi, core).
Axes of the slice: x: 4, y: 4 (y_hi: 2, y_lo: 2; y = y_hi * 2 + y_lo), z: 16, core: 2. Of those that a mesh axis runs over, the one named last changes fastest.
Arguments:
- hidden: bfloat16 [2048, 4096], P(('dp', 'tensor')), may hold values from -6 to 6
- joined_in: bfloat16 [2048, 8192], P(('dp', 'tensor')), may hold values from -6 to 6
- gate_act: bfloat16 [2048, 28672], P(('dp', 'tensor')), may hold values from -6 to 6
- up_act: bfloat16 [2048, 28672], P(('dp', 'tensor')), may hold values from -6 to 6
- product_grad: bfloat16 [2048, 28672], P(('dp', 'tensor')), may hold values from -6 to 6
- resid_grad: bfloat16 [2048, 4096], P(('dp', 'tensor')), may hold values from -6 to 6
- norm_gain: float32 [4096], replicated, may hold values from 0.1 to 1.9
- gate_weight: bfloat16 [28672, 4096], P('tensor', 'dp'), may hold values from -0.09375 to 0.09375
- up_weight: bfloat16 [28672, 4096], P('tensor', 'dp'), may hold values from -0.09375 to 0.09375
- join_weight: bfloat16 [8192, 4096], P('tensor', 'dp'), may hold values from -0.09375 to 0.09375
Outputs:
- joined_grad: bfloat16 [2048, 8192], P(('dp', 'tensor'))
- gate_weight_grad: float32 [28672, 4096], P('tensor', 'dp')
- up_weight_grad: float32 [28672, 4096], P('tensor', 'dp')
- join_weight_grad: float32 [8192, 4096], P('tensor', 'dp')
- gain_grad: float32 [4096], replicated
All inputs are finite; a program needn't handle non-finite values.
Results may differ from a plain program's by a relative error of at most 0.0057.
Values may be sent and summed in bfloat16 or wider, within the bound.
No kernel may reach another device: no remote copies, remote signals or barrier semaphores. Data moves between devices by JAX's collectives and lax.ppermute only.
A program may use at most 64 MiB of HBM per device.

v0:
```python
import jax
import jax.numpy as jnp
from jax import lax
from jax.sharding import PartitionSpec as P

epsilon = 1e-05


def swiglu_back(gate_act, up_act, product_grad):
    gate_wide = gate_act.astype(jnp.float32)
    logistic = jax.nn.sigmoid(gate_wide)
    product_wide = product_grad.astype(jnp.float32)
    gate_grad = (
        product_wide * up_act.astype(jnp.float32) * logistic * (1.0 + gate_wide * (1.0 - logistic))
    )
    up_grad = product_wide * gate_wide * logistic
    return (gate_grad.astype(jnp.bfloat16), up_grad.astype(jnp.bfloat16))


def token_sum(left, right):
    return lax.dot_general(
        left, right, (((0,), (0,)), ((), ())), preferred_element_type=jnp.float32
    )


def spread_columns(rows_in):
    group_block = lax.all_gather(rows_in, "tensor", axis=0, tiled=True)
    spread_out = lax.all_to_all(group_block, "dp", split_axis=1, concat_axis=0, tiled=True)
    return spread_out


def shards(
    hidden,
    joined_in,
    gate_act,
    up_act,
    product_grad,
    resid_grad,
    norm_gain,
    gate_weight,
    up_weight,
    join_weight,
):
    tensor_count = lax.axis_size("tensor")
    dp_count = lax.axis_size("dp")
    row_count = hidden.shape[0]
    hidden_wide = hidden.astype(jnp.float32)
    row_scale = lax.rsqrt(jnp.mean(hidden_wide * hidden_wide, axis=1, keepdims=True) + epsilon)
    normed = hidden_wide * row_scale
    mlp_input = (normed * norm_gain).astype(jnp.bfloat16)
    gate_cols, up_cols, product_cols, joined_cols = (
        lax.all_to_all(gate_act, "tensor", split_axis=1, concat_axis=0, tiled=True),
        lax.all_to_all(up_act, "tensor", split_axis=1, concat_axis=0, tiled=True),
        lax.all_to_all(product_grad, "tensor", split_axis=1, concat_axis=0, tiled=True),
        lax.all_to_all(joined_in, "tensor", split_axis=1, concat_axis=0, tiled=True),
    )
    gate_grad, up_grad = swiglu_back(gate_cols, up_cols, product_cols)
    gate_all, up_all, joined_all = (
        lax.all_gather(gate_grad, "dp", axis=0, tiled=True),
        lax.all_gather(up_grad, "dp", axis=0, tiled=True),
        lax.all_gather(joined_cols, "dp", axis=0, tiled=True),
    )
    input_all = spread_columns(mlp_input)
    gate_weight_grad = token_sum(gate_all, input_all)
    up_weight_grad = token_sum(up_all, input_all)
    partial_value = jnp.dot(gate_all, gate_weight, preferred_element_type=jnp.float32) + jnp.dot(
        up_all, up_weight, preferred_element_type=jnp.float32
    )
    partial_value = partial_value.reshape(dp_count, tensor_count, row_count, partial_value.shape[1])
    summed = lax.psum_scatter(partial_value, "tensor", scatter_dimension=1, tiled=True)
    summed = summed.reshape(dp_count, row_count, summed.shape[3])
    input_grad = lax.all_to_all(summed, "dp", split_axis=0, concat_axis=2, tiled=True).reshape(
        row_count, -1
    )
    lifted = input_grad * norm_gain
    inner_mean = jnp.mean(lifted * normed, axis=1, keepdims=True)
    hidden_grad = (
        resid_grad.astype(jnp.float32) + row_scale * (lifted - normed * inner_mean)
    ).astype(jnp.bfloat16)
    gain_grad = lax.psum(jnp.sum(input_grad * normed, axis=0), ("tensor", "dp"))
    grad_all = spread_columns(hidden_grad)
    join_weight_grad = token_sum(joined_all, grad_all)
    joined_total = lax.psum_scatter(
        lax.dot_general(
            grad_all, join_weight, (((1,), (1,)), ((), ())), preferred_element_type=jnp.float32
        ),
        "dp",
        scatter_dimension=0,
        tiled=True,
    )
    joined_grad = lax.all_to_all(
        joined_total.astype(jnp.bfloat16), "tensor", split_axis=0, concat_axis=1, tiled=True
    )
    return (joined_grad, gate_weight_grad, up_weight_grad, join_weight_grad, gain_grad)


def solution(mesh):
    in_specs = (
        P(("dp", "tensor"), None),
        P(("dp", "tensor"), None),
        P(("dp", "tensor"), None),
        P(("dp", "tensor"), None),
        P(("dp", "tensor"), None),
        P(("dp", "tensor"), None),
        P(),
        P("tensor", "dp"),
        P("tensor", "dp"),
        P("tensor", "dp"),
    )
    out_specs = (
        P(("dp", "tensor"), None),
        P("tensor", "dp"),
        P("tensor", "dp"),
        P("tensor", "dp"),
        P(),
    )
    return jax.shard_map(shards, mesh=mesh, in_specs=in_specs, out_specs=out_specs, check_vma=False)
```

profile of v0, /device:TPU:1, one launch (start us, length us, event | category | flops | bytes accessed | tf_op | source)
XLA Modules:
  0.0 826.4 jit_solution(5630265549092731015)
XLA Ops:
  7.2 35.9 %all_to_all.130 = bf16[4,32,896]{2,0,1:T(4,128)(2,1)S(1)} all-to-all(bf16[4,32,896]{2,0,1:T(4,128)(2,1)} %bitcast.52), channel_id=1, replica_groups=mesh['tensor'=32,'dp'=16] {'tensor'}, dimensions={1} | all-to-all | bytes 458752 | tf_op jit(solution)/shard_map/all_to_all | solution.py:54
  43.0 22.3 %all_to_all.131 = bf16[4,32,896]{2,0,1:T(4,128)(2,1)S(1)} all-to-all(bf16[4,32,896]{2,0,1:T(4,128)(2,1)} %bitcast.53), channel_id=1, replica_groups=mesh['tensor'=32,'dp'=16] {'tensor'}, dimensions={1} | all-to-all | bytes 458752 | tf_op jit(solution)/shard_map/all_to_all | solution.py:53
  65.3 5.0 all-to-all-start.2
  70.8 16.4 %all-to-all-done.2 = bf16[4,32,896]{2,0,1:T(4,128)(2,1)S(1)} async-done(((bf16[4,32,896]{2,0,1:T(4,128)(2,1)}), bf16[4,32,896]{2,0,1:T(4,128)(2,1)S(1)}, u32[]{:S(2)}, u32[]{:S(2)}) %all-to-all-start.2) | async-done | bytes 229408 | tf_op jit(solution)/shard_map/all_to_all | solution.py:52
  87.5 1.0 multiply_convert_fusion
  89.3 65.2 %all-gather.8.cloned.1.call-done = bf16[2048,896]{1,0:T(8,128)(2,1)} async-done(((bf16[128,896]{1,0:T(8,128)(2,1)}), bf16[2048,896]{1,0:T(8,128)(2,1)}) %all-gather.8.cloned.1.call-update) | async-done | bytes 3670032 | tf_op jit(solution)/shard_map/all_gather | solution.py:59
  154.4 3.3 fusion.14
  157.7 69.0 %all-gather.10.cloned.1.call-done = bf16[2048,896]{1,0:T(8,128)(2,1)} async-done(((bf16[128,896]{1,0:T(8,128)(2,1)}), bf16[2048,896]{1,0:T(8,128)(2,1)}) %all-gather.10.cloned.1.call-update) | async-done | bytes 3670032 | tf_op jit(solution)/shard_map/all_gather | solution.py:60
  226.7 4.7 convolution_add_fusion
  231.4 1.9 reshape.60
  233.4 2.6 copy.46
  236.2 114.0 %reduce-scatter.3.cloned.1.call-done = f32[16,1,4,256]{3,0,2,1:T(8,128)} async-done(((f32[16,32,4,256]{3,0,2,1:T(8,128)}), f32[16,1,4,256]{3,0,2,1:T(8,128)}) %reduce-scatter.3.cloned.1.call-update) | async-done | bytes 65552 | tf_op jit(solution)/shard_map/reduce_scatter | solution.py:70
  350.2 1.5 copy.47
  351.7 30.0 %all-to-all-start.3 = ((f32[16,4,256]{2,1,0:T(4,128)}), f32[16,4,256]{2,1,0:T(4,128)S(1)}, u32[]{:S(2)}, u32[]{:S(2)}) async-start(f32[16,4,256]{2,1,0:T(4,128)} %copy.47), calls=%async_computation.4 | async-start | bytes 131072 | tf_op jit(solution)/shard_map/all_to_all | solution.py:72
  381.8 7.3 all-to-all-done.3
  391.3 18.4 %all_to_all.132 = bf16[4,32,256]{2,0,1:T(4,128)(2,1)S(1)} all-to-all(bf16[4,32,256]{2,0,1:T(4,128)(2,1)S(1)} %bitcast.55), channel_id=1, replica_groups=mesh['tensor'=32,'dp'=16] {'tensor'}, dimensions={1} | all-to-all | bytes 131072 | tf_op jit(solution)/shard_map/all_to_all | solution.py:55
  410.4 78.1 %all-gather.14.cloned.1.call-done = bf16[32,4,4096]{2,1,0:T(4,128)(2,1)} async-done(((bf16[1,4,4096]{2,1,0:T(4,128)(2,1)}), bf16[32,4,4096]{2,1,0:T(4,128)(2,1)}) %all-gather.14.cloned.1.call-update) | async-done | bytes 1048592 | tf_op jit(solution)/shard_map/all_gather | solution.py:27
  488.5 1.8 all_to_all.106
  490.7 44.7 %all_to_all.133 = bf16[128,16,256]{2,0,1:T(8,128)(2,1)S(1)} all-to-all(bf16[128,16,256]{2,0,1:T(8,128)(2,1)S(1)} %copy.48), channel_id=1, replica_groups=mesh['tensor'=32,'dp'=16] {'dp'}, dimensions={1} | all-to-all | bytes 2097152 | tf_op jit(solution)/shard_map/all_to_all | solution.py:28
  535.4 1.9 fusion.15
  537.3 78.2 %all-gather.16.cloned.1.call-done = bf16[32,4,4096]{2,1,0:T(4,128)(2,1)} async-done(((bf16[1,4,4096]{2,1,0:T(4,128)(2,1)}), bf16[32,4,4096]{2,1,0:T(4,128)(2,1)}) %all-gather.16.cloned.1.call-update) | async-done | bytes 1048592 | tf_op jit(solution)/shard_map/all_gather | solution.py:27
  615.4 1.8 all_to_all.114
  617.2 1.3 copy.50
  618.5 28.7 %all-to-all-start.6 = ((bf16[128,16,256]{2,0,1:T(8,128)(2,1)}), bf16[128,16,256]{2,0,1:T(8,128)(2,1)S(1)}, u32[]{:S(2)}, u32[]{:S(2)}) async-start(bf16[128,16,256]{2,0,1:T(8,128)(2,1)} %copy.50), calls=%async_computation.8 | async-start | bytes 2097152 | tf_op jit(solution)/shard_map/all_to_all | solution.py:28
  647.3 109.4 %psum.7 = f32[4096]{0:T(1024)} all-reduce(f32[4096]{0:T(1024)S(1)} %get-tuple-element.30), channel_id=1, replica_groups=mesh['tensor'=32,'dp'=16] {'tensor','dp'}, use_global_device_ids=true, to_apply=%region_5.0 | all-reduce | flops 4096 | bytes 32768 | tf_op jit(solution)/shard_map/psum | solution.py:80
  756.7 1.7 convolution_bitcast_fusion
  759.2 4.2 fusion.16
  763.4 28.1 %reduce-scatter.5.cloned.1.call-done = f32[128,256]{1,0:T(8,128)} async-done(((f32[2048,256]{1,0:T(8,128)}), f32[128,256]{1,0:T(8,128)}) %reduce-scatter.5.cloned.1.call-update) | async-done | bytes 131088 | tf_op jit(solution)/shard_map/reduce_scatter | solution.py:83
  791.4 0.9 convert_element_type.62
  793.0 12.7 %all-to-all-start.5 = ((bf16[32,4,256]{2,1,0:T(4,128)(2,1)}), bf16[32,4,256]{2,1,0:T(4,128)(2,1)S(1)}, u32[]{:S(2)}, u32[]{:S(2)}) async-start(bf16[32,4,256]{2,1,0:T(4,128)(2,1)} %all_to_all.110), calls=%async_computation.7 | async-start | bytes 131072 | tf_op jit(solution)/shard_map/all_to_all | solution.py:91
  805.7 4.1 fusion.17
  809.8 9.1 %all-to-all-done.5 = bf16[32,4,256]{2,1,0:T(4,128)(2,1)S(1)} async-done(((bf16[32,4,256]{2,1,0:T(4,128)(2,1)}), bf16[32,4,256]{2,1,0:T(4,128)(2,1)S(1)}, u32[]{:S(2)}, u32[]{:S(2)}) %all-to-all-start.5) | async-done | bytes 65568 | tf_op jit(solution)/shard_map/all_to_all | solution.py:91
  (46 shorter events, 7.0 us)
Async XLA Ops:
  7.2 147.3 %copy-start = (bf16[896,256]{1,0:T(8,128)(2,1)S(1)}, bf16[896,256]{1,0:T(8,128)(2,1)}, u32[]{:S(2)}) copy-start(bf16[896,256]{1,0:T(8,128)(2,1)} %param.17) | copy-start | bytes 1376260
  65.3 21.9 %all-to-all-start.2 = ((bf16[4,32,896]{2,0,1:T(4,128)(2,1)}), bf16[4,32,896]{2,0,1:T(4,128)(2,1)S(1)}, u32[]{:S(2)}, u32[]{:S(2)}) async-start(bf16[4,32,896]{2,0,1:T(4,128)(2,1)} %bitcast.54), calls=%async_computation.2 | async-start | bytes 458752 | tf_op jit(solution)/shard_map/all_to_all | solution.py:52
  70.3 84.1 %all-gather.8.cloned.1.call-start = ((), (), s32[]{:S(2)}) async-start(), calls=%async_computation.10 | async-start | bytes 3899392 | tf_op jit(solution)/shard_map/all_gather | solution.py:59
  88.5 138.3 %all-gather.10.cloned.1.call-start = ((), (), s32[]{:S(2)}) async-start(), calls=%async_computation.11 | async-start | bytes 3899392 | tf_op jit(solution)/shard_map/all_gather | solution.py:60
  89.2 137.5 %copy-start.1 = (bf16[896,256]{1,0:T(8,128)(2,1)S(1)}, bf16[896,256]{1,0:T(8,128)(2,1)}, u32[]{:S(2)}) copy-start(bf16[896,256]{1,0:T(8,128)(2,1)} %param.18) | copy-start | bytes 1376260
  89.2 261.0 %reduce-scatter.3.cloned.1.call-start = ((), (), s32[]{:S(2)}) async-start(), calls=%async_computation.12 | async-start | bytes 2162688 | tf_op jit(solution)/shard_map/reduce_scatter | solution.py:70
  233.3 2.7 copy-start.2
  233.3 155.8 %copy-start.5 = (f32[4096]{0:T(1024)S(1)}, f32[4096]{0:T(1024)}, u32[]{:S(2)}) copy-start(f32[4096]{0:T(1024)} %param.16) | copy-start | bytes 49156
  233.3 156.6 %copy-start.6 = (bf16[4,4096]{1,0:T(4,128)(2,1)S(1)}, bf16[4,4096]{1,0:T(4,128)(2,1)}, u32[]{:S(2)}) copy-start(bf16[4,4096]{1,0:T(4,128)(2,1)} %param.15) | copy-start | bytes 98308
  233.3 158.0 %copy-start.4 = (bf16[4,8192]{1,0:T(4,128)(2,1)S(1)}, bf16[4,8192]{1,0:T(4,128)(2,1)}, u32[]{:S(2)}) copy-start(bf16[4,8192]{1,0:T(4,128)(2,1)} %param.11) | copy-start | bytes 196612
  236.0 299.3 %copy-start.3 = (bf16[256,256]{1,0:T(8,128)(2,1)S(1)}, bf16[256,256]{1,0:T(8,128)(2,1)}, u32[]{:S(2)}) copy-start(bf16[256,256]{1,0:T(8,128)(2,1)} %param.19) | copy-start | bytes 393220
  351.7 37.4 %all-to-all-start.3 = ((f32[16,4,256]{2,1,0:T(4,128)}), f32[16,4,256]{2,1,0:T(4,128)S(1)}, u32[]{:S(2)}, u32[]{:S(2)}) async-start(f32[16,4,256]{2,1,0:T(4,128)} %copy.47), calls=%async_computation.4 | async-start | bytes 131072 | tf_op jit(solution)/shard_map/all_to_all | solution.py:72
  381.7 106.8 %all-gather.14.cloned.1.call-start = ((), (), s32[]{:S(2)}) async-start(), calls=%async_computation.15 | async-start | bytes 1081344 | tf_op jit(solution)/shard_map/all_gather | solution.py:27
  390.7 224.8 %all-gather.16.cloned.1.call-start = ((), (), s32[]{:S(2)}) async-start(), calls=%async_computation.16 | async-start | bytes 1081344 | tf_op jit(solution)/shard_map/all_gather | solution.py:27
  391.3 365.4 %all-gather.12.cloned.1.call-start = ((), (), s32[]{:S(2)}) async-start(), calls=%async_computation.14 | async-start | bytes 1114112 | tf_op jit(solution)/shard_map/all_gather | solution.py:61
  410.4 381.1 %reduce-scatter.5.cloned.1.call-start = ((), (), s32[]{:S(2)}) async-start(), calls=%async_computation.13 | async-start | bytes 2228224 | tf_op jit(solution)/shard_map/reduce_scatter | solution.py:83
  618.5 140.7 %all-to-all-start.6 = ((bf16[128,16,256]{2,0,1:T(8,128)(2,1)}), bf16[128,16,256]{2,0,1:T(8,128)(2,1)S(1)}, u32[]{:S(2)}, u32[]{:S(2)}) async-start(bf16[128,16,256]{2,0,1:T(8,128)(2,1)} %copy.50), calls=%async_computation.8 | async-start | bytes 2097152 | tf_op jit(solution)/shard_map/all_to_all | solution.py:28
  793.0 25.9 %all-to-all-start.5 = ((bf16[32,4,256]{2,1,0:T(4,128)(2,1)}), bf16[32,4,256]{2,1,0:T(4,128)(2,1)S(1)}, u32[]{:S(2)}, u32[]{:S(2)}) async-start(bf16[32,4,256]{2,1,0:T(4,128)(2,1)} %all_to_all.110), calls=%async_computation.7 | async-start | bytes 131072 | tf_op jit(solution)/shard_map/all_to_all | solution.py:91
Sparse Core Ops, SparseCore 0:
  88.6 65.7 all-gather.7
  158.3 68.4 all-gather.9
  236.1 114.0 reduce-scatter.2
  390.8 97.7 all-gather.13
  491.2 124.1 all-gather.15
  619.6 75.5 all-gather.11
  700.8 90.5 reduce-scatter.4
where the time goes:
time: 829 us; the launch traced here: 826 us
  waiting for transfers between devices  467 us (56%)
  blocking collectives  231 us (28%)
  starting transfers between devices  76.7 us (9%)
  matrix products  19.8 us (2%)
  local copies, waits for them, and re-layouts  14.5 us (2%)
  between operations  14.3 us (2%)
    all_gather x2, waiting for transfers between devices, spread_columns(): group_block = lax.all_gather(rows_in, 'tensor', axis=0, tiled=True)  156 us
    reduce_scatter x1, waiting for transfers between devices, shards(): lax.psum_scatter(partial_value, 'tensor', scatter_dimension=1, tiled=True)  114 us
    psum x1, blocking collectives, shards(): gain_grad = lax.psum(jnp.sum(input_grad * normed, axis=0), ('tensor', 'dp'))  109 us
    all_gather x1, waiting for transfers between devices, shards(): lax.all_gather(up_grad, 'dp', axis=0, tiled=True)  69 us
    all_gather x1, waiting for transfers between devices, shards(): lax.all_gather(gate_grad, 'dp', axis=0, tiled=True)  65.2 us
    all_to_all x1, blocking collectives, spread_columns(): lax.all_to_all(group_block, 'dp', split_axis=1, concat_axis=0, tiled=True)  44.7 us
    all_to_all x1, blocking collectives, shards(): lax.all_to_all(product_grad, 'tensor', split_axis=1, concat_axis=0, tiled...  35.9 us
    all_to_all x1, starting transfers between devices, shards(): lax.all_to_all(summed, 'dp', split_axis=0, concat_axis=2, tiled=True)  30 us
  transfers between devices with their start and end apart: 11, of which 9 were waited for; matrix products, arithmetic and copies ran while one was open for 2% of the time, Pallas kernels for 0%

commit v1 on v0

v1 whole, which is shorter than its diff:
```python
import jax
import jax.numpy as jnp
from jax import lax
from jax.sharding import Mesh
from jax.sharding import PartitionSpec as P

epsilon = 1e-05
narrow = jnp.bfloat16
wide = jnp.float32


def swiglu_back(gate_act, up_act, product_grad):
    gate_wide = gate_act.astype(wide)
    logistic = jax.nn.sigmoid(gate_wide)
    product_wide = product_grad.astype(wide)
    gate_grad = (
        product_wide * up_act.astype(wide) * logistic * (1.0 + gate_wide * (1.0 - logistic))
    )
    up_grad = product_wide * gate_wide * logistic
    return (gate_grad.astype(narrow), up_grad.astype(narrow))


def token_sum(left, right):
    return lax.dot_general(left, right, (((0,), (0,)), ((), ())), preferred_element_type=wide)


def exchange(blocks, axes):
    return lax.all_to_all(blocks, axes, split_axis=0, concat_axis=0, tiled=True)


def swap_cores(value):
    return lax.ppermute(value, "core", [(0, 1), (1, 0)])


def split_three(value):
    high = value.astype(narrow)
    rest = value - high.astype(wide)
    middle = rest.astype(narrow)
    low = (rest - middle.astype(wide)).astype(narrow)
    return (high, middle, low)


def shards(
    hidden,
    joined_in,
    gate_act,
    up_act,
    product_grad,
    resid_grad,
    norm_gain,
    gate_weight,
    up_weight,
    join_weight,
):
    tensor_axes = ("y_lo", "z")
    dp_axes = ("x", "y_hi", "core")
    z_count = lax.axis_size("z")
    tensor_count = lax.axis_size("y_lo") * z_count
    core_count = lax.axis_size("core")
    dp_count = lax.axis_size("x") * lax.axis_size("y_hi") * core_count
    row_count, width = hidden.shape
    units, features = gate_weight.shape
    inputs = join_weight.shape[0]
    half_inputs = inputs // 2
    group_rows = tensor_count * row_count
    block_rows = dp_count * row_count
    tokens = dp_count * group_rows
    on_first = lax.axis_index("core") == 0

    weight_kept = jnp.where(on_first, gate_weight, up_weight)
    weight_other = swap_cores(jnp.where(on_first, up_weight, gate_weight))
    weight_pair = jnp.concatenate(
        [
            jnp.where(on_first, weight_kept, weight_other),
            jnp.where(on_first, weight_other, weight_kept),
        ],
        axis=1,
    )

    hidden_wide = hidden.astype(wide)
    row_scale = lax.rsqrt(jnp.mean(hidden_wide * hidden_wide, axis=1, keepdims=True) + epsilon)
    scale_parts = jnp.concatenate(split_three(row_scale), axis=1)
    scale_parts = jnp.pad(scale_parts, ((0, 0), (0, features - scale_parts.shape[1])))
    norm_rows = jnp.stack(
        [
            hidden.reshape(row_count, dp_count, features),
            resid_grad.reshape(row_count, dp_count, features),
            jnp.broadcast_to(scale_parts[:, None, :], (row_count, dp_count, features)),
        ]
    )
    norm_block = exchange(norm_rows.transpose(2, 0, 1, 3), dp_axes)
    hidden_block = norm_block[:, 0].reshape(block_rows, features).astype(wide)
    resid_block = norm_block[:, 1].reshape(block_rows, features).astype(wide)
    scale_block = norm_block[:, 2, :, :3].astype(wide).reshape(block_rows, 3)
    scale_block = (scale_block[:, 0:1] + scale_block[:, 1:2]) + scale_block[:, 2:3]
    gain_block = lax.dynamic_slice_in_dim(
        norm_gain, lax.axis_index(dp_axes) * features, features, 0
    )
    normed = hidden_block * scale_block
    mlp_block = (normed * gain_block).astype(narrow)
    mlp_all = lax.all_gather(mlp_block, tensor_axes, axis=0, tiled=True)
    mlp_all = (
        mlp_all.reshape(tensor_count, dp_count, row_count, features)
        .transpose(1, 0, 2, 3)
        .reshape(tokens, features)
    )
    mlp_other = swap_cores(mlp_all)
    mlp_pair = jnp.concatenate(
        [jnp.where(on_first, mlp_all, mlp_other), jnp.where(on_first, mlp_other, mlp_all)],
        axis=1,
    )

    gate_grad, up_grad = swiglu_back(gate_act, up_act, product_grad)
    joined_rows = joined_in.reshape(row_count, tensor_count, 2, half_inputs)
    half_width = units + half_inputs
    gate_rows = jnp.concatenate(
        [gate_grad.reshape(row_count, tensor_count, units), joined_rows[:, :, 0]], axis=2
    )
    up_rows = jnp.concatenate(
        [up_grad.reshape(row_count, tensor_count, units), joined_rows[:, :, 1]], axis=2
    )
    unit_rows = jnp.stack([gate_rows, up_rows]).transpose(2, 0, 1, 3)
    unit_group = exchange(
        unit_rows.reshape(tensor_count, 2 * row_count, half_width), tensor_axes
    )
    unit_halves = (
        unit_group.reshape(tensor_count, 2, row_count, half_width)
        .transpose(1, 0, 2, 3)
        .reshape(2, group_rows, half_width)
    )
    unit_halves = jnp.broadcast_to(
        unit_halves[None], (dp_count // core_count, core_count, group_rows, half_width)
    ).reshape(dp_count, group_rows, half_width)
    half_all = exchange(unit_halves, dp_axes).reshape(tokens, half_width)
    grad_half = half_all[:, :units]
    joined_half = half_all[:, units:]

    partial_value = jnp.dot(grad_half, weight_pair, preferred_element_type=wide).astype(narrow)
    partial_value = partial_value.reshape(
        dp_count, 2, z_count, row_count, core_count, features
    ).transpose(1, 4, 2, 0, 3, 5)
    near = exchange(
        partial_value.reshape(2 * core_count, z_count * block_rows, features), ("y_lo", "core")
    )
    near_sum = jnp.sum(near.astype(wide), axis=0).astype(narrow)
    far = exchange(near_sum.reshape(z_count, block_rows, features), "z")
    input_grad = jnp.sum(far.astype(wide), axis=0)

    lifted = input_grad * gain_block
    mean_part = jnp.sum(lifted * normed, axis=1)
    mean_all = exchange(
        jnp.broadcast_to(mean_part[None, None], (dp_count, 1, block_rows)), dp_axes
    )
    inner_mean = (jnp.sum(mean_all, axis=(0, 1)) / width)[:, None]
    hidden_grad = (resid_block + scale_block * (lifted - normed * inner_mean)).astype(narrow)
    gain_part = jnp.sum(input_grad * normed, axis=0, keepdims=True)
    gain_parts = lax.all_gather(gain_part, tensor_axes, axis=0, tiled=True)
    gain_sum = jnp.sum(gain_parts, axis=0, keepdims=True)

    grad_far = exchange(
        jnp.broadcast_to(hidden_grad[None], (z_count, block_rows, features)), "z"
    ).reshape(1, z_count * block_rows, features)
    grad_all = exchange(
        jnp.broadcast_to(grad_far, (2, z_count * block_rows, features)), "y_lo"
    )
    grad_all = (
        grad_all.reshape(tensor_count, dp_count, row_count, features)
        .transpose(1, 0, 2, 3)
        .reshape(tokens, features)
    )
    joined_part = lax.dot_general(
        grad_all, join_weight, (((1,), (1,)), ((), ())), preferred_element_type=wide
    ).astype(narrow)
    gain_rows = jnp.concatenate(
        list(split_three(gain_sum)) + [jnp.zeros((13, features), narrow)], axis=0
    )
    joined_part = jnp.concatenate(
        [
            joined_part.reshape(dp_count, group_rows, inputs),
            jnp.broadcast_to(gain_rows[None], (dp_count, 16, features)),
        ],
        axis=1,
    )
    joined_blocks = exchange(joined_part, dp_axes)
    gain_grad = joined_blocks[:, group_rows : group_rows + 3].astype(wide)
    gain_grad = ((gain_grad[:, 0] + gain_grad[:, 1]) + gain_grad[:, 2]).reshape(width)
    joined_total = jnp.sum(joined_blocks[:, :group_rows].astype(wide), axis=0).astype(narrow)
    joined_grad = exchange(joined_total.reshape(tensor_count, row_count, inputs), tensor_axes)
    joined_grad = joined_grad.transpose(1, 0, 2).reshape(row_count, tensor_count * inputs)

    unit_weight_grad = token_sum(grad_half, mlp_pair)
    grad_first = unit_weight_grad[:, :features]
    grad_second = unit_weight_grad[:, features:]
    own_grad = jnp.where(on_first, grad_first, grad_second)
    other_grad = swap_cores(jnp.where(on_first, grad_second, grad_first))
    gate_weight_grad = jnp.where(on_first, own_grad, other_grad)
    up_weight_grad = jnp.where(on_first, other_grad, own_grad)
    joined_other = swap_cores(joined_half)
    joined_all = jnp.concatenate(
        [
            jnp.where(on_first, joined_half, joined_other),
            jnp.where(on_first, joined_other, joined_half),
        ],
        axis=1,
    )
    join_weight_grad = token_sum(joined_all, grad_all)
    return (joined_grad, gate_weight_grad, up_weight_grad, join_weight_grad, gain_grad)


def solution(mesh):
    tensor_count, dp_count = mesh.shape["tensor"], mesh.shape["dp"]
    fine = Mesh(
        mesh.devices.reshape(2, tensor_count // 2, dp_count // 4, 2, 2),
        ("y_lo", "z", "x", "y_hi", "core"),
    )
    tensor_axes = ("y_lo", "z")
    dp_axes = ("x", "y_hi", "core")
    rows = P(dp_axes + tensor_axes, None)
    blocks = P(tensor_axes, dp_axes)
    in_specs = (rows, rows, rows, rows, rows, rows, P(), blocks, blocks, blocks)
    out_specs = (rows, blocks, blocks, blocks, P())
    return jax.shard_map(shards, mesh=fine, in_specs=in_specs, out_specs=out_specs, check_vma=False)
```

time: 829 us -> 496 us (0.60)
  waiting for transfers between devices: 467 us -> 230 us
  blocking collectives: 231 us -> 96.1 us
  starting transfers between devices: 76.7 us -> 101 us
  local copies, waits for them, and re-layouts: 14.5 us -> 26.8 us
  other arithmetic: 3.69 us -> 14.5 us
  matrix products: 19.8 us -> 11.5 us
    all_gather x5 -> x1, waiting for transfers between devices: 290 us -> 103 us  [shards(): mlp_all = lax.all_gather(mlp_block, tensor_axes, axis=0, tiled=True)]
    reduce_scatter x2 -> x0, waiting for transfers between devices: 142 us -> none  [the longest x1 114 us: shards(): lax.psum_scatter(partial_value, 'tensor', scatter_dimension=1, tiled=True)]
    psum x1 -> x0, blocking collectives: 109 us -> none  [shards(): gain_grad = lax.psum(jnp.sum(input_grad * normed, axis=0), ('tensor', 'dp'))]
    all_to_all x4 -> x9, waiting for transfers between devices: 32.9 us -> 126 us  [exchange(): return lax.all_to_all(blocks, axes, split_axis=0, concat_axis=0, tiled=True)]
    all_to_all x4 -> x1, blocking collectives: 121 us -> 47.5 us  [exchange(): return lax.all_to_all(blocks, axes, split_axis=0, concat_axis=0, tiled=True)]
    all_gather x0 -> x1, blocking collectives: none -> 48.6 us  [shards(): gain_parts = lax.all_gather(gain_part, tensor_axes, axis=0, tiled=True)]
    ppermute x0 -> x4, starting transfers between devices: none -> 26.5 us  [swap_cores(): return lax.ppermute(value, 'core', [(0, 1), (1, 0)])]
    reshape x3 -> x11, local copies, waits for them, and re-layouts: 6 us -> 14.6 us  [the longest x2 5.1 us: shards(): partial_value.reshape(dp_count, 2, z_count, row_count, core_count, features)]
  transfers between devices with their start and end apart: 11 -> 14, of which waited for: 9 -> 9; matrix products, arithmetic and copies ran while one was open for 2% -> 5% of each run, Pallas kernels for 0% -> 0%
where the time goes in v1:
time: 496 us; the launch traced here: 495 us
  waiting for transfers between devices  230 us (46%)
  starting transfers between devices  101 us (20%)
  blocking collectives  96.1 us (19%)
  local copies, waits for them, and re-layouts  26.8 us (5%)
  other arithmetic  14.5 us (3%)
  between operations  14.5 us (3%)
  matrix products  11.5 us (2%)
    all_to_all x9, waiting for transfers between devices, exchange(): return lax.all_to_all(blocks, axes, split_axis=0, concat_axis=0, tiled=True)  126 us
    all_gather x1, waiting for transfers between devices, shards(): mlp_all = lax.all_gather(mlp_block, tensor_axes, axis=0, tiled=True)  103 us
    all_to_all x9, starting transfers between devices, exchange(): return lax.all_to_all(blocks, axes, split_axis=0, concat_axis=0, tiled=True)  74.6 us
    all_gather x1, blocking collectives, shards(): gain_parts = lax.all_gather(gain_part, tensor_axes, axis=0, tiled=True)  48.6 us
    all_to_all x1, blocking collectives, exchange(): return lax.all_to_all(blocks, axes, split_axis=0, concat_axis=0, tiled=True)  47.5 us
    ppermute x4, starting transfers between devices, swap_cores(): return lax.ppermute(value, 'core', [(0, 1), (1, 0)])  26.5 us
  transfers between devices with their start and end apart: 14, of which 9 were waited for; matrix products, arithmetic and copies ran while one was open for 5% of the time, Pallas kernels for 0%

profile of v1, /device:TPU:1, one launch (start us, length us, event | category | flops | bytes accessed | tf_op | source)
XLA Modules:
  0.0 494.9 jit_solution(15079677616514319674)
XLA Ops:
  8.3 1.7 fusion.19
  10.8 47.5 %all_to_all.50 = bf16[32,8,1024]{2,1,0:T(8,128)(2,1)S(1)} all-to-all(bf16[32,8,1024]{2,1,0:T(8,128)(2,1)S(1)} %reshape.290), channel_id=1, replica_groups=mesh['y_lo'=2,'z'=16,'x'=4,'y_hi'=2,'core'=2] {'y_lo','z'}, dimensions={0} | all-to-all | bytes 1048576 | tf_op jit(solution)/shard_map/all_to_all | solution.py:28
  59.2 2.5 broadcast_in_dim.21
  61.8 8.3 %all-to-all-start.2 = ((bf16[16,128,1024]{2,1,0:T(8,128)(2,1)}), bf16[16,128,1024]{2,1,0:T(8,128)(2,1)}, u32[]{:S(2)}, u32[]{:S(2)}) async-start(bf16[16,128,1024]{2,1,0:T(8,128)(2,1)} %bitcast.71), calls=%async_computation.2 | async-start | bytes 8388608 | tf_op jit(solution)/shard_map/all_to_all | solution.py:28
  70.1 2.1 collective-permute-start
  73.9 48.9 %all-to-all-done.2 = bf16[16,128,1024]{2,1,0:T(8,128)(2,1)} async-done(((bf16[16,128,1024]{2,1,0:T(8,128)(2,1)}), bf16[16,128,1024]{2,1,0:T(8,128)(2,1)}, u32[]{:S(2)}, u32[]{:S(2)}) %all-to-all-start.2) | async-done | bytes 4194336 | tf_op jit(solution)/shard_map/all_to_all | solution.py:28
  122.8 5.7 %fusion.4 = bf16[2048,512]{1,0:T(8,128)(2,1)} fusion(bf16[2048,1024]{1,0:T(8,128)(2,1)} %bitcast.16, bf16[896,256]{1,0:T(8,128)(2,1)S(1)} %get-tuple-element.16, bf16[896,256]{1,0:T(8,128)(2,1)S(1)} %get-tuple-element.15), kind=kOutput, calls=%fused_computation.4 | convolution fusion | flops 1881931776 | bytes 6684672 | tf_op jit(solution)/shard_map/dot_general | solution.py:138
  128.5 2.5 reshape.294
  131.1 2.6 copy.100
  133.6 4.0 reshape.295
  137.6 3.7 all-to-all-start.3
  142.4 23.6 %all-to-all-done.3 = bf16[4,1024,256]{2,1,0:T(8,128)(2,1)S(1)} async-done(((bf16[4,1024,256]{2,1,0:T(8,128)(2,1)}), bf16[4,1024,256]{2,1,0:T(8,128)(2,1)S(1)}, u32[]{:S(2)}, u32[]{:S(2)}) %all-to-all-start.3) | async-done | bytes 2097184 | tf_op jit(solution)/shard_map/all_to_all | solution.py:28
  166.0 14.0 %all-to-all-start = ((bf16[16,3,4,256]{3,2,1,0:T(4,128)(2,1)}), bf16[16,3,4,256]{3,2,1,0:T(4,128)(2,1)S(1)}, u32[]{:S(2)}, u32[]{:S(2)}) async-start(bf16[16,3,4,256]{3,2,1,0:T(4,128)(2,1)} %maximum_bitcast_fusion.3), calls=%async_computation | async-start | bytes 196608 | tf_op jit(solution)/shard_map/all_to_all | solution.py:28
  181.2 6.2 %all-to-all-done = bf16[16,3,4,256]{3,2,1,0:T(4,128)(2,1)S(1)} async-done(((bf16[16,3,4,256]{3,2,1,0:T(4,128)(2,1)}), bf16[16,3,4,256]{3,2,1,0:T(4,128)(2,1)S(1)}, u32[]{:S(2)}, u32[]{:S(2)}) %all-to-all-start) | async-done | bytes 98336 | tf_op jit(solution)/shard_map/all_to_all | solution.py:28
  187.4 4.6 all-to-all-start.4
  194.4 20.5 %all-to-all-done.4 = bf16[16,64,256]{2,1,0:T(8,128)(2,1)S(1)} async-done(((bf16[16,64,256]{2,1,0:T(8,128)(2,1)}), bf16[16,64,256]{2,1,0:T(8,128)(2,1)S(1)}, u32[]{:S(2)}, u32[]{:S(2)}) %all-to-all-start.4) | async-done | bytes 524320 | tf_op jit(solution)/shard_map/all_to_all | solution.py:28
  215.9 10.4 %all-to-all-start.5 = ((f32[16,1,64]{2,1,0:T(1,128)}), f32[16,1,64]{2,1,0:T(1,128)S(1)}, u32[]{:S(2)}, u32[]{:S(2)}) async-start(f32[16,1,64]{2,1,0:T(1,128)} %broadcast_in_dim.23), calls=%async_computation.5 | async-start | bytes 16384 | tf_op jit(solution)/shard_map/all_to_all | solution.py:28
  226.4 6.8 %all-to-all-done.5 = f32[16,1,64]{2,1,0:T(1,128)S(1)} async-done(((f32[16,1,64]{2,1,0:T(1,128)}), f32[16,1,64]{2,1,0:T(1,128)S(1)}, u32[]{:S(2)}, u32[]{:S(2)}) %all-to-all-start.5) | async-done | bytes 4128 | tf_op jit(solution)/shard_map/all_to_all | solution.py:28
  234.8 6.1 %all-to-all-start.6 = ((bf16[16,64,256]{2,1,0:T(8,128)(2,1)}), bf16[16,64,256]{2,1,0:T(8,128)(2,1)S(1)}, u32[]{:S(2)}, u32[]{:S(2)}) async-start(bf16[16,64,256]{2,1,0:T(8,128)(2,1)} %broadcast_in_dim.24), calls=%async_computation.6 | async-start | bytes 1048576 | tf_op jit(solution)/shard_map/all_to_all | solution.py:28
  240.9 102.7 %all-gather.4.cloned.1.call-done = bf16[2048,256]{1,0:T(8,128)(2,1)} async-done(((bf16[64,256]{1,0:T(8,128)(2,1)}), bf16[2048,256]{1,0:T(8,128)(2,1)}) %all-gather.4.cloned.1.call-update) | async-done | bytes 1048592 | tf_op jit(solution)/shard_map/all_gather | solution.py:101
  345.8 20.5 %collective-permute-start.1 = (bf16[2048,256]{1,0:T(8,128)(2,1)S(1)}, bf16[2048,256]{1,0:T(8,128)(2,1)}, u32[]{:S(2)}, u32[]{:S(2)}) collective-permute-start(bf16[2048,256]{1,0:T(8,128)(2,1)S(1)} %reshape.303), channel_id=1, source_target_pairs={{0,1},{1,0},{2,3},{3,2},{4,5},{5,4},{6,7},{7,6},{8,9},{9,8},{10,11... | collective-permute-start | bytes 3145736 | tf_op jit(solution)/shard_map/ppermute | solution.py:32
  367.3 3.6 all-to-all-start.7
  371.0 1.9 slice.77
  372.8 1.9 collective-permute-start.3
  374.8 48.6 %all-gather.1 = f32[32,1,256]{2,1,0:T(1,128)S(1)} all-gather(f32[1,1,256]{2,1,0:T(1,128)S(1)} %bitcast.88), channel_id=2, replica_groups=mesh['y_lo'=2,'z'=16,'x'=4,'y_hi'=2,'core'=2] {'y_lo','z'}, dimensions={0}, use_global_device_ids=true | all-gather | bytes 33792 | tf_op jit(solution)/shard_map/all_gather | solution.py:157
  428.3 20.1 %all-to-all-start.8 = ((bf16[16,144,256]{2,1,0:T(8,128)(2,1)}), bf16[16,144,256]{2,1,0:T(8,128)(2,1)S(1)}, u32[]{:S(2)}, u32[]{:S(2)}) async-start(bf16[16,144,256]{2,1,0:T(8,128)(2,1)} %pad_maximum_fusion), calls=%async_computation.8 | async-start | bytes 2359296 | tf_op jit(solution)/shard_map/all_to_all | solution.py:28
  449.8 4.1 fusion
  455.0 2.0 collective-permute-start.2
  459.5 7.6 %all-to-all-done.8 = bf16[16,144,256]{2,1,0:T(8,128)(2,1)S(1)} async-done(((bf16[16,144,256]{2,1,0:T(8,128)(2,1)}), bf16[16,144,256]{2,1,0:T(8,128)(2,1)S(1)}, u32[]{:S(2)}, u32[]{:S(2)}) %all-to-all-start.8) | async-done | bytes 1179680 | tf_op jit(solution)/shard_map/all_to_all | solution.py:28
  467.8 3.9 all-to-all-start.9
  472.3 12.5 %all-to-all-done.9 = bf16[32,4,256]{2,1,0:T(4,128)(2,1)S(1)} async-done(((bf16[32,4,256]{2,1,0:T(4,128)(2,1)}), bf16[32,4,256]{2,1,0:T(4,128)(2,1)S(1)}, u32[]{:S(2)}, u32[]{:S(2)}) %all-to-all-start.9) | async-done | bytes 65568 | tf_op jit(solution)/shard_map/all_to_all | solution.py:28
  484.9 2.6 broadcast_select_fusion.4
  (88 shorter events, 26.8 us)
Async XLA Ops:
  7.2 419.5 %copy-start = (bf16[256,256]{1,0:T(8,128)(2,1)S(1)}, bf16[256,256]{1,0:T(8,128)(2,1)}, u32[]{:S(2)}) copy-start(bf16[256,256]{1,0:T(8,128)(2,1)} %param.19) | copy-start | bytes 393220
  61.8 8.3 %copy-start.3 = (bf16[896,256]{1,0:T(8,128)(2,1)S(1)}, bf16[896,256]{1,0:T(8,128)(2,1)}, u32[]{:S(2)}) copy-start(bf16[896,256]{1,0:T(8,128)(2,1)} %param.18) | copy-start | bytes 1376260
  61.8 8.3 %copy-start.4 = (bf16[896,256]{1,0:T(8,128)(2,1)S(1)}, bf16[896,256]{1,0:T(8,128)(2,1)}, u32[]{:S(2)}) copy-start(bf16[896,256]{1,0:T(8,128)(2,1)} %param.17) | copy-start | bytes 1376260
  61.8 61.0 %all-to-all-start.2 = ((bf16[16,128,1024]{2,1,0:T(8,128)(2,1)}), bf16[16,128,1024]{2,1,0:T(8,128)(2,1)}, u32[]{:S(2)}, u32[]{:S(2)}) async-start(bf16[16,128,1024]{2,1,0:T(8,128)(2,1)} %bitcast.71), calls=%async_computation.2 | async-start | bytes 8388608 | tf_op jit(solution)/shard_map/all_to_all | solution.py:28
  70.1 3.7 collective-permute-start
  137.6 3.7 copy-start.5
  137.6 4.1 copy-start.6
  137.6 28.4 %all-to-all-start.3 = ((bf16[4,1024,256]{2,1,0:T(8,128)(2,1)}), bf16[4,1024,256]{2,1,0:T(8,128)(2,1)S(1)}, u32[]{:S(2)}, u32[]{:S(2)}) async-start(bf16[4,1024,256]{2,1,0:T(8,128)(2,1)} %reshape.295), calls=%async_computation.3 | async-start | bytes 4194304 | tf_op jit(solution)/shard_map/all_to_all | solution.py:28
  166.0 21.4 %all-to-all-start = ((bf16[16,3,4,256]{3,2,1,0:T(4,128)(2,1)}), bf16[16,3,4,256]{3,2,1,0:T(4,128)(2,1)S(1)}, u32[]{:S(2)}, u32[]{:S(2)}) async-start(bf16[16,3,4,256]{3,2,1,0:T(4,128)(2,1)} %maximum_bitcast_fusion.3), calls=%async_computation | async-start | bytes 196608 | tf_op jit(solution)/shard_map/all_to_all | solution.py:28
  187.4 27.5 %all-to-all-start.4 = ((bf16[16,64,256]{2,1,0:T(8,128)(2,1)}), bf16[16,64,256]{2,1,0:T(8,128)(2,1)S(1)}, u32[]{:S(2)}, u32[]{:S(2)}) async-start(bf16[16,64,256]{2,1,0:T(8,128)(2,1)} %bitcast.18), calls=%async_computation.4 | async-start | bytes 1048576 | tf_op jit(solution)/shard_map/all_to_all | solution.py:28
  215.9 17.3 %all-to-all-start.5 = ((f32[16,1,64]{2,1,0:T(1,128)}), f32[16,1,64]{2,1,0:T(1,128)S(1)}, u32[]{:S(2)}, u32[]{:S(2)}) async-start(f32[16,1,64]{2,1,0:T(1,128)} %broadcast_in_dim.23), calls=%async_computation.5 | async-start | bytes 16384 | tf_op jit(solution)/shard_map/all_to_all | solution.py:28
  226.2 117.4 %all-gather.4.cloned.1.call-start = ((), (), s32[]{:S(2)}) async-start(), calls=%async_computation.10 | async-start | bytes 1081344 | tf_op jit(solution)/shard_map/all_gather | solution.py:101
  234.8 131.4 %all-to-all-start.6 = ((bf16[16,64,256]{2,1,0:T(8,128)(2,1)}), bf16[16,64,256]{2,1,0:T(8,128)(2,1)S(1)}, u32[]{:S(2)}, u32[]{:S(2)}) async-start(bf16[16,64,256]{2,1,0:T(8,128)(2,1)} %broadcast_in_dim.24), calls=%async_computation.6 | async-start | bytes 1048576 | tf_op jit(solution)/shard_map/all_to_all | solution.py:28
  345.8 102.7 %collective-permute-start.1 = (bf16[2048,256]{1,0:T(8,128)(2,1)S(1)}, bf16[2048,256]{1,0:T(8,128)(2,1)}, u32[]{:S(2)}, u32[]{:S(2)}) collective-permute-start(bf16[2048,256]{1,0:T(8,128)(2,1)S(1)} %reshape.303), channel_id=1, source_target_pairs={{0,1},{1,0},{2,3},{3,2},{4,5},{5,4},{6,7},{7,6},{8,9},{9,8},{10,11... | collective-permute-start | bytes 3145736 | tf_op jit(solution)/shard_map/ppermute | solution.py:32
  367.3 56.2 %all-to-all-start.7 = ((bf16[2,1024,256]{2,1,0:T(8,128)(2,1)}), bf16[2,1024,256]{2,1,0:T(8,128)(2,1)S(1)}, u32[]{:S(2)}, u32[]{:S(2)}) async-start(bf16[2,1024,256]{2,1,0:T(8,128)(2,1)} %broadcast_in_dim.52), calls=%async_computation.7 | async-start | bytes 2097152 | tf_op jit(solution)/shard_map/all_to_all | solution.py:28
  372.8 84.1 %collective-permute-start.3 = (bf16[2048,128]{1,0:T(8,128)(2,1)}, bf16[2048,128]{1,0:T(8,128)(2,1)}, u32[]{:S(2)}, u32[]{:S(2)}) collective-permute-start(bf16[2048,128]{1,0:T(8,128)(2,1)} %slice.77), channel_id=1, source_target_pairs={{0,1},{1,0},{2,3},{3,2},{4,5},{5,4},{6,7},{7,6},{8,9},{9,8},{10,11... | collective-permute-start | bytes 1572872 | tf_op jit(solution)/shard_map/ppermute | solution.py:32
  426.7 1.6 copy-start.1
  428.3 38.7 %all-to-all-start.8 = ((bf16[16,144,256]{2,1,0:T(8,128)(2,1)}), bf16[16,144,256]{2,1,0:T(8,128)(2,1)S(1)}, u32[]{:S(2)}, u32[]{:S(2)}) async-start(bf16[16,144,256]{2,1,0:T(8,128)(2,1)} %pad_maximum_fusion), calls=%async_computation.8 | async-start | bytes 2359296 | tf_op jit(solution)/shard_map/all_to_all | solution.py:28
  453.9 4.4 copy-start.2
  455.0 29.9 %collective-permute-start.2 = (f32[896,256]{1,0:T(8,128)}, f32[896,256]{1,0:T(8,128)}, u32[]{:S(2)}, u32[]{:S(2)}) collective-permute-start(f32[896,256]{1,0:T(8,128)} %slice_select_fusion), channel_id=1, source_target_pairs={{0,1},{1,0},{2,3},{3,2},{4,5},{5,4},{6,7},{7,6},{8,9},{9,8},{10,11... | collective-permute-start | bytes 2752520 | tf_op jit(solution)/shard_map/ppermute | solution.py:32
  467.8 17.1 %all-to-all-start.9 = ((bf16[32,4,256]{2,1,0:T(4,128)(2,1)}), bf16[32,4,256]{2,1,0:T(4,128)(2,1)S(1)}, u32[]{:S(2)}, u32[]{:S(2)}) async-start(bf16[32,4,256]{2,1,0:T(4,128)(2,1)} %reshape.300), calls=%async_computation.9 | async-start | bytes 131072 | tf_op jit(solution)/shard_map/all_to_all | solution.py:28
Sparse Core Ops, SparseCore 0:
  234.1 109.4 all-gather.3

commit v2 on v1

--- a/solution.py
+++ b/solution.py
@@ -30,6 +30,10 @@
 
 def swap_cores(value):
     return lax.ppermute(value, "core", [(0, 1), (1, 0)])
+
+
+def swap_near(value):
+    return lax.ppermute(value, "y_lo", [(0, 1), (1, 0)])
 
 
 def split_three(value):
@@ -69,13 +73,6 @@
 
     weight_kept = jnp.where(on_first, gate_weight, up_weight)
     weight_other = swap_cores(jnp.where(on_first, up_weight, gate_weight))
-    weight_pair = jnp.concatenate(
-        [
-            jnp.where(on_first, weight_kept, weight_other),
-            jnp.where(on_first, weight_other, weight_kept),
-        ],
-        axis=1,
-    )
 
     hidden_wide = hidden.astype(wide)
     row_scale = lax.rsqrt(jnp.mean(hidden_wide * hidden_wide, axis=1, keepdims=True) + epsilon)
@@ -98,17 +95,6 @@
     )
     normed = hidden_block * scale_block
     mlp_block = (normed * gain_block).astype(narrow)
-    mlp_all = lax.all_gather(mlp_block, tensor_axes, axis=0, tiled=True)
-    mlp_all = (
-        mlp_all.reshape(tensor_count, dp_count, row_count, features)
-        .transpose(1, 0, 2, 3)
-        .reshape(tokens, features)
-    )
-    mlp_other = swap_cores(mlp_all)
-    mlp_pair = jnp.concatenate(
-        [jnp.where(on_first, mlp_all, mlp_other), jnp.where(on_first, mlp_other, mlp_all)],
-        axis=1,
-    )
 
     gate_grad, up_grad = swiglu_back(gate_act, up_act, product_grad)
     joined_rows = joined_in.reshape(row_count, tensor_count, 2, half_inputs)
@@ -120,9 +106,17 @@
         [up_grad.reshape(row_count, tensor_count, units), joined_rows[:, :, 1]], axis=2
     )
     unit_rows = jnp.stack([gate_rows, up_rows]).transpose(2, 0, 1, 3)
+    unit_rows, mlp_sent = lax.optimization_barrier((unit_rows, mlp_block))
     unit_group = exchange(
         unit_rows.reshape(tensor_count, 2 * row_count, half_width), tensor_axes
     )
+    mlp_all = lax.all_gather(mlp_sent, tensor_axes, axis=0, tiled=True)
+    mlp_all = (
+        mlp_all.reshape(tensor_count, dp_count, row_count, features)
+        .transpose(1, 0, 2, 3)
+        .reshape(tokens, features)
+    )
+    mlp_other = swap_cores(mlp_all)
     unit_halves = (
         unit_group.reshape(tensor_count, 2, row_count, half_width)
         .transpose(1, 0, 2, 3)
@@ -135,15 +129,22 @@
     grad_half = half_all[:, :units]
     joined_half = half_all[:, units:]
 
-    partial_value = jnp.dot(grad_half, weight_pair, preferred_element_type=wide).astype(narrow)
-    partial_value = partial_value.reshape(
-        dp_count, 2, z_count, row_count, core_count, features
-    ).transpose(1, 4, 2, 0, 3, 5)
-    near = exchange(
-        partial_value.reshape(2 * core_count, z_count * block_rows, features), ("y_lo", "core")
-    )
-    near_sum = jnp.sum(near.astype(wide), axis=0).astype(narrow)
-    far = exchange(near_sum.reshape(z_count, block_rows, features), "z")
+    partial_other = jnp.dot(grad_half, weight_other, preferred_element_type=wide)
+    partial_own = jnp.dot(grad_half, weight_kept, preferred_element_type=wide)
+    partial_value = (partial_own + swap_cores(partial_other)).reshape(
+        dp_count, 2, z_count * row_count, features
+    )
+    here = lax.axis_index("y_lo")
+    near_kept = lax.dynamic_index_in_dim(partial_value, here, 1, keepdims=False)
+    near_sent = lax.dynamic_index_in_dim(partial_value, 1 - here, 1, keepdims=False)
+    near_sum = near_kept + swap_near(near_sent.astype(narrow)).astype(wide)
+    near_sum = (
+        near_sum.astype(narrow)
+        .reshape(dp_count, z_count, row_count, features)
+        .transpose(1, 0, 2, 3)
+        .reshape(z_count, block_rows, features)
+    )
+    far = exchange(near_sum, "z")
     input_grad = jnp.sum(far.astype(wide), axis=0)
 
     lifted = input_grad * gain_block
@@ -154,17 +155,21 @@
     inner_mean = (jnp.sum(mean_all, axis=(0, 1)) / width)[:, None]
     hidden_grad = (resid_block + scale_block * (lifted - normed * inner_mean)).astype(narrow)
     gain_part = jnp.sum(input_grad * normed, axis=0, keepdims=True)
-    gain_parts = lax.all_gather(gain_part, tensor_axes, axis=0, tiled=True)
-    gain_sum = jnp.sum(gain_parts, axis=0, keepdims=True)
-
-    grad_far = exchange(
-        jnp.broadcast_to(hidden_grad[None], (z_count, block_rows, features)), "z"
-    ).reshape(1, z_count * block_rows, features)
-    grad_all = exchange(
-        jnp.broadcast_to(grad_far, (2, z_count * block_rows, features)), "y_lo"
-    )
+
+    sent_rows = block_rows + 8
+    grad_sent = jnp.concatenate(
+        [hidden_grad] + list(split_three(gain_part)) + [jnp.zeros((5, features), narrow)], axis=0
+    )
+    grad_far = exchange(jnp.broadcast_to(grad_sent[None], (z_count, sent_rows, features)), "z")
+    grad_near = swap_near(grad_far)
+    grad_pair = jnp.stack(
+        [jnp.where(here == 0, grad_far, grad_near), jnp.where(here == 0, grad_near, grad_far)]
+    )
+    gain_parts = grad_pair[:, :, block_rows : block_rows + 3].astype(wide)
+    gain_sum = jnp.sum(gain_parts, axis=(0, 1, 2))[None]
     grad_all = (
-        grad_all.reshape(tensor_count, dp_count, row_count, features)
+        grad_pair[:, :, :block_rows]
+        .reshape(tensor_count, dp_count, row_count, features)
         .transpose(1, 0, 2, 3)
         .reshape(tokens, features)
     )
@@ -188,22 +193,17 @@
     joined_grad = exchange(joined_total.reshape(tensor_count, row_count, inputs), tensor_axes)
     joined_grad = joined_grad.transpose(1, 0, 2).reshape(row_count, tensor_count * inputs)
 
-    unit_weight_grad = token_sum(grad_half, mlp_pair)
-    grad_first = unit_weight_grad[:, :features]
-    grad_second = unit_weight_grad[:, features:]
-    own_grad = jnp.where(on_first, grad_first, grad_second)
-    other_grad = swap_cores(jnp.where(on_first, grad_second, grad_first))
-    gate_weight_grad = jnp.where(on_first, own_grad, other_grad)
-    up_weight_grad = jnp.where(on_first, other_grad, own_grad)
+    kept_grad = token_sum(grad_half, mlp_all)
+    other_grad = swap_cores(token_sum(grad_half, mlp_other))
+    gate_weight_grad = jnp.where(on_first, kept_grad, other_grad)
+    up_weight_grad = jnp.where(on_first, other_grad, kept_grad)
     joined_other = swap_cores(joined_half)
-    joined_all = jnp.concatenate(
-        [
-            jnp.where(on_first, joined_half, joined_other),
-            jnp.where(on_first, joined_other, joined_half),
-        ],
-        axis=1,
-    )
-    join_weight_grad = token_sum(joined_all, grad_all)
+    join_kept = token_sum(joined_half, grad_all)
+    join_other = token_sum(joined_other, grad_all)
+    join_weight_grad = jnp.concatenate(
+        [jnp.where(on_first, join_kept, join_other), jnp.where(on_first, join_other, join_kept)],
+        axis=0,
+    )
     return (joined_grad, gate_weight_grad, up_weight_grad, join_weight_grad, gain_grad)
 
 

time: 496 us -> 397 us (0.80)
  blocking collectives: 96.1 us -> 44 us
  waiting for transfers between devices: 230 us -> 198 us
  local copies, waits for them, and re-layouts: 26.8 us -> 15.7 us
  starting transfers between devices: 101 us -> 92.7 us
  matrix products: 11.5 us -> 16.5 us
    all_gather x1 -> x0, blocking collectives: 48.6 us -> none  [shards(): gain_parts = lax.all_gather(gain_part, tensor_axes, axis=0, tiled=True)]
    all_gather x1, waiting for transfers between devices: 103 us -> 72.9 us  [shards(): mlp_all = lax.all_gather(mlp_sent, tensor_axes, axis=0, tiled=True)]
    all_to_all x9 -> x7, waiting for transfers between devices: 126 us -> 101 us  [exchange(): return lax.all_to_all(blocks, axes, split_axis=0, concat_axis=0, tiled=True)]
    ppermute x0 -> x2, waiting for transfers between devices: none -> 20.7 us  [swap_near(): return lax.ppermute(value, 'y_lo', [(0, 1), (1, 0)])]
    all_to_all x9 -> x7, starting transfers between devices: 74.6 us -> 58.5 us  [exchange(): return lax.all_to_all(blocks, axes, split_axis=0, concat_axis=0, tiled=True)]
    reshape x5 -> x2, local copies, waits for them, and re-layouts: 10.7 us -> 1.24 us  [the longest x1 0.95 us: shards(): near_sum = near_sum.astype(narrow).reshape(dp_count, z_count, row_count,...]
    ppermute x4 -> x5, starting transfers between devices: 26.5 us -> 29.7 us  [swap_cores(): return lax.ppermute(value, 'core', [(0, 1), (1, 0)])]
  transfers between devices with their start and end apart: 14 -> 15, of which waited for: 9 -> 12; matrix products, arithmetic and copies ran while one was open for 5% -> 7% of each run, Pallas kernels for 0% -> 0%
where the time goes in v2:
time: 397 us; the launch traced here: 396 us
  waiting for transfers between devices  198 us (50%)
  starting transfers between devices  92.7 us (23%)
  blocking collectives  44 us (11%)
  matrix products  16.5 us (4%)
  local copies, waits for them, and re-layouts  15.7 us (4%)
  other arithmetic  14.5 us (4%)
  between operations  14.5 us (4%)
    all_to_all x7, waiting for transfers between devices, exchange(): return lax.all_to_all(blocks, axes, split_axis=0, concat_axis=0, tiled=True)  101 us
    all_gather x1, waiting for transfers between devices, shards(): mlp_all = lax.all_gather(mlp_sent, tensor_axes, axis=0, tiled=True)  72.9 us
    all_to_all x7, starting transfers between devices, exchange(): return lax.all_to_all(blocks, axes, split_axis=0, concat_axis=0, tiled=True)  58.5 us
    all_to_all x1, blocking collectives, exchange(): return lax.all_to_all(blocks, axes, split_axis=0, concat_axis=0, tiled=True)  44 us
    ppermute x5, starting transfers between devices, swap_cores(): return lax.ppermute(value, 'core', [(0, 1), (1, 0)])  29.7 us
    ppermute x2, waiting for transfers between devices, swap_near(): return lax.ppermute(value, 'y_lo', [(0, 1), (1, 0)])  20.7 us
    dot_general x4, matrix products, token_sum(): lax.dot_general(left, right, (((0,), (0,)), ((), ())), preferred_element_...  9.33 us
  transfers between devices with their start and end apart: 15, of which 12 were waited for; matrix products, arithmetic and copies ran while one was open for 7% of the time, Pallas kernels for 0%

profile of v2, /device:TPU:1, one launch (start us, length us, event | category | flops | bytes accessed | tf_op | source)
XLA Modules:
  0.0 395.7 jit_solution(7176789795445613335)
XLA Ops:
  9.8 10.2 %all-to-all-start = ((bf16[16,3,4,256]{3,2,1,0:T(4,128)(2,1)}), bf16[16,3,4,256]{3,2,1,0:T(4,128)(2,1)S(1)}, u32[]{:S(2)}, u32[]{:S(2)}) async-start(bf16[16,3,4,256]{3,2,1,0:T(4,128)(2,1)} %maximum_bitcast_fusion.3), calls=%async_computation | async-start | bytes 196608 | tf_op jit(solution)/shard_map/all_to_all | solution.py:28
  21.9 1.7 fusion.13
  24.1 3.3 all-to-all-done
  29.8 44.0 %all_to_all.40 = bf16[32,8,1024]{2,1,0:T(8,128)(2,1)S(1)} all-to-all(bf16[32,8,1024]{2,1,0:T(8,128)(2,1)S(1)} %reshape.259), channel_id=1, replica_groups=mesh['y_lo'=2,'z'=16,'x'=4,'y_hi'=2,'core'=2] {'y_lo','z'}, dimensions={0} | all-to-all | bytes 1048576 | tf_op jit(solution)/shard_map/all_to_all | solution.py:28
  74.8 2.5 broadcast_in_dim.17
  77.3 5.8 %all-to-all-start.2 = ((bf16[16,128,1024]{2,1,0:T(8,128)(2,1)}), bf16[16,128,1024]{2,1,0:T(8,128)(2,1)}, u32[]{:S(2)}, u32[]{:S(2)}) async-start(bf16[16,128,1024]{2,1,0:T(8,128)(2,1)} %bitcast.91), calls=%async_computation.2 | async-start | bytes 8388608 | tf_op jit(solution)/shard_map/all_to_all | solution.py:28
  83.2 2.2 collective-permute-start
  87.0 48.8 %all-to-all-done.2 = bf16[16,128,1024]{2,1,0:T(8,128)(2,1)} async-done(((bf16[16,128,1024]{2,1,0:T(8,128)(2,1)}), bf16[16,128,1024]{2,1,0:T(8,128)(2,1)}, u32[]{:S(2)}, u32[]{:S(2)}) %all-to-all-start.2) | async-done | bytes 4194336 | tf_op jit(solution)/shard_map/all_to_all | solution.py:28
  135.9 3.4 fusion.4
  139.3 1.9 collective-permute-start.1
  141.2 3.3 fusion.6
  145.4 1.9 add.80
  147.7 2.3 collective-permute-start.2
  150.1 12.8 %collective-permute-done.2 = bf16[16,64,256]{2,0,1:T(8,128)(2,1)S(1)} collective-permute-done((bf16[16,64,256]{2,0,1:T(8,128)(2,1)S(1)}, bf16[16,64,256]{2,0,1:T(8,128)(2,1)S(1)}, u32[]{:S(2)}, u32[]{:S(2)}) %collective-permute-start.2) | collective-permute-done | bytes 524320 | tf_op jit(solution)/shard_map/ppermute | solution.py:36
  164.8 4.7 %all-to-all-start.3 = ((bf16[16,64,256]{2,1,0:T(8,128)(2,1)}), bf16[16,64,256]{2,1,0:T(8,128)(2,1)S(1)}, u32[]{:S(2)}, u32[]{:S(2)}) async-start(bf16[16,64,256]{2,1,0:T(8,128)(2,1)} %copy.113), calls=%async_computation.3 | async-start | bytes 1048576 | tf_op jit(solution)/shard_map/all_to_all | solution.py:28
  170.3 22.1 %all-to-all-done.3 = bf16[16,64,256]{2,1,0:T(8,128)(2,1)S(1)} async-done(((bf16[16,64,256]{2,1,0:T(8,128)(2,1)}), bf16[16,64,256]{2,1,0:T(8,128)(2,1)S(1)}, u32[]{:S(2)}, u32[]{:S(2)}) %all-to-all-start.3) | async-done | bytes 524320 | tf_op jit(solution)/shard_map/all_to_all | solution.py:28
  193.4 19.3 %all-to-all-start.4 = ((f32[16,1,64]{2,1,0:T(1,128)}), f32[16,1,64]{2,1,0:T(1,128)S(1)}, u32[]{:S(2)}, u32[]{:S(2)}) async-start(f32[16,1,64]{2,1,0:T(1,128)} %broadcast_in_dim.19), calls=%async_computation.4 | async-start | bytes 16384 | tf_op jit(solution)/shard_map/all_to_all | solution.py:28
  212.6 6.9 %all-to-all-done.4 = f32[16,1,64]{2,1,0:T(1,128)S(1)} async-done(((f32[16,1,64]{2,1,0:T(1,128)}), f32[16,1,64]{2,1,0:T(1,128)S(1)}, u32[]{:S(2)}, u32[]{:S(2)}) %all-to-all-start.4) | async-done | bytes 4128 | tf_op jit(solution)/shard_map/all_to_all | solution.py:28
  220.6 6.6 %all-to-all-start.5 = ((bf16[16,72,256]{2,1,0:T(8,128)(2,1)}), bf16[16,72,256]{2,1,0:T(8,128)(2,1)S(1)}, u32[]{:S(2)}, u32[]{:S(2)}) async-start(bf16[16,72,256]{2,1,0:T(8,128)(2,1)} %broadcast_in_dim.21), calls=%async_computation.5 | async-start | bytes 1179648 | tf_op jit(solution)/shard_map/all_to_all | solution.py:28
  227.1 72.9 %all-gather.2.cloned.1.call-done = bf16[2048,256]{1,0:T(8,128)(2,1)} async-done(((bf16[64,256]{1,0:T(8,128)(2,1)}), bf16[2048,256]{1,0:T(8,128)(2,1)}) %all-gather.2.cloned.1.call-update) | async-done | bytes 1048592 | tf_op jit(solution)/shard_map/all_gather | solution.py:113
  302.1 21.3 %collective-permute-start.4 = (bf16[2048,256]{1,0:T(8,128)(2,1)S(1)}, bf16[2048,256]{1,0:T(8,128)(2,1)}, u32[]{:S(2)}, u32[]{:S(2)}) collective-permute-start(bf16[2048,256]{1,0:T(8,128)(2,1)S(1)} %reshape.272), channel_id=1, source_target_pairs={{0,1},{1,0},{2,3},{3,2},{4,5},{5,4},{6,7},{7,6},{8,9},{9,8},{10,11... | collective-permute-start | bytes 3145736 | tf_op jit(solution)/shard_map/ppermute | solution.py:32
  323.6 2.1 collective-permute-start.3
  325.8 4.4 %fusion = f32[896,256]{1,0:T(8,128)} fusion(bf16[2048,256]{1,0:T(8,128)(2,1)} %collective-permute-done.4, bf16[2048,1024]{1,0:T(8,128)(2,1)} %bitcast.16), kind=kOutput, calls=%fused_computation.1 | convolution fusion | flops 939524096 | bytes 5636096 | tf_op jit(solution)/shard_map/dot_general | solution.py:24
  330.2 2.3 collective-permute-start.5
  332.5 7.9 %collective-permute-done.3 = bf16[16,72,256]{2,0,1:T(8,128)(2,1)S(1)} collective-permute-done((bf16[16,72,256]{2,0,1:T(8,128)(2,1)S(1)}, bf16[16,72,256]{2,0,1:T(8,128)(2,1)S(1)}, u32[]{:S(2)}, u32[]{:S(2)}) %collective-permute-start.3) | collective-permute-done | bytes 589856 | tf_op jit(solution)/shard_map/ppermute | solution.py:36
  343.6 7.9 %all-to-all-start.6 = ((bf16[16,144,256]{2,1,0:T(8,128)(2,1)}), bf16[16,144,256]{2,1,0:T(8,128)(2,1)S(1)}, u32[]{:S(2)}, u32[]{:S(2)}) async-start(bf16[16,144,256]{2,1,0:T(8,128)(2,1)} %pad_maximum_fusion), calls=%async_computation.6 | async-start | bytes 2359296 | tf_op jit(solution)/shard_map/all_to_all | solution.py:28
  351.6 3.2 fusion.2
  355.8 2.0 collective-permute-start.6
  357.9 2.5 broadcast_select_fusion
  362.9 7.3 %all-to-all-done.6 = bf16[16,144,256]{2,1,0:T(8,128)(2,1)S(1)} async-done(((bf16[16,144,256]{2,1,0:T(8,128)(2,1)}), bf16[16,144,256]{2,1,0:T(8,128)(2,1)S(1)}, u32[]{:S(2)}, u32[]{:S(2)}) %all-to-all-start.6) | async-done | bytes 1179680 | tf_op jit(solution)/shard_map/all_to_all | solution.py:28
  371.0 4.0 %all-to-all-start.7 = ((bf16[32,4,256]{2,1,0:T(4,128)(2,1)}), bf16[32,4,256]{2,1,0:T(4,128)(2,1)S(1)}, u32[]{:S(2)}, u32[]{:S(2)}) async-start(bf16[32,4,256]{2,1,0:T(4,128)(2,1)} %reshape.269), calls=%async_computation.7 | async-start | bytes 131072 | tf_op jit(solution)/shard_map/all_to_all | solution.py:28
  375.7 12.6 %all-to-all-done.7 = bf16[32,4,256]{2,1,0:T(4,128)(2,1)S(1)} async-done(((bf16[32,4,256]{2,1,0:T(4,128)(2,1)}), bf16[32,4,256]{2,1,0:T(4,128)(2,1)S(1)}, u32[]{:S(2)}, u32[]{:S(2)}) %all-to-all-start.7) | async-done | bytes 65568 | tf_op jit(solution)/shard_map/all_to_all | solution.py:28
  (94 shorter events, 27.1 us)
Async XLA Ops:
  7.2 334.8 %copy-start = (bf16[256,256]{1,0:T(8,128)(2,1)S(1)}, bf16[256,256]{1,0:T(8,128)(2,1)}, u32[]{:S(2)}) copy-start(bf16[256,256]{1,0:T(8,128)(2,1)} %param.19) | copy-start | bytes 393220
  9.8 17.6 %all-to-all-start = ((bf16[16,3,4,256]{3,2,1,0:T(4,128)(2,1)}), bf16[16,3,4,256]{3,2,1,0:T(4,128)(2,1)S(1)}, u32[]{:S(2)}, u32[]{:S(2)}) async-start(bf16[16,3,4,256]{3,2,1,0:T(4,128)(2,1)} %maximum_bitcast_fusion.3), calls=%async_computation | async-start | bytes 196608 | tf_op jit(solution)/shard_map/all_to_all | solution.py:28
  77.3 5.8 %copy-start.3 = (bf16[896,256]{1,0:T(8,128)(2,1)S(1)}, bf16[896,256]{1,0:T(8,128)(2,1)}, u32[]{:S(2)}) copy-start(bf16[896,256]{1,0:T(8,128)(2,1)} %param.17) | copy-start | bytes 1376260
  77.3 5.8 %copy-start.4 = (bf16[896,256]{1,0:T(8,128)(2,1)S(1)}, bf16[896,256]{1,0:T(8,128)(2,1)}, u32[]{:S(2)}) copy-start(bf16[896,256]{1,0:T(8,128)(2,1)} %param.18) | copy-start | bytes 1376260
  77.3 58.6 %all-to-all-start.2 = ((bf16[16,128,1024]{2,1,0:T(8,128)(2,1)}), bf16[16,128,1024]{2,1,0:T(8,128)(2,1)}, u32[]{:S(2)}, u32[]{:S(2)}) async-start(bf16[16,128,1024]{2,1,0:T(8,128)(2,1)} %bitcast.91), calls=%async_computation.2 | async-start | bytes 8388608 | tf_op jit(solution)/shard_map/all_to_all | solution.py:28
  83.2 3.8 collective-permute-start
  139.3 6.2 %collective-permute-start.1 = (f32[2048,256]{1,0:T(8,128)S(1)}, f32[2048,256]{1,0:T(8,128)}, u32[]{:S(2)}, u32[]{:S(2)}) collective-permute-start(f32[2048,256]{1,0:T(8,128)S(1)} %fusion.4), channel_id=1, source_target_pairs={{0,1},{1,0},{2,3},{3,2},{4,5},{5,4},{6,7},{7,6},{8,9},{9,8},{10,11... | collective-permute-start | bytes 6291464 | tf_op jit(solution)/shard_map/ppermute | solution.py:32
  147.7 15.3 %collective-permute-start.2 = (bf16[16,64,256]{2,0,1:T(8,128)(2,1)S(1)}, bf16[16,64,256]{2,0,1:T(8,128)(2,1)S(1)}, u32[]{:S(2)}, u32[]{:S(2)}) collective-permute-start(bf16[16,64,256]{2,0,1:T(8,128)(2,1)S(1)} %bitcast.103), channel_id=1, source_target_pairs={{0,256},{256,0},{1,257},{257,1},{2,258},{258,2},{3,259},{259,3},{4... | collective-permute-start | bytes 1572872 | tf_op jit(solution)/shard_map/ppermute | solution.py:36
  164.8 27.5 %all-to-all-start.3 = ((bf16[16,64,256]{2,1,0:T(8,128)(2,1)}), bf16[16,64,256]{2,1,0:T(8,128)(2,1)S(1)}, u32[]{:S(2)}, u32[]{:S(2)}) async-start(bf16[16,64,256]{2,1,0:T(8,128)(2,1)} %copy.113), calls=%async_computation.3 | async-start | bytes 1048576 | tf_op jit(solution)/shard_map/all_to_all | solution.py:28
  169.5 130.5 %all-gather.2.cloned.1.call-start = ((), (), s32[]{:S(2)}) async-start(), calls=%async_computation.8 | async-start | bytes 1081344 | tf_op jit(solution)/shard_map/all_gather | solution.py:113
  193.4 26.2 %all-to-all-start.4 = ((f32[16,1,64]{2,1,0:T(1,128)}), f32[16,1,64]{2,1,0:T(1,128)S(1)}, u32[]{:S(2)}, u32[]{:S(2)}) async-start(f32[16,1,64]{2,1,0:T(1,128)} %broadcast_in_dim.19), calls=%async_computation.4 | async-start | bytes 16384 | tf_op jit(solution)/shard_map/all_to_all | solution.py:28
  220.6 102.9 %all-to-all-start.5 = ((bf16[16,72,256]{2,1,0:T(8,128)(2,1)}), bf16[16,72,256]{2,1,0:T(8,128)(2,1)S(1)}, u32[]{:S(2)}, u32[]{:S(2)}) async-start(bf16[16,72,256]{2,1,0:T(8,128)(2,1)} %broadcast_in_dim.21), calls=%async_computation.5 | async-start | bytes 1179648 | tf_op jit(solution)/shard_map/all_to_all | solution.py:28
  302.1 28.1 %copy-start.1 = (bf16[2048,256]{1,0:T(8,128)(2,1)}, bf16[2048,256]{1,0:T(8,128)(2,1)S(1)}, u32[]{:S(2)}) copy-start(bf16[2048,256]{1,0:T(8,128)(2,1)S(1)} %reshape.272) | copy-start | bytes 3145732
  302.1 23.7 %collective-permute-start.4 = (bf16[2048,256]{1,0:T(8,128)(2,1)S(1)}, bf16[2048,256]{1,0:T(8,128)(2,1)}, u32[]{:S(2)}, u32[]{:S(2)}) collective-permute-start(bf16[2048,256]{1,0:T(8,128)(2,1)S(1)} %reshape.272), channel_id=1, source_target_pairs={{0,1},{1,0},{2,3},{3,2},{4,5},{5,4},{6,7},{7,6},{8,9},{9,8},{10,11... | collective-permute-start | bytes 3145736 | tf_op jit(solution)/shard_map/ppermute | solution.py:32
  323.6 16.8 %collective-permute-start.3 = (bf16[16,72,256]{2,0,1:T(8,128)(2,1)S(1)}, bf16[16,72,256]{2,0,1:T(8,128)(2,1)S(1)}, u32[]{:S(2)}, u32[]{:S(2)}) collective-permute-start(bf16[16,72,256]{2,0,1:T(8,128)(2,1)S(1)} %copy.116), channel_id=1, source_target_pairs={{0,256},{256,0},{1,257},{257,1},{2,258},{258,2},{3,259},{259,3},{4... | collective-permute-start | bytes 1769480 | tf_op jit(solution)/shard_map/ppermute | solution.py:36
  330.2 27.6 %collective-permute-start.5 = (f32[896,256]{1,0:T(8,128)}, f32[896,256]{1,0:T(8,128)}, u32[]{:S(2)}, u32[]{:S(2)}) collective-permute-start(f32[896,256]{1,0:T(8,128)} %fusion), channel_id=1, source_target_pairs={{0,1},{1,0},{2,3},{3,2},{4,5},{5,4},{6,7},{7,6},{8,9},{9,8},{10,11... | collective-permute-start | bytes 2752520 | tf_op jit(solution)/shard_map/ppermute | solution.py:32
  342.5 9.1 %copy-start.2 = (bf16[2048,256]{1,0:T(8,128)(2,1)S(1)}, bf16[2048,256]{1,0:T(8,128)(2,1)}, u32[]{:S(2)}) copy-start(bf16[2048,256]{1,0:T(8,128)(2,1)} %copy-done.1) | copy-start | bytes 3145732
  343.6 26.6 %all-to-all-start.6 = ((bf16[16,144,256]{2,1,0:T(8,128)(2,1)}), bf16[16,144,256]{2,1,0:T(8,128)(2,1)S(1)}, u32[]{:S(2)}, u32[]{:S(2)}) async-start(bf16[16,144,256]{2,1,0:T(8,128)(2,1)} %pad_maximum_fusion), calls=%async_computation.6 | async-start | bytes 2359296 | tf_op jit(solution)/shard_map/all_to_all | solution.py:28
  355.8 6.0 %collective-permute-start.6 = (bf16[2048,128]{1,0:T(8,128)(2,1)S(1)}, bf16[2048,128]{1,0:T(8,128)(2,1)S(1)}, u32[]{:S(2)}, u32[]{:S(2)}) collective-permute-start(bf16[2048,128]{1,0:T(8,128)(2,1)S(1)} %slice.77), channel_id=1, source_target_pairs={{0,1},{1,0},{2,3},{3,2},{4,5},{5,4},{6,7},{7,6},{8,9},{9,8},{10,11... | collective-permute-start | bytes 1572872 | tf_op jit(solution)/shard_map/ppermute | solution.py:32
  371.0 17.3 %all-to-all-start.7 = ((bf16[32,4,256]{2,1,0:T(4,128)(2,1)}), bf16[32,4,256]{2,1,0:T(4,128)(2,1)S(1)}, u32[]{:S(2)}, u32[]{:S(2)}) async-start(bf16[32,4,256]{2,1,0:T(4,128)(2,1)} %reshape.269), calls=%async_computation.7 | async-start | bytes 131072 | tf_op jit(solution)/shard_map/all_to_all | solution.py:28
Sparse Core Ops, SparseCore 0:
  173.0 126.9 all-gather.1

commit v3 on v2

--- a/solution.py
+++ b/solution.py
@@ -34,6 +34,27 @@
 
 def swap_near(value):
     return lax.ppermute(value, "y_lo", [(0, 1), (1, 0)])
+
+
+def from_above(value, distance):
+    count = lax.axis_size("z")
+    return lax.ppermute(value, "z", [((i + distance) % count, i) for i in range(count)])
+
+
+def gather_blocks(block):
+    near = swap_near(block)
+    first = lax.axis_index("y_lo") == 0
+    pair = jnp.stack([jnp.where(first, block, near), jnp.where(first, near, block)])
+    z_count = lax.axis_size("z")
+    quarter = z_count // 4
+    strided = jnp.stack([pair] + [from_above(pair, 4 * step) for step in range(1, quarter)])
+    below = from_above(strided, z_count - 1)
+    below = jnp.concatenate([below[1:], below[:1]])
+    all_pairs = jnp.stack(
+        [strided, from_above(strided, 1), from_above(strided, 2), below], axis=1
+    ).reshape(z_count, *pair.shape)
+    twice = jnp.concatenate([all_pairs, all_pairs])
+    return lax.dynamic_slice_in_dim(twice, z_count - lax.axis_index("z"), z_count, 0)
 
 
 def split_three(value):
@@ -106,17 +127,10 @@
         [up_grad.reshape(row_count, tensor_count, units), joined_rows[:, :, 1]], axis=2
     )
     unit_rows = jnp.stack([gate_rows, up_rows]).transpose(2, 0, 1, 3)
-    unit_rows, mlp_sent = lax.optimization_barrier((unit_rows, mlp_block))
     unit_group = exchange(
         unit_rows.reshape(tensor_count, 2 * row_count, half_width), tensor_axes
     )
-    mlp_all = lax.all_gather(mlp_sent, tensor_axes, axis=0, tiled=True)
-    mlp_all = (
-        mlp_all.reshape(tensor_count, dp_count, row_count, features)
-        .transpose(1, 0, 2, 3)
-        .reshape(tokens, features)
-    )
-    mlp_other = swap_cores(mlp_all)
+    mlp_all = gather_blocks(mlp_block)
     unit_halves = (
         unit_group.reshape(tensor_count, 2, row_count, half_width)
         .transpose(1, 0, 2, 3)
@@ -126,6 +140,13 @@
         unit_halves[None], (dp_count // core_count, core_count, group_rows, half_width)
     ).reshape(dp_count, group_rows, half_width)
     half_all = exchange(unit_halves, dp_axes).reshape(tokens, half_width)
+    half_all, mlp_all = lax.optimization_barrier((half_all, mlp_all))
+    mlp_all = (
+        mlp_all.reshape(z_count, 2, dp_count, row_count, features)
+        .transpose(2, 1, 0, 3, 4)
+        .reshape(tokens, features)
+    )
+    mlp_other = swap_cores(mlp_all)
     grad_half = half_all[:, :units]
     joined_half = half_all[:, units:]
 

time: 397 us -> 364 us (0.917)
  starting transfers between devices: 92.7 us -> 158 us
  blocking collectives: 44 us -> 0 us
  waiting for transfers between devices: 198 us -> 154 us
  between operations: 14.5 us -> 1.33 us
    all_gather x1 -> x0, waiting for transfers between devices: 72.9 us -> none  [shards(): mlp_all = lax.all_gather(mlp_sent, tensor_axes, axis=0, tiled=True)]
    all_to_all x7 -> x8, starting transfers between devices: 58.5 us -> 104 us  [exchange(): return lax.all_to_all(blocks, axes, split_axis=0, concat_axis=0, tiled=True)]
    all_to_all x1 -> x0, blocking collectives: 44 us -> none  [exchange(): return lax.all_to_all(blocks, axes, split_axis=0, concat_axis=0, tiled=True)]
    ppermute x0 -> x6, starting transfers between devices: none -> 26.7 us  [from_above(): lax.ppermute(value, 'z', [((i + distance) % count, i) for i in range(coun...]
    ppermute x0 -> x6, waiting for transfers between devices: none -> 20.1 us  [from_above(): lax.ppermute(value, 'z', [((i + distance) % count, i) for i in range(coun...]
    ppermute x5, starting transfers between devices: 29.7 us -> 20.6 us  [swap_cores(): return lax.ppermute(value, 'core', [(0, 1), (1, 0)])]
    ppermute x2 -> x3, waiting for transfers between devices: 20.7 us -> 26.6 us  [swap_near(): return lax.ppermute(value, 'y_lo', [(0, 1), (1, 0)])]
    all_to_all x7 -> x8, waiting for transfers between devices: 101 us -> 107 us  [exchange(): return lax.all_to_all(blocks, axes, split_axis=0, concat_axis=0, tiled=True)]
  transfers between devices with their start and end apart: 15 -> 22, of which waited for: 12 -> 12; matrix products, arithmetic and copies ran while one was open for 7% -> 8% of each run, Pallas kernels for 0% -> 0%
where the time goes in v3:
time: 364 us; the launch traced here: 362 us
  starting transfers between devices  158 us (43%)
  waiting for transfers between devices  154 us (42%)
  matrix products  17.6 us (5%)
  local copies, waits for them, and re-layouts  16.5 us (5%)
  other arithmetic  14.1 us (4%)
    all_to_all x8, waiting for transfers between devices, exchange(): return lax.all_to_all(blocks, axes, split_axis=0, concat_axis=0, tiled=True)  107 us
    all_to_all x8, starting transfers between devices, exchange(): return lax.all_to_all(blocks, axes, split_axis=0, concat_axis=0, tiled=True)  104 us
    ppermute x6, starting transfers between devices, from_above(): lax.ppermute(value, 'z', [((i + distance) % count, i) for i in range(coun...  26.7 us
    ppermute x3, waiting for transfers between devices, swap_near(): return lax.ppermute(value, 'y_lo', [(0, 1), (1, 0)])  26.6 us
    ppermute x5, starting transfers between devices, swap_cores(): return lax.ppermute(value, 'core', [(0, 1), (1, 0)])  20.6 us
    ppermute x6, waiting for transfers between devices, from_above(): lax.ppermute(value, 'z', [((i + distance) % count, i) for i in range(coun...  20.1 us
    dot_general x4, matrix products, token_sum(): lax.dot_general(left, right, (((0,), (0,)), ((), ())), preferred_element_...  9.06 us
  transfers between devices with their start and end apart: 22, of which 12 were waited for; matrix products, arithmetic and copies ran while one was open for 8% of the time, Pallas kernels for 0%

profile of v3, /device:TPU:1, one launch (start us, length us, event | category | flops | bytes accessed | tf_op | source)
XLA Modules:
  0.0 362.0 jit_solution(12227869629930781740)
XLA Ops:
  5.0 17.0 %all-to-all-start.1 = ((bf16[32,8,1024]{2,1,0:T(8,128)(2,1)}), bf16[32,8,1024]{2,1,0:T(8,128)(2,1)S(1)}, u32[]{:S(2)}, u32[]{:S(2)}) async-start(bf16[32,8,1024]{2,1,0:T(8,128)(2,1)} %reshape.262), calls=%async_computation.1 | async-start | bytes 1048576 | tf_op jit(solution)/shard_map/all_to_all | solution.py:28
  23.1 29.6 %all-to-all-done.1 = bf16[32,8,1024]{2,1,0:T(8,128)(2,1)S(1)} async-done(((bf16[32,8,1024]{2,1,0:T(8,128)(2,1)}), bf16[32,8,1024]{2,1,0:T(8,128)(2,1)S(1)}, u32[]{:S(2)}, u32[]{:S(2)}) %all-to-all-start.1) | async-done | bytes 524320 | tf_op jit(solution)/shard_map/all_to_all | solution.py:28
  52.8 8.2 %all-to-all-start = ((bf16[16,3,4,256]{3,2,1,0:T(4,128)(2,1)}), bf16[16,3,4,256]{3,2,1,0:T(4,128)(2,1)S(1)}, u32[]{:S(2)}, u32[]{:S(2)}) async-start(bf16[16,3,4,256]{3,2,1,0:T(4,128)(2,1)} %maximum_bitcast_fusion.4), calls=%async_computation | async-start | bytes 196608 | tf_op jit(solution)/shard_map/all_to_all | solution.py:28
  61.9 6.5 %all-to-all-done = bf16[16,3,4,256]{3,2,1,0:T(4,128)(2,1)S(1)} async-done(((bf16[16,3,4,256]{3,2,1,0:T(4,128)(2,1)}), bf16[16,3,4,256]{3,2,1,0:T(4,128)(2,1)S(1)}, u32[]{:S(2)}, u32[]{:S(2)}) %all-to-all-start) | async-done | bytes 98336 | tf_op jit(solution)/shard_map/all_to_all | solution.py:28
  70.9 4.9 %all-to-all-start.2 = ((bf16[16,128,1024]{2,1,0:T(8,128)(2,1)}), bf16[16,128,1024]{2,1,0:T(8,128)(2,1)}, u32[]{:S(2)}, u32[]{:S(2)}) async-start(bf16[16,128,1024]{2,1,0:T(8,128)(2,1)} %bitcast.109), calls=%async_computation.2 | async-start | bytes 8388608 | tf_op jit(solution)/shard_map/all_to_all | solution.py:28
  80.1 14.3 %collective-permute-done = bf16[64,256]{1,0:T(8,128)(2,1)S(1)} collective-permute-done((bf16[64,256]{1,0:T(8,128)(2,1)S(1)}, bf16[64,256]{1,0:T(8,128)(2,1)S(1)}, u32[]{:S(2)}, u32[]{:S(2)}) %collective-permute-start) | collective-permute-done | bytes 32800 | tf_op jit(solution)/shard_map/ppermute | solution.py:36
  94.6 4.1 %collective-permute-start.1 = (bf16[2,64,256]{2,1,0:T(8,128)(2,1)S(1)}, bf16[2,64,256]{2,1,0:T(8,128)(2,1)S(1)}, u32[]{:S(2)}, u32[]{:S(2)}) collective-permute-start(bf16[2,64,256]{2,1,0:T(8,128)(2,1)S(1)} %get-tuple-element.26), channel_id=1, source_target_pairs={{64,0},{80,16},{96,32},{112,48},{128,64},{144,80},{160,96},{176,11... | collective-permute-start | bytes 196616 | tf_op jit(solution)/shard_map/ppermute | solution.py:41
  98.7 6.2 %collective-permute-start.2 = (bf16[2,64,256]{2,1,0:T(8,128)(2,1)S(1)}, bf16[2,64,256]{2,1,0:T(8,128)(2,1)S(1)}, u32[]{:S(2)}, u32[]{:S(2)}) collective-permute-start(bf16[2,64,256]{2,1,0:T(8,128)(2,1)S(1)} %get-tuple-element.26), channel_id=1, source_target_pairs={{128,0},{144,16},{160,32},{176,48},{192,64},{208,80},{224,96},{240... | collective-permute-start | bytes 196616 | tf_op jit(solution)/shard_map/ppermute | solution.py:41
  104.9 3.5 collective-permute-start.3
  108.5 7.6 %collective-permute-done.2 = bf16[2,64,256]{2,1,0:T(8,128)(2,1)S(1)} collective-permute-done((bf16[2,64,256]{2,1,0:T(8,128)(2,1)S(1)}, bf16[2,64,256]{2,1,0:T(8,128)(2,1)S(1)}, u32[]{:S(2)}, u32[]{:S(2)}) %collective-permute-start.2) | collective-permute-done | bytes 65568 | tf_op jit(solution)/shard_map/ppermute | solution.py:41
  116.2 7.0 %collective-permute-start.6 = (bf16[4,2,64,256]{3,2,1,0:T(8,128)(2,1)S(1)}, bf16[4,2,64,256]{3,2,1,0:T(8,128)(2,1)S(1)}, u32[]{:S(2)}, u32[]{:S(2)}) collective-permute-start(bf16[4,2,64,256]{3,2,1,0:T(8,128)(2,1)S(1)} %get-tuple-element.22), channel_id=1, source_target_pairs={{240,0},{0,16},{16,32},{32,48},{48,64},{64,80},{80,96},{96,112},{1... | collective-permute-start | bytes 786440 | tf_op jit(solution)/shard_map/ppermute | solution.py:41
  125.9 3.1 collective-permute-start.5
  129.1 3.9 %collective-permute-start.7 = (bf16[896,256]{1,0:T(8,128)(2,1)S(1)}, bf16[896,256]{1,0:T(8,128)(2,1)}, u32[]{:S(2)}, u32[]{:S(2)}) collective-permute-start(bf16[896,256]{1,0:T(8,128)(2,1)S(1)} %broadcast_select_fusion.2), channel_id=1, source_target_pairs={{0,1},{1,0},{2,3},{3,2},{4,5},{5,4},{6,7},{7,6},{8,9},{9,8},{10,11... | collective-permute-start | bytes 1376264 | tf_op jit(solution)/shard_map/ppermute | solution.py:32
  133.1 12.4 %collective-permute-done.5 = bf16[4,2,64,256]{3,2,1,0:T(8,128)(2,1)S(1)} collective-permute-done((bf16[4,2,64,256]{3,2,1,0:T(8,128)(2,1)S(1)}, bf16[4,2,64,256]{3,2,1,0:T(8,128)(2,1)S(1)}, u32[]{:S(2)}, u32[]{:S(2)}) %collective-permute-start.5) | collective-permute-done | bytes 262176 | tf_op jit(solution)/shard_map/ppermute | solution.py:41
  146.2 4.7 %fusion.4 = f32[2048,256]{1,0:T(8,128)} fusion(bf16[896,256]{1,0:T(8,128)(2,1)} %collective-permute-done.7, bf16[2048,1024]{1,0:T(8,128)(2,1)} %bitcast.16), kind=kOutput, calls=%fused_computation.5 | convolution fusion | flops 939524096 | bytes 6225920 | tf_op jit(solution)/shard_map/dot_general | solution.py:153
  150.9 3.2 collective-permute-start.8
  154.2 3.3 fusion.6
  164.3 12.3 %collective-permute-done.9 = bf16[16,64,256]{2,0,1:T(8,128)(2,1)} collective-permute-done((bf16[16,64,256]{2,0,1:T(8,128)(2,1)}, bf16[16,64,256]{2,0,1:T(8,128)(2,1)}, u32[]{:S(2)}, u32[]{:S(2)}) %collective-permute-start.9) | collective-permute-done | bytes 524320 | tf_op jit(solution)/shard_map/ppermute | solution.py:36
  179.5 5.8 %all-to-all-start.3 = ((bf16[16,64,256]{2,1,0:T(8,128)(2,1)}), bf16[16,64,256]{2,1,0:T(8,128)(2,1)S(1)}, u32[]{:S(2)}, u32[]{:S(2)}) async-start(bf16[16,64,256]{2,1,0:T(8,128)(2,1)} %copy.119), calls=%async_computation.3 | async-start | bytes 1048576 | tf_op jit(solution)/shard_map/all_to_all | solution.py:28
  185.4 22.7 %all-to-all-done.3 = bf16[16,64,256]{2,1,0:T(8,128)(2,1)S(1)} async-done(((bf16[16,64,256]{2,1,0:T(8,128)(2,1)}), bf16[16,64,256]{2,1,0:T(8,128)(2,1)S(1)}, u32[]{:S(2)}, u32[]{:S(2)}) %all-to-all-start.3) | async-done | bytes 524320 | tf_op jit(solution)/shard_map/all_to_all | solution.py:28
  209.1 42.3 %all-to-all-start.4 = ((f32[16,1,64]{2,1,0:T(1,128)}), f32[16,1,64]{2,1,0:T(1,128)S(1)}, u32[]{:S(2)}, u32[]{:S(2)}) async-start(f32[16,1,64]{2,1,0:T(1,128)} %broadcast_in_dim.19), calls=%async_computation.4 | async-start | bytes 16384 | tf_op jit(solution)/shard_map/all_to_all | solution.py:28
  251.4 6.9 %all-to-all-done.4 = f32[16,1,64]{2,1,0:T(1,128)S(1)} async-done(((f32[16,1,64]{2,1,0:T(1,128)}), f32[16,1,64]{2,1,0:T(1,128)S(1)}, u32[]{:S(2)}, u32[]{:S(2)}) %all-to-all-start.4) | async-done | bytes 4128 | tf_op jit(solution)/shard_map/all_to_all | solution.py:28
  259.3 6.3 %all-to-all-start.5 = ((bf16[16,72,256]{2,1,0:T(8,128)(2,1)}), bf16[16,72,256]{2,1,0:T(8,128)(2,1)S(1)}, u32[]{:S(2)}, u32[]{:S(2)}) async-start(bf16[16,72,256]{2,1,0:T(8,128)(2,1)} %broadcast_in_dim.21), calls=%async_computation.5 | async-start | bytes 1179648 | tf_op jit(solution)/shard_map/all_to_all | solution.py:28
  266.8 3.0 collective-permute-start.11
  269.8 21.1 %all-to-all-done.5 = bf16[16,72,256]{2,1,0:T(8,128)(2,1)S(1)} async-done(((bf16[16,72,256]{2,1,0:T(8,128)(2,1)}), bf16[16,72,256]{2,1,0:T(8,128)(2,1)S(1)}, u32[]{:S(2)}, u32[]{:S(2)}) %all-to-all-start.5) | async-done | bytes 589856 | tf_op jit(solution)/shard_map/all_to_all | solution.py:28
  293.1 4.1 %fusion = f32[896,256]{1,0:T(8,128)} fusion(bf16[2048,256]{1,0:T(8,128)(2,1)S(1)} %collective-permute-done.11, bf16[2048,1024]{1,0:T(8,128)(2,1)} %bitcast.16), kind=kOutput, calls=%fused_computation.1 | convolution fusion | flops 939524096 | bytes 5636096 | tf_op jit(solution)/shard_map/dot_general | solution.py:24
  297.2 8.4 %collective-permute-start.12 = (f32[896,256]{1,0:T(8,128)}, f32[896,256]{1,0:T(8,128)}, u32[]{:S(2)}, u32[]{:S(2)}) collective-permute-start(f32[896,256]{1,0:T(8,128)} %fusion), channel_id=1, source_target_pairs={{0,1},{1,0},{2,3},{3,2},{4,5},{5,4},{6,7},{7,6},{8,9},{9,8},{10,11... | collective-permute-start | bytes 2752520 | tf_op jit(solution)/shard_map/ppermute | solution.py:32
  308.8 7.2 %all-to-all-start.6 = ((bf16[16,144,256]{2,1,0:T(8,128)(2,1)}), bf16[16,144,256]{2,1,0:T(8,128)(2,1)S(1)}, u32[]{:S(2)}, u32[]{:S(2)}) async-start(bf16[16,144,256]{2,1,0:T(8,128)(2,1)} %pad_maximum_fusion), calls=%async_computation.6 | async-start | bytes 2359296 | tf_op jit(solution)/shard_map/all_to_all | solution.py:28
  316.0 3.2 fusion.2
  327.4 7.2 %all-to-all-done.6 = bf16[16,144,256]{2,1,0:T(8,128)(2,1)S(1)} async-done(((bf16[16,144,256]{2,1,0:T(8,128)(2,1)}), bf16[16,144,256]{2,1,0:T(8,128)(2,1)S(1)}, u32[]{:S(2)}, u32[]{:S(2)}) %all-to-all-start.6) | async-done | bytes 1179680 | tf_op jit(solution)/shard_map/all_to_all | solution.py:28
  335.5 12.7 %all-to-all-start.7 = ((bf16[32,4,256]{2,1,0:T(4,128)(2,1)}), bf16[32,4,256]{2,1,0:T(4,128)(2,1)S(1)}, u32[]{:S(2)}, u32[]{:S(2)}) async-start(bf16[32,4,256]{2,1,0:T(4,128)(2,1)} %reshape.273), calls=%async_computation.7 | async-start | bytes 131072 | tf_op jit(solution)/shard_map/all_to_all | solution.py:28
  348.8 12.6 %all-to-all-done.7 = bf16[32,4,256]{2,1,0:T(4,128)(2,1)S(1)} async-done(((bf16[32,4,256]{2,1,0:T(4,128)(2,1)}), bf16[32,4,256]{2,1,0:T(4,128)(2,1)S(1)}, u32[]{:S(2)}, u32[]{:S(2)}) %all-to-all-start.7) | async-done | bytes 65568 | tf_op jit(solution)/shard_map/all_to_all | solution.py:28
  (119 shorter events, 45.2 us)
Async XLA Ops:
  0.6 306.5 %copy-start = (bf16[256,256]{1,0:T(8,128)(2,1)S(1)}, bf16[256,256]{1,0:T(8,128)(2,1)}, u32[]{:S(2)}) copy-start(bf16[256,256]{1,0:T(8,128)(2,1)} %param.19) | copy-start | bytes 393220
  3.5 18.6 %copy-start.5 = (bf16[4,4096]{1,0:T(4,128)(2,1)S(1)}, bf16[4,4096]{1,0:T(4,128)(2,1)}, u32[]{:S(2)}) copy-start(bf16[4,4096]{1,0:T(4,128)(2,1)} %param.10) | copy-start | bytes 98308
  3.5 18.9 %copy-start.6 = (bf16[4,4096]{1,0:T(4,128)(2,1)S(1)}, bf16[4,4096]{1,0:T(4,128)(2,1)}, u32[]{:S(2)}) copy-start(bf16[4,4096]{1,0:T(4,128)(2,1)} %param.15) | copy-start | bytes 98308
  5.0 47.7 %all-to-all-start.1 = ((bf16[32,8,1024]{2,1,0:T(8,128)(2,1)}), bf16[32,8,1024]{2,1,0:T(8,128)(2,1)S(1)}, u32[]{:S(2)}, u32[]{:S(2)}) async-start(bf16[32,8,1024]{2,1,0:T(8,128)(2,1)} %reshape.262), calls=%async_computation.1 | async-start | bytes 1048576 | tf_op jit(solution)/shard_map/all_to_all | solution.py:28
  52.8 15.6 %all-to-all-start = ((bf16[16,3,4,256]{3,2,1,0:T(4,128)(2,1)}), bf16[16,3,4,256]{3,2,1,0:T(4,128)(2,1)S(1)}, u32[]{:S(2)}, u32[]{:S(2)}) async-start(bf16[16,3,4,256]{3,2,1,0:T(4,128)(2,1)} %maximum_bitcast_fusion.4), calls=%async_computation | async-start | bytes 196608 | tf_op jit(solution)/shard_map/all_to_all | solution.py:28
  70.9 58.1 %copy-start.3 = (bf16[896,256]{1,0:T(8,128)(2,1)S(1)}, bf16[896,256]{1,0:T(8,128)(2,1)}, u32[]{:S(2)}) copy-start(bf16[896,256]{1,0:T(8,128)(2,1)} %param.17) | copy-start | bytes 1376260
  70.9 58.2 %copy-start.4 = (bf16[896,256]{1,0:T(8,128)(2,1)S(1)}, bf16[896,256]{1,0:T(8,128)(2,1)}, u32[]{:S(2)}) copy-start(bf16[896,256]{1,0:T(8,128)(2,1)} %param.18) | copy-start | bytes 1376260
  70.9 75.3 %all-to-all-start.2 = ((bf16[16,128,1024]{2,1,0:T(8,128)(2,1)}), bf16[16,128,1024]{2,1,0:T(8,128)(2,1)}, u32[]{:S(2)}, u32[]{:S(2)}) async-start(bf16[16,128,1024]{2,1,0:T(8,128)(2,1)} %bitcast.109), calls=%async_computation.2 | async-start | bytes 8388608 | tf_op jit(solution)/shard_map/all_to_all | solution.py:28
  78.2 16.3 %collective-permute-start = (bf16[64,256]{1,0:T(8,128)(2,1)S(1)}, bf16[64,256]{1,0:T(8,128)(2,1)S(1)}, u32[]{:S(2)}, u32[]{:S(2)}) collective-permute-start(bf16[64,256]{1,0:T(8,128)(2,1)S(1)} %multiply_convert_fusion), channel_id=1, source_target_pairs={{0,256},{256,0},{1,257},{257,1},{2,258},{258,2},{3,259},{259,3},{4... | collective-permute-start | bytes 98312 | tf_op jit(solution)/shard_map/ppermute | solution.py:36
  94.6 13.9 %collective-permute-start.1 = (bf16[2,64,256]{2,1,0:T(8,128)(2,1)S(1)}, bf16[2,64,256]{2,1,0:T(8,128)(2,1)S(1)}, u32[]{:S(2)}, u32[]{:S(2)}) collective-permute-start(bf16[2,64,256]{2,1,0:T(8,128)(2,1)S(1)} %get-tuple-element.26), channel_id=1, source_target_pairs={{64,0},{80,16},{96,32},{112,48},{128,64},{144,80},{160,96},{176,11... | collective-permute-start | bytes 196616 | tf_op jit(solution)/shard_map/ppermute | solution.py:41
  98.7 17.5 %collective-permute-start.2 = (bf16[2,64,256]{2,1,0:T(8,128)(2,1)S(1)}, bf16[2,64,256]{2,1,0:T(8,128)(2,1)S(1)}, u32[]{:S(2)}, u32[]{:S(2)}) collective-permute-start(bf16[2,64,256]{2,1,0:T(8,128)(2,1)S(1)} %get-tuple-element.26), channel_id=1, source_target_pairs={{128,0},{144,16},{160,32},{176,48},{192,64},{208,80},{224,96},{240... | collective-permute-start | bytes 196616 | tf_op jit(solution)/shard_map/ppermute | solution.py:41
  104.9 11.2 %collective-permute-start.3 = (bf16[2,64,256]{2,1,0:T(8,128)(2,1)S(1)}, bf16[2,64,256]{2,1,0:T(8,128)(2,1)S(1)}, u32[]{:S(2)}, u32[]{:S(2)}) collective-permute-start(bf16[2,64,256]{2,1,0:T(8,128)(2,1)S(1)} %get-tuple-element.26), channel_id=1, source_target_pairs={{192,0},{208,16},{224,32},{240,48},{0,64},{16,80},{32,96},{48,112}... | collective-permute-start | bytes 196616 | tf_op jit(solution)/shard_map/ppermute | solution.py:41
  116.2 16.8 %collective-permute-start.6 = (bf16[4,2,64,256]{3,2,1,0:T(8,128)(2,1)S(1)}, bf16[4,2,64,256]{3,2,1,0:T(8,128)(2,1)S(1)}, u32[]{:S(2)}, u32[]{:S(2)}) collective-permute-start(bf16[4,2,64,256]{3,2,1,0:T(8,128)(2,1)S(1)} %get-tuple-element.22), channel_id=1, source_target_pairs={{240,0},{0,16},{16,32},{32,48},{48,64},{64,80},{80,96},{96,112},{1... | collective-permute-start | bytes 786440 | tf_op jit(solution)/shard_map/ppermute | solution.py:41
  123.3 9.8 %collective-permute-start.4 = (bf16[4,2,64,256]{3,2,1,0:T(8,128)(2,1)S(1)}, bf16[4,2,64,256]{3,2,1,0:T(8,128)(2,1)S(1)}, u32[]{:S(2)}, u32[]{:S(2)}) collective-permute-start(bf16[4,2,64,256]{3,2,1,0:T(8,128)(2,1)S(1)} %get-tuple-element.22), channel_id=1, source_target_pairs={{16,0},{32,16},{48,32},{64,48},{80,64},{96,80},{112,96},{128,112},... | collective-permute-start | bytes 786440 | tf_op jit(solution)/shard_map/ppermute | solution.py:41
  125.9 19.6 %collective-permute-start.5 = (bf16[4,2,64,256]{3,2,1,0:T(8,128)(2,1)S(1)}, bf16[4,2,64,256]{3,2,1,0:T(8,128)(2,1)S(1)}, u32[]{:S(2)}, u32[]{:S(2)}) collective-permute-start(bf16[4,2,64,256]{3,2,1,0:T(8,128)(2,1)S(1)} %get-tuple-element.22), channel_id=1, source_target_pairs={{32,0},{48,16},{64,32},{80,48},{96,64},{112,80},{128,96},{144,112}... | collective-permute-start | bytes 786440 | tf_op jit(solution)/shard_map/ppermute | solution.py:41
  129.1 17.1 %collective-permute-start.7 = (bf16[896,256]{1,0:T(8,128)(2,1)S(1)}, bf16[896,256]{1,0:T(8,128)(2,1)}, u32[]{:S(2)}, u32[]{:S(2)}) collective-permute-start(bf16[896,256]{1,0:T(8,128)(2,1)S(1)} %broadcast_select_fusion.2), channel_id=1, source_target_pairs={{0,1},{1,0},{2,3},{3,2},{4,5},{5,4},{6,7},{7,6},{8,9},{9,8},{10,11... | collective-permute-start | bytes 1376264 | tf_op jit(solution)/shard_map/ppermute | solution.py:32
  150.9 7.4 %collective-permute-start.8 = (f32[2048,256]{1,0:T(8,128)}, f32[2048,256]{1,0:T(8,128)}, u32[]{:S(2)}, u32[]{:S(2)}) collective-permute-start(f32[2048,256]{1,0:T(8,128)} %fusion.4), channel_id=1, source_target_pairs={{0,1},{1,0},{2,3},{3,2},{4,5},{5,4},{6,7},{7,6},{8,9},{9,8},{10,11... | collective-permute-start | bytes 6291464 | tf_op jit(solution)/shard_map/ppermute | solution.py:32
  161.3 15.3 %collective-permute-start.9 = (bf16[16,64,256]{2,0,1:T(8,128)(2,1)}, bf16[16,64,256]{2,0,1:T(8,128)(2,1)}, u32[]{:S(2)}, u32[]{:S(2)}) collective-permute-start(bf16[16,64,256]{2,0,1:T(8,128)(2,1)} %bitcast.108), channel_id=1, source_target_pairs={{0,256},{256,0},{1,257},{257,1},{2,258},{258,2},{3,259},{259,3},{4... | collective-permute-start | bytes 1572872 | tf_op jit(solution)/shard_map/ppermute | solution.py:36
  179.5 28.6 %all-to-all-start.3 = ((bf16[16,64,256]{2,1,0:T(8,128)(2,1)}), bf16[16,64,256]{2,1,0:T(8,128)(2,1)S(1)}, u32[]{:S(2)}, u32[]{:S(2)}) async-start(bf16[16,64,256]{2,1,0:T(8,128)(2,1)} %copy.119), calls=%async_computation.3 | async-start | bytes 1048576 | tf_op jit(solution)/shard_map/all_to_all | solution.py:28
  209.1 49.2 %all-to-all-start.4 = ((f32[16,1,64]{2,1,0:T(1,128)}), f32[16,1,64]{2,1,0:T(1,128)S(1)}, u32[]{:S(2)}, u32[]{:S(2)}) async-start(f32[16,1,64]{2,1,0:T(1,128)} %broadcast_in_dim.19), calls=%async_computation.4 | async-start | bytes 16384 | tf_op jit(solution)/shard_map/all_to_all | solution.py:28
  259.3 31.6 %all-to-all-start.5 = ((bf16[16,72,256]{2,1,0:T(8,128)(2,1)}), bf16[16,72,256]{2,1,0:T(8,128)(2,1)S(1)}, u32[]{:S(2)}, u32[]{:S(2)}) async-start(bf16[16,72,256]{2,1,0:T(8,128)(2,1)} %broadcast_in_dim.21), calls=%async_computation.5 | async-start | bytes 1179648 | tf_op jit(solution)/shard_map/all_to_all | solution.py:28
  266.8 30.4 %copy-start.1 = (bf16[2048,256]{1,0:T(8,128)(2,1)}, bf16[2048,256]{1,0:T(8,128)(2,1)S(1)}, u32[]{:S(2)}) copy-start(bf16[2048,256]{1,0:T(8,128)(2,1)S(1)} %reshape.276) | copy-start | bytes 3145732
  266.8 26.3 %collective-permute-start.11 = (bf16[2048,256]{1,0:T(8,128)(2,1)S(1)}, bf16[2048,256]{1,0:T(8,128)(2,1)S(1)}, u32[]{:S(2)}, u32[]{:S(2)}) collective-permute-start(bf16[2048,256]{1,0:T(8,128)(2,1)S(1)} %reshape.276), channel_id=1, source_target_pairs={{0,1},{1,0},{2,3},{3,2},{4,5},{5,4},{6,7},{7,6},{8,9},{9,8},{10,11... | collective-permute-start | bytes 3145736 | tf_op jit(solution)/shard_map/ppermute | solution.py:32
  291.0 14.5 %collective-permute-start.10 = (bf16[16,72,256]{2,0,1:T(8,128)(2,1)S(1)}, bf16[16,72,256]{2,0,1:T(8,128)(2,1)S(1)}, u32[]{:S(2)}, u32[]{:S(2)}) collective-permute-start(bf16[16,72,256]{2,0,1:T(8,128)(2,1)S(1)} %copy.122), channel_id=1, source_target_pairs={{0,256},{256,0},{1,257},{257,1},{2,258},{258,2},{3,259},{259,3},{4... | collective-permute-start | bytes 1769480 | tf_op jit(solution)/shard_map/ppermute | solution.py:36
  297.2 25.2 %collective-permute-start.12 = (f32[896,256]{1,0:T(8,128)}, f32[896,256]{1,0:T(8,128)}, u32[]{:S(2)}, u32[]{:S(2)}) collective-permute-start(f32[896,256]{1,0:T(8,128)} %fusion), channel_id=1, source_target_pairs={{0,1},{1,0},{2,3},{3,2},{4,5},{5,4},{6,7},{7,6},{8,9},{9,8},{10,11... | collective-permute-start | bytes 2752520 | tf_op jit(solution)/shard_map/ppermute | solution.py:32
  307.6 8.3 %copy-start.2 = (bf16[2048,256]{1,0:T(8,128)(2,1)S(1)}, bf16[2048,256]{1,0:T(8,128)(2,1)}, u32[]{:S(2)}) copy-start(bf16[2048,256]{1,0:T(8,128)(2,1)} %copy-done.1) | copy-start | bytes 3145732
  308.8 25.9 %all-to-all-start.6 = ((bf16[16,144,256]{2,1,0:T(8,128)(2,1)}), bf16[16,144,256]{2,1,0:T(8,128)(2,1)S(1)}, u32[]{:S(2)}, u32[]{:S(2)}) async-start(bf16[16,144,256]{2,1,0:T(8,128)(2,1)} %pad_maximum_fusion), calls=%async_computation.6 | async-start | bytes 2359296 | tf_op jit(solution)/shard_map/all_to_all | solution.py:28
  320.2 6.1 %collective-permute-start.13 = (bf16[2048,128]{1,0:T(8,128)(2,1)S(1)}, bf16[2048,128]{1,0:T(8,128)(2,1)S(1)}, u32[]{:S(2)}, u32[]{:S(2)}) collective-permute-start(bf16[2048,128]{1,0:T(8,128)(2,1)S(1)} %slice.71), channel_id=1, source_target_pairs={{0,1},{1,0},{2,3},{3,2},{4,5},{5,4},{6,7},{7,6},{8,9},{9,8},{10,11... | collective-permute-start | bytes 1572872 | tf_op jit(solution)/shard_map/ppermute | solution.py:32
  335.5 25.9 %all-to-all-start.7 = ((bf16[32,4,256]{2,1,0:T(4,128)(2,1)}), bf16[32,4,256]{2,1,0:T(4,128)(2,1)S(1)}, u32[]{:S(2)}, u32[]{:S(2)}) async-start(bf16[32,4,256]{2,1,0:T(4,128)(2,1)} %reshape.273), calls=%async_computation.7 | async-start | bytes 131072 | tf_op jit(solution)/shard_map/all_to_all | solution.py:28

commit v4 on v3

--- a/solution.py
+++ b/solution.py
@@ -41,20 +41,40 @@
     return lax.ppermute(value, "z", [((i + distance) % count, i) for i in range(count)])
 
 
-def gather_blocks(block):
-    near = swap_near(block)
-    first = lax.axis_index("y_lo") == 0
-    pair = jnp.stack([jnp.where(first, block, near), jnp.where(first, near, block)])
+def gather_z(block):
     z_count = lax.axis_size("z")
     quarter = z_count // 4
-    strided = jnp.stack([pair] + [from_above(pair, 4 * step) for step in range(1, quarter)])
+    strided = jnp.stack([block] + [from_above(block, 4 * step) for step in range(1, quarter)])
     below = from_above(strided, z_count - 1)
     below = jnp.concatenate([below[1:], below[:1]])
-    all_pairs = jnp.stack(
+    all_blocks = jnp.stack(
         [strided, from_above(strided, 1), from_above(strided, 2), below], axis=1
-    ).reshape(z_count, *pair.shape)
-    twice = jnp.concatenate([all_pairs, all_pairs])
+    ).reshape(z_count, *block.shape)
+    twice = jnp.concatenate([all_blocks, all_blocks])
     return lax.dynamic_slice_in_dim(twice, z_count - lax.axis_index("z"), z_count, 0)
+
+
+def trade_pair(blocks, axis_name):
+    first = lax.axis_index(axis_name) == 0
+    kept = jnp.where(first, blocks[0], blocks[1])
+    sent = jnp.where(first, blocks[1], blocks[0])
+    other = lax.ppermute(sent, axis_name, [(0, 1), (1, 0)])
+    return jnp.stack([jnp.where(first, kept, other), jnp.where(first, other, kept)])
+
+
+def trade_x(blocks):
+    count, here = lax.axis_size("x"), lax.axis_index("x")
+    turned = lax.dynamic_slice_in_dim(jnp.concatenate([blocks, blocks]), here, count, 0)
+    pieces = [turned[0]] + [
+        lax.ppermute(turned[step], "x", [(i, (i + step) % count) for i in range(count)])
+        for step in range(1, count)
+    ]
+    back = jnp.stack([pieces[(count - step) % count] for step in range(count)])
+    return lax.dynamic_slice_in_dim(jnp.concatenate([back, back]), count - here, count, 0)
+
+
+def other_first(pair):
+    return jnp.where(lax.axis_index("y_lo") == 0, pair[::-1], pair)
 
 
 def split_three(value):
@@ -106,7 +126,14 @@
             jnp.broadcast_to(scale_parts[:, None, :], (row_count, dp_count, features)),
         ]
     )
-    norm_block = exchange(norm_rows.transpose(2, 0, 1, 3), dp_axes)
+    norm_sent = norm_rows.transpose(2, 0, 1, 3).reshape(
+        lax.axis_size("x"), 2, 2, 3 * row_count, features
+    )
+    norm_block = trade_pair(norm_sent.transpose(2, 0, 1, 3, 4), "core")
+    norm_block = trade_pair(norm_block.transpose(2, 0, 1, 3, 4), "y_hi")
+    norm_block = trade_x(norm_block.transpose(2, 0, 1, 3, 4)).reshape(
+        dp_count, 3, row_count, features
+    )
     hidden_block = norm_block[:, 0].reshape(block_rows, features).astype(wide)
     resid_block = norm_block[:, 1].reshape(block_rows, features).astype(wide)
     scale_block = norm_block[:, 2, :, :3].astype(wide).reshape(block_rows, 3)
@@ -130,35 +157,44 @@
     unit_group = exchange(
         unit_rows.reshape(tensor_count, 2 * row_count, half_width), tensor_axes
     )
-    mlp_all = gather_blocks(mlp_block)
+    unit_group, mlp_block = lax.optimization_barrier((unit_group, mlp_block))
+    mlp_z = gather_z(mlp_block)
     unit_halves = (
-        unit_group.reshape(tensor_count, 2, row_count, half_width)
-        .transpose(1, 0, 2, 3)
+        other_first(unit_group.reshape(2, z_count, 2, row_count, half_width))
+        .transpose(2, 0, 1, 3, 4)
         .reshape(2, group_rows, half_width)
     )
     unit_halves = jnp.broadcast_to(
         unit_halves[None], (dp_count // core_count, core_count, group_rows, half_width)
     ).reshape(dp_count, group_rows, half_width)
     half_all = exchange(unit_halves, dp_axes).reshape(tokens, half_width)
-    half_all, mlp_all = lax.optimization_barrier((half_all, mlp_all))
+    half_all, mlp_z = lax.optimization_barrier((half_all, mlp_z))
     mlp_all = (
-        mlp_all.reshape(z_count, 2, dp_count, row_count, features)
-        .transpose(2, 1, 0, 3, 4)
+        jnp.stack([swap_near(mlp_z), mlp_z])
+        .reshape(2, z_count, dp_count, row_count, features)
+        .transpose(2, 0, 1, 3, 4)
         .reshape(tokens, features)
     )
     mlp_other = swap_cores(mlp_all)
     grad_half = half_all[:, :units]
     joined_half = half_all[:, units:]
 
-    partial_other = jnp.dot(grad_half, weight_other, preferred_element_type=wide)
-    partial_own = jnp.dot(grad_half, weight_kept, preferred_element_type=wide)
-    partial_value = (partial_own + swap_cores(partial_other)).reshape(
-        dp_count, 2, z_count * row_count, features
-    )
-    here = lax.axis_index("y_lo")
-    near_kept = lax.dynamic_index_in_dim(partial_value, here, 1, keepdims=False)
-    near_sent = lax.dynamic_index_in_dim(partial_value, 1 - here, 1, keepdims=False)
-    near_sum = near_kept + swap_near(near_sent.astype(narrow)).astype(wide)
+    sent_rows, kept_rows = (
+        half_all.reshape(dp_count, 2, z_count * row_count, half_width)[:, side].reshape(
+            -1, half_width
+        )
+        for side in range(2)
+    )
+    weight_other, weight_kept = (
+        jnp.pad(weight, ((0, half_width - units), (0, 0)))
+        for weight in (weight_other, weight_kept)
+    )
+    sent_other = swap_cores(jnp.dot(sent_rows, weight_other, preferred_element_type=wide))
+    sent_own = jnp.dot(sent_rows, weight_kept, preferred_element_type=wide)
+    near_part = swap_near((sent_own + sent_other).astype(narrow))
+    kept_other = swap_cores(jnp.dot(kept_rows, weight_other, preferred_element_type=wide))
+    kept_own = jnp.dot(kept_rows, weight_kept, preferred_element_type=wide)
+    near_sum = kept_own + kept_other + near_part.astype(wide)
     near_sum = (
         near_sum.astype(narrow)
         .reshape(dp_count, z_count, row_count, features)
@@ -177,15 +213,13 @@
     hidden_grad = (resid_block + scale_block * (lifted - normed * inner_mean)).astype(narrow)
     gain_part = jnp.sum(input_grad * normed, axis=0, keepdims=True)
 
-    sent_rows = block_rows + 8
+    rows_sent = block_rows + 8
     grad_sent = jnp.concatenate(
         [hidden_grad] + list(split_three(gain_part)) + [jnp.zeros((5, features), narrow)], axis=0
     )
-    grad_far = exchange(jnp.broadcast_to(grad_sent[None], (z_count, sent_rows, features)), "z")
+    grad_far = exchange(jnp.broadcast_to(grad_sent[None], (z_count, rows_sent, features)), "z")
     grad_near = swap_near(grad_far)
-    grad_pair = jnp.stack(
-        [jnp.where(here == 0, grad_far, grad_near), jnp.where(here == 0, grad_near, grad_far)]
-    )
+    grad_pair = jnp.stack([grad_near, grad_far])
     gain_parts = grad_pair[:, :, block_rows : block_rows + 3].astype(wide)
     gain_sum = jnp.sum(gain_parts, axis=(0, 1, 2))[None]
     grad_all = (
@@ -211,7 +245,8 @@
     gain_grad = joined_blocks[:, group_rows : group_rows + 3].astype(wide)
     gain_grad = ((gain_grad[:, 0] + gain_grad[:, 1]) + gain_grad[:, 2]).reshape(width)
     joined_total = jnp.sum(joined_blocks[:, :group_rows].astype(wide), axis=0).astype(narrow)
-    joined_grad = exchange(joined_total.reshape(tensor_count, row_count, inputs), tensor_axes)
+    joined_sent = other_first(joined_total.reshape(2, z_count, row_count, inputs))
+    joined_grad = exchange(joined_sent.reshape(tensor_count, row_count, inputs), tensor_axes)
     joined_grad = joined_grad.transpose(1, 0, 2).reshape(row_count, tensor_count * inputs)
 
     kept_grad = token_sum(grad_half, mlp_all)

time: 364 us -> 309 us (0.85)
  waiting for transfers between devices: 154 us -> 122 us
  starting transfers between devices: 158 us -> 137 us
  matrix products: 17.6 us -> 13.4 us
    all_to_all x8 -> x7, starting transfers between devices: 104 us -> 65.2 us  [exchange(): return lax.all_to_all(blocks, axes, split_axis=0, concat_axis=0, tiled=True)]
    all_to_all x8 -> x7, waiting for transfers between devices: 107 us -> 78.4 us  [exchange(): return lax.all_to_all(blocks, axes, split_axis=0, concat_axis=0, tiled=True)]
    ppermute x0 -> x5, starting transfers between devices: none -> 22.6 us  [the longest x2 13.3 us: trade_pair(): other = lax.ppermute(sent, axis_name, [(0, 1), (1, 0)])]
    ppermute x6, waiting for transfers between devices: 20.1 us -> 13.8 us  [from_above(): lax.ppermute(value, 'z', [((i + distance) % count, i) for i in range(coun...]
    dot_general x2 -> x4, matrix products: 8.04 us -> 2.85 us  [the longest x1 0.71 us: shards(): sent_own = jnp.dot(sent_rows, weight_kept, preferred_element_type=wide)]
    ppermute x0 -> x5, waiting for transfers between devices: none -> 4.75 us  [the longest x3 2.95 us: trade_x(): lax.ppermute(turned[step], 'x', [(i, (i + step) % count) for i in range(c...]
    ppermute x6, starting transfers between devices: 26.7 us -> 22.3 us  [from_above(): lax.ppermute(value, 'z', [((i + distance) % count, i) for i in range(coun...]
    ppermute x5 -> x6, starting transfers between devices: 20.6 us -> 21.4 us  [swap_cores(): return lax.ppermute(value, 'core', [(0, 1), (1, 0)])]
  transfers between devices with their start and end apart: 22 -> 27, of which waited for: 12 -> 15; matrix products, arithmetic and copies ran while one was open for 8% -> 11% of each run, Pallas kernels for 0% -> 0%
where the time goes in v4:
time: 309 us; the launch traced here: 307 us
  starting transfers between devices  137 us (44%)
  waiting for transfers between devices  122 us (39%)
  local copies, waits for them, and re-layouts  19.7 us (6%)
  matrix products  13.4 us (4%)
  other arithmetic  12.9 us (4%)
    all_to_all x7, waiting for transfers between devices, exchange(): return lax.all_to_all(blocks, axes, split_axis=0, concat_axis=0, tiled=True)  78.4 us
    all_to_all x7, starting transfers between devices, exchange(): return lax.all_to_all(blocks, axes, split_axis=0, concat_axis=0, tiled=True)  65.2 us
    ppermute x3, waiting for transfers between devices, swap_near(): return lax.ppermute(value, 'y_lo', [(0, 1), (1, 0)])  25 us
    ppermute x6, starting transfers between devices, from_above(): lax.ppermute(value, 'z', [((i + distance) % count, i) for i in range(coun...  22.3 us
    ppermute x6, starting transfers between devices, swap_cores(): return lax.ppermute(value, 'core', [(0, 1), (1, 0)])  21.4 us
    ppermute x6, waiting for transfers between devices, from_above(): lax.ppermute(value, 'z', [((i + distance) % count, i) for i in range(coun...  13.8 us
    ppermute x2, starting transfers between devices, trade_pair(): other = lax.ppermute(sent, axis_name, [(0, 1), (1, 0)])  13.3 us
    dot_general x4, matrix products, token_sum(): lax.dot_general(left, right, (((0,), (0,)), ((), ())), preferred_element_...  10.1 us
  transfers between devices with their start and end apart: 27, of which 15 were waited for; matrix products, arithmetic and copies ran while one was open for 11% of the time, Pallas kernels for 0%

profile of v4, /device:TPU:1, one launch (start us, length us, event | category | flops | bytes accessed | tf_op | source)
XLA Modules:
  0.0 307.0 jit_solution(12793262018963768321)
XLA Ops:
  2.9 8.8 %collective-permute-start = (bf16[4,2,12,256]{3,1,2,0:T(2,128)(2,1)S(1)}, bf16[4,2,12,256]{3,1,2,0:T(2,128)(2,1)S(1)}, u32[]{:S(2)}, u32[]{:S(2)}) collective-permute-start(bf16[4,2,12,256]{3,1,2,0:T(2,128)(2,1)S(1)} %bitcast.166), channel_id=1, source_target_pairs={{0,1},{1,0},{2,3},{3,2},{4,5},{5,4},{6,7},{7,6},{8,9},{9,8},{10,11... | collective-permute-start | bytes 147464 | tf_op jit(solution)/shard_map/ppermute | solution.py:61
  16.1 10.8 %all-to-all-start = ((bf16[32,8,1024]{2,1,0:T(8,128)(2,1)}), bf16[32,8,1024]{2,1,0:T(8,128)(2,1)S(1)}, u32[]{:S(2)}, u32[]{:S(2)}) async-start(bf16[32,8,1024]{2,1,0:T(8,128)(2,1)} %reshape.283), calls=%async_computation | async-start | bytes 1048576 | tf_op jit(solution)/shard_map/all_to_all | solution.py:28
  27.5 4.5 %collective-permute-start.1 = (bf16[2,4,12,256]{3,1,2,0:T(4,128)(2,1)S(1)}, bf16[2,4,12,256]{3,1,2,0:T(4,128)(2,1)S(1)}, u32[]{:S(2)}, u32[]{:S(2)}) collective-permute-start(bf16[2,4,12,256]{3,1,2,0:T(4,128)(2,1)S(1)} %bitcast.167), channel_id=1, source_target_pairs={{0,2},{2,0},{1,3},{3,1},{4,6},{6,4},{5,7},{7,5},{8,10},{10,8},{9,1... | collective-permute-start | bytes 147464 | tf_op jit(solution)/shard_map/ppermute | solution.py:61
  34.3 4.4 %collective-permute-start.2 = (bf16[2,2,12,256]{3,1,2,0:T(2,128)(2,1)S(1)}, bf16[2,2,12,256]{3,1,2,0:T(2,128)(2,1)S(1)}, u32[]{:S(2)}, u32[]{:S(2)}) collective-permute-start(bf16[2,2,12,256]{3,1,2,0:T(2,128)(2,1)S(1)} %bitcast.173), channel_id=1, source_target_pairs={{0,12},{4,0},{8,4},{12,8},{1,13},{5,1},{9,5},{13,9},{2,14},{6,2},{... | collective-permute-start | bytes 73736 | tf_op jit(solution)/shard_map/ppermute | solution.py:69
  45.0 2.5 collective-permute-done.4
  50.1 7.5 %all-to-all-done = bf16[32,8,1024]{2,1,0:T(8,128)(2,1)S(1)} async-done(((bf16[32,8,1024]{2,1,0:T(8,128)(2,1)}), bf16[32,8,1024]{2,1,0:T(8,128)(2,1)S(1)}, u32[]{:S(2)}, u32[]{:S(2)}) %all-to-all-start) | async-done | bytes 524320 | tf_op jit(solution)/shard_map/all_to_all | solution.py:28
  58.8 2.6 broadcast_in_dim.17
  61.3 7.8 %all-to-all-start.1 = ((bf16[16,128,1024]{2,1,0:T(8,128)(2,1)}), bf16[16,128,1024]{2,1,0:T(8,128)(2,1)}, u32[]{:S(2)}, u32[]{:S(2)}) async-start(bf16[16,128,1024]{2,1,0:T(8,128)(2,1)} %bitcast.143), calls=%async_computation.1 | async-start | bytes 8388608 | tf_op jit(solution)/shard_map/all_to_all | solution.py:28
  71.5 9.2 %collective-permute-start.6 = (bf16[64,256]{1,0:T(8,128)(2,1)S(1)}, bf16[64,256]{1,0:T(8,128)(2,1)S(1)}, u32[]{:S(2)}, u32[]{:S(2)}) collective-permute-start(bf16[64,256]{1,0:T(8,128)(2,1)S(1)} %multiply_convert_fusion), channel_id=1, source_target_pairs={{128,0},{144,16},{160,32},{176,48},{192,64},{208,80},{224,96},{240... | collective-permute-start | bytes 98312 | tf_op jit(solution)/shard_map/ppermute | solution.py:41
  84.8 8.0 %collective-permute-done.5 = bf16[64,256]{1,0:T(8,128)(2,1)S(1)} collective-permute-done((bf16[64,256]{1,0:T(8,128)(2,1)S(1)}, bf16[64,256]{1,0:T(8,128)(2,1)S(1)}, u32[]{:S(2)}, u32[]{:S(2)}) %collective-permute-start.5) | collective-permute-done | bytes 32800 | tf_op jit(solution)/shard_map/ppermute | solution.py:41
  97.3 4.0 %collective-permute-start.8 = (bf16[4,64,256]{2,1,0:T(8,128)(2,1)S(1)}, bf16[4,64,256]{2,1,0:T(8,128)(2,1)S(1)}, u32[]{:S(2)}, u32[]{:S(2)}) collective-permute-start(bf16[4,64,256]{2,1,0:T(8,128)(2,1)S(1)} %get-tuple-element.34), channel_id=1, source_target_pairs={{16,0},{32,16},{48,32},{64,48},{80,64},{96,80},{112,96},{128,112},... | collective-permute-start | bytes 393224 | tf_op jit(solution)/shard_map/ppermute | solution.py:41
  101.4 2.9 collective-permute-start.11
  104.4 4.0 %collective-permute-done.8 = bf16[4,64,256]{2,1,0:T(8,128)(2,1)S(1)} collective-permute-done((bf16[4,64,256]{2,1,0:T(8,128)(2,1)S(1)}, bf16[4,64,256]{2,1,0:T(8,128)(2,1)S(1)}, u32[]{:S(2)}, u32[]{:S(2)}) %collective-permute-start.8) | collective-permute-done | bytes 131104 | tf_op jit(solution)/shard_map/ppermute | solution.py:41
  108.7 13.1 %all-to-all-done.1 = bf16[16,128,1024]{2,1,0:T(8,128)(2,1)} async-done(((bf16[16,128,1024]{2,1,0:T(8,128)(2,1)}), bf16[16,128,1024]{2,1,0:T(8,128)(2,1)}, u32[]{:S(2)}, u32[]{:S(2)}) %all-to-all-start.1) | async-done | bytes 4194336 | tf_op jit(solution)/shard_map/all_to_all | solution.py:28
  121.8 2.7 fusion.40
  134.1 12.6 %collective-permute-done.14 = bf16[1024,256]{1,0:T(8,128)(2,1)S(1)} collective-permute-done((bf16[1024,256]{1,0:T(8,128)(2,1)S(1)}, bf16[1024,256]{1,0:T(8,128)(2,1)S(1)}, u32[]{:S(2)}, u32[]{:S(2)}) %collective-permute-start.14) | collective-permute-done | bytes 524320 | tf_op jit(solution)/shard_map/ppermute | solution.py:36
  148.1 5.0 %all-to-all-start.2 = ((bf16[16,64,256]{2,1,0:T(8,128)(2,1)}), bf16[16,64,256]{2,1,0:T(8,128)(2,1)S(1)}, u32[]{:S(2)}, u32[]{:S(2)}) async-start(bf16[16,64,256]{2,1,0:T(8,128)(2,1)} %copy.309), calls=%async_computation.2 | async-start | bytes 1048576 | tf_op jit(solution)/shard_map/all_to_all | solution.py:28
  153.4 22.7 %all-to-all-done.2 = bf16[16,64,256]{2,1,0:T(8,128)(2,1)S(1)} async-done(((bf16[16,64,256]{2,1,0:T(8,128)(2,1)}), bf16[16,64,256]{2,1,0:T(8,128)(2,1)S(1)}, u32[]{:S(2)}, u32[]{:S(2)}) %all-to-all-start.2) | async-done | bytes 524320 | tf_op jit(solution)/shard_map/all_to_all | solution.py:28
  177.1 19.4 %all-to-all-start.3 = ((f32[16,1,64]{2,1,0:T(1,128)}), f32[16,1,64]{2,1,0:T(1,128)S(1)}, u32[]{:S(2)}, u32[]{:S(2)}) async-start(f32[16,1,64]{2,1,0:T(1,128)} %broadcast_in_dim.19), calls=%async_computation.3 | async-start | bytes 16384 | tf_op jit(solution)/shard_map/all_to_all | solution.py:28
  196.6 6.9 %all-to-all-done.3 = f32[16,1,64]{2,1,0:T(1,128)S(1)} async-done(((f32[16,1,64]{2,1,0:T(1,128)}), f32[16,1,64]{2,1,0:T(1,128)S(1)}, u32[]{:S(2)}, u32[]{:S(2)}) %all-to-all-start.3) | async-done | bytes 4128 | tf_op jit(solution)/shard_map/all_to_all | solution.py:28
  204.5 6.2 %all-to-all-start.4 = ((bf16[16,72,256]{2,1,0:T(8,128)(2,1)}), bf16[16,72,256]{2,1,0:T(8,128)(2,1)S(1)}, u32[]{:S(2)}, u32[]{:S(2)}) async-start(bf16[16,72,256]{2,1,0:T(8,128)(2,1)} %broadcast_in_dim.21), calls=%async_computation.4 | async-start | bytes 1179648 | tf_op jit(solution)/shard_map/all_to_all | solution.py:28
  212.8 12.3 %collective-permute-done.16 = bf16[16,64,256]{2,1,0:T(8,128)(2,1)S(1)} collective-permute-done((bf16[16,64,256]{2,1,0:T(8,128)(2,1)S(1)}, bf16[16,64,256]{2,1,0:T(8,128)(2,1)S(1)}, u32[]{:S(2)}, u32[]{:S(2)}) %collective-permute-start.16) | collective-permute-done | bytes 524320 | tf_op jit(solution)/shard_map/ppermute | solution.py:36
  226.1 3.8 %collective-permute-start.17 = (bf16[2048,256]{1,0:T(8,128)(2,1)S(1)}, bf16[2048,256]{1,0:T(8,128)(2,1)S(1)}, u32[]{:S(2)}, u32[]{:S(2)}) collective-permute-start(bf16[2048,256]{1,0:T(8,128)(2,1)S(1)} %reshape.297), channel_id=1, source_target_pairs={{0,1},{1,0},{2,3},{3,2},{4,5},{5,4},{6,7},{7,6},{8,9},{9,8},{10,11... | collective-permute-start | bytes 3145736 | tf_op jit(solution)/shard_map/ppermute | solution.py:32
  229.9 6.1 %all-to-all-done.4 = bf16[16,72,256]{2,1,0:T(8,128)(2,1)S(1)} async-done(((bf16[16,72,256]{2,1,0:T(8,128)(2,1)}), bf16[16,72,256]{2,1,0:T(8,128)(2,1)S(1)}, u32[]{:S(2)}, u32[]{:S(2)}) %all-to-all-start.4) | async-done | bytes 589856 | tf_op jit(solution)/shard_map/all_to_all | solution.py:28
  240.0 8.5 %collective-permute-start.19 = (bf16[2048,128]{1,0:T(8,128)(2,1)}, bf16[2048,128]{1,0:T(8,128)(2,1)}, u32[]{:S(2)}, u32[]{:S(2)}) collective-permute-start(bf16[2048,128]{1,0:T(8,128)(2,1)} %slice.115), channel_id=1, source_target_pairs={{0,1},{1,0},{2,3},{3,2},{4,5},{5,4},{6,7},{7,6},{8,9},{9,8},{10,11... | collective-permute-start | bytes 1572872 | tf_op jit(solution)/shard_map/ppermute | solution.py:32
  248.6 4.1 %fusion = f32[896,256]{1,0:T(8,128)} fusion(bf16[2048,256]{1,0:T(8,128)(2,1)S(1)} %collective-permute-done.17, bf16[2048,1024]{1,0:T(8,128)(2,1)} %bitcast.31), kind=kOutput, calls=%fused_computation | convolution fusion | flops 939524096 | bytes 5636096 | tf_op jit(solution)/shard_map/dot_general | solution.py:24
  257.7 4.0 %all-to-all-start.5 = ((bf16[16,144,256]{2,1,0:T(8,128)(2,1)}), bf16[16,144,256]{2,1,0:T(8,128)(2,1)S(1)}, u32[]{:S(2)}, u32[]{:S(2)}) async-start(bf16[16,144,256]{2,1,0:T(8,128)(2,1)} %pad_maximum_fusion), calls=%async_computation.5 | async-start | bytes 2359296 | tf_op jit(solution)/shard_map/all_to_all | solution.py:28
  261.6 3.2 %fusion.2 = f32[896,256]{1,0:T(8,128)S(1)} fusion(bf16[2048,256]{1,0:T(8,128)(2,1)S(1)} %reshape.297, bf16[2048,1024]{1,0:T(8,128)(2,1)} %bitcast.31), kind=kOutput, calls=%fused_computation.2 | convolution fusion | flops 939524096 | bytes 5636096 | tf_op jit(solution)/shard_map/dot_general | solution.py:24
  264.9 2.5 broadcast_select_fusion
  270.9 9.4 %all-to-all-done.5 = bf16[16,144,256]{2,1,0:T(8,128)(2,1)S(1)} async-done(((bf16[16,144,256]{2,1,0:T(8,128)(2,1)}), bf16[16,144,256]{2,1,0:T(8,128)(2,1)S(1)}, u32[]{:S(2)}, u32[]{:S(2)}) %all-to-all-start.5) | async-done | bytes 1179680 | tf_op jit(solution)/shard_map/all_to_all | solution.py:28
  281.2 12.0 %all-to-all-start.6 = ((bf16[32,4,256]{2,1,0:T(4,128)(2,1)}), bf16[32,4,256]{2,1,0:T(4,128)(2,1)S(1)}, u32[]{:S(2)}, u32[]{:S(2)}) async-start(bf16[32,4,256]{2,1,0:T(4,128)(2,1)} %bitcast.54), calls=%async_computation.6 | async-start | bytes 131072 | tf_op jit(solution)/shard_map/all_to_all | solution.py:28
  293.8 12.6 %all-to-all-done.6 = bf16[32,4,256]{2,1,0:T(4,128)(2,1)S(1)} async-done(((bf16[32,4,256]{2,1,0:T(4,128)(2,1)}), bf16[32,4,256]{2,1,0:T(4,128)(2,1)S(1)}, u32[]{:S(2)}, u32[]{:S(2)}) %all-to-all-start.6) | async-done | bytes 65568 | tf_op jit(solution)/shard_map/all_to_all | solution.py:28
  (147 shorter events, 61.2 us)
Async XLA Ops:
  0.6 255.4 %copy-start = (bf16[256,256]{1,0:T(8,128)(2,1)S(1)}, bf16[256,256]{1,0:T(8,128)(2,1)}, u32[]{:S(2)}) copy-start(bf16[256,256]{1,0:T(8,128)(2,1)} %param.19) | copy-start | bytes 393220
  2.9 24.0 %collective-permute-start = (bf16[4,2,12,256]{3,1,2,0:T(2,128)(2,1)S(1)}, bf16[4,2,12,256]{3,1,2,0:T(2,128)(2,1)S(1)}, u32[]{:S(2)}, u32[]{:S(2)}) collective-permute-start(bf16[4,2,12,256]{3,1,2,0:T(2,128)(2,1)S(1)} %bitcast.166), channel_id=1, source_target_pairs={{0,1},{1,0},{2,3},{3,2},{4,5},{5,4},{6,7},{7,6},{8,9},{9,8},{10,11... | collective-permute-start | bytes 147464 | tf_op jit(solution)/shard_map/ppermute | solution.py:61
  16.1 41.6 %all-to-all-start = ((bf16[32,8,1024]{2,1,0:T(8,128)(2,1)}), bf16[32,8,1024]{2,1,0:T(8,128)(2,1)S(1)}, u32[]{:S(2)}, u32[]{:S(2)}) async-start(bf16[32,8,1024]{2,1,0:T(8,128)(2,1)} %reshape.283), calls=%async_computation | async-start | bytes 1048576 | tf_op jit(solution)/shard_map/all_to_all | solution.py:28
  27.5 6.3 %collective-permute-start.1 = (bf16[2,4,12,256]{3,1,2,0:T(4,128)(2,1)S(1)}, bf16[2,4,12,256]{3,1,2,0:T(4,128)(2,1)S(1)}, u32[]{:S(2)}, u32[]{:S(2)}) collective-permute-start(bf16[2,4,12,256]{3,1,2,0:T(4,128)(2,1)S(1)} %bitcast.167), channel_id=1, source_target_pairs={{0,2},{2,0},{1,3},{3,1},{4,6},{6,4},{5,7},{7,5},{8,10},{10,8},{9,1... | collective-permute-start | bytes 147464 | tf_op jit(solution)/shard_map/ppermute | solution.py:61
  34.3 10.2 %collective-permute-start.2 = (bf16[2,2,12,256]{3,1,2,0:T(2,128)(2,1)S(1)}, bf16[2,2,12,256]{3,1,2,0:T(2,128)(2,1)S(1)}, u32[]{:S(2)}, u32[]{:S(2)}) collective-permute-start(bf16[2,2,12,256]{3,1,2,0:T(2,128)(2,1)S(1)} %bitcast.173), channel_id=1, source_target_pairs={{0,12},{4,0},{8,4},{12,8},{1,13},{5,1},{9,5},{13,9},{2,14},{6,2},{... | collective-permute-start | bytes 73736 | tf_op jit(solution)/shard_map/ppermute | solution.py:69
  38.7 6.2 %collective-permute-start.3 = (bf16[2,2,12,256]{3,1,2,0:T(2,128)(2,1)S(1)}, bf16[2,2,12,256]{3,1,2,0:T(2,128)(2,1)S(1)}, u32[]{:S(2)}, u32[]{:S(2)}) collective-permute-start(bf16[2,2,12,256]{3,1,2,0:T(2,128)(2,1)S(1)} %bitcast.175), channel_id=1, source_target_pairs={{0,8},{4,12},{8,0},{12,4},{1,9},{5,13},{9,1},{13,5},{2,10},{6,14},... | collective-permute-start | bytes 73736 | tf_op jit(solution)/shard_map/ppermute | solution.py:69
  41.2 6.3 %collective-permute-start.4 = (bf16[2,2,12,256]{3,1,2,0:T(2,128)(2,1)S(1)}, bf16[2,2,12,256]{3,1,2,0:T(2,128)(2,1)S(1)}, u32[]{:S(2)}, u32[]{:S(2)}) collective-permute-start(bf16[2,2,12,256]{3,1,2,0:T(2,128)(2,1)S(1)} %bitcast.177), channel_id=1, source_target_pairs={{0,4},{4,8},{8,12},{12,0},{1,5},{5,9},{9,13},{13,1},{2,6},{6,10},{... | collective-permute-start | bytes 73736 | tf_op jit(solution)/shard_map/ppermute | solution.py:69
  61.3 40.0 %copy-start.1 = (bf16[896,256]{1,0:T(8,128)(2,1)S(1)}, bf16[896,256]{1,0:T(8,128)(2,1)}, u32[]{:S(2)}) copy-start(bf16[896,256]{1,0:T(8,128)(2,1)} %param.18) | copy-start | bytes 1376260
  61.3 40.0 %copy-start.2 = (bf16[896,256]{1,0:T(8,128)(2,1)S(1)}, bf16[896,256]{1,0:T(8,128)(2,1)}, u32[]{:S(2)}) copy-start(bf16[896,256]{1,0:T(8,128)(2,1)} %param.17) | copy-start | bytes 1376260
  61.3 60.5 %all-to-all-start.1 = ((bf16[16,128,1024]{2,1,0:T(8,128)(2,1)}), bf16[16,128,1024]{2,1,0:T(8,128)(2,1)}, u32[]{:S(2)}, u32[]{:S(2)}) async-start(bf16[16,128,1024]{2,1,0:T(8,128)(2,1)} %bitcast.143), calls=%async_computation.1 | async-start | bytes 8388608 | tf_op jit(solution)/shard_map/all_to_all | solution.py:28
  69.1 13.9 %collective-permute-start.7 = (bf16[64,256]{1,0:T(8,128)(2,1)S(1)}, bf16[64,256]{1,0:T(8,128)(2,1)S(1)}, u32[]{:S(2)}, u32[]{:S(2)}) collective-permute-start(bf16[64,256]{1,0:T(8,128)(2,1)S(1)} %multiply_convert_fusion), channel_id=1, source_target_pairs={{192,0},{208,16},{224,32},{240,48},{0,64},{16,80},{32,96},{48,112}... | collective-permute-start | bytes 98312 | tf_op jit(solution)/shard_map/ppermute | solution.py:41
  71.5 13.4 %collective-permute-start.6 = (bf16[64,256]{1,0:T(8,128)(2,1)S(1)}, bf16[64,256]{1,0:T(8,128)(2,1)S(1)}, u32[]{:S(2)}, u32[]{:S(2)}) collective-permute-start(bf16[64,256]{1,0:T(8,128)(2,1)S(1)} %multiply_convert_fusion), channel_id=1, source_target_pairs={{128,0},{144,16},{160,32},{176,48},{192,64},{208,80},{224,96},{240... | collective-permute-start | bytes 98312 | tf_op jit(solution)/shard_map/ppermute | solution.py:41
  80.7 12.2 %collective-permute-start.5 = (bf16[64,256]{1,0:T(8,128)(2,1)S(1)}, bf16[64,256]{1,0:T(8,128)(2,1)S(1)}, u32[]{:S(2)}, u32[]{:S(2)}) collective-permute-start(bf16[64,256]{1,0:T(8,128)(2,1)S(1)} %multiply_convert_fusion), channel_id=1, source_target_pairs={{64,0},{80,16},{96,32},{112,48},{128,64},{144,80},{160,96},{176,11... | collective-permute-start | bytes 98312 | tf_op jit(solution)/shard_map/ppermute | solution.py:41
  92.9 11.4 %collective-permute-start.10 = (bf16[4,64,256]{2,1,0:T(8,128)(2,1)S(1)}, bf16[4,64,256]{2,1,0:T(8,128)(2,1)S(1)}, u32[]{:S(2)}, u32[]{:S(2)}) collective-permute-start(bf16[4,64,256]{2,1,0:T(8,128)(2,1)S(1)} %get-tuple-element.34), channel_id=1, source_target_pairs={{240,0},{0,16},{16,32},{32,48},{48,64},{64,80},{80,96},{96,112},{1... | collective-permute-start | bytes 393224 | tf_op jit(solution)/shard_map/ppermute | solution.py:41
  94.9 9.5 %collective-permute-start.9 = (bf16[4,64,256]{2,1,0:T(8,128)(2,1)S(1)}, bf16[4,64,256]{2,1,0:T(8,128)(2,1)S(1)}, u32[]{:S(2)}, u32[]{:S(2)}) collective-permute-start(bf16[4,64,256]{2,1,0:T(8,128)(2,1)S(1)} %get-tuple-element.34), channel_id=1, source_target_pairs={{32,0},{48,16},{64,32},{80,48},{96,64},{112,80},{128,96},{144,112}... | collective-permute-start | bytes 393224 | tf_op jit(solution)/shard_map/ppermute | solution.py:41
  97.3 11.0 %collective-permute-start.8 = (bf16[4,64,256]{2,1,0:T(8,128)(2,1)S(1)}, bf16[4,64,256]{2,1,0:T(8,128)(2,1)S(1)}, u32[]{:S(2)}, u32[]{:S(2)}) collective-permute-start(bf16[4,64,256]{2,1,0:T(8,128)(2,1)S(1)} %get-tuple-element.34), channel_id=1, source_target_pairs={{16,0},{32,16},{48,32},{64,48},{80,64},{96,80},{112,96},{128,112},... | collective-permute-start | bytes 393224 | tf_op jit(solution)/shard_map/ppermute | solution.py:41
  101.4 23.2 %collective-permute-start.11 = (bf16[896,256]{1,0:T(8,128)(2,1)S(1)}, bf16[896,256]{1,0:T(8,128)(2,1)S(1)}, u32[]{:S(2)}, u32[]{:S(2)}) collective-permute-start(bf16[896,256]{1,0:T(8,128)(2,1)S(1)} %get-tuple-element.21), channel_id=1, source_target_pairs={{0,1},{1,0},{2,3},{3,2},{4,5},{5,4},{6,7},{7,6},{8,9},{9,8},{10,11... | collective-permute-start | bytes 1376264 | tf_op jit(solution)/shard_map/ppermute | solution.py:32
  125.3 5.8 %collective-permute-start.13 = (f32[1024,256]{1,0:T(8,128)S(1)}, f32[1024,256]{1,0:T(8,128)S(1)}, u32[]{:S(2)}, u32[]{:S(2)}) collective-permute-start(f32[1024,256]{1,0:T(8,128)S(1)} %fusion.7), channel_id=1, source_target_pairs={{0,1},{1,0},{2,3},{3,2},{4,5},{5,4},{6,7},{7,6},{8,9},{9,8},{10,11... | collective-permute-start | bytes 3145736 | tf_op jit(solution)/shard_map/ppermute | solution.py:32
  127.9 6.1 %collective-permute-start.12 = (f32[1024,256]{1,0:T(8,128)S(1)}, f32[1024,256]{1,0:T(8,128)S(1)}, u32[]{:S(2)}, u32[]{:S(2)}) collective-permute-start(f32[1024,256]{1,0:T(8,128)S(1)} %fusion.9), channel_id=1, source_target_pairs={{0,1},{1,0},{2,3},{3,2},{4,5},{5,4},{6,7},{7,6},{8,9},{9,8},{10,11... | collective-permute-start | bytes 3145736 | tf_op jit(solution)/shard_map/ppermute | solution.py:32
  131.3 15.4 %collective-permute-start.14 = (bf16[1024,256]{1,0:T(8,128)(2,1)S(1)}, bf16[1024,256]{1,0:T(8,128)(2,1)S(1)}, u32[]{:S(2)}, u32[]{:S(2)}) collective-permute-start(bf16[1024,256]{1,0:T(8,128)(2,1)S(1)} %add_convert_fusion.1), channel_id=1, source_target_pairs={{0,256},{256,0},{1,257},{257,1},{2,258},{258,2},{3,259},{259,3},{4... | collective-permute-start | bytes 1572872 | tf_op jit(solution)/shard_map/ppermute | solution.py:36
  148.1 28.0 %all-to-all-start.2 = ((bf16[16,64,256]{2,1,0:T(8,128)(2,1)}), bf16[16,64,256]{2,1,0:T(8,128)(2,1)S(1)}, u32[]{:S(2)}, u32[]{:S(2)}) async-start(bf16[16,64,256]{2,1,0:T(8,128)(2,1)} %copy.309), calls=%async_computation.2 | async-start | bytes 1048576 | tf_op jit(solution)/shard_map/all_to_all | solution.py:28
  177.1 26.3 %all-to-all-start.3 = ((f32[16,1,64]{2,1,0:T(1,128)}), f32[16,1,64]{2,1,0:T(1,128)S(1)}, u32[]{:S(2)}, u32[]{:S(2)}) async-start(f32[16,1,64]{2,1,0:T(1,128)} %broadcast_in_dim.19), calls=%async_computation.3 | async-start | bytes 16384 | tf_op jit(solution)/shard_map/all_to_all | solution.py:28
  204.5 31.6 %all-to-all-start.4 = ((bf16[16,72,256]{2,1,0:T(8,128)(2,1)}), bf16[16,72,256]{2,1,0:T(8,128)(2,1)S(1)}, u32[]{:S(2)}, u32[]{:S(2)}) async-start(bf16[16,72,256]{2,1,0:T(8,128)(2,1)} %broadcast_in_dim.21), calls=%async_computation.4 | async-start | bytes 1179648 | tf_op jit(solution)/shard_map/all_to_all | solution.py:28
  210.7 14.4 %collective-permute-start.16 = (bf16[16,64,256]{2,1,0:T(8,128)(2,1)S(1)}, bf16[16,64,256]{2,1,0:T(8,128)(2,1)S(1)}, u32[]{:S(2)}, u32[]{:S(2)}) collective-permute-start(bf16[16,64,256]{2,1,0:T(8,128)(2,1)S(1)} %fusion.6), channel_id=1, source_target_pairs={{0,256},{256,0},{1,257},{257,1},{2,258},{258,2},{3,259},{259,3},{4... | collective-permute-start | bytes 1572872 | tf_op jit(solution)/shard_map/ppermute | solution.py:36
  226.1 22.4 %collective-permute-start.17 = (bf16[2048,256]{1,0:T(8,128)(2,1)S(1)}, bf16[2048,256]{1,0:T(8,128)(2,1)S(1)}, u32[]{:S(2)}, u32[]{:S(2)}) collective-permute-start(bf16[2048,256]{1,0:T(8,128)(2,1)S(1)} %reshape.297), channel_id=1, source_target_pairs={{0,1},{1,0},{2,3},{3,2},{4,5},{5,4},{6,7},{7,6},{8,9},{9,8},{10,11... | collective-permute-start | bytes 3145736 | tf_op jit(solution)/shard_map/ppermute | solution.py:32
  236.1 18.5 %collective-permute-start.15 = (bf16[16,72,256]{2,0,1:T(8,128)(2,1)S(1)}, bf16[16,72,256]{2,0,1:T(8,128)(2,1)S(1)}, u32[]{:S(2)}, u32[]{:S(2)}) collective-permute-start(bf16[16,72,256]{2,0,1:T(8,128)(2,1)S(1)} %copy.353), channel_id=1, source_target_pairs={{0,256},{256,0},{1,257},{257,1},{2,258},{258,2},{3,259},{259,3},{4... | collective-permute-start | bytes 1769480 | tf_op jit(solution)/shard_map/ppermute | solution.py:36
  240.0 28.7 %collective-permute-start.19 = (bf16[2048,128]{1,0:T(8,128)(2,1)}, bf16[2048,128]{1,0:T(8,128)(2,1)}, u32[]{:S(2)}, u32[]{:S(2)}) collective-permute-start(bf16[2048,128]{1,0:T(8,128)(2,1)} %slice.115), channel_id=1, source_target_pairs={{0,1},{1,0},{2,3},{3,2},{4,5},{5,4},{6,7},{7,6},{8,9},{9,8},{10,11... | collective-permute-start | bytes 1572872 | tf_op jit(solution)/shard_map/ppermute | solution.py:32
  252.7 12.2 %collective-permute-start.18 = (f32[896,256]{1,0:T(8,128)}, f32[896,256]{1,0:T(8,128)}, u32[]{:S(2)}, u32[]{:S(2)}) collective-permute-start(f32[896,256]{1,0:T(8,128)} %fusion), channel_id=1, source_target_pairs={{0,1},{1,0},{2,3},{3,2},{4,5},{5,4},{6,7},{7,6},{8,9},{9,8},{10,11... | collective-permute-start | bytes 2752520 | tf_op jit(solution)/shard_map/ppermute | solution.py:32
  257.7 22.7 %all-to-all-start.5 = ((bf16[16,144,256]{2,1,0:T(8,128)(2,1)}), bf16[16,144,256]{2,1,0:T(8,128)(2,1)S(1)}, u32[]{:S(2)}, u32[]{:S(2)}) async-start(bf16[16,144,256]{2,1,0:T(8,128)(2,1)} %pad_maximum_fusion), calls=%async_computation.5 | async-start | bytes 2359296 | tf_op jit(solution)/shard_map/all_to_all | solution.py:28
  281.2 25.2 %all-to-all-start.6 = ((bf16[32,4,256]{2,1,0:T(4,128)(2,1)}), bf16[32,4,256]{2,1,0:T(4,128)(2,1)S(1)}, u32[]{:S(2)}, u32[]{:S(2)}) async-start(bf16[32,4,256]{2,1,0:T(4,128)(2,1)} %bitcast.54), calls=%async_computation.6 | async-start | bytes 131072 | tf_op jit(solution)/shard_map/all_to_all | solution.py:28

commit v5 on v4

--- a/solution.py
+++ b/solution.py
@@ -115,6 +115,21 @@
     weight_kept = jnp.where(on_first, gate_weight, up_weight)
     weight_other = swap_cores(jnp.where(on_first, up_weight, gate_weight))
 
+    gate_grad, up_grad = swiglu_back(gate_act, up_act, product_grad)
+    joined_rows = joined_in.reshape(row_count, tensor_count, 2, half_inputs)
+    half_width = units + half_inputs
+    gate_rows = jnp.concatenate(
+        [gate_grad.reshape(row_count, tensor_count, units), joined_rows[:, :, 0]], axis=2
+    )
+    up_rows = jnp.concatenate(
+        [up_grad.reshape(row_count, tensor_count, units), joined_rows[:, :, 1]], axis=2
+    )
+    unit_rows = jnp.stack([gate_rows, up_rows]).transpose(2, 0, 1, 3)
+    unit_rows, hidden, resid_grad = lax.optimization_barrier((unit_rows, hidden, resid_grad))
+    unit_group = exchange(
+        unit_rows.reshape(tensor_count, 2 * row_count, half_width), tensor_axes
+    )
+
     hidden_wide = hidden.astype(wide)
     row_scale = lax.rsqrt(jnp.mean(hidden_wide * hidden_wide, axis=1, keepdims=True) + epsilon)
     scale_parts = jnp.concatenate(split_three(row_scale), axis=1)
@@ -144,19 +159,6 @@
     normed = hidden_block * scale_block
     mlp_block = (normed * gain_block).astype(narrow)
 
-    gate_grad, up_grad = swiglu_back(gate_act, up_act, product_grad)
-    joined_rows = joined_in.reshape(row_count, tensor_count, 2, half_inputs)
-    half_width = units + half_inputs
-    gate_rows = jnp.concatenate(
-        [gate_grad.reshape(row_count, tensor_count, units), joined_rows[:, :, 0]], axis=2
-    )
-    up_rows = jnp.concatenate(
-        [up_grad.reshape(row_count, tensor_count, units), joined_rows[:, :, 1]], axis=2
-    )
-    unit_rows = jnp.stack([gate_rows, up_rows]).transpose(2, 0, 1, 3)
-    unit_group = exchange(
-        unit_rows.reshape(tensor_count, 2 * row_count, half_width), tensor_axes
-    )
     unit_group, mlp_block = lax.optimization_barrier((unit_group, mlp_block))
     mlp_z = gather_z(mlp_block)
     unit_halves = (
@@ -213,14 +215,13 @@
     hidden_grad = (resid_block + scale_block * (lifted - normed * inner_mean)).astype(narrow)
     gain_part = jnp.sum(input_grad * normed, axis=0, keepdims=True)
 
-    rows_sent = block_rows + 8
     grad_sent = jnp.concatenate(
         [hidden_grad] + list(split_three(gain_part)) + [jnp.zeros((5, features), narrow)], axis=0
     )
-    grad_far = exchange(jnp.broadcast_to(grad_sent[None], (z_count, rows_sent, features)), "z")
+    grad_far = gather_z(grad_sent)
     grad_near = swap_near(grad_far)
     grad_pair = jnp.stack([grad_near, grad_far])
-    gain_parts = grad_pair[:, :, block_rows : block_rows + 3].astype(wide)
+    gain_parts = other_first(grad_pair[:, :, block_rows : block_rows + 3]).astype(wide)
     gain_sum = jnp.sum(gain_parts, axis=(0, 1, 2))[None]
     grad_all = (
         grad_pair[:, :, :block_rows]

time: 309 us -> 309 us (level)
  starting transfers between devices: 137 us -> 155 us
  waiting for transfers between devices: 122 us -> 106 us
    ppermute x6 -> x12, starting transfers between devices: 22.3 us -> 47.7 us  [from_above(): lax.ppermute(value, 'z', [((i + distance) % count, i) for i in range(coun...]
    all_to_all x7 -> x6, waiting for transfers between devices: 78.4 us -> 53.3 us  [exchange(): return lax.all_to_all(blocks, axes, split_axis=0, concat_axis=0, tiled=True)]
    all_to_all x7 -> x6, starting transfers between devices: 65.2 us -> 58.4 us  [exchange(): return lax.all_to_all(blocks, axes, split_axis=0, concat_axis=0, tiled=True)]
    ppermute x6 -> x12, waiting for transfers between devices: 13.8 us -> 19.7 us  [from_above(): lax.ppermute(value, 'z', [((i + distance) % count, i) for i in range(coun...]
  transfers between devices with their start and end apart: 27 -> 32, of which waited for: 15 -> 18; matrix products, arithmetic and copies ran while one was open for 11% -> 11% of each run, Pallas kernels for 0% -> 0%
where the time goes in v5:
time: 309 us; the launch traced here: 307 us
  starting transfers between devices  155 us (50%)
  waiting for transfers between devices  106 us (34%)
  local copies, waits for them, and re-layouts  18 us (6%)
  matrix products  13.7 us (4%)
  other arithmetic  12.8 us (4%)
    all_to_all x6, starting transfers between devices, exchange(): return lax.all_to_all(blocks, axes, split_axis=0, concat_axis=0, tiled=True)  58.4 us
    all_to_all x6, waiting for transfers between devices, exchange(): return lax.all_to_all(blocks, axes, split_axis=0, concat_axis=0, tiled=True)  53.3 us
    ppermute x12, starting transfers between devices, from_above(): lax.ppermute(value, 'z', [((i + distance) % count, i) for i in range(coun...  47.7 us
    ppermute x3, waiting for transfers between devices, swap_near(): return lax.ppermute(value, 'y_lo', [(0, 1), (1, 0)])  27.8 us
    ppermute x6, starting transfers between devices, swap_cores(): return lax.ppermute(value, 'core', [(0, 1), (1, 0)])  20.3 us
    ppermute x12, waiting for transfers between devices, from_above(): lax.ppermute(value, 'z', [((i + distance) % count, i) for i in range(coun...  19.7 us
    ppermute x2, starting transfers between devices, trade_pair(): other = lax.ppermute(sent, axis_name, [(0, 1), (1, 0)])  13.3 us
    dot_general x4, matrix products, token_sum(): lax.dot_general(left, right, (((0,), (0,)), ((), ())), preferred_element_...  10.4 us
  transfers between devices with their start and end apart: 32, of which 18 were waited for; matrix products, arithmetic and copies ran while one was open for 11% of the time, Pallas kernels for 0%

profile of v5, /device:TPU:1, one launch (start us, length us, event | category | flops | bytes accessed | tf_op | source)
XLA Modules:
  0.0 306.9 jit_solution(14974094881928973387)
XLA Ops:
  4.9 8.8 %collective-permute-start = (bf16[4,2,12,256]{3,1,2,0:T(2,128)(2,1)S(1)}, bf16[4,2,12,256]{3,1,2,0:T(2,128)(2,1)S(1)}, u32[]{:S(2)}, u32[]{:S(2)}) collective-permute-start(bf16[4,2,12,256]{3,1,2,0:T(2,128)(2,1)S(1)} %bitcast.184), channel_id=1, source_target_pairs={{0,1},{1,0},{2,3},{3,2},{4,5},{5,4},{6,7},{7,6},{8,9},{9,8},{10,11... | collective-permute-start | bytes 147464 | tf_op jit(solution)/shard_map/ppermute | solution.py:61
  14.6 10.8 %all-to-all-start = ((bf16[32,8,1024]{2,1,0:T(8,128)(2,1)}), bf16[32,8,1024]{2,1,0:T(8,128)(2,1)S(1)}, u32[]{:S(2)}, u32[]{:S(2)}) async-start(bf16[32,8,1024]{2,1,0:T(8,128)(2,1)} %reshape.285), calls=%async_computation | async-start | bytes 1048576 | tf_op jit(solution)/shard_map/all_to_all | solution.py:28
  26.0 4.5 %collective-permute-start.1 = (bf16[2,4,12,256]{3,1,2,0:T(4,128)(2,1)S(1)}, bf16[2,4,12,256]{3,1,2,0:T(4,128)(2,1)S(1)}, u32[]{:S(2)}, u32[]{:S(2)}) collective-permute-start(bf16[2,4,12,256]{3,1,2,0:T(4,128)(2,1)S(1)} %bitcast.185), channel_id=1, source_target_pairs={{0,2},{2,0},{1,3},{3,1},{4,6},{6,4},{5,7},{7,5},{8,10},{10,8},{9,1... | collective-permute-start | bytes 147464 | tf_op jit(solution)/shard_map/ppermute | solution.py:61
  32.8 4.4 %collective-permute-start.2 = (bf16[2,2,12,256]{3,1,2,0:T(2,128)(2,1)S(1)}, bf16[2,2,12,256]{3,1,2,0:T(2,128)(2,1)S(1)}, u32[]{:S(2)}, u32[]{:S(2)}) collective-permute-start(bf16[2,2,12,256]{3,1,2,0:T(2,128)(2,1)S(1)} %bitcast.194), channel_id=1, source_target_pairs={{0,12},{4,0},{8,4},{12,8},{1,13},{5,1},{9,5},{13,9},{2,14},{6,2},{... | collective-permute-start | bytes 73736 | tf_op jit(solution)/shard_map/ppermute | solution.py:69
  48.6 7.5 %all-to-all-done = bf16[32,8,1024]{2,1,0:T(8,128)(2,1)S(1)} async-done(((bf16[32,8,1024]{2,1,0:T(8,128)(2,1)}), bf16[32,8,1024]{2,1,0:T(8,128)(2,1)S(1)}, u32[]{:S(2)}, u32[]{:S(2)}) %all-to-all-start) | async-done | bytes 524320 | tf_op jit(solution)/shard_map/all_to_all | solution.py:28
  59.9 7.8 %all-to-all-start.1 = ((bf16[16,128,1024]{2,1,0:T(8,128)(2,1)}), bf16[16,128,1024]{2,1,0:T(8,128)(2,1)}, u32[]{:S(2)}, u32[]{:S(2)}) async-start(bf16[16,128,1024]{2,1,0:T(8,128)(2,1)} %bitcast.158), calls=%async_computation.1 | async-start | bytes 8388608 | tf_op jit(solution)/shard_map/all_to_all | solution.py:28
  70.0 9.2 %collective-permute-start.6 = (bf16[64,256]{1,0:T(8,128)(2,1)S(1)}, bf16[64,256]{1,0:T(8,128)(2,1)S(1)}, u32[]{:S(2)}, u32[]{:S(2)}) collective-permute-start(bf16[64,256]{1,0:T(8,128)(2,1)S(1)} %multiply_convert_fusion), channel_id=1, source_target_pairs={{128,0},{144,16},{160,32},{176,48},{192,64},{208,80},{224,96},{240... | collective-permute-start | bytes 98312 | tf_op jit(solution)/shard_map/ppermute | solution.py:41
  83.4 8.0 %collective-permute-done.5 = bf16[64,256]{1,0:T(8,128)(2,1)S(1)} collective-permute-done((bf16[64,256]{1,0:T(8,128)(2,1)S(1)}, bf16[64,256]{1,0:T(8,128)(2,1)S(1)}, u32[]{:S(2)}, u32[]{:S(2)}) %collective-permute-start.5) | collective-permute-done | bytes 32800 | tf_op jit(solution)/shard_map/ppermute | solution.py:41
  95.9 4.0 %collective-permute-start.8 = (bf16[4,64,256]{2,1,0:T(8,128)(2,1)S(1)}, bf16[4,64,256]{2,1,0:T(8,128)(2,1)S(1)}, u32[]{:S(2)}, u32[]{:S(2)}) collective-permute-start(bf16[4,64,256]{2,1,0:T(8,128)(2,1)S(1)} %get-tuple-element.40), channel_id=1, source_target_pairs={{16,0},{32,16},{48,32},{64,48},{80,64},{96,80},{112,96},{128,112},... | collective-permute-start | bytes 393224 | tf_op jit(solution)/shard_map/ppermute | solution.py:41
  102.9 4.0 %collective-permute-done.8 = bf16[4,64,256]{2,1,0:T(8,128)(2,1)S(1)} collective-permute-done((bf16[4,64,256]{2,1,0:T(8,128)(2,1)S(1)}, bf16[4,64,256]{2,1,0:T(8,128)(2,1)S(1)}, u32[]{:S(2)}, u32[]{:S(2)}) %collective-permute-start.8) | collective-permute-done | bytes 131104 | tf_op jit(solution)/shard_map/ppermute | solution.py:41
  107.3 13.1 %all-to-all-done.1 = bf16[16,128,1024]{2,1,0:T(8,128)(2,1)} async-done(((bf16[16,128,1024]{2,1,0:T(8,128)(2,1)}), bf16[16,128,1024]{2,1,0:T(8,128)(2,1)}, u32[]{:S(2)}, u32[]{:S(2)}) %all-to-all-start.1) | async-done | bytes 4194336 | tf_op jit(solution)/shard_map/all_to_all | solution.py:28
  132.6 12.6 %collective-permute-done.14 = bf16[1024,256]{1,0:T(8,128)(2,1)S(1)} collective-permute-done((bf16[1024,256]{1,0:T(8,128)(2,1)S(1)}, bf16[1024,256]{1,0:T(8,128)(2,1)S(1)}, u32[]{:S(2)}, u32[]{:S(2)}) %collective-permute-start.14) | collective-permute-done | bytes 524320 | tf_op jit(solution)/shard_map/ppermute | solution.py:36
  146.6 5.0 %all-to-all-start.2 = ((bf16[16,64,256]{2,1,0:T(8,128)(2,1)}), bf16[16,64,256]{2,1,0:T(8,128)(2,1)S(1)}, u32[]{:S(2)}, u32[]{:S(2)}) async-start(bf16[16,64,256]{2,1,0:T(8,128)(2,1)} %copy.307), calls=%async_computation.2 | async-start | bytes 1048576 | tf_op jit(solution)/shard_map/all_to_all | solution.py:28
  154.2 11.7 %collective-permute-done.22 = bf16[16,64,256]{2,1,0:T(8,128)(2,1)S(1)} collective-permute-done((bf16[16,64,256]{2,1,0:T(8,128)(2,1)S(1)}, bf16[16,64,256]{2,1,0:T(8,128)(2,1)S(1)}, u32[]{:S(2)}, u32[]{:S(2)}) %collective-permute-start.22) | collective-permute-done | bytes 524320 | tf_op jit(solution)/shard_map/ppermute | solution.py:36
  166.9 3.9 %collective-permute-start.23 = (bf16[2048,256]{1,0:T(8,128)(2,1)S(1)}, bf16[2048,256]{1,0:T(8,128)(2,1)}, u32[]{:S(2)}, u32[]{:S(2)}) collective-permute-start(bf16[2048,256]{1,0:T(8,128)(2,1)S(1)} %reshape.300), channel_id=1, source_target_pairs={{0,1},{1,0},{2,3},{3,2},{4,5},{5,4},{6,7},{7,6},{8,9},{9,8},{10,11... | collective-permute-start | bytes 3145736 | tf_op jit(solution)/shard_map/ppermute | solution.py:32
  170.9 3.7 %all-to-all-done.2 = bf16[16,64,256]{2,1,0:T(8,128)(2,1)S(1)} async-done(((bf16[16,64,256]{2,1,0:T(8,128)(2,1)}), bf16[16,64,256]{2,1,0:T(8,128)(2,1)S(1)}, u32[]{:S(2)}, u32[]{:S(2)}) %all-to-all-start.2) | async-done | bytes 524320 | tf_op jit(solution)/shard_map/all_to_all | solution.py:28
  175.7 19.4 %all-to-all-start.3 = ((f32[16,1,64]{2,1,0:T(1,128)}), f32[16,1,64]{2,1,0:T(1,128)S(1)}, u32[]{:S(2)}, u32[]{:S(2)}) async-start(f32[16,1,64]{2,1,0:T(1,128)} %broadcast_in_dim.17), calls=%async_computation.3 | async-start | bytes 16384 | tf_op jit(solution)/shard_map/all_to_all | solution.py:28
  195.1 6.9 %all-to-all-done.3 = f32[16,1,64]{2,1,0:T(1,128)S(1)} async-done(((f32[16,1,64]{2,1,0:T(1,128)}), f32[16,1,64]{2,1,0:T(1,128)S(1)}, u32[]{:S(2)}, u32[]{:S(2)}) %all-to-all-start.3) | async-done | bytes 4128 | tf_op jit(solution)/shard_map/all_to_all | solution.py:28
  202.2 5.8 %collective-permute-start.17 = (bf16[72,256]{1,0:T(8,128)(2,1)S(1)}, bf16[72,256]{1,0:T(8,128)(2,1)S(1)}, u32[]{:S(2)}, u32[]{:S(2)}) collective-permute-start(bf16[72,256]{1,0:T(8,128)(2,1)S(1)} %concatenate.48), channel_id=1, source_target_pairs={{192,0},{208,16},{224,32},{240,48},{0,64},{16,80},{32,96},{48,112}... | collective-permute-start | bytes 110600 | tf_op jit(solution)/shard_map/ppermute | solution.py:41
  207.9 6.8 %collective-permute-start.16 = (bf16[72,256]{1,0:T(8,128)(2,1)S(1)}, bf16[72,256]{1,0:T(8,128)(2,1)S(1)}, u32[]{:S(2)}, u32[]{:S(2)}) collective-permute-start(bf16[72,256]{1,0:T(8,128)(2,1)S(1)} %concatenate.48), channel_id=1, source_target_pairs={{128,0},{144,16},{160,32},{176,48},{192,64},{208,80},{224,96},{240... | collective-permute-start | bytes 110600 | tf_op jit(solution)/shard_map/ppermute | solution.py:41
  214.7 3.4 %collective-permute-start.15 = (bf16[72,256]{1,0:T(8,128)(2,1)S(1)}, bf16[72,256]{1,0:T(8,128)(2,1)S(1)}, u32[]{:S(2)}, u32[]{:S(2)}) collective-permute-start(bf16[72,256]{1,0:T(8,128)(2,1)S(1)} %concatenate.48), channel_id=1, source_target_pairs={{64,0},{80,16},{96,32},{112,48},{128,64},{144,80},{160,96},{176,11... | collective-permute-start | bytes 110600 | tf_op jit(solution)/shard_map/ppermute | solution.py:41
  218.1 3.2 %collective-permute-done.16 = bf16[72,256]{1,0:T(8,128)(2,1)S(1)} collective-permute-done((bf16[72,256]{1,0:T(8,128)(2,1)S(1)}, bf16[72,256]{1,0:T(8,128)(2,1)S(1)}, u32[]{:S(2)}, u32[]{:S(2)}) %collective-permute-start.16) | collective-permute-done | bytes 36896 | tf_op jit(solution)/shard_map/ppermute | solution.py:41
  224.0 3.5 %collective-permute-start.20 = (bf16[4,72,256]{2,1,0:T(8,128)(2,1)S(1)}, bf16[4,72,256]{2,1,0:T(8,128)(2,1)S(1)}, u32[]{:S(2)}, u32[]{:S(2)}) collective-permute-start(bf16[4,72,256]{2,1,0:T(8,128)(2,1)S(1)} %get-tuple-element.34), channel_id=1, source_target_pairs={{240,0},{0,16},{16,32},{32,48},{48,64},{64,80},{80,96},{96,112},{1... | collective-permute-start | bytes 442376 | tf_op jit(solution)/shard_map/ppermute | solution.py:41
  230.1 3.4 %collective-permute-start.18 = (bf16[4,72,256]{2,1,0:T(8,128)(2,1)S(1)}, bf16[4,72,256]{2,1,0:T(8,128)(2,1)S(1)}, u32[]{:S(2)}, u32[]{:S(2)}) collective-permute-start(bf16[4,72,256]{2,1,0:T(8,128)(2,1)S(1)} %get-tuple-element.34), channel_id=1, source_target_pairs={{16,0},{32,16},{48,32},{64,48},{80,64},{96,80},{112,96},{128,112},... | collective-permute-start | bytes 442376 | tf_op jit(solution)/shard_map/ppermute | solution.py:41
  235.4 4.9 %collective-permute-start.25 = (bf16[2048,128]{1,0:T(8,128)(2,1)}, bf16[2048,128]{1,0:T(8,128)(2,1)}, u32[]{:S(2)}, u32[]{:S(2)}) collective-permute-start(bf16[2048,128]{1,0:T(8,128)(2,1)} %slice.123), channel_id=1, source_target_pairs={{0,1},{1,0},{2,3},{3,2},{4,5},{5,4},{6,7},{7,6},{8,9},{9,8},{10,11... | collective-permute-start | bytes 1572872 | tf_op jit(solution)/shard_map/ppermute | solution.py:32
  242.7 4.4 %fusion = f32[896,256]{1,0:T(8,128)} fusion(bf16[2048,256]{1,0:T(8,128)(2,1)} %collective-permute-done.23, bf16[2048,1024]{1,0:T(8,128)(2,1)} %bitcast.31), kind=kOutput, calls=%fused_computation | convolution fusion | flops 939524096 | bytes 5636096 | tf_op jit(solution)/shard_map/dot_general | solution.py:24
  247.2 4.4 %collective-permute-start.24 = (f32[896,256]{1,0:T(8,128)}, f32[896,256]{1,0:T(8,128)}, u32[]{:S(2)}, u32[]{:S(2)}) collective-permute-start(f32[896,256]{1,0:T(8,128)} %fusion), channel_id=1, source_target_pairs={{0,1},{1,0},{2,3},{3,2},{4,5},{5,4},{6,7},{7,6},{8,9},{9,8},{10,11... | collective-permute-start | bytes 2752520 | tf_op jit(solution)/shard_map/ppermute | solution.py:32
  251.8 3.4 %collective-permute-done.21 = bf16[16,72,256]{2,1,0:T(8,128)(2,1)S(1)} collective-permute-done((bf16[16,72,256]{2,1,0:T(8,128)(2,1)S(1)}, bf16[16,72,256]{2,1,0:T(8,128)(2,1)S(1)}, u32[]{:S(2)}, u32[]{:S(2)}) %collective-permute-start.21) | collective-permute-done | bytes 589856 | tf_op jit(solution)/shard_map/ppermute | solution.py:36
  258.2 6.7 %all-to-all-start.4 = ((bf16[16,144,256]{2,1,0:T(8,128)(2,1)}), bf16[16,144,256]{2,1,0:T(8,128)(2,1)S(1)}, u32[]{:S(2)}, u32[]{:S(2)}) async-start(bf16[16,144,256]{2,1,0:T(8,128)(2,1)} %pad_maximum_fusion), calls=%async_computation.4 | async-start | bytes 2359296 | tf_op jit(solution)/shard_map/all_to_all | solution.py:28
  274.2 9.4 %all-to-all-done.4 = bf16[16,144,256]{2,1,0:T(8,128)(2,1)S(1)} async-done(((bf16[16,144,256]{2,1,0:T(8,128)(2,1)}), bf16[16,144,256]{2,1,0:T(8,128)(2,1)S(1)}, u32[]{:S(2)}, u32[]{:S(2)}) %all-to-all-start.4) | async-done | bytes 1179680 | tf_op jit(solution)/shard_map/all_to_all | solution.py:28
  284.5 8.6 %all-to-all-start.5 = ((bf16[32,4,256]{2,1,0:T(4,128)(2,1)}), bf16[32,4,256]{2,1,0:T(4,128)(2,1)S(1)}, u32[]{:S(2)}, u32[]{:S(2)}) async-start(bf16[32,4,256]{2,1,0:T(4,128)(2,1)} %bitcast.62), calls=%async_computation.5 | async-start | bytes 131072 | tf_op jit(solution)/shard_map/all_to_all | solution.py:28
  293.7 12.6 %all-to-all-done.5 = bf16[32,4,256]{2,1,0:T(4,128)(2,1)S(1)} async-done(((bf16[32,4,256]{2,1,0:T(4,128)(2,1)}), bf16[32,4,256]{2,1,0:T(4,128)(2,1)S(1)}, u32[]{:S(2)}, u32[]{:S(2)}) %all-to-all-start.5) | async-done | bytes 65568 | tf_op jit(solution)/shard_map/all_to_all | solution.py:28
  (174 shorter events, 79.2 us)
Async XLA Ops:
  4.9 20.6 %collective-permute-start = (bf16[4,2,12,256]{3,1,2,0:T(2,128)(2,1)S(1)}, bf16[4,2,12,256]{3,1,2,0:T(2,128)(2,1)S(1)}, u32[]{:S(2)}, u32[]{:S(2)}) collective-permute-start(bf16[4,2,12,256]{3,1,2,0:T(2,128)(2,1)S(1)} %bitcast.184), channel_id=1, source_target_pairs={{0,1},{1,0},{2,3},{3,2},{4,5},{5,4},{6,7},{7,6},{8,9},{9,8},{10,11... | collective-permute-start | bytes 147464 | tf_op jit(solution)/shard_map/ppermute | solution.py:61
  14.6 41.6 %all-to-all-start = ((bf16[32,8,1024]{2,1,0:T(8,128)(2,1)}), bf16[32,8,1024]{2,1,0:T(8,128)(2,1)S(1)}, u32[]{:S(2)}, u32[]{:S(2)}) async-start(bf16[32,8,1024]{2,1,0:T(8,128)(2,1)} %reshape.285), calls=%async_computation | async-start | bytes 1048576 | tf_op jit(solution)/shard_map/all_to_all | solution.py:28
  26.0 6.3 %collective-permute-start.1 = (bf16[2,4,12,256]{3,1,2,0:T(4,128)(2,1)S(1)}, bf16[2,4,12,256]{3,1,2,0:T(4,128)(2,1)S(1)}, u32[]{:S(2)}, u32[]{:S(2)}) collective-permute-start(bf16[2,4,12,256]{3,1,2,0:T(4,128)(2,1)S(1)} %bitcast.185), channel_id=1, source_target_pairs={{0,2},{2,0},{1,3},{3,1},{4,6},{6,4},{5,7},{7,5},{8,10},{10,8},{9,1... | collective-permute-start | bytes 147464 | tf_op jit(solution)/shard_map/ppermute | solution.py:61
  32.8 10.2 %collective-permute-start.2 = (bf16[2,2,12,256]{3,1,2,0:T(2,128)(2,1)S(1)}, bf16[2,2,12,256]{3,1,2,0:T(2,128)(2,1)S(1)}, u32[]{:S(2)}, u32[]{:S(2)}) collective-permute-start(bf16[2,2,12,256]{3,1,2,0:T(2,128)(2,1)S(1)} %bitcast.194), channel_id=1, source_target_pairs={{0,12},{4,0},{8,4},{12,8},{1,13},{5,1},{9,5},{13,9},{2,14},{6,2},{... | collective-permute-start | bytes 73736 | tf_op jit(solution)/shard_map/ppermute | solution.py:69
  37.3 6.2 %collective-permute-start.3 = (bf16[2,2,12,256]{3,1,2,0:T(2,128)(2,1)S(1)}, bf16[2,2,12,256]{3,1,2,0:T(2,128)(2,1)S(1)}, u32[]{:S(2)}, u32[]{:S(2)}) collective-permute-start(bf16[2,2,12,256]{3,1,2,0:T(2,128)(2,1)S(1)} %bitcast.196), channel_id=1, source_target_pairs={{0,8},{4,12},{8,0},{12,4},{1,9},{5,13},{9,1},{13,5},{2,10},{6,14},... | collective-permute-start | bytes 73736 | tf_op jit(solution)/shard_map/ppermute | solution.py:69
  39.7 6.3 %collective-permute-start.4 = (bf16[2,2,12,256]{3,1,2,0:T(2,128)(2,1)S(1)}, bf16[2,2,12,256]{3,1,2,0:T(2,128)(2,1)S(1)}, u32[]{:S(2)}, u32[]{:S(2)}) collective-permute-start(bf16[2,2,12,256]{3,1,2,0:T(2,128)(2,1)S(1)} %bitcast.198), channel_id=1, source_target_pairs={{0,4},{4,8},{8,12},{12,0},{1,5},{5,9},{9,13},{13,1},{2,6},{6,10},{... | collective-permute-start | bytes 73736 | tf_op jit(solution)/shard_map/ppermute | solution.py:69
  59.9 60.5 %all-to-all-start.1 = ((bf16[16,128,1024]{2,1,0:T(8,128)(2,1)}), bf16[16,128,1024]{2,1,0:T(8,128)(2,1)}, u32[]{:S(2)}, u32[]{:S(2)}) async-start(bf16[16,128,1024]{2,1,0:T(8,128)(2,1)} %bitcast.158), calls=%async_computation.1 | async-start | bytes 8388608 | tf_op jit(solution)/shard_map/all_to_all | solution.py:28
  67.6 13.9 %collective-permute-start.7 = (bf16[64,256]{1,0:T(8,128)(2,1)S(1)}, bf16[64,256]{1,0:T(8,128)(2,1)S(1)}, u32[]{:S(2)}, u32[]{:S(2)}) collective-permute-start(bf16[64,256]{1,0:T(8,128)(2,1)S(1)} %multiply_convert_fusion), channel_id=1, source_target_pairs={{192,0},{208,16},{224,32},{240,48},{0,64},{16,80},{32,96},{48,112}... | collective-permute-start | bytes 98312 | tf_op jit(solution)/shard_map/ppermute | solution.py:41
  70.0 13.4 %collective-permute-start.6 = (bf16[64,256]{1,0:T(8,128)(2,1)S(1)}, bf16[64,256]{1,0:T(8,128)(2,1)S(1)}, u32[]{:S(2)}, u32[]{:S(2)}) collective-permute-start(bf16[64,256]{1,0:T(8,128)(2,1)S(1)} %multiply_convert_fusion), channel_id=1, source_target_pairs={{128,0},{144,16},{160,32},{176,48},{192,64},{208,80},{224,96},{240... | collective-permute-start | bytes 98312 | tf_op jit(solution)/shard_map/ppermute | solution.py:41
  79.2 12.2 %collective-permute-start.5 = (bf16[64,256]{1,0:T(8,128)(2,1)S(1)}, bf16[64,256]{1,0:T(8,128)(2,1)S(1)}, u32[]{:S(2)}, u32[]{:S(2)}) collective-permute-start(bf16[64,256]{1,0:T(8,128)(2,1)S(1)} %multiply_convert_fusion), channel_id=1, source_target_pairs={{64,0},{80,16},{96,32},{112,48},{128,64},{144,80},{160,96},{176,11... | collective-permute-start | bytes 98312 | tf_op jit(solution)/shard_map/ppermute | solution.py:41
  91.4 11.4 %collective-permute-start.10 = (bf16[4,64,256]{2,1,0:T(8,128)(2,1)S(1)}, bf16[4,64,256]{2,1,0:T(8,128)(2,1)S(1)}, u32[]{:S(2)}, u32[]{:S(2)}) collective-permute-start(bf16[4,64,256]{2,1,0:T(8,128)(2,1)S(1)} %get-tuple-element.40), channel_id=1, source_target_pairs={{240,0},{0,16},{16,32},{32,48},{48,64},{64,80},{80,96},{96,112},{1... | collective-permute-start | bytes 393224 | tf_op jit(solution)/shard_map/ppermute | solution.py:41
  93.4 9.5 %collective-permute-start.9 = (bf16[4,64,256]{2,1,0:T(8,128)(2,1)S(1)}, bf16[4,64,256]{2,1,0:T(8,128)(2,1)S(1)}, u32[]{:S(2)}, u32[]{:S(2)}) collective-permute-start(bf16[4,64,256]{2,1,0:T(8,128)(2,1)S(1)} %get-tuple-element.40), channel_id=1, source_target_pairs={{32,0},{48,16},{64,32},{80,48},{96,64},{112,80},{128,96},{144,112}... | collective-permute-start | bytes 393224 | tf_op jit(solution)/shard_map/ppermute | solution.py:41
  95.9 11.0 %collective-permute-start.8 = (bf16[4,64,256]{2,1,0:T(8,128)(2,1)S(1)}, bf16[4,64,256]{2,1,0:T(8,128)(2,1)S(1)}, u32[]{:S(2)}, u32[]{:S(2)}) collective-permute-start(bf16[4,64,256]{2,1,0:T(8,128)(2,1)S(1)} %get-tuple-element.40), channel_id=1, source_target_pairs={{16,0},{32,16},{48,32},{64,48},{80,64},{96,80},{112,96},{128,112},... | collective-permute-start | bytes 393224 | tf_op jit(solution)/shard_map/ppermute | solution.py:41
  99.9 23.2 %collective-permute-start.11 = (bf16[896,256]{1,0:T(8,128)(2,1)S(1)}, bf16[896,256]{1,0:T(8,128)(2,1)S(1)}, u32[]{:S(2)}, u32[]{:S(2)}) collective-permute-start(bf16[896,256]{1,0:T(8,128)(2,1)S(1)} %get-tuple-element.27), channel_id=1, source_target_pairs={{0,1},{1,0},{2,3},{3,2},{4,5},{5,4},{6,7},{7,6},{8,9},{9,8},{10,11... | collective-permute-start | bytes 1376264 | tf_op jit(solution)/shard_map/ppermute | solution.py:32
  123.8 5.8 %collective-permute-start.13 = (f32[1024,256]{1,0:T(8,128)S(1)}, f32[1024,256]{1,0:T(8,128)S(1)}, u32[]{:S(2)}, u32[]{:S(2)}) collective-permute-start(f32[1024,256]{1,0:T(8,128)S(1)} %fusion.8), channel_id=1, source_target_pairs={{0,1},{1,0},{2,3},{3,2},{4,5},{5,4},{6,7},{7,6},{8,9},{9,8},{10,11... | collective-permute-start | bytes 3145736 | tf_op jit(solution)/shard_map/ppermute | solution.py:32
  126.5 6.1 %collective-permute-start.12 = (f32[1024,256]{1,0:T(8,128)S(1)}, f32[1024,256]{1,0:T(8,128)S(1)}, u32[]{:S(2)}, u32[]{:S(2)}) collective-permute-start(f32[1024,256]{1,0:T(8,128)S(1)} %fusion.10), channel_id=1, source_target_pairs={{0,1},{1,0},{2,3},{3,2},{4,5},{5,4},{6,7},{7,6},{8,9},{9,8},{10,11... | collective-permute-start | bytes 3145736 | tf_op jit(solution)/shard_map/ppermute | solution.py:32
  129.8 15.4 %collective-permute-start.14 = (bf16[1024,256]{1,0:T(8,128)(2,1)S(1)}, bf16[1024,256]{1,0:T(8,128)(2,1)S(1)}, u32[]{:S(2)}, u32[]{:S(2)}) collective-permute-start(bf16[1024,256]{1,0:T(8,128)(2,1)S(1)} %add_convert_fusion.1), channel_id=1, source_target_pairs={{0,256},{256,0},{1,257},{257,1},{2,258},{258,2},{3,259},{259,3},{4... | collective-permute-start | bytes 1572872 | tf_op jit(solution)/shard_map/ppermute | solution.py:36
  146.6 28.0 %all-to-all-start.2 = ((bf16[16,64,256]{2,1,0:T(8,128)(2,1)}), bf16[16,64,256]{2,1,0:T(8,128)(2,1)S(1)}, u32[]{:S(2)}, u32[]{:S(2)}) async-start(bf16[16,64,256]{2,1,0:T(8,128)(2,1)} %copy.307), calls=%async_computation.2 | async-start | bytes 1048576 | tf_op jit(solution)/shard_map/all_to_all | solution.py:28
  151.7 14.2 %collective-permute-start.22 = (bf16[16,64,256]{2,1,0:T(8,128)(2,1)S(1)}, bf16[16,64,256]{2,1,0:T(8,128)(2,1)S(1)}, u32[]{:S(2)}, u32[]{:S(2)}) collective-permute-start(bf16[16,64,256]{2,1,0:T(8,128)(2,1)S(1)} %fusion.7), channel_id=1, source_target_pairs={{0,256},{256,0},{1,257},{257,1},{2,258},{258,2},{3,259},{259,3},{4... | collective-permute-start | bytes 1572872 | tf_op jit(solution)/shard_map/ppermute | solution.py:36
  166.9 75.8 %collective-permute-start.23 = (bf16[2048,256]{1,0:T(8,128)(2,1)S(1)}, bf16[2048,256]{1,0:T(8,128)(2,1)}, u32[]{:S(2)}, u32[]{:S(2)}) collective-permute-start(bf16[2048,256]{1,0:T(8,128)(2,1)S(1)} %reshape.300), channel_id=1, source_target_pairs={{0,1},{1,0},{2,3},{3,2},{4,5},{5,4},{6,7},{7,6},{8,9},{9,8},{10,11... | collective-permute-start | bytes 3145736 | tf_op jit(solution)/shard_map/ppermute | solution.py:32
  175.7 26.3 %all-to-all-start.3 = ((f32[16,1,64]{2,1,0:T(1,128)}), f32[16,1,64]{2,1,0:T(1,128)S(1)}, u32[]{:S(2)}, u32[]{:S(2)}) async-start(f32[16,1,64]{2,1,0:T(1,128)} %broadcast_in_dim.17), calls=%async_computation.3 | async-start | bytes 16384 | tf_op jit(solution)/shard_map/all_to_all | solution.py:28
  202.2 16.0 %collective-permute-start.17 = (bf16[72,256]{1,0:T(8,128)(2,1)S(1)}, bf16[72,256]{1,0:T(8,128)(2,1)S(1)}, u32[]{:S(2)}, u32[]{:S(2)}) collective-permute-start(bf16[72,256]{1,0:T(8,128)(2,1)S(1)} %concatenate.48), channel_id=1, source_target_pairs={{192,0},{208,16},{224,32},{240,48},{0,64},{16,80},{32,96},{48,112}... | collective-permute-start | bytes 110600 | tf_op jit(solution)/shard_map/ppermute | solution.py:41
  207.9 13.4 %collective-permute-start.16 = (bf16[72,256]{1,0:T(8,128)(2,1)S(1)}, bf16[72,256]{1,0:T(8,128)(2,1)S(1)}, u32[]{:S(2)}, u32[]{:S(2)}) collective-permute-start(bf16[72,256]{1,0:T(8,128)(2,1)S(1)} %concatenate.48), channel_id=1, source_target_pairs={{128,0},{144,16},{160,32},{176,48},{192,64},{208,80},{224,96},{240... | collective-permute-start | bytes 110600 | tf_op jit(solution)/shard_map/ppermute | solution.py:41
  214.7 9.2 %collective-permute-start.15 = (bf16[72,256]{1,0:T(8,128)(2,1)S(1)}, bf16[72,256]{1,0:T(8,128)(2,1)S(1)}, u32[]{:S(2)}, u32[]{:S(2)}) collective-permute-start(bf16[72,256]{1,0:T(8,128)(2,1)S(1)} %concatenate.48), channel_id=1, source_target_pairs={{64,0},{80,16},{96,32},{112,48},{128,64},{144,80},{160,96},{176,11... | collective-permute-start | bytes 110600 | tf_op jit(solution)/shard_map/ppermute | solution.py:41
  224.0 16.3 %collective-permute-start.20 = (bf16[4,72,256]{2,1,0:T(8,128)(2,1)S(1)}, bf16[4,72,256]{2,1,0:T(8,128)(2,1)S(1)}, u32[]{:S(2)}, u32[]{:S(2)}) collective-permute-start(bf16[4,72,256]{2,1,0:T(8,128)(2,1)S(1)} %get-tuple-element.34), channel_id=1, source_target_pairs={{240,0},{0,16},{16,32},{32,48},{48,64},{64,80},{80,96},{96,112},{1... | collective-permute-start | bytes 442376 | tf_op jit(solution)/shard_map/ppermute | solution.py:41
  227.5 12.9 %collective-permute-start.19 = (bf16[4,72,256]{2,1,0:T(8,128)(2,1)S(1)}, bf16[4,72,256]{2,1,0:T(8,128)(2,1)S(1)}, u32[]{:S(2)}, u32[]{:S(2)}) collective-permute-start(bf16[4,72,256]{2,1,0:T(8,128)(2,1)S(1)} %get-tuple-element.34), channel_id=1, source_target_pairs={{32,0},{48,16},{64,32},{80,48},{96,64},{112,80},{128,96},{144,112}... | collective-permute-start | bytes 442376 | tf_op jit(solution)/shard_map/ppermute | solution.py:41
  230.1 10.4 %collective-permute-start.18 = (bf16[4,72,256]{2,1,0:T(8,128)(2,1)S(1)}, bf16[4,72,256]{2,1,0:T(8,128)(2,1)S(1)}, u32[]{:S(2)}, u32[]{:S(2)}) collective-permute-start(bf16[4,72,256]{2,1,0:T(8,128)(2,1)S(1)} %get-tuple-element.34), channel_id=1, source_target_pairs={{16,0},{32,16},{48,32},{64,48},{80,64},{96,80},{112,96},{128,112},... | collective-permute-start | bytes 442376 | tf_op jit(solution)/shard_map/ppermute | solution.py:41
  235.4 36.7 %collective-permute-start.25 = (bf16[2048,128]{1,0:T(8,128)(2,1)}, bf16[2048,128]{1,0:T(8,128)(2,1)}, u32[]{:S(2)}, u32[]{:S(2)}) collective-permute-start(bf16[2048,128]{1,0:T(8,128)(2,1)} %slice.123), channel_id=1, source_target_pairs={{0,1},{1,0},{2,3},{3,2},{4,5},{5,4},{6,7},{7,6},{8,9},{9,8},{10,11... | collective-permute-start | bytes 1572872 | tf_op jit(solution)/shard_map/ppermute | solution.py:32
  240.8 14.4 %collective-permute-start.21 = (bf16[16,72,256]{2,1,0:T(8,128)(2,1)S(1)}, bf16[16,72,256]{2,1,0:T(8,128)(2,1)S(1)}, u32[]{:S(2)}, u32[]{:S(2)}) collective-permute-start(bf16[16,72,256]{2,1,0:T(8,128)(2,1)S(1)} %fusion.5), channel_id=1, source_target_pairs={{0,256},{256,0},{1,257},{257,1},{2,258},{258,2},{3,259},{259,3},{4... | collective-permute-start | bytes 1769480 | tf_op jit(solution)/shard_map/ppermute | solution.py:36
  247.2 21.0 %collective-permute-start.24 = (f32[896,256]{1,0:T(8,128)}, f32[896,256]{1,0:T(8,128)}, u32[]{:S(2)}, u32[]{:S(2)}) collective-permute-start(f32[896,256]{1,0:T(8,128)} %fusion), channel_id=1, source_target_pairs={{0,1},{1,0},{2,3},{3,2},{4,5},{5,4},{6,7},{7,6},{8,9},{9,8},{10,11... | collective-permute-start | bytes 2752520 | tf_op jit(solution)/shard_map/ppermute | solution.py:32
  258.2 25.4 %all-to-all-start.4 = ((bf16[16,144,256]{2,1,0:T(8,128)(2,1)}), bf16[16,144,256]{2,1,0:T(8,128)(2,1)S(1)}, u32[]{:S(2)}, u32[]{:S(2)}) async-start(bf16[16,144,256]{2,1,0:T(8,128)(2,1)} %pad_maximum_fusion), calls=%async_computation.4 | async-start | bytes 2359296 | tf_op jit(solution)/shard_map/all_to_all | solution.py:28
  284.5 21.8 %all-to-all-start.5 = ((bf16[32,4,256]{2,1,0:T(4,128)(2,1)}), bf16[32,4,256]{2,1,0:T(4,128)(2,1)S(1)}, u32[]{:S(2)}, u32[]{:S(2)}) async-start(bf16[32,4,256]{2,1,0:T(4,128)(2,1)} %bitcast.62), calls=%async_computation.5 | async-start | bytes 131072 | tf_op jit(solution)/shard_map/all_to_all | solution.py:28
  (7 other events, 424.6 us)

commit v6 on v5

v6 whole, which is shorter than its diff:
```python
import jax
import jax.numpy as jnp
from jax import lax
from jax.sharding import Mesh
from jax.sharding import PartitionSpec as P

epsilon = 1e-05
narrow = jnp.bfloat16
wide = jnp.float32


def swiglu_back(gate_act, up_act, product_grad):
    gate_wide = gate_act.astype(wide)
    logistic = jax.nn.sigmoid(gate_wide)
    product_wide = product_grad.astype(wide)
    gate_grad = (
        product_wide * up_act.astype(wide) * logistic * (1.0 + gate_wide * (1.0 - logistic))
    )
    up_grad = product_wide * gate_wide * logistic
    return (gate_grad.astype(narrow), up_grad.astype(narrow))


def token_sum(left, right):
    return lax.dot_general(left, right, (((0,), (0,)), ((), ())), preferred_element_type=wide)


def exchange(blocks, axes):
    return lax.all_to_all(blocks, axes, split_axis=0, concat_axis=0, tiled=True)


def swap_cores(value):
    return lax.ppermute(value, "core", [(0, 1), (1, 0)])


def swap_near(value):
    return lax.ppermute(value, "y_lo", [(0, 1), (1, 0)])


def from_above(value, distance):
    count = lax.axis_size("z")
    return lax.ppermute(value, "z", [((i + distance) % count, i) for i in range(count)])


def gather_z(block):
    z_count = lax.axis_size("z")
    quarter = z_count // 4
    strided = jnp.stack([block] + [from_above(block, 4 * step) for step in range(1, quarter)])
    below = from_above(strided, z_count - 1)
    below = jnp.concatenate([below[1:], below[:1]])
    all_blocks = jnp.stack(
        [strided, from_above(strided, 1), from_above(strided, 2), below], axis=1
    ).reshape(z_count, *block.shape)
    twice = jnp.concatenate([all_blocks, all_blocks])
    return lax.dynamic_slice_in_dim(twice, z_count - lax.axis_index("z"), z_count, 0)


def trade_pair(blocks, axis_name):
    first = lax.axis_index(axis_name) == 0
    kept = jnp.where(first, blocks[0], blocks[1])
    sent = jnp.where(first, blocks[1], blocks[0])
    other = lax.ppermute(sent, axis_name, [(0, 1), (1, 0)])
    return jnp.stack([jnp.where(first, kept, other), jnp.where(first, other, kept)])


def trade_x(blocks):
    count, here = lax.axis_size("x"), lax.axis_index("x")
    turned = lax.dynamic_slice_in_dim(jnp.concatenate([blocks, blocks]), here, count, 0)
    pieces = [turned[0]] + [
        lax.ppermute(turned[step], "x", [(i, (i + step) % count) for i in range(count)])
        for step in range(1, count)
    ]
    back = jnp.stack([pieces[(count - step) % count] for step in range(count)])
    return lax.dynamic_slice_in_dim(jnp.concatenate([back, back]), count - here, count, 0)


def split_three(value):
    high = value.astype(narrow)
    rest = value - high.astype(wide)
    middle = rest.astype(narrow)
    low = (rest - middle.astype(wide)).astype(narrow)
    return (high, middle, low)


def shards(
    hidden,
    joined_in,
    gate_act,
    up_act,
    product_grad,
    resid_grad,
    norm_gain,
    gate_weight,
    up_weight,
    join_weight,
):
    dp_axes = ("x", "y_hi", "core")
    z_count = lax.axis_size("z")
    core_count = lax.axis_size("core")
    dp_count = lax.axis_size("x") * lax.axis_size("y_hi") * core_count
    row_count, width = hidden.shape
    units, features = gate_weight.shape
    inputs = join_weight.shape[0]
    half_inputs = inputs // 2
    part_width = units + half_inputs
    plane_rows = z_count * row_count
    block_rows = dp_count * row_count
    tokens = dp_count * plane_rows
    on_first = lax.axis_index("core") == 0
    here = lax.axis_index("y_lo")
    near_first = here == 0

    def by_near(own, near):
        return jnp.stack([jnp.where(near_first, own, near), jnp.where(near_first, near, own)])

    def by_core(own, other):
        return jnp.stack([jnp.where(on_first, own, other), jnp.where(on_first, other, own)])

    gate_grad, up_grad = swiglu_back(gate_act, up_act, product_grad)
    joined_rows = joined_in.reshape(row_count, 2, z_count, 2, half_inputs)
    gate_rows = jnp.concatenate(
        [gate_grad.reshape(row_count, 2, z_count, units), joined_rows[:, :, :, 0]], axis=3
    )
    up_rows = jnp.concatenate(
        [up_grad.reshape(row_count, 2, z_count, units), joined_rows[:, :, :, 1]], axis=3
    )
    unit_rows = jnp.stack([gate_rows, up_rows]).transpose(3, 0, 1, 2, 4)
    unit_rows = unit_rows.reshape(z_count, 2 * row_count, 2 * part_width)
    unit_rows, hidden, resid_grad = lax.optimization_barrier((unit_rows, hidden, resid_grad))
    unit_group = exchange(unit_rows, "z")

    weight_own = jnp.where(on_first, gate_weight, up_weight)
    weight_other = swap_cores(jnp.where(on_first, up_weight, gate_weight))
    near_own, near_other = swap_near(weight_own), swap_near(weight_other)
    near_join = swap_near(join_weight)

    hidden_wide = hidden.astype(wide)
    row_scale = lax.rsqrt(jnp.mean(hidden_wide * hidden_wide, axis=1, keepdims=True) + epsilon)
    scale_parts = jnp.concatenate(split_three(row_scale), axis=1)
    scale_parts = jnp.pad(scale_parts, ((0, 0), (0, features - scale_parts.shape[1])))
    norm_rows = jnp.stack(
        [
            hidden.reshape(row_count, dp_count, features),
            resid_grad.reshape(row_count, dp_count, features),
            jnp.broadcast_to(scale_parts[:, None, :], (row_count, dp_count, features)),
        ]
    )
    norm_sent = norm_rows.transpose(2, 0, 1, 3).reshape(
        lax.axis_size("x"), 2, 2, 3 * row_count, features
    )
    norm_block = trade_pair(norm_sent.transpose(2, 0, 1, 3, 4), "core")
    norm_block = trade_pair(norm_block.transpose(2, 0, 1, 3, 4), "y_hi")
    norm_block = trade_x(norm_block.transpose(2, 0, 1, 3, 4)).reshape(
        dp_count, 3, row_count, features
    )
    hidden_block = norm_block[:, 0].reshape(block_rows, features).astype(wide)
    resid_block = norm_block[:, 1].reshape(block_rows, features).astype(wide)
    scale_block = norm_block[:, 2, :, :3].astype(wide).reshape(block_rows, 3)
    scale_block = (scale_block[:, 0:1] + scale_block[:, 1:2]) + scale_block[:, 2:3]
    gain_block = lax.dynamic_slice_in_dim(
        norm_gain, lax.axis_index(dp_axes) * features, features, 0
    )
    normed = hidden_block * scale_block
    mlp_block = (normed * gain_block).astype(narrow)

    unit_group, mlp_block, near_own, near_other = lax.optimization_barrier(
        (unit_group, mlp_block, near_own, near_other)
    )
    mlp_z = gather_z(mlp_block)
    unit_halves = (
        unit_group.reshape(z_count, 2, row_count, 2 * part_width)
        .transpose(1, 0, 2, 3)
        .reshape(2, plane_rows, 2 * part_width)
    )
    unit_halves = jnp.broadcast_to(
        unit_halves[None], (dp_count // core_count, core_count, plane_rows, 2 * part_width)
    ).reshape(dp_count, plane_rows, 2 * part_width)
    half_all = exchange(unit_halves, dp_axes).reshape(tokens, 2 * part_width)
    half_all, mlp_z = lax.optimization_barrier((half_all, mlp_z))

    def both_near(own, near):
        both = jnp.pad(by_near(own, near), ((0, 0), (0, half_inputs), (0, 0)))
        return both.reshape(2 * part_width, features)

    partial_other = jnp.dot(
        half_all, both_near(weight_other, near_other), preferred_element_type=wide
    )
    partial_own = jnp.dot(half_all, both_near(weight_own, near_own), preferred_element_type=wide)
    partial_value = partial_own + swap_cores(partial_other)
    partial_value = (
        partial_value.astype(narrow)
        .reshape(dp_count, z_count, row_count, features)
        .transpose(1, 0, 2, 3)
        .reshape(z_count, block_rows, features)
    )
    input_grad = jnp.sum(exchange(partial_value, "z").astype(wide), axis=0)

    lifted = input_grad * gain_block
    mean_part = jnp.sum(lifted * normed, axis=1)
    mean_all = exchange(
        jnp.broadcast_to(mean_part[None, None], (dp_count, 1, block_rows)), dp_axes
    )
    inner_mean = (jnp.sum(mean_all, axis=(0, 1)) / width)[:, None]
    hidden_grad = (resid_block + scale_block * (lifted - normed * inner_mean)).astype(narrow)
    gain_part = jnp.sum(input_grad * normed, axis=0, keepdims=True)

    sent_rows = block_rows + 8
    grad_sent = jnp.concatenate(
        [hidden_grad] + list(split_three(gain_part)) + [jnp.zeros((5, features), narrow)], axis=0
    )
    grad_z = exchange(jnp.broadcast_to(grad_sent[None], (z_count, sent_rows, features)), "z")
    gain_sum = jnp.sum(grad_z[:, block_rows : block_rows + 3].astype(wide), axis=(0, 1))[None]
    grad_all = (
        grad_z[:, :block_rows]
        .reshape(z_count, dp_count, row_count, features)
        .transpose(1, 0, 2, 3)
        .reshape(tokens, features)
    )

    join_both = by_near(join_weight, near_join).reshape(2 * inputs, features)
    joined_part = lax.dot_general(
        grad_all, join_both, (((1,), (1,)), ((), ())), preferred_element_type=wide
    ).astype(narrow)
    gain_rows = jnp.concatenate(
        list(split_three(gain_sum)) + [jnp.zeros((13, features), narrow)], axis=0
    ).reshape(8, 2 * features)
    joined_part = jnp.concatenate(
        [
            joined_part.reshape(dp_count, plane_rows, 2 * inputs),
            jnp.broadcast_to(gain_rows[None], (dp_count, 8, 2 * features)),
        ],
        axis=1,
    )
    joined_blocks = exchange(joined_part, dp_axes)
    gain_blocks = joined_blocks[:, plane_rows : plane_rows + 2].astype(wide)
    gain_own = (gain_blocks[:, 0, :features] + gain_blocks[:, 0, features:]) + gain_blocks[
        :, 1, :features
    ]
    gain_grad = (gain_own + swap_near(gain_own)).reshape(width)
    joined_total = jnp.sum(joined_blocks[:, :plane_rows].astype(wide), axis=0).astype(narrow)
    joined_grad = exchange(joined_total.reshape(z_count, row_count, 2 * inputs), "z")
    joined_grad = (
        joined_grad.reshape(z_count, row_count, 2, inputs)
        .transpose(1, 2, 0, 3)
        .reshape(row_count, 2 * z_count * inputs)
    )

    mlp_own = (
        mlp_z.reshape(z_count, dp_count, row_count, features)
        .transpose(1, 0, 2, 3)
        .reshape(tokens, features)
    )

    def add_near(sums):
        kept = lax.dynamic_index_in_dim(sums, here, 0, keepdims=False)
        sent = lax.dynamic_index_in_dim(sums, 1 - here, 0, keepdims=False)
        return kept + swap_near(sent)

    def unit_sums(mlp_input):
        sums = token_sum(half_all, mlp_input).reshape(2, part_width, features)
        return add_near(sums[:, :units])

    other_grad = swap_cores(unit_sums(swap_cores(mlp_own)))
    own_grad = unit_sums(mlp_own)
    gate_weight_grad = jnp.where(on_first, own_grad, other_grad)
    up_weight_grad = jnp.where(on_first, other_grad, own_grad)

    joined_half = jnp.concatenate(
        [half_all[:, units:part_width], half_all[:, part_width + units :]], axis=1
    )
    join_sums = by_core(
        token_sum(joined_half, grad_all).reshape(2, half_inputs, features),
        token_sum(swap_cores(joined_half), grad_all).reshape(2, half_inputs, features),
    )
    join_weight_grad = add_near(join_sums.transpose(1, 0, 2, 3)).reshape(inputs, features)
    return (joined_grad, gate_weight_grad, up_weight_grad, join_weight_grad, gain_grad)


def solution(mesh):
    tensor_count, dp_count = mesh.shape["tensor"], mesh.shape["dp"]
    fine = Mesh(
        mesh.devices.reshape(2, tensor_count // 2, dp_count // 4, 2, 2),
        ("y_lo", "z", "x", "y_hi", "core"),
    )
    tensor_axes = ("y_lo", "z")
    dp_axes = ("x", "y_hi", "core")
    rows = P(dp_axes + tensor_axes, None)
    blocks = P(tensor_axes, dp_axes)
    in_specs = (rows, rows, rows, rows, rows, rows, P(), blocks, blocks, blocks)
    out_specs = (rows, blocks, blocks, blocks, P())
    return jax.shard_map(shards, mesh=fine, in_specs=in_specs, out_specs=out_specs, check_vma=False)
```

time: 309 us -> 305 us (0.987); the launches traced: 307 us -> 299 us
  waiting for transfers between devices: 106 us -> 83.1 us
  local copies, waits for them, and re-layouts: 18 us -> 28.3 us
    ppermute x12 -> x6, starting transfers between devices: 47.7 us -> 32.3 us  [from_above(): lax.ppermute(value, 'z', [((i + distance) % count, i) for i in range(coun...]
    ppermute x12 -> x6, waiting for transfers between devices: 19.7 us -> 8.23 us  [from_above(): lax.ppermute(value, 'z', [((i + distance) % count, i) for i in range(coun...]
    ppermute x3 -> x7, starting transfers between devices: 6.11 us -> 17.1 us  [swap_near(): return lax.ppermute(value, 'y_lo', [(0, 1), (1, 0)])]
    all_to_all x6 -> x7, starting transfers between devices: 58.4 us -> 69.2 us  [exchange(): return lax.all_to_all(blocks, axes, split_axis=0, concat_axis=0, tiled=True)]
    all_to_all x6 -> x7, waiting for transfers between devices: 53.3 us -> 45 us  [exchange(): return lax.all_to_all(blocks, axes, split_axis=0, concat_axis=0, tiled=True)]
    dot_general x0 -> x3, local copies, waits for them, and re-layouts: none -> 7.95 us  [token_sum(): lax.dot_general(left, right, (((0,), (0,)), ((), ())), preferred_element_...]
    ppermute x6 -> x5, starting transfers between devices: 20.3 us -> 15.4 us  [swap_cores(): return lax.ppermute(value, 'core', [(0, 1), (1, 0)])]
    dot_general x5 -> x3, matrix products: 3.31 us -> 7.35 us  [the longest x1 3.44 us: shards(): jnp.dot(half_all, both_near(weight_other, near_other), preferred_element_...]
  transfers between devices with their start and end apart: 32 -> 30, of which waited for: 18 -> 14; matrix products, arithmetic and copies ran while one was open for 11% -> 13% of each run, Pallas kernels for 0% -> 0%
where the time goes in v6:
time: 305 us; the launch traced here: 299 us
  starting transfers between devices  157 us (51%)
  waiting for transfers between devices  83.1 us (27%)
  local copies, waits for them, and re-layouts  28.3 us (9%)
  matrix products  14.8 us (5%)
  other arithmetic  14.4 us (5%)
    all_to_all x7, starting transfers between devices, exchange(): return lax.all_to_all(blocks, axes, split_axis=0, concat_axis=0, tiled=True)  69.2 us
    all_to_all x7, waiting for transfers between devices, exchange(): return lax.all_to_all(blocks, axes, split_axis=0, concat_axis=0, tiled=True)  45 us
    ppermute x6, starting transfers between devices, from_above(): lax.ppermute(value, 'z', [((i + distance) % count, i) for i in range(coun...  32.3 us
    ppermute x7, waiting for transfers between devices, swap_near(): return lax.ppermute(value, 'y_lo', [(0, 1), (1, 0)])  27.2 us
    ppermute x7, starting transfers between devices, swap_near(): return lax.ppermute(value, 'y_lo', [(0, 1), (1, 0)])  17.1 us
    ppermute x5, starting transfers between devices, swap_cores(): return lax.ppermute(value, 'core', [(0, 1), (1, 0)])  15.4 us
    ppermute x2, starting transfers between devices, trade_pair(): other = lax.ppermute(sent, axis_name, [(0, 1), (1, 0)])  13.6 us
    ppermute x3, starting transfers between devices, trade_x(): lax.ppermute(turned[step], 'x', [(i, (i + step) % count) for i in range(c...  9.33 us
  transfers between devices with their start and end apart: 30, of which 14 were waited for; matrix products, arithmetic and copies ran while one was open for 13% of the time, Pallas kernels for 0%

profile of v6, /device:TPU:1, one launch (start us, length us, event | category | flops | bytes accessed | tf_op | source)
XLA Modules:
  0.0 299.3 jit_solution(2659811008605551553)
XLA Ops:
  7.1 8.8 %collective-permute-start = (bf16[4,2,12,256]{3,1,2,0:T(2,128)(2,1)S(1)}, bf16[4,2,12,256]{3,1,2,0:T(2,128)(2,1)S(1)}, u32[]{:S(2)}, u32[]{:S(2)}) collective-permute-start(bf16[4,2,12,256]{3,1,2,0:T(2,128)(2,1)S(1)} %bitcast.229), channel_id=1, source_target_pairs={{0,1},{1,0},{2,3},{3,2},{4,5},{5,4},{6,7},{7,6},{8,9},{9,8},{10,11... | collective-permute-start | bytes 147464 | tf_op jit(solution)/shard_map/ppermute | solution.py:61
  15.9 9.6 %all-to-all-start = ((bf16[16,8,2048]{2,1,0:T(8,128)(2,1)}), bf16[16,8,2048]{2,1,0:T(8,128)(2,1)S(1)}, u32[]{:S(2)}, u32[]{:S(2)}) async-start(bf16[16,8,2048]{2,1,0:T(8,128)(2,1)} %reshape.299), calls=%async_computation | async-start | bytes 1048576 | tf_op jit(solution)/shard_map/all_to_all | solution.py:28
  26.0 4.8 %collective-permute-start.1 = (bf16[2,4,12,256]{3,1,2,0:T(4,128)(2,1)S(1)}, bf16[2,4,12,256]{3,1,2,0:T(4,128)(2,1)S(1)}, u32[]{:S(2)}, u32[]{:S(2)}) collective-permute-start(bf16[2,4,12,256]{3,1,2,0:T(4,128)(2,1)S(1)} %bitcast.228), channel_id=1, source_target_pairs={{0,2},{2,0},{1,3},{3,1},{4,6},{6,4},{5,7},{7,5},{8,10},{10,8},{9,1... | collective-permute-start | bytes 147464 | tf_op jit(solution)/shard_map/ppermute | solution.py:61
  34.0 4.4 %collective-permute-start.2 = (bf16[2,2,12,256]{3,1,2,0:T(2,128)(2,1)S(1)}, bf16[2,2,12,256]{3,1,2,0:T(2,128)(2,1)S(1)}, u32[]{:S(2)}, u32[]{:S(2)}) collective-permute-start(bf16[2,2,12,256]{3,1,2,0:T(2,128)(2,1)S(1)} %bitcast.239), channel_id=1, source_target_pairs={{0,12},{4,0},{8,4},{12,8},{1,13},{5,1},{9,5},{13,9},{2,14},{6,2},{... | collective-permute-start | bytes 73736 | tf_op jit(solution)/shard_map/ppermute | solution.py:69
  52.2 3.9 %collective-permute-done.5 = bf16[896,256]{1,0:T(8,128)(2,1)S(1)} collective-permute-done((bf16[896,256]{1,0:T(8,128)(2,1)S(1)}, bf16[896,256]{1,0:T(8,128)(2,1)S(1)}, u32[]{:S(2)}, u32[]{:S(2)}) %collective-permute-start.5) | collective-permute-done | bytes 458784 | tf_op jit(solution)/shard_map/ppermute | solution.py:36
  56.1 9.8 %collective-permute-done.7 = bf16[896,256]{1,0:T(8,128)(2,1)S(1)} collective-permute-done((bf16[896,256]{1,0:T(8,128)(2,1)S(1)}, bf16[896,256]{1,0:T(8,128)(2,1)S(1)}, u32[]{:S(2)}, u32[]{:S(2)}) %collective-permute-start.7) | collective-permute-done | bytes 458784 | tf_op jit(solution)/shard_map/ppermute | solution.py:36
  69.5 7.6 %all-to-all-start.1 = ((bf16[16,64,2048]{2,1,0:T(8,128)(2,1)}), bf16[16,64,2048]{2,1,0:T(8,128)(2,1)}, u32[]{:S(2)}, u32[]{:S(2)}) async-start(bf16[16,64,2048]{2,1,0:T(8,128)(2,1)} %bitcast.200), calls=%async_computation.1 | async-start | bytes 8388608 | tf_op jit(solution)/shard_map/all_to_all | solution.py:28
  77.1 6.9 %collective-permute-start.10 = (bf16[64,256]{1,0:T(8,128)(2,1)S(1)}, bf16[64,256]{1,0:T(8,128)(2,1)S(1)}, u32[]{:S(2)}, u32[]{:S(2)}) collective-permute-start(bf16[64,256]{1,0:T(8,128)(2,1)S(1)} %multiply_convert_fusion), channel_id=1, source_target_pairs={{192,0},{208,16},{224,32},{240,48},{0,64},{16,80},{32,96},{48,112}... | collective-permute-start | bytes 98312 | tf_op jit(solution)/shard_map/ppermute | solution.py:41
  84.0 7.3 %collective-permute-start.9 = (bf16[64,256]{1,0:T(8,128)(2,1)S(1)}, bf16[64,256]{1,0:T(8,128)(2,1)S(1)}, u32[]{:S(2)}, u32[]{:S(2)}) collective-permute-start(bf16[64,256]{1,0:T(8,128)(2,1)S(1)} %multiply_convert_fusion), channel_id=1, source_target_pairs={{128,0},{144,16},{160,32},{176,48},{192,64},{208,80},{224,96},{240... | collective-permute-start | bytes 98312 | tf_op jit(solution)/shard_map/ppermute | solution.py:41
  91.3 7.0 %collective-permute-start.8 = (bf16[64,256]{1,0:T(8,128)(2,1)S(1)}, bf16[64,256]{1,0:T(8,128)(2,1)S(1)}, u32[]{:S(2)}, u32[]{:S(2)}) collective-permute-start(bf16[64,256]{1,0:T(8,128)(2,1)S(1)} %multiply_convert_fusion), channel_id=1, source_target_pairs={{64,0},{80,16},{96,32},{112,48},{128,64},{144,80},{160,96},{176,11... | collective-permute-start | bytes 98312 | tf_op jit(solution)/shard_map/ppermute | solution.py:41
  101.3 5.8 %collective-permute-start.12 = (bf16[4,64,256]{2,1,0:T(8,128)(2,1)S(1)}, bf16[4,64,256]{2,1,0:T(8,128)(2,1)S(1)}, u32[]{:S(2)}, u32[]{:S(2)}) collective-permute-start(bf16[4,64,256]{2,1,0:T(8,128)(2,1)S(1)} %get-tuple-element.50), channel_id=1, source_target_pairs={{32,0},{48,16},{64,32},{80,48},{96,64},{112,80},{128,96},{144,112}... | collective-permute-start | bytes 393224 | tf_op jit(solution)/shard_map/ppermute | solution.py:41
  107.1 3.4 %collective-permute-start.11 = (bf16[4,64,256]{2,1,0:T(8,128)(2,1)S(1)}, bf16[4,64,256]{2,1,0:T(8,128)(2,1)S(1)}, u32[]{:S(2)}, u32[]{:S(2)}) collective-permute-start(bf16[4,64,256]{2,1,0:T(8,128)(2,1)S(1)} %get-tuple-element.50), channel_id=1, source_target_pairs={{16,0},{32,16},{48,32},{64,48},{80,64},{96,80},{112,96},{128,112},... | collective-permute-start | bytes 393224 | tf_op jit(solution)/shard_map/ppermute | solution.py:41
  112.6 5.3 %collective-permute-done.13 = bf16[4,64,256]{2,1,0:T(8,128)(2,1)S(1)} collective-permute-done((bf16[4,64,256]{2,1,0:T(8,128)(2,1)S(1)}, bf16[4,64,256]{2,1,0:T(8,128)(2,1)S(1)}, u32[]{:S(2)}, u32[]{:S(2)}) %collective-permute-start.13) | collective-permute-done | bytes 131104 | tf_op jit(solution)/shard_map/ppermute | solution.py:41
  118.3 11.6 %all-to-all-done.1 = bf16[16,64,2048]{2,1,0:T(8,128)(2,1)} async-done(((bf16[16,64,2048]{2,1,0:T(8,128)(2,1)}), bf16[16,64,2048]{2,1,0:T(8,128)(2,1)}, u32[]{:S(2)}, u32[]{:S(2)}) %all-to-all-start.1) | async-done | bytes 4194336 | tf_op jit(solution)/shard_map/all_to_all | solution.py:28
  129.8 3.4 %fusion.38 = f32[1024,256]{1,0:T(8,128)S(1)} fusion(bf16[1024,2048]{1,0:T(8,128)(2,1)} %bitcast.29, bf16[2048,256]{1,0:T(8,128)(2,1)S(1)} %bitcast.213), kind=kOutput, calls=%fused_computation.127 | convolution fusion | flops 1073741824 | bytes 6291456 | tf_op jit(solution)/shard_map/dot_general | solution.py:184
  137.8 3.4 %fusion.6 = bf16[1024,256]{1,0:T(8,128)(2,1)S(1)} fusion(f32[1024,256]{1,0:T(8,128)S(1)} %collective-permute-done.14, bf16[1024,2048]{1,0:T(8,128)(2,1)} %bitcast.29, bf16[2048,256]{1,0:T(8,128)(2,1)S(1)} %bitcast.214), kind=kOutput, calls=%fused_computation.9 | convolution fusion | flops 1074266112 | bytes 6815744 | tf_op jit(solution)/shard_map/dot_general | solution.py:187
  142.5 11.5 %all-to-all-start.2 = ((bf16[16,64,256]{2,1,0:T(8,128)(2,1)}), bf16[16,64,256]{2,1,0:T(8,128)(2,1)S(1)}, u32[]{:S(2)}, u32[]{:S(2)}) async-start(bf16[16,64,256]{2,1,0:T(8,128)(2,1)} %copy.348), calls=%async_computation.2 | async-start | bytes 1048576 | tf_op jit(solution)/shard_map/all_to_all | solution.py:28
  159.9 17.1 %all-to-all-done.2 = bf16[16,64,256]{2,1,0:T(8,128)(2,1)S(1)} async-done(((bf16[16,64,256]{2,1,0:T(8,128)(2,1)}), bf16[16,64,256]{2,1,0:T(8,128)(2,1)S(1)}, u32[]{:S(2)}, u32[]{:S(2)}) %all-to-all-start.2) | async-done | bytes 524320 | tf_op jit(solution)/shard_map/all_to_all | solution.py:28
  178.0 19.5 %all-to-all-start.3 = ((f32[16,1,64]{2,1,0:T(1,128)}), f32[16,1,64]{2,1,0:T(1,128)S(1)}, u32[]{:S(2)}, u32[]{:S(2)}) async-start(f32[16,1,64]{2,1,0:T(1,128)} %broadcast_in_dim.21), calls=%async_computation.3 | async-start | bytes 16384 | tf_op jit(solution)/shard_map/all_to_all | solution.py:28
  197.6 6.9 %all-to-all-done.3 = f32[16,1,64]{2,1,0:T(1,128)S(1)} async-done(((f32[16,1,64]{2,1,0:T(1,128)}), f32[16,1,64]{2,1,0:T(1,128)S(1)}, u32[]{:S(2)}, u32[]{:S(2)}) %all-to-all-start.3) | async-done | bytes 4128 | tf_op jit(solution)/shard_map/all_to_all | solution.py:28
  205.5 6.2 %all-to-all-start.4 = ((bf16[16,72,256]{2,1,0:T(8,128)(2,1)}), bf16[16,72,256]{2,1,0:T(8,128)(2,1)S(1)}, u32[]{:S(2)}, u32[]{:S(2)}) async-start(bf16[16,72,256]{2,1,0:T(8,128)(2,1)} %broadcast_in_dim.46), calls=%async_computation.4 | async-start | bytes 1179648 | tf_op jit(solution)/shard_map/all_to_all | solution.py:28
  212.8 3.5 %fusion.39 = f32[2048,256]{1,0:T(8,128)S(1)} fusion(bf16[1024,2048]{1,0:T(8,128)(2,1)} %bitcast.29, bf16[1024,256]{1,0:T(8,128)(2,1)S(1)} %collective-permute-done.17), kind=kOutput, calls=%fused_computation.128 | convolution fusion | flops 1073741824 | bytes 6815744 | tf_op jit(solution)/shard_map/dot_general | solution.py:24
  221.8 3.1 %collective-permute-start.20 = (bf16[1024,256]{1,0:T(8,128)(2,1)}, bf16[1024,256]{1,0:T(8,128)(2,1)}, u32[]{:S(2)}, u32[]{:S(2)}) collective-permute-start(bf16[1024,256]{1,0:T(8,128)(2,1)} %get-tuple-element.39), channel_id=1, source_target_pairs={{0,1},{1,0},{2,3},{3,2},{4,5},{5,4},{6,7},{7,6},{8,9},{9,8},{10,11... | collective-permute-start | bytes 1572872 | tf_op jit(solution)/shard_map/ppermute | solution.py:32
  224.9 6.5 %copy.365 = bf16[2048,1024]{1,0:T(8,128)(2,1)} copy(bf16[2048,1024]{0,1:T(8,128)(2,1)} %bitcast.58) | data formatting | bytes 8388608 | tf_op jit(solution)/shard_map/dot_general | solution.py:24
  231.4 3.3 %fusion = f32[2,896,256]{2,1,0:T(8,128)S(1)} fusion(bf16[1024,256,1]{1,0,2:T(8,128)(2,1)} %reshape.325, bf16[2,1024,1024]{2,1,0:T(8,128)(2,1)} %bitcast.202), kind=kOutput, calls=%fused_computation | convolution fusion | flops 939524096 | bytes 6029312 | tf_op jit(solution)/shard_map/dot_general | solution.py:24
  242.8 5.1 %collective-permute-start.19 = (f32[896,256]{1,0:T(8,128)}, f32[896,256]{1,0:T(8,128)}, u32[]{:S(2)}, u32[]{:S(2)}) collective-permute-start(f32[896,256]{1,0:T(8,128)} %bitcast_add_fusion), channel_id=1, source_target_pairs={{0,1},{1,0},{2,3},{3,2},{4,5},{5,4},{6,7},{7,6},{8,9},{9,8},{10,11... | collective-permute-start | bytes 2752520 | tf_op jit(solution)/shard_map/ppermute | solution.py:32
  250.4 3.6 %all-to-all-start.5 = ((bf16[16,72,512]{2,1,0:T(8,128)(2,1)}), bf16[16,72,512]{2,1,0:T(8,128)(2,1)S(1)}, u32[]{:S(2)}, u32[]{:S(2)}) async-start(bf16[16,72,512]{2,1,0:T(8,128)(2,1)} %pad_maximum_fusion), calls=%async_computation.5 | async-start | bytes 2359296 | tf_op jit(solution)/shard_map/all_to_all | solution.py:28
  255.5 9.8 %collective-permute-done.16 = f32[896,256]{1,0:T(8,128)} collective-permute-done((f32[896,256]{1,0:T(8,128)}, f32[896,256]{1,0:T(8,128)}, u32[]{:S(2)}, u32[]{:S(2)}) %collective-permute-start.16) | collective-permute-done | bytes 917536 | tf_op jit(solution)/shard_map/ppermute | solution.py:36
  265.3 3.1 %broadcast_select_fusion = (f32[896,256]{1,0:T(8,128)}, f32[896,256]{1,0:T(8,128)}) fusion(f32[896,256]{1,0:T(8,128)} %collective-permute-done.19, pred[]{:T(512)S(6)} %eq.11, f32[896,256]{1,0:T(8,128)} %collective-permute-done.16, f32[2,896,256]{2,1,0:T(8,128)} %copy-done, s32[]{:T(128)S(6)} %select_n.175), kind=kLoop, calls=%fused_computation.46 | loop fusion | flops 688128 | bytes 4587525 | tf_op jit(solution)/shard_map/jit(_where)/select_n | solution.py:265
  271.8 3.1 %all-to-all-done.5 = bf16[16,72,512]{2,1,0:T(8,128)(2,1)S(1)} async-done(((bf16[16,72,512]{2,1,0:T(8,128)(2,1)}), bf16[16,72,512]{2,1,0:T(8,128)(2,1)S(1)}, u32[]{:S(2)}, u32[]{:S(2)}) %all-to-all-start.5) | async-done | bytes 1179680 | tf_op jit(solution)/shard_map/all_to_all | solution.py:28
  275.7 11.3 %all-to-all-start.6 = ((bf16[16,4,512]{2,1,0:T(4,128)(2,1)}), bf16[16,4,512]{2,1,0:T(4,128)(2,1)S(1)}, u32[]{:S(2)}, u32[]{:S(2)}) async-start(bf16[16,4,512]{2,1,0:T(4,128)(2,1)} %reshape.314), calls=%async_computation.6 | async-start | bytes 131072 | tf_op jit(solution)/shard_map/all_to_all | solution.py:28
  292.2 6.4 %all-to-all-done.6 = bf16[16,4,512]{2,1,0:T(4,128)(2,1)S(1)} async-done(((bf16[16,4,512]{2,1,0:T(4,128)(2,1)}), bf16[16,4,512]{2,1,0:T(4,128)(2,1)S(1)}, u32[]{:S(2)}, u32[]{:S(2)}) %all-to-all-start.6) | async-done | bytes 65568 | tf_op jit(solution)/shard_map/all_to_all | solution.py:28
  (179 shorter events, 74.5 us)
Async XLA Ops:
  5.2 25.7 %copy-start.1 = (bf16[896,256]{1,0:T(8,128)(2,1)S(1)}, bf16[896,256]{1,0:T(8,128)(2,1)}, u32[]{:S(2)}) copy-start(bf16[896,256]{1,0:T(8,128)(2,1)} %param.18) | copy-start | bytes 1376260
  5.2 25.7 %copy-start.2 = (bf16[896,256]{1,0:T(8,128)(2,1)S(1)}, bf16[896,256]{1,0:T(8,128)(2,1)}, u32[]{:S(2)}) copy-start(bf16[896,256]{1,0:T(8,128)(2,1)} %param.17) | copy-start | bytes 1376260
  7.1 18.4 %collective-permute-start = (bf16[4,2,12,256]{3,1,2,0:T(2,128)(2,1)S(1)}, bf16[4,2,12,256]{3,1,2,0:T(2,128)(2,1)S(1)}, u32[]{:S(2)}, u32[]{:S(2)}) collective-permute-start(bf16[4,2,12,256]{3,1,2,0:T(2,128)(2,1)S(1)} %bitcast.229), channel_id=1, source_target_pairs={{0,1},{1,0},{2,3},{3,2},{4,5},{5,4},{6,7},{7,6},{8,9},{9,8},{10,11... | collective-permute-start | bytes 147464 | tf_op jit(solution)/shard_map/ppermute | solution.py:61
  15.9 50.0 %all-to-all-start = ((bf16[16,8,2048]{2,1,0:T(8,128)(2,1)}), bf16[16,8,2048]{2,1,0:T(8,128)(2,1)S(1)}, u32[]{:S(2)}, u32[]{:S(2)}) async-start(bf16[16,8,2048]{2,1,0:T(8,128)(2,1)} %reshape.299), calls=%async_computation | async-start | bytes 1048576 | tf_op jit(solution)/shard_map/all_to_all | solution.py:28
  26.0 7.4 %collective-permute-start.1 = (bf16[2,4,12,256]{3,1,2,0:T(4,128)(2,1)S(1)}, bf16[2,4,12,256]{3,1,2,0:T(4,128)(2,1)S(1)}, u32[]{:S(2)}, u32[]{:S(2)}) collective-permute-start(bf16[2,4,12,256]{3,1,2,0:T(4,128)(2,1)S(1)} %bitcast.228), channel_id=1, source_target_pairs={{0,2},{2,0},{1,3},{3,1},{4,6},{6,4},{5,7},{7,5},{8,10},{10,8},{9,1... | collective-permute-start | bytes 147464 | tf_op jit(solution)/shard_map/ppermute | solution.py:61
  31.0 16.9 %collective-permute-start.6 = (bf16[896,256]{1,0:T(8,128)(2,1)S(1)}, bf16[896,256]{1,0:T(8,128)(2,1)S(1)}, u32[]{:S(2)}, u32[]{:S(2)}) collective-permute-start(bf16[896,256]{1,0:T(8,128)(2,1)S(1)} %get-tuple-element.35), channel_id=1, source_target_pairs={{0,1},{1,0},{2,3},{3,2},{4,5},{5,4},{6,7},{7,6},{8,9},{9,8},{10,11... | collective-permute-start | bytes 1376264 | tf_op jit(solution)/shard_map/ppermute | solution.py:32
  34.0 12.6 %collective-permute-start.2 = (bf16[2,2,12,256]{3,1,2,0:T(2,128)(2,1)S(1)}, bf16[2,2,12,256]{3,1,2,0:T(2,128)(2,1)S(1)}, u32[]{:S(2)}, u32[]{:S(2)}) collective-permute-start(bf16[2,2,12,256]{3,1,2,0:T(2,128)(2,1)S(1)} %bitcast.239), channel_id=1, source_target_pairs={{0,12},{4,0},{8,4},{12,8},{1,13},{5,1},{9,5},{13,9},{2,14},{6,2},{... | collective-permute-start | bytes 73736 | tf_op jit(solution)/shard_map/ppermute | solution.py:69
  38.4 8.2 %collective-permute-start.3 = (bf16[2,2,12,256]{3,1,2,0:T(2,128)(2,1)S(1)}, bf16[2,2,12,256]{3,1,2,0:T(2,128)(2,1)S(1)}, u32[]{:S(2)}, u32[]{:S(2)}) collective-permute-start(bf16[2,2,12,256]{3,1,2,0:T(2,128)(2,1)S(1)} %bitcast.235), channel_id=1, source_target_pairs={{0,8},{4,12},{8,0},{12,4},{1,9},{5,13},{9,1},{13,5},{2,10},{6,14},... | collective-permute-start | bytes 73736 | tf_op jit(solution)/shard_map/ppermute | solution.py:69
  40.9 6.1 %collective-permute-start.4 = (bf16[2,2,12,256]{3,1,2,0:T(2,128)(2,1)S(1)}, bf16[2,2,12,256]{3,1,2,0:T(2,128)(2,1)S(1)}, u32[]{:S(2)}, u32[]{:S(2)}) collective-permute-start(bf16[2,2,12,256]{3,1,2,0:T(2,128)(2,1)S(1)} %bitcast.237), channel_id=1, source_target_pairs={{0,4},{4,8},{8,12},{12,0},{1,5},{5,9},{9,13},{13,1},{2,6},{6,10},{... | collective-permute-start | bytes 73736 | tf_op jit(solution)/shard_map/ppermute | solution.py:69
  43.4 12.7 %collective-permute-start.5 = (bf16[896,256]{1,0:T(8,128)(2,1)S(1)}, bf16[896,256]{1,0:T(8,128)(2,1)S(1)}, u32[]{:S(2)}, u32[]{:S(2)}) collective-permute-start(bf16[896,256]{1,0:T(8,128)(2,1)S(1)} %get-tuple-element.36), channel_id=1, source_target_pairs={{0,256},{256,0},{1,257},{257,1},{2,258},{258,2},{3,259},{259,3},{4... | collective-permute-start | bytes 1376264 | tf_op jit(solution)/shard_map/ppermute | solution.py:36
  47.9 18.1 %collective-permute-start.7 = (bf16[896,256]{1,0:T(8,128)(2,1)S(1)}, bf16[896,256]{1,0:T(8,128)(2,1)S(1)}, u32[]{:S(2)}, u32[]{:S(2)}) collective-permute-start(bf16[896,256]{1,0:T(8,128)(2,1)S(1)} %collective-permute-done.6), channel_id=1, source_target_pairs={{0,256},{256,0},{1,257},{257,1},{2,258},{258,2},{3,259},{259,3},{4... | collective-permute-start | bytes 1376264 | tf_op jit(solution)/shard_map/ppermute | solution.py:36
  69.5 60.3 %all-to-all-start.1 = ((bf16[16,64,2048]{2,1,0:T(8,128)(2,1)}), bf16[16,64,2048]{2,1,0:T(8,128)(2,1)}, u32[]{:S(2)}, u32[]{:S(2)}) async-start(bf16[16,64,2048]{2,1,0:T(8,128)(2,1)} %bitcast.200), calls=%async_computation.1 | async-start | bytes 8388608 | tf_op jit(solution)/shard_map/all_to_all | solution.py:28
  77.1 21.3 %collective-permute-start.10 = (bf16[64,256]{1,0:T(8,128)(2,1)S(1)}, bf16[64,256]{1,0:T(8,128)(2,1)S(1)}, u32[]{:S(2)}, u32[]{:S(2)}) collective-permute-start(bf16[64,256]{1,0:T(8,128)(2,1)S(1)} %multiply_convert_fusion), channel_id=1, source_target_pairs={{192,0},{208,16},{224,32},{240,48},{0,64},{16,80},{32,96},{48,112}... | collective-permute-start | bytes 98312 | tf_op jit(solution)/shard_map/ppermute | solution.py:41
  84.0 14.4 %collective-permute-start.9 = (bf16[64,256]{1,0:T(8,128)(2,1)S(1)}, bf16[64,256]{1,0:T(8,128)(2,1)S(1)}, u32[]{:S(2)}, u32[]{:S(2)}) collective-permute-start(bf16[64,256]{1,0:T(8,128)(2,1)S(1)} %multiply_convert_fusion), channel_id=1, source_target_pairs={{128,0},{144,16},{160,32},{176,48},{192,64},{208,80},{224,96},{240... | collective-permute-start | bytes 98312 | tf_op jit(solution)/shard_map/ppermute | solution.py:41
  91.3 10.0 %collective-permute-start.8 = (bf16[64,256]{1,0:T(8,128)(2,1)S(1)}, bf16[64,256]{1,0:T(8,128)(2,1)S(1)}, u32[]{:S(2)}, u32[]{:S(2)}) collective-permute-start(bf16[64,256]{1,0:T(8,128)(2,1)S(1)} %multiply_convert_fusion), channel_id=1, source_target_pairs={{64,0},{80,16},{96,32},{112,48},{128,64},{144,80},{160,96},{176,11... | collective-permute-start | bytes 98312 | tf_op jit(solution)/shard_map/ppermute | solution.py:41
  101.3 16.6 %collective-permute-start.12 = (bf16[4,64,256]{2,1,0:T(8,128)(2,1)S(1)}, bf16[4,64,256]{2,1,0:T(8,128)(2,1)S(1)}, u32[]{:S(2)}, u32[]{:S(2)}) collective-permute-start(bf16[4,64,256]{2,1,0:T(8,128)(2,1)S(1)} %get-tuple-element.50), channel_id=1, source_target_pairs={{32,0},{48,16},{64,32},{80,48},{96,64},{112,80},{128,96},{144,112}... | collective-permute-start | bytes 393224 | tf_op jit(solution)/shard_map/ppermute | solution.py:41
  107.1 10.8 %collective-permute-start.11 = (bf16[4,64,256]{2,1,0:T(8,128)(2,1)S(1)}, bf16[4,64,256]{2,1,0:T(8,128)(2,1)S(1)}, u32[]{:S(2)}, u32[]{:S(2)}) collective-permute-start(bf16[4,64,256]{2,1,0:T(8,128)(2,1)S(1)} %get-tuple-element.50), channel_id=1, source_target_pairs={{16,0},{32,16},{48,32},{64,48},{80,64},{96,80},{112,96},{128,112},... | collective-permute-start | bytes 393224 | tf_op jit(solution)/shard_map/ppermute | solution.py:41
  110.6 7.3 %collective-permute-start.13 = (bf16[4,64,256]{2,1,0:T(8,128)(2,1)S(1)}, bf16[4,64,256]{2,1,0:T(8,128)(2,1)S(1)}, u32[]{:S(2)}, u32[]{:S(2)}) collective-permute-start(bf16[4,64,256]{2,1,0:T(8,128)(2,1)S(1)} %get-tuple-element.50), channel_id=1, source_target_pairs={{240,0},{0,16},{16,32},{32,48},{48,64},{64,80},{80,96},{96,112},{1... | collective-permute-start | bytes 393224 | tf_op jit(solution)/shard_map/ppermute | solution.py:41
  133.3 4.6 %collective-permute-start.14 = (f32[1024,256]{1,0:T(8,128)S(1)}, f32[1024,256]{1,0:T(8,128)S(1)}, u32[]{:S(2)}, u32[]{:S(2)}) collective-permute-start(f32[1024,256]{1,0:T(8,128)S(1)} %fusion.38), channel_id=1, source_target_pairs={{0,1},{1,0},{2,3},{3,2},{4,5},{5,4},{6,7},{7,6},{8,9},{9,8},{10,11... | collective-permute-start | bytes 3145736 | tf_op jit(solution)/shard_map/ppermute | solution.py:32
  142.5 34.5 %all-to-all-start.2 = ((bf16[16,64,256]{2,1,0:T(8,128)(2,1)}), bf16[16,64,256]{2,1,0:T(8,128)(2,1)S(1)}, u32[]{:S(2)}, u32[]{:S(2)}) async-start(bf16[16,64,256]{2,1,0:T(8,128)(2,1)} %copy.348), calls=%async_computation.2 | async-start | bytes 1048576 | tf_op jit(solution)/shard_map/all_to_all | solution.py:28
  153.9 57.9 %collective-permute-start.15 = (bf16[256,256]{1,0:T(8,128)(2,1)S(1)}, bf16[256,256]{1,0:T(8,128)(2,1)S(1)}, u32[]{:S(2)}, u32[]{:S(2)}) collective-permute-start(bf16[256,256]{1,0:T(8,128)(2,1)S(1)} %copy-done.3), channel_id=1, source_target_pairs={{0,256},{256,0},{1,257},{257,1},{2,258},{258,2},{3,259},{259,3},{4... | collective-permute-start | bytes 393224 | tf_op jit(solution)/shard_map/ppermute | solution.py:36
  157.2 55.6 %collective-permute-start.17 = (bf16[1024,256]{1,0:T(8,128)(2,1)S(1)}, bf16[1024,256]{1,0:T(8,128)(2,1)S(1)}, u32[]{:S(2)}, u32[]{:S(2)}) collective-permute-start(bf16[1024,256]{1,0:T(8,128)(2,1)S(1)} %reshape.318), channel_id=1, source_target_pairs={{0,1},{1,0},{2,3},{3,2},{4,5},{5,4},{6,7},{7,6},{8,9},{9,8},{10,11... | collective-permute-start | bytes 1572872 | tf_op jit(solution)/shard_map/ppermute | solution.py:32
  178.0 26.4 %all-to-all-start.3 = ((f32[16,1,64]{2,1,0:T(1,128)}), f32[16,1,64]{2,1,0:T(1,128)S(1)}, u32[]{:S(2)}, u32[]{:S(2)}) async-start(f32[16,1,64]{2,1,0:T(1,128)} %broadcast_in_dim.21), calls=%async_computation.3 | async-start | bytes 16384 | tf_op jit(solution)/shard_map/all_to_all | solution.py:28
  205.5 42.4 %all-to-all-start.4 = ((bf16[16,72,256]{2,1,0:T(8,128)(2,1)}), bf16[16,72,256]{2,1,0:T(8,128)(2,1)S(1)}, u32[]{:S(2)}, u32[]{:S(2)}) async-start(bf16[16,72,256]{2,1,0:T(8,128)(2,1)} %broadcast_in_dim.46), calls=%async_computation.4 | async-start | bytes 1179648 | tf_op jit(solution)/shard_map/all_to_all | solution.py:28
  217.5 23.1 %collective-permute-start.18 = (f32[896,256]{1,0:T(8,128)}, f32[896,256]{1,0:T(8,128)}, u32[]{:S(2)}, u32[]{:S(2)}) collective-permute-start(f32[896,256]{1,0:T(8,128)} %dynamic-slice_bitcast_fusion), channel_id=1, source_target_pairs={{0,256},{256,0},{1,257},{257,1},{2,258},{258,2},{3,259},{259,3},{4... | collective-permute-start | bytes 2752520 | tf_op jit(solution)/shard_map/ppermute | solution.py:36
  221.8 32.5 %collective-permute-start.20 = (bf16[1024,256]{1,0:T(8,128)(2,1)}, bf16[1024,256]{1,0:T(8,128)(2,1)}, u32[]{:S(2)}, u32[]{:S(2)}) collective-permute-start(bf16[1024,256]{1,0:T(8,128)(2,1)} %get-tuple-element.39), channel_id=1, source_target_pairs={{0,1},{1,0},{2,3},{3,2},{4,5},{5,4},{6,7},{7,6},{8,9},{9,8},{10,11... | collective-permute-start | bytes 1572872 | tf_op jit(solution)/shard_map/ppermute | solution.py:32
  235.8 29.5 %collective-permute-start.16 = (f32[896,256]{1,0:T(8,128)}, f32[896,256]{1,0:T(8,128)}, u32[]{:S(2)}, u32[]{:S(2)}) collective-permute-start(f32[896,256]{1,0:T(8,128)} %dynamic-slice_bitcast_fusion.1), channel_id=1, source_target_pairs={{0,256},{256,0},{1,257},{257,1},{2,258},{258,2},{3,259},{259,3},{4... | collective-permute-start | bytes 2752520 | tf_op jit(solution)/shard_map/ppermute | solution.py:36
  242.8 22.5 %collective-permute-start.19 = (f32[896,256]{1,0:T(8,128)}, f32[896,256]{1,0:T(8,128)}, u32[]{:S(2)}, u32[]{:S(2)}) collective-permute-start(f32[896,256]{1,0:T(8,128)} %bitcast_add_fusion), channel_id=1, source_target_pairs={{0,1},{1,0},{2,3},{3,2},{4,5},{5,4},{6,7},{7,6},{8,9},{9,8},{10,11... | collective-permute-start | bytes 2752520 | tf_op jit(solution)/shard_map/ppermute | solution.py:32
  250.4 24.5 %all-to-all-start.5 = ((bf16[16,72,512]{2,1,0:T(8,128)(2,1)}), bf16[16,72,512]{2,1,0:T(8,128)(2,1)S(1)}, u32[]{:S(2)}, u32[]{:S(2)}) async-start(bf16[16,72,512]{2,1,0:T(8,128)(2,1)} %pad_maximum_fusion), calls=%async_computation.5 | async-start | bytes 2359296 | tf_op jit(solution)/shard_map/all_to_all | solution.py:28
  269.2 19.8 %collective-permute-start.21 = (f32[2,128,256]{2,1,0:T(8,128)S(1)}, f32[2,128,256]{2,1,0:T(8,128)S(1)}, u32[]{:S(2)}, u32[]{:S(2)}) collective-permute-start(f32[2,128,256]{2,1,0:T(8,128)S(1)} %fusion.20), channel_id=1, source_target_pairs={{0,256},{256,0},{1,257},{257,1},{2,258},{258,2},{3,259},{259,3},{4... | collective-permute-start | bytes 786440 | tf_op jit(solution)/shard_map/ppermute | solution.py:36
  275.7 22.8 %all-to-all-start.6 = ((bf16[16,4,512]{2,1,0:T(4,128)(2,1)}), bf16[16,4,512]{2,1,0:T(4,128)(2,1)S(1)}, u32[]{:S(2)}, u32[]{:S(2)}) async-start(bf16[16,4,512]{2,1,0:T(4,128)(2,1)} %reshape.314), calls=%async_computation.6 | async-start | bytes 131072 | tf_op jit(solution)/shard_map/all_to_all | solution.py:28
  287.1 4.5 %collective-permute-start.22 = (f32[16,256]{1,0:T(8,128)S(1)}, f32[16,256]{1,0:T(8,128)S(1)}, u32[]{:S(2)}, u32[]{:S(2)}) collective-permute-start(f32[16,256]{1,0:T(8,128)S(1)} %bitcast.242), channel_id=1, source_target_pairs={{0,256},{256,0},{1,257},{257,1},{2,258},{258,2},{3,259},{259,3},{4... | collective-permute-start | bytes 49160 | tf_op jit(solution)/shard_map/ppermute | solution.py:36
  (4 other events, 26.7 us)

commit v7 on v6

--- a/solution.py
+++ b/solution.py
@@ -130,7 +130,6 @@
 
     weight_own = jnp.where(on_first, gate_weight, up_weight)
     weight_other = swap_cores(jnp.where(on_first, up_weight, gate_weight))
-    near_own, near_other = swap_near(weight_own), swap_near(weight_other)
     near_join = swap_near(join_weight)
 
     hidden_wide = hidden.astype(wide)
@@ -148,7 +147,10 @@
         lax.axis_size("x"), 2, 2, 3 * row_count, features
     )
     norm_block = trade_pair(norm_sent.transpose(2, 0, 1, 3, 4), "core")
+    norm_block, near_own = lax.optimization_barrier((norm_block, swap_near(weight_own)))
     norm_block = trade_pair(norm_block.transpose(2, 0, 1, 3, 4), "y_hi")
+    norm_block, weight_other = lax.optimization_barrier((norm_block, weight_other))
+    near_other = swap_near(weight_other)
     norm_block = trade_x(norm_block.transpose(2, 0, 1, 3, 4)).reshape(
         dp_count, 3, row_count, features
     )
@@ -162,8 +164,8 @@
     normed = hidden_block * scale_block
     mlp_block = (normed * gain_block).astype(narrow)
 
-    unit_group, mlp_block, near_own, near_other = lax.optimization_barrier(
-        (unit_group, mlp_block, near_own, near_other)
+    unit_group, mlp_block, near_other = lax.optimization_barrier(
+        (unit_group, mlp_block, near_other)
     )
     mlp_z = gather_z(mlp_block)
     unit_halves = (
@@ -192,7 +194,20 @@
         .transpose(1, 0, 2, 3)
         .reshape(z_count, block_rows, features)
     )
-    input_grad = jnp.sum(exchange(partial_value, "z").astype(wide), axis=0)
+
+    mlp_own = (
+        mlp_z.reshape(z_count, dp_count, row_count, features)
+        .transpose(1, 0, 2, 3)
+        .reshape(tokens, features)
+    )
+    unit_sums = token_sum(half_all, jnp.concatenate([mlp_own, swap_cores(mlp_own)], axis=1))
+    partial_far, unit_sums = lax.optimization_barrier((exchange(partial_value, "z"), unit_sums))
+    unit_sums = unit_sums.reshape(2, part_width, 2 * features)[:, :units]
+    unit_kept = lax.dynamic_index_in_dim(unit_sums, here, 0, keepdims=False)
+    unit_near = swap_near(
+        lax.dynamic_index_in_dim(unit_sums, 1 - here, 0, keepdims=False).astype(narrow)
+    )
+    input_grad = jnp.sum(partial_far.astype(wide), axis=0)
 
     lifted = input_grad * gain_block
     mean_part = jnp.sum(lifted * normed, axis=1)
@@ -208,6 +223,7 @@
         [hidden_grad] + list(split_three(gain_part)) + [jnp.zeros((5, features), narrow)], axis=0
     )
     grad_z = exchange(jnp.broadcast_to(grad_sent[None], (z_count, sent_rows, features)), "z")
+    grad_z, unit_near = lax.optimization_barrier((grad_z, unit_near))
     gain_sum = jnp.sum(grad_z[:, block_rows : block_rows + 3].astype(wide), axis=(0, 1))[None]
     grad_all = (
         grad_z[:, :block_rows]
@@ -244,25 +260,16 @@
         .reshape(row_count, 2 * z_count * inputs)
     )
 
-    mlp_own = (
-        mlp_z.reshape(z_count, dp_count, row_count, features)
-        .transpose(1, 0, 2, 3)
-        .reshape(tokens, features)
-    )
+    unit_grad = unit_kept + unit_near.astype(wide)
+    own_grad = unit_grad[:, :features]
+    other_grad = swap_cores(unit_grad[:, features:])
+    gate_weight_grad = jnp.where(on_first, own_grad, other_grad)
+    up_weight_grad = jnp.where(on_first, other_grad, own_grad)
 
     def add_near(sums):
         kept = lax.dynamic_index_in_dim(sums, here, 0, keepdims=False)
         sent = lax.dynamic_index_in_dim(sums, 1 - here, 0, keepdims=False)
         return kept + swap_near(sent)
-
-    def unit_sums(mlp_input):
-        sums = token_sum(half_all, mlp_input).reshape(2, part_width, features)
-        return add_near(sums[:, :units])
-
-    other_grad = swap_cores(unit_sums(swap_cores(mlp_own)))
-    own_grad = unit_sums(mlp_own)
-    gate_weight_grad = jnp.where(on_first, own_grad, other_grad)
-    up_weight_grad = jnp.where(on_first, other_grad, own_grad)
 
     joined_half = jnp.concatenate(
         [half_all[:, units:part_width], half_all[:, part_width + units :]], axis=1

time: 305 us -> 294 us (0.964); the launches traced: 299 us -> 292 us
  local copies, waits for them, and re-layouts: 28.3 us -> 21.7 us
    all_to_all x7, waiting for transfers between devices: 45 us -> 35.6 us  [exchange(): return lax.all_to_all(blocks, axes, split_axis=0, concat_axis=0, tiled=True)]
    ppermute x7 -> x6, waiting for transfers between devices: 27.2 us -> 35.2 us  [swap_near(): return lax.ppermute(value, 'y_lo', [(0, 1), (1, 0)])]
    dot_general x3 -> x2, local copies, waits for them, and re-layouts: 7.95 us -> 0.41 us  [token_sum(): lax.dot_general(left, right, (((0,), (0,)), ((), ())), preferred_element_...]
    all_to_all x7, starting transfers between devices: 69.2 us -> 74.3 us  [exchange(): return lax.all_to_all(blocks, axes, split_axis=0, concat_axis=0, tiled=True)]
    ppermute x5, starting transfers between devices: 15.4 us -> 11.9 us  [swap_cores(): return lax.ppermute(value, 'core', [(0, 1), (1, 0)])]
    slice x1 -> x2, local copies, waits for them, and re-layouts: 0.12 us -> 3.42 us  [the longest x1 2.42 us: shards(): unit_sums = unit_sums.reshape(2, part_width, 2 * features)[:, :units]]
    ppermute x7 -> x6, starting transfers between devices: 17.1 us -> 16.4 us  [swap_near(): return lax.ppermute(value, 'y_lo', [(0, 1), (1, 0)])]
    dot_general x4 -> x3, matrix products: 7.43 us -> 7.21 us  [token_sum(): lax.dot_general(left, right, (((0,), (0,)), ((), ())), preferred_element_...]
  transfers between devices with their start and end apart: 30 -> 29, of which waited for: 14 -> 13; matrix products, arithmetic and copies ran while one was open for 13% -> 10% of each run, Pallas kernels for 0% -> 0%
where the time goes in v7:
time: 294 us; the launch traced here: 292 us
  starting transfers between devices  156 us (53%)
  waiting for transfers between devices  85 us (29%)
  local copies, waits for them, and re-layouts  21.7 us (7%)
  matrix products  14.6 us (5%)
  other arithmetic  12.4 us (4%)
    all_to_all x7, starting transfers between devices, exchange(): return lax.all_to_all(blocks, axes, split_axis=0, concat_axis=0, tiled=True)  74.3 us
    all_to_all x7, waiting for transfers between devices, exchange(): return lax.all_to_all(blocks, axes, split_axis=0, concat_axis=0, tiled=True)  35.6 us
    ppermute x6, waiting for transfers between devices, swap_near(): return lax.ppermute(value, 'y_lo', [(0, 1), (1, 0)])  35.2 us
    ppermute x6, starting transfers between devices, from_above(): lax.ppermute(value, 'z', [((i + distance) % count, i) for i in range(coun...  33 us
    ppermute x6, starting transfers between devices, swap_near(): return lax.ppermute(value, 'y_lo', [(0, 1), (1, 0)])  16.4 us
    ppermute x5, starting transfers between devices, swap_cores(): return lax.ppermute(value, 'core', [(0, 1), (1, 0)])  11.9 us
    ppermute x2, starting transfers between devices, trade_pair(): other = lax.ppermute(sent, axis_name, [(0, 1), (1, 0)])  11.2 us
    ppermute x3, starting transfers between devices, trade_x(): lax.ppermute(turned[step], 'x', [(i, (i + step) % count) for i in range(c...  9.33 us
  transfers between devices with their start and end apart: 29, of which 13 were waited for; matrix products, arithmetic and copies ran while one was open for 10% of the time, Pallas kernels for 0%

profile of v7, /device:TPU:1, one launch (start us, length us, event | category | flops | bytes accessed | tf_op | source)
XLA Modules:
  0.0 291.6 jit_solution(6288300095567559659)
XLA Ops:
  2.0 4.0 %collective-permute-start.1 = (bf16[896,256]{1,0:T(8,128)(2,1)S(1)}, bf16[896,256]{1,0:T(8,128)(2,1)S(1)}, u32[]{:S(2)}, u32[]{:S(2)}) collective-permute-start(bf16[896,256]{1,0:T(8,128)(2,1)S(1)} %get-tuple-element.50), channel_id=1, source_target_pairs={{0,256},{256,0},{1,257},{257,1},{2,258},{258,2},{3,259},{259,3},{4... | collective-permute-start | bytes 1376264 | tf_op jit(solution)/shard_map/ppermute | solution.py:36
  11.3 6.7 %collective-permute-start = (bf16[4,2,12,256]{3,1,2,0:T(2,128)(2,1)S(1)}, bf16[4,2,12,256]{3,1,2,0:T(2,128)(2,1)S(1)}, u32[]{:S(2)}, u32[]{:S(2)}) collective-permute-start(bf16[4,2,12,256]{3,1,2,0:T(2,128)(2,1)S(1)} %bitcast.216), channel_id=1, source_target_pairs={{0,1},{1,0},{2,3},{3,2},{4,5},{5,4},{6,7},{7,6},{8,9},{9,8},{10,11... | collective-permute-start | bytes 147464 | tf_op jit(solution)/shard_map/ppermute | solution.py:61
  18.0 11.1 %all-to-all-start = ((bf16[16,8,2048]{2,1,0:T(8,128)(2,1)}), bf16[16,8,2048]{2,1,0:T(8,128)(2,1)S(1)}, u32[]{:S(2)}, u32[]{:S(2)}) async-start(bf16[16,8,2048]{2,1,0:T(8,128)(2,1)} %reshape.298), calls=%async_computation | async-start | bytes 1048576 | tf_op jit(solution)/shard_map/all_to_all | solution.py:28
  31.9 4.5 %collective-permute-start.2 = (bf16[2,4,12,256]{3,1,2,0:T(4,128)(2,1)S(1)}, bf16[2,4,12,256]{3,1,2,0:T(4,128)(2,1)S(1)}, u32[]{:S(2)}, u32[]{:S(2)}) collective-permute-start(bf16[2,4,12,256]{3,1,2,0:T(4,128)(2,1)S(1)} %bitcast.217), channel_id=1, source_target_pairs={{0,2},{2,0},{1,3},{3,1},{4,6},{6,4},{5,7},{7,5},{8,10},{10,8},{9,1... | collective-permute-start | bytes 147464 | tf_op jit(solution)/shard_map/ppermute | solution.py:61
  39.1 4.4 %collective-permute-start.4 = (bf16[2,2,12,256]{3,1,2,0:T(2,128)(2,1)S(1)}, bf16[2,2,12,256]{3,1,2,0:T(2,128)(2,1)S(1)}, u32[]{:S(2)}, u32[]{:S(2)}) collective-permute-start(bf16[2,2,12,256]{3,1,2,0:T(2,128)(2,1)S(1)} %bitcast.227), channel_id=1, source_target_pairs={{0,12},{4,0},{8,4},{12,8},{1,13},{5,1},{9,5},{13,9},{2,14},{6,2},{... | collective-permute-start | bytes 73736 | tf_op jit(solution)/shard_map/ppermute | solution.py:69
  54.6 6.6 %collective-permute-done.7 = bf16[896,256]{1,0:T(8,128)(2,1)S(1)} collective-permute-done((bf16[896,256]{1,0:T(8,128)(2,1)S(1)}, bf16[896,256]{1,0:T(8,128)(2,1)S(1)}, u32[]{:S(2)}, u32[]{:S(2)}) %collective-permute-start.7) | collective-permute-done | bytes 458784 | tf_op jit(solution)/shard_map/ppermute | solution.py:36
  64.8 8.8 %all-to-all-start.1 = ((bf16[16,64,2048]{2,1,0:T(8,128)(2,1)}), bf16[16,64,2048]{2,1,0:T(8,128)(2,1)}, u32[]{:S(2)}, u32[]{:S(2)}) async-start(bf16[16,64,2048]{2,1,0:T(8,128)(2,1)} %bitcast.186), calls=%async_computation.1 | async-start | bytes 8388608 | tf_op jit(solution)/shard_map/all_to_all | solution.py:28
  73.6 7.6 %collective-permute-start.10 = (bf16[64,256]{1,0:T(8,128)(2,1)S(1)}, bf16[64,256]{1,0:T(8,128)(2,1)S(1)}, u32[]{:S(2)}, u32[]{:S(2)}) collective-permute-start(bf16[64,256]{1,0:T(8,128)(2,1)S(1)} %multiply_convert_fusion), channel_id=1, source_target_pairs={{192,0},{208,16},{224,32},{240,48},{0,64},{16,80},{32,96},{48,112}... | collective-permute-start | bytes 98312 | tf_op jit(solution)/shard_map/ppermute | solution.py:41
  81.2 7.0 %collective-permute-start.9 = (bf16[64,256]{1,0:T(8,128)(2,1)S(1)}, bf16[64,256]{1,0:T(8,128)(2,1)S(1)}, u32[]{:S(2)}, u32[]{:S(2)}) collective-permute-start(bf16[64,256]{1,0:T(8,128)(2,1)S(1)} %multiply_convert_fusion), channel_id=1, source_target_pairs={{128,0},{144,16},{160,32},{176,48},{192,64},{208,80},{224,96},{240... | collective-permute-start | bytes 98312 | tf_op jit(solution)/shard_map/ppermute | solution.py:41
  88.2 7.0 %collective-permute-start.8 = (bf16[64,256]{1,0:T(8,128)(2,1)S(1)}, bf16[64,256]{1,0:T(8,128)(2,1)S(1)}, u32[]{:S(2)}, u32[]{:S(2)}) collective-permute-start(bf16[64,256]{1,0:T(8,128)(2,1)S(1)} %multiply_convert_fusion), channel_id=1, source_target_pairs={{64,0},{80,16},{96,32},{112,48},{128,64},{144,80},{160,96},{176,11... | collective-permute-start | bytes 98312 | tf_op jit(solution)/shard_map/ppermute | solution.py:41
  95.3 2.6 collective-permute-done.8
  98.0 6.1 %collective-permute-start.12 = (bf16[4,64,256]{2,1,0:T(8,128)(2,1)S(1)}, bf16[4,64,256]{2,1,0:T(8,128)(2,1)S(1)}, u32[]{:S(2)}, u32[]{:S(2)}) collective-permute-start(bf16[4,64,256]{2,1,0:T(8,128)(2,1)S(1)} %get-tuple-element.64), channel_id=1, source_target_pairs={{32,0},{48,16},{64,32},{80,48},{96,64},{112,80},{128,96},{144,112}... | collective-permute-start | bytes 393224 | tf_op jit(solution)/shard_map/ppermute | solution.py:41
  104.1 3.4 %collective-permute-start.11 = (bf16[4,64,256]{2,1,0:T(8,128)(2,1)S(1)}, bf16[4,64,256]{2,1,0:T(8,128)(2,1)S(1)}, u32[]{:S(2)}, u32[]{:S(2)}) collective-permute-start(bf16[4,64,256]{2,1,0:T(8,128)(2,1)S(1)} %get-tuple-element.64), channel_id=1, source_target_pairs={{16,0},{32,16},{48,32},{64,48},{80,64},{96,80},{112,96},{128,112},... | collective-permute-start | bytes 393224 | tf_op jit(solution)/shard_map/ppermute | solution.py:41
  109.5 5.3 %collective-permute-done.13 = bf16[4,64,256]{2,1,0:T(8,128)(2,1)S(1)} collective-permute-done((bf16[4,64,256]{2,1,0:T(8,128)(2,1)S(1)}, bf16[4,64,256]{2,1,0:T(8,128)(2,1)S(1)}, u32[]{:S(2)}, u32[]{:S(2)}) %collective-permute-start.13) | collective-permute-done | bytes 131104 | tf_op jit(solution)/shard_map/ppermute | solution.py:41
  115.2 11.2 %all-to-all-done.1 = bf16[16,64,2048]{2,1,0:T(8,128)(2,1)} async-done(((bf16[16,64,2048]{2,1,0:T(8,128)(2,1)}), bf16[16,64,2048]{2,1,0:T(8,128)(2,1)}, u32[]{:S(2)}, u32[]{:S(2)}) %all-to-all-start.1) | async-done | bytes 4194336 | tf_op jit(solution)/shard_map/all_to_all | solution.py:28
  126.4 3.4 %fusion.42 = f32[1024,256]{1,0:T(8,128)S(1)} fusion(bf16[1024,2048]{1,0:T(8,128)(2,1)} %bitcast.29, bf16[2048,256]{1,0:T(8,128)(2,1)S(1)} %bitcast.198), kind=kOutput, calls=%fused_computation.130 | convolution fusion | flops 1073741824 | bytes 6291456 | tf_op jit(solution)/shard_map/dot_general | solution.py:186
  134.4 3.4 %fusion.4 = bf16[1024,256]{1,0:T(8,128)(2,1)S(1)} fusion(f32[1024,256]{1,0:T(8,128)S(1)} %collective-permute-done.14, bf16[1024,2048]{1,0:T(8,128)(2,1)} %bitcast.29, bf16[2048,256]{1,0:T(8,128)(2,1)S(1)} %bitcast.199), kind=kOutput, calls=%fused_computation.9 | convolution fusion | flops 1074266112 | bytes 6815744 | tf_op jit(solution)/shard_map/dot_general | solution.py:189
  139.0 11.9 %all-to-all-start.2 = ((bf16[16,64,256]{2,1,0:T(8,128)(2,1)}), bf16[16,64,256]{2,1,0:T(8,128)(2,1)S(1)}, u32[]{:S(2)}, u32[]{:S(2)}) async-start(bf16[16,64,256]{2,1,0:T(8,128)(2,1)} %copy.333), calls=%async_computation.2 | async-start | bytes 1048576 | tf_op jit(solution)/shard_map/all_to_all | solution.py:28
  155.2 6.6 %fusion.7 = f32[2048,512]{1,0:T(8,128)} fusion(bf16[1024,2048]{1,0:T(8,128)(2,1)} %bitcast.29, bf16[1024,256]{1,0:T(8,128)(2,1)S(1)} %collective-permute-done.15, bf16[1024,256]{1,0:T(8,128)(2,1)S(1)} %reshape.310), kind=kOutput, calls=%fused_computation.16 | convolution fusion | flops 2149580800 | bytes 9437184 | tf_op jit(solution)/shard_map/dot_general | solution.py:24
  161.8 12.0 %all-to-all-done.2 = bf16[16,64,256]{2,1,0:T(8,128)(2,1)S(1)} async-done(((bf16[16,64,256]{2,1,0:T(8,128)(2,1)}), bf16[16,64,256]{2,1,0:T(8,128)(2,1)S(1)}, u32[]{:S(2)}, u32[]{:S(2)}) %all-to-all-start.2) | async-done | bytes 524320 | tf_op jit(solution)/shard_map/all_to_all | solution.py:28
  174.9 19.5 %all-to-all-start.3 = ((f32[16,1,64]{2,1,0:T(1,128)}), f32[16,1,64]{2,1,0:T(1,128)S(1)}, u32[]{:S(2)}, u32[]{:S(2)}) async-start(f32[16,1,64]{2,1,0:T(1,128)} %broadcast_in_dim.21), calls=%async_computation.3 | async-start | bytes 16384 | tf_op jit(solution)/shard_map/all_to_all | solution.py:28
  194.5 6.9 %all-to-all-done.3 = f32[16,1,64]{2,1,0:T(1,128)S(1)} async-done(((f32[16,1,64]{2,1,0:T(1,128)}), f32[16,1,64]{2,1,0:T(1,128)S(1)}, u32[]{:S(2)}, u32[]{:S(2)}) %all-to-all-start.3) | async-done | bytes 4128 | tf_op jit(solution)/shard_map/all_to_all | solution.py:28
  202.4 6.2 %all-to-all-start.4 = ((bf16[16,72,256]{2,1,0:T(8,128)(2,1)}), bf16[16,72,256]{2,1,0:T(8,128)(2,1)S(1)}, u32[]{:S(2)}, u32[]{:S(2)}) async-start(bf16[16,72,256]{2,1,0:T(8,128)(2,1)} %broadcast_in_dim.46), calls=%async_computation.4 | async-start | bytes 1179648 | tf_op jit(solution)/shard_map/all_to_all | solution.py:28
  215.3 3.0 %collective-permute-start.19 = (bf16[1024,256]{1,0:T(8,128)(2,1)S(1)}, bf16[1024,256]{1,0:T(8,128)(2,1)S(1)}, u32[]{:S(2)}, u32[]{:S(2)}) collective-permute-start(bf16[1024,256]{1,0:T(8,128)(2,1)S(1)} %get-tuple-element.53), channel_id=1, source_target_pairs={{0,1},{1,0},{2,3},{3,2},{4,5},{5,4},{6,7},{7,6},{8,9},{9,8},{10,11... | collective-permute-start | bytes 1572872 | tf_op jit(solution)/shard_map/ppermute | solution.py:32
  218.3 3.5 %collective-permute-start.17 = (bf16[256,256]{1,0:T(8,128)(2,1)S(1)}, bf16[256,256]{1,0:T(8,128)(2,1)S(1)}, u32[]{:S(2)}, u32[]{:S(2)}) collective-permute-start(bf16[256,256]{1,0:T(8,128)(2,1)S(1)} %copy-done.5), channel_id=1, source_target_pairs={{0,256},{256,0},{1,257},{257,1},{2,258},{258,2},{3,259},{259,3},{4... | collective-permute-start | bytes 393224 | tf_op jit(solution)/shard_map/ppermute | solution.py:36
  221.9 16.2 %collective-permute-done.17 = bf16[256,256]{1,0:T(8,128)(2,1)S(1)} collective-permute-done((bf16[256,256]{1,0:T(8,128)(2,1)S(1)}, bf16[256,256]{1,0:T(8,128)(2,1)S(1)}, u32[]{:S(2)}, u32[]{:S(2)}) %collective-permute-start.17) | collective-permute-done | bytes 131104 | tf_op jit(solution)/shard_map/ppermute | solution.py:36
  241.1 5.3 %all-to-all-start.5 = ((bf16[16,72,512]{2,1,0:T(8,128)(2,1)}), bf16[16,72,512]{2,1,0:T(8,128)(2,1)S(1)}, u32[]{:S(2)}, u32[]{:S(2)}) async-start(bf16[16,72,512]{2,1,0:T(8,128)(2,1)} %pad_maximum_fusion), calls=%async_computation.5 | async-start | bytes 2359296 | tf_op jit(solution)/shard_map/all_to_all | solution.py:28
  254.0 12.3 %collective-permute-done.20 = f32[2,128,256]{2,1,0:T(8,128)S(1)} collective-permute-done((f32[2,128,256]{2,1,0:T(8,128)S(1)}, f32[2,128,256]{2,1,0:T(8,128)S(1)}, u32[]{:S(2)}, u32[]{:S(2)}) %collective-permute-start.20) | collective-permute-done | bytes 262176 | tf_op jit(solution)/shard_map/ppermute | solution.py:36
  267.8 11.4 %all-to-all-start.6 = ((bf16[16,4,512]{2,1,0:T(4,128)(2,1)}), bf16[16,4,512]{2,1,0:T(4,128)(2,1)S(1)}, u32[]{:S(2)}, u32[]{:S(2)}) async-start(bf16[16,4,512]{2,1,0:T(4,128)(2,1)} %reshape.316), calls=%async_computation.6 | async-start | bytes 131072 | tf_op jit(solution)/shard_map/all_to_all | solution.py:28
  279.3 2.8 collective-permute-start.21
  282.1 2.6 slice_select_fusion
  285.3 5.5 %all-to-all-done.6 = bf16[16,4,512]{2,1,0:T(4,128)(2,1)S(1)} async-done(((bf16[16,4,512]{2,1,0:T(4,128)(2,1)}), bf16[16,4,512]{2,1,0:T(4,128)(2,1)S(1)}, u32[]{:S(2)}, u32[]{:S(2)}) %all-to-all-start.6) | async-done | bytes 65568 | tf_op jit(solution)/shard_map/all_to_all | solution.py:28
  (178 shorter events, 60.7 us)
Async XLA Ops:
  0.6 6.4 %copy-start.2 = (bf16[4,28672]{1,0:T(4,128)(2,1)S(1)}, bf16[4,28672]{1,0:T(4,128)(2,1)}, u32[]{:S(2)}) copy-start(bf16[4,28672]{1,0:T(4,128)(2,1)} %param.14) | copy-start | bytes 688132
  0.6 6.4 %copy-start.4 = (bf16[4,28672]{1,0:T(4,128)(2,1)S(1)}, bf16[4,28672]{1,0:T(4,128)(2,1)}, u32[]{:S(2)}) copy-start(bf16[4,28672]{1,0:T(4,128)(2,1)} %param.13) | copy-start | bytes 688132
  2.0 29.7 %collective-permute-start.1 = (bf16[896,256]{1,0:T(8,128)(2,1)S(1)}, bf16[896,256]{1,0:T(8,128)(2,1)S(1)}, u32[]{:S(2)}, u32[]{:S(2)}) collective-permute-start(bf16[896,256]{1,0:T(8,128)(2,1)S(1)} %get-tuple-element.50), channel_id=1, source_target_pairs={{0,256},{256,0},{1,257},{257,1},{2,258},{258,2},{3,259},{259,3},{4... | collective-permute-start | bytes 1376264 | tf_op jit(solution)/shard_map/ppermute | solution.py:36
  11.3 20.0 %collective-permute-start = (bf16[4,2,12,256]{3,1,2,0:T(2,128)(2,1)S(1)}, bf16[4,2,12,256]{3,1,2,0:T(2,128)(2,1)S(1)}, u32[]{:S(2)}, u32[]{:S(2)}) collective-permute-start(bf16[4,2,12,256]{3,1,2,0:T(2,128)(2,1)S(1)} %bitcast.216), channel_id=1, source_target_pairs={{0,1},{1,0},{2,3},{3,2},{4,5},{5,4},{6,7},{7,6},{8,9},{9,8},{10,11... | collective-permute-start | bytes 147464 | tf_op jit(solution)/shard_map/ppermute | solution.py:61
  18.0 43.2 %all-to-all-start = ((bf16[16,8,2048]{2,1,0:T(8,128)(2,1)}), bf16[16,8,2048]{2,1,0:T(8,128)(2,1)S(1)}, u32[]{:S(2)}, u32[]{:S(2)}) async-start(bf16[16,8,2048]{2,1,0:T(8,128)(2,1)} %reshape.298), calls=%async_computation | async-start | bytes 1048576 | tf_op jit(solution)/shard_map/all_to_all | solution.py:28
  29.2 9.5 %collective-permute-start.3 = (bf16[896,256]{1,0:T(8,128)(2,1)S(1)}, bf16[896,256]{1,0:T(8,128)(2,1)S(1)}, u32[]{:S(2)}, u32[]{:S(2)}) collective-permute-start(bf16[896,256]{1,0:T(8,128)(2,1)S(1)} %get-tuple-element.49), channel_id=1, source_target_pairs={{0,1},{1,0},{2,3},{3,2},{4,5},{5,4},{6,7},{7,6},{8,9},{9,8},{10,11... | collective-permute-start | bytes 1376264 | tf_op jit(solution)/shard_map/ppermute | solution.py:32
  31.9 6.6 %collective-permute-start.2 = (bf16[2,4,12,256]{3,1,2,0:T(4,128)(2,1)S(1)}, bf16[2,4,12,256]{3,1,2,0:T(4,128)(2,1)S(1)}, u32[]{:S(2)}, u32[]{:S(2)}) collective-permute-start(bf16[2,4,12,256]{3,1,2,0:T(4,128)(2,1)S(1)} %bitcast.217), channel_id=1, source_target_pairs={{0,2},{2,0},{1,3},{3,1},{4,6},{6,4},{5,7},{7,5},{8,10},{10,8},{9,1... | collective-permute-start | bytes 147464 | tf_op jit(solution)/shard_map/ppermute | solution.py:61
  39.1 12.2 %collective-permute-start.4 = (bf16[2,2,12,256]{3,1,2,0:T(2,128)(2,1)S(1)}, bf16[2,2,12,256]{3,1,2,0:T(2,128)(2,1)S(1)}, u32[]{:S(2)}, u32[]{:S(2)}) collective-permute-start(bf16[2,2,12,256]{3,1,2,0:T(2,128)(2,1)S(1)} %bitcast.227), channel_id=1, source_target_pairs={{0,12},{4,0},{8,4},{12,8},{1,13},{5,1},{9,5},{13,9},{2,14},{6,2},{... | collective-permute-start | bytes 73736 | tf_op jit(solution)/shard_map/ppermute | solution.py:69
  43.5 7.9 %collective-permute-start.5 = (bf16[2,2,12,256]{3,1,2,0:T(2,128)(2,1)S(1)}, bf16[2,2,12,256]{3,1,2,0:T(2,128)(2,1)S(1)}, u32[]{:S(2)}, u32[]{:S(2)}) collective-permute-start(bf16[2,2,12,256]{3,1,2,0:T(2,128)(2,1)S(1)} %bitcast.223), channel_id=1, source_target_pairs={{0,8},{4,12},{8,0},{12,4},{1,9},{5,13},{9,1},{13,5},{2,10},{6,14},... | collective-permute-start | bytes 73736 | tf_op jit(solution)/shard_map/ppermute | solution.py:69
  46.0 6.1 %collective-permute-start.6 = (bf16[2,2,12,256]{3,1,2,0:T(2,128)(2,1)S(1)}, bf16[2,2,12,256]{3,1,2,0:T(2,128)(2,1)S(1)}, u32[]{:S(2)}, u32[]{:S(2)}) collective-permute-start(bf16[2,2,12,256]{3,1,2,0:T(2,128)(2,1)S(1)} %bitcast.225), channel_id=1, source_target_pairs={{0,4},{4,8},{8,12},{12,0},{1,5},{5,9},{9,13},{13,1},{2,6},{6,10},{... | collective-permute-start | bytes 73736 | tf_op jit(solution)/shard_map/ppermute | solution.py:69
  49.3 12.0 %collective-permute-start.7 = (bf16[896,256]{1,0:T(8,128)(2,1)S(1)}, bf16[896,256]{1,0:T(8,128)(2,1)S(1)}, u32[]{:S(2)}, u32[]{:S(2)}) collective-permute-start(bf16[896,256]{1,0:T(8,128)(2,1)S(1)} %collective-permute-done.3), channel_id=1, source_target_pairs={{0,256},{256,0},{1,257},{257,1},{2,258},{258,2},{3,259},{259,3},{4... | collective-permute-start | bytes 1376264 | tf_op jit(solution)/shard_map/ppermute | solution.py:36
  64.8 61.5 %all-to-all-start.1 = ((bf16[16,64,2048]{2,1,0:T(8,128)(2,1)}), bf16[16,64,2048]{2,1,0:T(8,128)(2,1)}, u32[]{:S(2)}, u32[]{:S(2)}) async-start(bf16[16,64,2048]{2,1,0:T(8,128)(2,1)} %bitcast.186), calls=%async_computation.1 | async-start | bytes 8388608 | tf_op jit(solution)/shard_map/all_to_all | solution.py:28
  73.6 21.7 %collective-permute-start.10 = (bf16[64,256]{1,0:T(8,128)(2,1)S(1)}, bf16[64,256]{1,0:T(8,128)(2,1)S(1)}, u32[]{:S(2)}, u32[]{:S(2)}) collective-permute-start(bf16[64,256]{1,0:T(8,128)(2,1)S(1)} %multiply_convert_fusion), channel_id=1, source_target_pairs={{192,0},{208,16},{224,32},{240,48},{0,64},{16,80},{32,96},{48,112}... | collective-permute-start | bytes 98312 | tf_op jit(solution)/shard_map/ppermute | solution.py:41
  81.2 14.1 %collective-permute-start.9 = (bf16[64,256]{1,0:T(8,128)(2,1)S(1)}, bf16[64,256]{1,0:T(8,128)(2,1)S(1)}, u32[]{:S(2)}, u32[]{:S(2)}) collective-permute-start(bf16[64,256]{1,0:T(8,128)(2,1)S(1)} %multiply_convert_fusion), channel_id=1, source_target_pairs={{128,0},{144,16},{160,32},{176,48},{192,64},{208,80},{224,96},{240... | collective-permute-start | bytes 98312 | tf_op jit(solution)/shard_map/ppermute | solution.py:41
  88.2 9.7 %collective-permute-start.8 = (bf16[64,256]{1,0:T(8,128)(2,1)S(1)}, bf16[64,256]{1,0:T(8,128)(2,1)S(1)}, u32[]{:S(2)}, u32[]{:S(2)}) collective-permute-start(bf16[64,256]{1,0:T(8,128)(2,1)S(1)} %multiply_convert_fusion), channel_id=1, source_target_pairs={{64,0},{80,16},{96,32},{112,48},{128,64},{144,80},{160,96},{176,11... | collective-permute-start | bytes 98312 | tf_op jit(solution)/shard_map/ppermute | solution.py:41
  98.0 16.9 %collective-permute-start.12 = (bf16[4,64,256]{2,1,0:T(8,128)(2,1)S(1)}, bf16[4,64,256]{2,1,0:T(8,128)(2,1)S(1)}, u32[]{:S(2)}, u32[]{:S(2)}) collective-permute-start(bf16[4,64,256]{2,1,0:T(8,128)(2,1)S(1)} %get-tuple-element.64), channel_id=1, source_target_pairs={{32,0},{48,16},{64,32},{80,48},{96,64},{112,80},{128,96},{144,112}... | collective-permute-start | bytes 393224 | tf_op jit(solution)/shard_map/ppermute | solution.py:41
  104.1 10.8 %collective-permute-start.11 = (bf16[4,64,256]{2,1,0:T(8,128)(2,1)S(1)}, bf16[4,64,256]{2,1,0:T(8,128)(2,1)S(1)}, u32[]{:S(2)}, u32[]{:S(2)}) collective-permute-start(bf16[4,64,256]{2,1,0:T(8,128)(2,1)S(1)} %get-tuple-element.64), channel_id=1, source_target_pairs={{16,0},{32,16},{48,32},{64,48},{80,64},{96,80},{112,96},{128,112},... | collective-permute-start | bytes 393224 | tf_op jit(solution)/shard_map/ppermute | solution.py:41
  107.5 7.3 %collective-permute-start.13 = (bf16[4,64,256]{2,1,0:T(8,128)(2,1)S(1)}, bf16[4,64,256]{2,1,0:T(8,128)(2,1)S(1)}, u32[]{:S(2)}, u32[]{:S(2)}) collective-permute-start(bf16[4,64,256]{2,1,0:T(8,128)(2,1)S(1)} %get-tuple-element.64), channel_id=1, source_target_pairs={{240,0},{0,16},{16,32},{32,48},{48,64},{64,80},{80,96},{96,112},{1... | collective-permute-start | bytes 393224 | tf_op jit(solution)/shard_map/ppermute | solution.py:41
  129.8 4.6 %collective-permute-start.14 = (f32[1024,256]{1,0:T(8,128)S(1)}, f32[1024,256]{1,0:T(8,128)S(1)}, u32[]{:S(2)}, u32[]{:S(2)}) collective-permute-start(f32[1024,256]{1,0:T(8,128)S(1)} %fusion.42), channel_id=1, source_target_pairs={{0,1},{1,0},{2,3},{3,2},{4,5},{5,4},{6,7},{7,6},{8,9},{9,8},{10,11... | collective-permute-start | bytes 3145736 | tf_op jit(solution)/shard_map/ppermute | solution.py:32
  139.0 34.9 %all-to-all-start.2 = ((bf16[16,64,256]{2,1,0:T(8,128)(2,1)}), bf16[16,64,256]{2,1,0:T(8,128)(2,1)S(1)}, u32[]{:S(2)}, u32[]{:S(2)}) async-start(bf16[16,64,256]{2,1,0:T(8,128)(2,1)} %copy.333), calls=%async_computation.2 | async-start | bytes 1048576 | tf_op jit(solution)/shard_map/all_to_all | solution.py:28
  151.4 3.9 %collective-permute-start.15 = (bf16[1024,256]{1,0:T(8,128)(2,1)S(1)}, bf16[1024,256]{1,0:T(8,128)(2,1)S(1)}, u32[]{:S(2)}, u32[]{:S(2)}) collective-permute-start(bf16[1024,256]{1,0:T(8,128)(2,1)S(1)} %reshape.310), channel_id=1, source_target_pairs={{0,1},{1,0},{2,3},{3,2},{4,5},{5,4},{6,7},{7,6},{8,9},{9,8},{10,11... | collective-permute-start | bytes 1572872 | tf_op jit(solution)/shard_map/ppermute | solution.py:32
  174.9 26.5 %all-to-all-start.3 = ((f32[16,1,64]{2,1,0:T(1,128)}), f32[16,1,64]{2,1,0:T(1,128)S(1)}, u32[]{:S(2)}, u32[]{:S(2)}) async-start(f32[16,1,64]{2,1,0:T(1,128)} %broadcast_in_dim.21), calls=%async_computation.3 | async-start | bytes 16384 | tf_op jit(solution)/shard_map/all_to_all | solution.py:28
  202.4 36.2 %all-to-all-start.4 = ((bf16[16,72,256]{2,1,0:T(8,128)(2,1)}), bf16[16,72,256]{2,1,0:T(8,128)(2,1)S(1)}, u32[]{:S(2)}, u32[]{:S(2)}) async-start(bf16[16,72,256]{2,1,0:T(8,128)(2,1)} %broadcast_in_dim.46), calls=%async_computation.4 | async-start | bytes 1179648 | tf_op jit(solution)/shard_map/all_to_all | solution.py:28
  211.1 7.1 %copy-start.5 = (bf16[256,256]{1,0:T(8,128)(2,1)S(1)}, bf16[256,256]{1,0:T(8,128)(2,1)}, u32[]{:S(2)}) copy-start(bf16[256,256]{1,0:T(8,128)(2,1)} %param.19) | copy-start | bytes 393220
  212.2 26.4 %collective-permute-start.16 = (bf16[896,512]{1,0:T(8,128)(2,1)}, bf16[896,512]{1,0:T(8,128)(2,1)}, u32[]{:S(2)}, u32[]{:S(2)}) collective-permute-start(bf16[896,512]{1,0:T(8,128)(2,1)} %fusion.11), channel_id=1, source_target_pairs={{0,256},{256,0},{1,257},{257,1},{2,258},{258,2},{3,259},{259,3},{4... | collective-permute-start | bytes 2752520 | tf_op jit(solution)/shard_map/ppermute | solution.py:36
  215.3 23.1 %collective-permute-start.19 = (bf16[1024,256]{1,0:T(8,128)(2,1)S(1)}, bf16[1024,256]{1,0:T(8,128)(2,1)S(1)}, u32[]{:S(2)}, u32[]{:S(2)}) collective-permute-start(bf16[1024,256]{1,0:T(8,128)(2,1)S(1)} %get-tuple-element.53), channel_id=1, source_target_pairs={{0,1},{1,0},{2,3},{3,2},{4,5},{5,4},{6,7},{7,6},{8,9},{9,8},{10,11... | collective-permute-start | bytes 1572872 | tf_op jit(solution)/shard_map/ppermute | solution.py:32
  218.3 19.8 %collective-permute-start.17 = (bf16[256,256]{1,0:T(8,128)(2,1)S(1)}, bf16[256,256]{1,0:T(8,128)(2,1)S(1)}, u32[]{:S(2)}, u32[]{:S(2)}) collective-permute-start(bf16[256,256]{1,0:T(8,128)(2,1)S(1)} %copy-done.5), channel_id=1, source_target_pairs={{0,256},{256,0},{1,257},{257,1},{2,258},{258,2},{3,259},{259,3},{4... | collective-permute-start | bytes 393224 | tf_op jit(solution)/shard_map/ppermute | solution.py:36
  241.1 26.0 %all-to-all-start.5 = ((bf16[16,72,512]{2,1,0:T(8,128)(2,1)}), bf16[16,72,512]{2,1,0:T(8,128)(2,1)S(1)}, u32[]{:S(2)}, u32[]{:S(2)}) async-start(bf16[16,72,512]{2,1,0:T(8,128)(2,1)} %pad_maximum_fusion), calls=%async_computation.5 | async-start | bytes 2359296 | tf_op jit(solution)/shard_map/all_to_all | solution.py:28
  247.0 19.3 %collective-permute-start.20 = (f32[2,128,256]{2,1,0:T(8,128)S(1)}, f32[2,128,256]{2,1,0:T(8,128)S(1)}, u32[]{:S(2)}, u32[]{:S(2)}) collective-permute-start(f32[2,128,256]{2,1,0:T(8,128)S(1)} %fusion.23), channel_id=1, source_target_pairs={{0,256},{256,0},{1,257},{257,1},{2,258},{258,2},{3,259},{259,3},{4... | collective-permute-start | bytes 786440 | tf_op jit(solution)/shard_map/ppermute | solution.py:36
  251.6 30.5 %collective-permute-start.18 = (f32[896,256]{1,0:T(8,128)}, f32[896,256]{1,0:T(8,128)}, u32[]{:S(2)}, u32[]{:S(2)}) collective-permute-start(f32[896,256]{1,0:T(8,128)} %slice.143), channel_id=1, source_target_pairs={{0,1},{1,0},{2,3},{3,2},{4,5},{5,4},{6,7},{7,6},{8,9},{9,8},{10,11... | collective-permute-start | bytes 2752520 | tf_op jit(solution)/shard_map/ppermute | solution.py:32
  267.8 23.0 %all-to-all-start.6 = ((bf16[16,4,512]{2,1,0:T(4,128)(2,1)}), bf16[16,4,512]{2,1,0:T(4,128)(2,1)S(1)}, u32[]{:S(2)}, u32[]{:S(2)}) async-start(bf16[16,4,512]{2,1,0:T(4,128)(2,1)} %reshape.316), calls=%async_computation.6 | async-start | bytes 131072 | tf_op jit(solution)/shard_map/all_to_all | solution.py:28
  279.3 5.4 %collective-permute-start.21 = (f32[16,256]{1,0:T(8,128)S(1)}, f32[16,256]{1,0:T(8,128)S(1)}, u32[]{:S(2)}, u32[]{:S(2)}) collective-permute-start(f32[16,256]{1,0:T(8,128)S(1)} %bitcast.230), channel_id=1, source_target_pairs={{0,256},{256,0},{1,257},{257,1},{2,258},{258,2},{3,259},{259,3},{4... | collective-permute-start | bytes 49160 | tf_op jit(solution)/shard_map/ppermute | solution.py:36
  (5 other events, 19.2 us)

commit v8 on v7

--- a/solution.py
+++ b/solution.py
@@ -50,8 +50,32 @@
     all_blocks = jnp.stack(
         [strided, from_above(strided, 1), from_above(strided, 2), below], axis=1
     ).reshape(z_count, *block.shape)
-    twice = jnp.concatenate([all_blocks, all_blocks])
-    return lax.dynamic_slice_in_dim(twice, z_count - lax.axis_index("z"), z_count, 0)
+    return from_first(all_blocks)
+
+
+def gather_z_relay(block):
+    z_count = lax.axis_size("z")
+    half = block.shape[0] // 2
+    above, below = from_above(block, 4), from_above(block, z_count - 4)
+    far = jnp.concatenate(
+        [from_above(above[:half], 4), from_above(below[half:], z_count - 4)]
+    )
+    strided = jnp.stack([block, above, far, below])
+    above, below = from_above(strided, 1), from_above(strided, z_count - 1)
+    far = jnp.concatenate(
+        [
+            from_above(above[:2], 1),
+            from_above(jnp.concatenate([below[3:], below[:1]]), z_count - 1),
+        ]
+    )
+    below = jnp.concatenate([below[1:], below[:1]])
+    return jnp.stack([strided, above, far, below], axis=1).reshape(z_count, *block.shape)
+
+
+def from_first(blocks):
+    twice = jnp.concatenate([blocks, blocks])
+    count = blocks.shape[0]
+    return lax.dynamic_slice_in_dim(twice, count - lax.axis_index("z"), count, 0)
 
 
 def trade_pair(blocks, axis_name):
@@ -128,10 +152,6 @@
     unit_rows, hidden, resid_grad = lax.optimization_barrier((unit_rows, hidden, resid_grad))
     unit_group = exchange(unit_rows, "z")
 
-    weight_own = jnp.where(on_first, gate_weight, up_weight)
-    weight_other = swap_cores(jnp.where(on_first, up_weight, gate_weight))
-    near_join = swap_near(join_weight)
-
     hidden_wide = hidden.astype(wide)
     row_scale = lax.rsqrt(jnp.mean(hidden_wide * hidden_wide, axis=1, keepdims=True) + epsilon)
     scale_parts = jnp.concatenate(split_three(row_scale), axis=1)
@@ -147,10 +167,10 @@
         lax.axis_size("x"), 2, 2, 3 * row_count, features
     )
     norm_block = trade_pair(norm_sent.transpose(2, 0, 1, 3, 4), "core")
-    norm_block, near_own = lax.optimization_barrier((norm_block, swap_near(weight_own)))
+    norm_block, near_gate, near_up = lax.optimization_barrier(
+        (norm_block, swap_near(gate_weight), swap_near(up_weight))
+    )
     norm_block = trade_pair(norm_block.transpose(2, 0, 1, 3, 4), "y_hi")
-    norm_block, weight_other = lax.optimization_barrier((norm_block, weight_other))
-    near_other = swap_near(weight_other)
     norm_block = trade_x(norm_block.transpose(2, 0, 1, 3, 4)).reshape(
         dp_count, 3, row_count, features
     )
@@ -164,10 +184,8 @@
     normed = hidden_block * scale_block
     mlp_block = (normed * gain_block).astype(narrow)
 
-    unit_group, mlp_block, near_other = lax.optimization_barrier(
-        (unit_group, mlp_block, near_other)
-    )
-    mlp_z = gather_z(mlp_block)
+    unit_group, mlp_block = lax.optimization_barrier((unit_group, mlp_block))
+    shared_z = gather_z_relay(jnp.concatenate([mlp_block, join_weight]))
     unit_halves = (
         unit_group.reshape(z_count, 2, row_count, 2 * part_width)
         .transpose(1, 0, 2, 3)
@@ -177,16 +195,21 @@
         unit_halves[None], (dp_count // core_count, core_count, plane_rows, 2 * part_width)
     ).reshape(dp_count, plane_rows, 2 * part_width)
     half_all = exchange(unit_halves, dp_axes).reshape(tokens, 2 * part_width)
-    half_all, mlp_z = lax.optimization_barrier((half_all, mlp_z))
 
     def both_near(own, near):
         both = jnp.pad(by_near(own, near), ((0, 0), (0, half_inputs), (0, 0)))
         return both.reshape(2 * part_width, features)
 
-    partial_other = jnp.dot(
-        half_all, both_near(weight_other, near_other), preferred_element_type=wide
-    )
-    partial_own = jnp.dot(half_all, both_near(weight_own, near_own), preferred_element_type=wide)
+    weight_own = both_near(
+        jnp.where(on_first, gate_weight, up_weight), jnp.where(on_first, near_gate, near_up)
+    )
+    weight_other = swap_cores(
+        both_near(
+            jnp.where(on_first, up_weight, gate_weight), jnp.where(on_first, near_up, near_gate)
+        )
+    )
+    partial_other = jnp.dot(half_all, weight_other, preferred_element_type=wide)
+    partial_own = jnp.dot(half_all, weight_own, preferred_element_type=wide)
     partial_value = partial_own + swap_cores(partial_other)
     partial_value = (
         partial_value.astype(narrow)
@@ -194,19 +217,31 @@
         .transpose(1, 0, 2, 3)
         .reshape(z_count, block_rows, features)
     )
+    partial_value, shared_z = lax.optimization_barrier((partial_value, shared_z))
+    join_z = shared_z[:, block_rows:]
 
     mlp_own = (
-        mlp_z.reshape(z_count, dp_count, row_count, features)
+        from_first(shared_z[:, :block_rows])
+        .reshape(z_count, dp_count, row_count, features)
         .transpose(1, 0, 2, 3)
         .reshape(tokens, features)
     )
     unit_sums = token_sum(half_all, jnp.concatenate([mlp_own, swap_cores(mlp_own)], axis=1))
-    partial_far, unit_sums = lax.optimization_barrier((exchange(partial_value, "z"), unit_sums))
     unit_sums = unit_sums.reshape(2, part_width, 2 * features)[:, :units]
     unit_kept = lax.dynamic_index_in_dim(unit_sums, here, 0, keepdims=False)
-    unit_near = swap_near(
-        lax.dynamic_index_in_dim(unit_sums, 1 - here, 0, keepdims=False).astype(narrow)
-    )
+    unit_sent = lax.dynamic_index_in_dim(unit_sums, 1 - here, 0, keepdims=False)
+    joined_half = jnp.concatenate(
+        [half_all[:, units:part_width], half_all[:, part_width + units :]], axis=1
+    )
+    partial_far, unit_sent, joined_half, joined_other = lax.optimization_barrier(
+        (
+            exchange(partial_value, "z"),
+            unit_sent.astype(narrow),
+            joined_half,
+            swap_cores(joined_half),
+        )
+    )
+    unit_near = swap_near(unit_sent)
     input_grad = jnp.sum(partial_far.astype(wide), axis=0)
 
     lifted = input_grad * gain_block
@@ -214,17 +249,43 @@
     mean_all = exchange(
         jnp.broadcast_to(mean_part[None, None], (dp_count, 1, block_rows)), dp_axes
     )
+    mean_all, unit_near = lax.optimization_barrier((mean_all, unit_near))
     inner_mean = (jnp.sum(mean_all, axis=(0, 1)) / width)[:, None]
     hidden_grad = (resid_block + scale_block * (lifted - normed * inner_mean)).astype(narrow)
+
+    grad_rows = jnp.stack(
+        [
+            rows.reshape(dp_count, row_count, features)
+            for rows in (hidden_grad, swap_near(hidden_grad))
+        ],
+        axis=1,
+    ).reshape(2 * block_rows, features)
+    joined_part = lax.dot_general(
+        grad_rows, join_z, (((1,), (2,)), ((), ())), preferred_element_type=wide
+    ).astype(narrow)
+    joined_blocks = exchange(
+        joined_part.reshape(dp_count, 2 * row_count, z_count * inputs), dp_axes
+    )
     gain_part = jnp.sum(input_grad * normed, axis=0, keepdims=True)
-
-    sent_rows = block_rows + 8
+    gain_part = gain_part + swap_near(gain_part)
     grad_sent = jnp.concatenate(
         [hidden_grad] + list(split_three(gain_part)) + [jnp.zeros((5, features), narrow)], axis=0
     )
-    grad_z = exchange(jnp.broadcast_to(grad_sent[None], (z_count, sent_rows, features)), "z")
-    grad_z, unit_near = lax.optimization_barrier((grad_z, unit_near))
-    gain_sum = jnp.sum(grad_z[:, block_rows : block_rows + 3].astype(wide), axis=(0, 1))[None]
+    grad_z = gather_z(grad_sent)
+    grad_z, joined_blocks = lax.optimization_barrier((grad_z, joined_blocks))
+    joined_total = jnp.sum(joined_blocks.astype(wide), axis=0).astype(narrow)
+    joined_total = joined_total.reshape(2, row_count, z_count, inputs).transpose(0, 2, 1, 3)
+    joined_total = by_near(joined_total[0], swap_near(joined_total[1]))
+    joined_grad = (
+        from_first(joined_total.transpose(1, 0, 2, 3))
+        .transpose(2, 1, 0, 3)
+        .reshape(row_count, 2 * z_count * inputs)
+    )
+
+    gain_sum = jnp.sum(grad_z[:, block_rows : block_rows + 3].astype(wide), axis=(0, 1))
+    gain_grad = exchange(
+        jnp.broadcast_to(gain_sum[None, None], (dp_count, 1, features)), dp_axes
+    ).reshape(width)
     grad_all = (
         grad_z[:, :block_rows]
         .reshape(z_count, dp_count, row_count, features)
@@ -232,34 +293,6 @@
         .reshape(tokens, features)
     )
 
-    join_both = by_near(join_weight, near_join).reshape(2 * inputs, features)
-    joined_part = lax.dot_general(
-        grad_all, join_both, (((1,), (1,)), ((), ())), preferred_element_type=wide
-    ).astype(narrow)
-    gain_rows = jnp.concatenate(
-        list(split_three(gain_sum)) + [jnp.zeros((13, features), narrow)], axis=0
-    ).reshape(8, 2 * features)
-    joined_part = jnp.concatenate(
-        [
-            joined_part.reshape(dp_count, plane_rows, 2 * inputs),
-            jnp.broadcast_to(gain_rows[None], (dp_count, 8, 2 * features)),
-        ],
-        axis=1,
-    )
-    joined_blocks = exchange(joined_part, dp_axes)
-    gain_blocks = joined_blocks[:, plane_rows : plane_rows + 2].astype(wide)
-    gain_own = (gain_blocks[:, 0, :features] + gain_blocks[:, 0, features:]) + gain_blocks[
-        :, 1, :features
-    ]
-    gain_grad = (gain_own + swap_near(gain_own)).reshape(width)
-    joined_total = jnp.sum(joined_blocks[:, :plane_rows].astype(wide), axis=0).astype(narrow)
-    joined_grad = exchange(joined_total.reshape(z_count, row_count, 2 * inputs), "z")
-    joined_grad = (
-        joined_grad.reshape(z_count, row_count, 2, inputs)
-        .transpose(1, 2, 0, 3)
-        .reshape(row_count, 2 * z_count * inputs)
-    )
-
     unit_grad = unit_kept + unit_near.astype(wide)
     own_grad = unit_grad[:, :features]
     other_grad = swap_cores(unit_grad[:, features:])
@@ -271,12 +304,9 @@
         sent = lax.dynamic_index_in_dim(sums, 1 - here, 0, keepdims=False)
         return kept + swap_near(sent)
 
-    joined_half = jnp.concatenate(
-        [half_all[:, units:part_width], half_all[:, part_width + units :]], axis=1
-    )
     join_sums = by_core(
         token_sum(joined_half, grad_all).reshape(2, half_inputs, features),
-        token_sum(swap_cores(joined_half), grad_all).reshape(2, half_inputs, features),
+        token_sum(joined_other, grad_all).reshape(2, half_inputs, features),
     )
     join_weight_grad = add_near(join_sums.transpose(1, 0, 2, 3)).reshape(inputs, features)
     return (joined_grad, gate_weight_grad, up_weight_grad, join_weight_grad, gain_grad)

time: 294 us -> 302 us (1.027)
  waiting for transfers between devices: 85 us -> 40.7 us
  starting transfers between devices: 156 us -> 184 us
  local copies, waits for them, and re-layouts: 21.7 us -> 40.8 us
  other arithmetic: 12.4 us -> 19.3 us
    ppermute x6 -> x14, starting transfers between devices: 33 us -> 68 us  [from_above(): lax.ppermute(value, 'z', [((i + distance) % count, i) for i in range(coun...]
    ppermute x6 -> x7, waiting for transfers between devices: 35.2 us -> 4.3 us  [swap_near(): return lax.ppermute(value, 'y_lo', [(0, 1), (1, 0)])]
    all_to_all x7 -> x6, waiting for transfers between devices: 35.6 us -> 8.55 us  [exchange(): return lax.all_to_all(blocks, axes, split_axis=0, concat_axis=0, tiled=True)]
    all_to_all x7 -> x6, starting transfers between devices: 74.3 us -> 53.9 us  [exchange(): return lax.all_to_all(blocks, axes, split_axis=0, concat_axis=0, tiled=True)]
    ppermute x6 -> x14, waiting for transfers between devices: 7.92 us -> 23.3 us  [from_above(): lax.ppermute(value, 'z', [((i + distance) % count, i) for i in range(coun...]
    dot_general x2 -> x3, local copies, waits for them, and re-layouts: 0.41 us -> 9.65 us  [token_sum(): lax.dot_general(left, right, (((0,), (0,)), ((), ())), preferred_element_...]
    ppermute x5, starting transfers between devices: 11.9 us -> 20.2 us  [swap_cores(): return lax.ppermute(value, 'core', [(0, 1), (1, 0)])]
    ppermute x5, waiting for transfers between devices: 3.56 us -> 0.01 us  [swap_cores(): return lax.ppermute(value, 'core', [(0, 1), (1, 0)])]
  transfers between devices with their start and end apart: 29 -> 37, of which waited for: 13 -> 14; matrix products, arithmetic and copies ran while one was open for 10% -> 20% of each run, Pallas kernels for 0% -> 0%
where the time goes in v8:
time: 302 us; the launch traced here: 300 us
  starting transfers between devices  184 us (61%)
  local copies, waits for them, and re-layouts  40.8 us (14%)
  waiting for transfers between devices  40.7 us (13%)
  other arithmetic  19.3 us (6%)
  matrix products  13 us (4%)
    ppermute x14, starting transfers between devices, from_above(): lax.ppermute(value, 'z', [((i + distance) % count, i) for i in range(coun...  68 us
    all_to_all x6, starting transfers between devices, exchange(): return lax.all_to_all(blocks, axes, split_axis=0, concat_axis=0, tiled=True)  53.9 us
    ppermute x14, waiting for transfers between devices, from_above(): lax.ppermute(value, 'z', [((i + distance) % count, i) for i in range(coun...  23.3 us
    ppermute x5, starting transfers between devices, swap_cores(): return lax.ppermute(value, 'core', [(0, 1), (1, 0)])  20.2 us
    ppermute x7, starting transfers between devices, swap_near(): return lax.ppermute(value, 'y_lo', [(0, 1), (1, 0)])  19.4 us
    ppermute x2, starting transfers between devices, trade_pair(): other = lax.ppermute(sent, axis_name, [(0, 1), (1, 0)])  13.5 us
    dot_general x3, local copies, waits for them, and re-layouts, token_sum(): lax.dot_general(left, right, (((0,), (0,)), ((), ())), preferred_element_...  9.65 us
    ppermute x3, starting transfers between devices, trade_x(): lax.ppermute(turned[step], 'x', [(i, (i + step) % count) for i in range(c...  9.33 us
  transfers between devices with their start and end apart: 37, of which 14 were waited for; matrix products, arithmetic and copies ran while one was open for 20% of the time, Pallas kernels for 0%

profile of v8, /device:TPU:1, one launch (start us, length us, event | category | flops | bytes accessed | tf_op | source)
XLA Modules:
  0.0 300.0 jit_solution(15600120863504993543)
XLA Ops:
  0.6 4.0 %collective-permute-start.1 = (bf16[896,256]{1,0:T(8,128)(2,1)}, bf16[896,256]{1,0:T(8,128)(2,1)S(1)}, u32[]{:S(2)}, u32[]{:S(2)}) collective-permute-start(bf16[896,256]{1,0:T(8,128)(2,1)} %param.17), channel_id=1, source_target_pairs={{0,256},{256,0},{1,257},{257,1},{2,258},{258,2},{3,259},{259,3},{4... | collective-permute-start | bytes 1376264 | tf_op jit(solution)/shard_map/ppermute | solution.py:36
  13.1 8.7 %collective-permute-start = (bf16[4,2,12,256]{3,1,2,0:T(2,128)(2,1)S(1)}, bf16[4,2,12,256]{3,1,2,0:T(2,128)(2,1)S(1)}, u32[]{:S(2)}, u32[]{:S(2)}) collective-permute-start(bf16[4,2,12,256]{3,1,2,0:T(2,128)(2,1)S(1)} %bitcast.243), channel_id=1, source_target_pairs={{0,1},{1,0},{2,3},{3,2},{4,5},{5,4},{6,7},{7,6},{8,9},{9,8},{10,11... | collective-permute-start | bytes 147464 | tf_op jit(solution)/shard_map/ppermute | solution.py:85
  21.8 9.6 %all-to-all-start = ((bf16[16,8,2048]{2,1,0:T(8,128)(2,1)}), bf16[16,8,2048]{2,1,0:T(8,128)(2,1)S(1)}, u32[]{:S(2)}, u32[]{:S(2)}) async-start(bf16[16,8,2048]{2,1,0:T(8,128)(2,1)} %reshape.245), calls=%async_computation | async-start | bytes 1048576 | tf_op jit(solution)/shard_map/all_to_all | solution.py:28
  31.9 4.8 %collective-permute-start.3 = (bf16[2,4,12,256]{3,1,2,0:T(4,128)(2,1)S(1)}, bf16[2,4,12,256]{3,1,2,0:T(4,128)(2,1)S(1)}, u32[]{:S(2)}, u32[]{:S(2)}) collective-permute-start(bf16[2,4,12,256]{3,1,2,0:T(4,128)(2,1)S(1)} %bitcast.242), channel_id=1, source_target_pairs={{0,2},{2,0},{1,3},{3,1},{4,6},{6,4},{5,7},{7,5},{8,10},{10,8},{9,1... | collective-permute-start | bytes 147464 | tf_op jit(solution)/shard_map/ppermute | solution.py:85
  38.8 4.4 %collective-permute-start.4 = (bf16[2,2,12,256]{3,1,2,0:T(2,128)(2,1)S(1)}, bf16[2,2,12,256]{3,1,2,0:T(2,128)(2,1)S(1)}, u32[]{:S(2)}, u32[]{:S(2)}) collective-permute-start(bf16[2,2,12,256]{3,1,2,0:T(2,128)(2,1)S(1)} %bitcast.250), channel_id=1, source_target_pairs={{0,12},{4,0},{8,4},{12,8},{1,13},{5,1},{9,5},{13,9},{2,14},{6,2},{... | collective-permute-start | bytes 73736 | tf_op jit(solution)/shard_map/ppermute | solution.py:93
  59.0 12.4 %all-to-all-start.1 = ((bf16[16,64,2048]{2,1,0:T(8,128)(2,1)}), bf16[16,64,2048]{2,1,0:T(8,128)(2,1)}, u32[]{:S(2)}, u32[]{:S(2)}) async-start(bf16[16,64,2048]{2,1,0:T(8,128)(2,1)} %bitcast.207), calls=%async_computation.1 | async-start | bytes 8388608 | tf_op jit(solution)/shard_map/all_to_all | solution.py:28
  71.5 4.3 %collective-permute-start.11 = (bf16[320,256]{1,0:T(8,128)(2,1)S(1)}, bf16[320,256]{1,0:T(8,128)(2,1)S(1)}, u32[]{:S(2)}, u32[]{:S(2)}) collective-permute-start(bf16[320,256]{1,0:T(8,128)(2,1)S(1)} %constant_dynamic-update-slice_fusion), channel_id=1, source_target_pairs={{192,0},{208,16},{224,32},{240,48},{0,64},{16,80},{32,96},{48,112}... | collective-permute-start | bytes 491528 | tf_op jit(solution)/shard_map/ppermute | solution.py:41
  75.8 4.9 %collective-permute-start.9 = (bf16[320,256]{1,0:T(8,128)(2,1)S(1)}, bf16[320,256]{1,0:T(8,128)(2,1)S(1)}, u32[]{:S(2)}, u32[]{:S(2)}) collective-permute-start(bf16[320,256]{1,0:T(8,128)(2,1)S(1)} %constant_dynamic-update-slice_fusion), channel_id=1, source_target_pairs={{64,0},{80,16},{96,32},{112,48},{128,64},{144,80},{160,96},{176,11... | collective-permute-start | bytes 491528 | tf_op jit(solution)/shard_map/ppermute | solution.py:41
  83.3 5.2 %collective-permute-start.12 = (bf16[160,256]{1,0:T(8,128)(2,1)S(1)}, bf16[160,256]{1,0:T(8,128)(2,1)S(1)}, u32[]{:S(2)}, u32[]{:S(2)}) collective-permute-start(bf16[160,256]{1,0:T(8,128)(2,1)S(1)} %slice.160), channel_id=1, source_target_pairs={{192,0},{208,16},{224,32},{240,48},{0,64},{16,80},{32,96},{48,112}... | collective-permute-start | bytes 245768 | tf_op jit(solution)/shard_map/ppermute | solution.py:41
  93.5 6.4 %collective-permute-start.7 = (bf16[2048,256]{1,0:T(8,128)(2,1)S(1)}, bf16[2048,256]{1,0:T(8,128)(2,1)}, u32[]{:S(2)}, u32[]{:S(2)}) collective-permute-start(bf16[2048,256]{1,0:T(8,128)(2,1)S(1)} %bitcast.221), channel_id=1, source_target_pairs={{0,1},{1,0},{2,3},{3,2},{4,5},{5,4},{6,7},{7,6},{8,9},{9,8},{10,11... | collective-permute-start | bytes 3145736 | tf_op jit(solution)/shard_map/ppermute | solution.py:32
  101.6 13.9 %collective-permute-start.13 = (bf16[4,320,256]{2,1,0:T(8,128)(2,1)S(1)}, bf16[4,320,256]{2,1,0:T(8,128)(2,1)S(1)}, u32[]{:S(2)}, u32[]{:S(2)}) collective-permute-start(bf16[4,320,256]{2,1,0:T(8,128)(2,1)S(1)} %get-tuple-element.54), channel_id=1, source_target_pairs={{16,0},{32,16},{48,32},{64,48},{80,64},{96,80},{112,96},{128,112},... | collective-permute-start | bytes 1966088 | tf_op jit(solution)/shard_map/ppermute | solution.py:41
  117.4 11.8 %collective-permute-done.13 = bf16[4,320,256]{2,1,0:T(8,128)(2,1)S(1)} collective-permute-done((bf16[4,320,256]{2,1,0:T(8,128)(2,1)S(1)}, bf16[4,320,256]{2,1,0:T(8,128)(2,1)S(1)}, u32[]{:S(2)}, u32[]{:S(2)}) %collective-permute-start.13) | collective-permute-done | bytes 655392 | tf_op jit(solution)/shard_map/ppermute | solution.py:41
  129.9 5.3 %collective-permute-start.14 = (bf16[2,320,256]{2,1,0:T(8,128)(2,1)}, bf16[2,320,256]{2,1,0:T(8,128)(2,1)}, u32[]{:S(2)}, u32[]{:S(2)}) collective-permute-start(bf16[2,320,256]{2,1,0:T(8,128)(2,1)} %slice.161), channel_id=1, source_target_pairs={{16,0},{32,16},{48,32},{64,48},{80,64},{96,80},{112,96},{128,112},... | collective-permute-start | bytes 983048 | tf_op jit(solution)/shard_map/ppermute | solution.py:41
  137.9 3.7 %fusion.49 = f32[1024,256]{1,0:T(8,128)S(1)} fusion(bf16[1024,2048]{1,0:T(8,128)(2,1)} %bitcast.29, bf16[2048,256]{1,0:T(8,128)(2,1)} %collective-permute-done.7), kind=kOutput, calls=%fused_computation.144 | convolution fusion | flops 1073741824 | bytes 6291456 | tf_op jit(solution)/shard_map/dot_general | solution.py:211
  141.7 3.6 %collective-permute-start.8 = (f32[1024,256]{1,0:T(8,128)S(1)}, f32[1024,256]{1,0:T(8,128)S(1)}, u32[]{:S(2)}, u32[]{:S(2)}) collective-permute-start(f32[1024,256]{1,0:T(8,128)S(1)} %fusion.49), channel_id=1, source_target_pairs={{0,1},{1,0},{2,3},{3,2},{4,5},{5,4},{6,7},{7,6},{8,9},{9,8},{10,11... | collective-permute-start | bytes 3145736 | tf_op jit(solution)/shard_map/ppermute | solution.py:32
  148.8 3.4 %fusion.48 = f32[1024,256]{1,0:T(8,128)S(1)} fusion(bf16[1024,2048]{1,0:T(8,128)(2,1)} %bitcast.29, bf16[2048,256]{1,0:T(8,128)(2,1)S(1)} %bitcast.222), kind=kOutput, calls=%fused_computation.143 | convolution fusion | flops 1073741824 | bytes 6291456 | tf_op jit(solution)/shard_map/dot_general | solution.py:212
  155.5 5.5 %all-to-all-start.2 = ((bf16[16,64,256]{2,1,0:T(8,128)(2,1)}), bf16[16,64,256]{2,1,0:T(8,128)(2,1)}, u32[]{:S(2)}, u32[]{:S(2)}) async-start(bf16[16,64,256]{2,1,0:T(8,128)(2,1)} %copy.337), calls=%async_computation.2 | async-start | bytes 1048576 | tf_op jit(solution)/shard_map/all_to_all | solution.py:28
  162.8 4.8 %collective-permute-start.17 = (bf16[1024,256]{1,0:T(8,128)(2,1)}, bf16[1024,256]{1,0:T(8,128)(2,1)}, u32[]{:S(2)}, u32[]{:S(2)}) collective-permute-start(bf16[1024,256]{1,0:T(8,128)(2,1)} %reshape.257), channel_id=1, source_target_pairs={{0,1},{1,0},{2,3},{3,2},{4,5},{5,4},{6,7},{7,6},{8,9},{9,8},{10,11... | collective-permute-start | bytes 1572872 | tf_op jit(solution)/shard_map/ppermute | solution.py:32
  170.7 6.4 %copy.338 = bf16[2048,1024]{1,0:T(8,128)(2,1)} copy(bf16[2048,1024]{0,1:T(8,128)(2,1)} %bitcast.47) | data formatting | bytes 8388608 | tf_op jit(solution)/shard_map/dot_general | solution.py:24
  177.1 4.4 %fusion = f32[2,896,512]{2,1,0:T(8,128)S(1)} fusion(bf16[2,1024,1024]{2,1,0:T(8,128)(2,1)} %bitcast.210, bf16[1024,256]{1,0:T(8,128)(2,1)} %collective-permute-done.17, bf16[1024,256]{1,0:T(8,128)(2,1)} %reshape.257), kind=kOutput, calls=%fused_computation | convolution fusion | flops 1881145344 | bytes 8388608 | tf_op jit(solution)/shard_map/dot_general | solution.py:24
  193.5 12.0 %all-to-all-start.3 = ((f32[16,1,64]{2,1,0:T(1,128)}), f32[16,1,64]{2,1,0:T(1,128)S(1)}, u32[]{:S(2)}, u32[]{:S(2)}) async-start(f32[16,1,64]{2,1,0:T(1,128)} %broadcast_in_dim.17), calls=%async_computation.3 | async-start | bytes 16384 | tf_op jit(solution)/shard_map/all_to_all | solution.py:28
  206.1 6.3 %all-to-all-done.3 = f32[16,1,64]{2,1,0:T(1,128)S(1)} async-done(((f32[16,1,64]{2,1,0:T(1,128)}), f32[16,1,64]{2,1,0:T(1,128)S(1)}, u32[]{:S(2)}, u32[]{:S(2)}) %all-to-all-start.3) | async-done | bytes 4128 | tf_op jit(solution)/shard_map/all_to_all | solution.py:28
  217.5 6.2 %collective-permute-start.23 = (bf16[72,256]{1,0:T(8,128)(2,1)S(1)}, bf16[72,256]{1,0:T(8,128)(2,1)S(1)}, u32[]{:S(2)}, u32[]{:S(2)}) collective-permute-start(bf16[72,256]{1,0:T(8,128)(2,1)S(1)} %concatenate.65), channel_id=1, source_target_pairs={{192,0},{208,16},{224,32},{240,48},{0,64},{16,80},{32,96},{48,112}... | collective-permute-start | bytes 110600 | tf_op jit(solution)/shard_map/ppermute | solution.py:41
  223.7 7.4 %collective-permute-start.22 = (bf16[72,256]{1,0:T(8,128)(2,1)S(1)}, bf16[72,256]{1,0:T(8,128)(2,1)}, u32[]{:S(2)}, u32[]{:S(2)}) collective-permute-start(bf16[72,256]{1,0:T(8,128)(2,1)S(1)} %concatenate.65), channel_id=1, source_target_pairs={{128,0},{144,16},{160,32},{176,48},{192,64},{208,80},{224,96},{240... | collective-permute-start | bytes 110600 | tf_op jit(solution)/shard_map/ppermute | solution.py:41
  231.1 5.3 %collective-permute-start.21 = (bf16[72,256]{1,0:T(8,128)(2,1)S(1)}, bf16[72,256]{1,0:T(8,128)(2,1)}, u32[]{:S(2)}, u32[]{:S(2)}) collective-permute-start(bf16[72,256]{1,0:T(8,128)(2,1)S(1)} %concatenate.65), channel_id=1, source_target_pairs={{64,0},{80,16},{96,32},{112,48},{128,64},{144,80},{160,96},{176,11... | collective-permute-start | bytes 110600 | tf_op jit(solution)/shard_map/ppermute | solution.py:41
  240.8 3.4 %collective-permute-start.29 = (f32[896,256]{1,0:T(8,128)}, f32[896,256]{1,0:T(8,128)}, u32[]{:S(2)}, u32[]{:S(2)}) collective-permute-start(f32[896,256]{1,0:T(8,128)} %slice.173), channel_id=1, source_target_pairs={{0,1},{1,0},{2,3},{3,2},{4,5},{5,4},{6,7},{7,6},{8,9},{9,8},{10,11... | collective-permute-start | bytes 2752520 | tf_op jit(solution)/shard_map/ppermute | solution.py:32
  247.0 6.4 %all-to-all-start.4 = ((bf16[16,8,4096]{2,1,0:T(8,128)(2,1)}), bf16[16,8,4096]{2,1,0:T(8,128)(2,1)S(1)}, u32[]{:S(2)}, u32[]{:S(2)}) async-start(bf16[16,8,4096]{2,1,0:T(8,128)(2,1)} %reshape.260), calls=%async_computation.4 | async-start | bytes 2097152 | tf_op jit(solution)/shard_map/all_to_all | solution.py:28
  257.1 3.8 %collective-permute-start.25 = (bf16[4,72,256]{2,1,0:T(8,128)(2,1)}, bf16[4,72,256]{2,1,0:T(8,128)(2,1)S(1)}, u32[]{:S(2)}, u32[]{:S(2)}) collective-permute-start(bf16[4,72,256]{2,1,0:T(8,128)(2,1)} %get-tuple-element.62), channel_id=1, source_target_pairs={{32,0},{48,16},{64,32},{80,48},{96,64},{112,80},{128,96},{144,112}... | collective-permute-start | bytes 442376 | tf_op jit(solution)/shard_map/ppermute | solution.py:41
  269.1 3.7 %collective-permute-done.24 = bf16[4,72,256]{2,1,0:T(8,128)(2,1)} collective-permute-done((bf16[4,72,256]{2,1,0:T(8,128)(2,1)}, bf16[4,72,256]{2,1,0:T(8,128)(2,1)}, u32[]{:S(2)}, u32[]{:S(2)}) %collective-permute-start.24) | collective-permute-done | bytes 147488 | tf_op jit(solution)/shard_map/ppermute | solution.py:41
  278.3 8.0 %all-to-all-start.5 = ((f32[16,1,256]{2,1,0:T(1,128)}), f32[16,1,256]{2,1,0:T(1,128)S(1)}, u32[]{:S(2)}, u32[]{:S(2)}) async-start(f32[16,1,256]{2,1,0:T(1,128)} %broadcast_in_dim.38), calls=%async_computation.5 | async-start | bytes 32768 | tf_op jit(solution)/shard_map/all_to_all | solution.py:28
  288.9 3.4 %collective-permute-start.30 = (f32[2,128,256]{2,1,0:T(8,128)S(1)}, f32[2,128,256]{2,1,0:T(8,128)S(1)}, u32[]{:S(2)}, u32[]{:S(2)}) collective-permute-start(f32[2,128,256]{2,1,0:T(8,128)S(1)} %fusion.28), channel_id=1, source_target_pairs={{0,256},{256,0},{1,257},{257,1},{2,258},{258,2},{3,259},{259,3},{4... | collective-permute-start | bytes 786440 | tf_op jit(solution)/shard_map/ppermute | solution.py:36
  294.4 4.3 %collective-permute-done.30 = f32[2,128,256]{2,1,0:T(8,128)S(1)} collective-permute-done((f32[2,128,256]{2,1,0:T(8,128)S(1)}, f32[2,128,256]{2,1,0:T(8,128)S(1)}, u32[]{:S(2)}, u32[]{:S(2)}) %collective-permute-start.30) | collective-permute-done | bytes 262176 | tf_op jit(solution)/shard_map/ppermute | solution.py:36
  (213 shorter events, 100.3 us)
Async XLA Ops:
  0.6 31.0 %collective-permute-start.1 = (bf16[896,256]{1,0:T(8,128)(2,1)}, bf16[896,256]{1,0:T(8,128)(2,1)S(1)}, u32[]{:S(2)}, u32[]{:S(2)}) collective-permute-start(bf16[896,256]{1,0:T(8,128)(2,1)} %param.17), channel_id=1, source_target_pairs={{0,256},{256,0},{1,257},{257,1},{2,258},{258,2},{3,259},{259,3},{4... | collective-permute-start | bytes 1376264 | tf_op jit(solution)/shard_map/ppermute | solution.py:36
  4.7 26.9 %collective-permute-start.2 = (bf16[896,256]{1,0:T(8,128)(2,1)}, bf16[896,256]{1,0:T(8,128)(2,1)S(1)}, u32[]{:S(2)}, u32[]{:S(2)}) collective-permute-start(bf16[896,256]{1,0:T(8,128)(2,1)} %param.18), channel_id=1, source_target_pairs={{0,256},{256,0},{1,257},{257,1},{2,258},{258,2},{3,259},{259,3},{4... | collective-permute-start | bytes 1376264 | tf_op jit(solution)/shard_map/ppermute | solution.py:36
  13.1 18.3 %collective-permute-start = (bf16[4,2,12,256]{3,1,2,0:T(2,128)(2,1)S(1)}, bf16[4,2,12,256]{3,1,2,0:T(2,128)(2,1)S(1)}, u32[]{:S(2)}, u32[]{:S(2)}) collective-permute-start(bf16[4,2,12,256]{3,1,2,0:T(2,128)(2,1)S(1)} %bitcast.243), channel_id=1, source_target_pairs={{0,1},{1,0},{2,3},{3,2},{4,5},{5,4},{6,7},{7,6},{8,9},{9,8},{10,11... | collective-permute-start | bytes 147464 | tf_op jit(solution)/shard_map/ppermute | solution.py:85
  21.8 33.7 %all-to-all-start = ((bf16[16,8,2048]{2,1,0:T(8,128)(2,1)}), bf16[16,8,2048]{2,1,0:T(8,128)(2,1)S(1)}, u32[]{:S(2)}, u32[]{:S(2)}) async-start(bf16[16,8,2048]{2,1,0:T(8,128)(2,1)} %reshape.245), calls=%async_computation | async-start | bytes 1048576 | tf_op jit(solution)/shard_map/all_to_all | solution.py:28
  38.8 10.2 %collective-permute-start.4 = (bf16[2,2,12,256]{3,1,2,0:T(2,128)(2,1)S(1)}, bf16[2,2,12,256]{3,1,2,0:T(2,128)(2,1)S(1)}, u32[]{:S(2)}, u32[]{:S(2)}) collective-permute-start(bf16[2,2,12,256]{3,1,2,0:T(2,128)(2,1)S(1)} %bitcast.250), channel_id=1, source_target_pairs={{0,12},{4,0},{8,4},{12,8},{1,13},{5,1},{9,5},{13,9},{2,14},{6,2},{... | collective-permute-start | bytes 73736 | tf_op jit(solution)/shard_map/ppermute | solution.py:93
  59.0 78.9 %all-to-all-start.1 = ((bf16[16,64,2048]{2,1,0:T(8,128)(2,1)}), bf16[16,64,2048]{2,1,0:T(8,128)(2,1)}, u32[]{:S(2)}, u32[]{:S(2)}) async-start(bf16[16,64,2048]{2,1,0:T(8,128)(2,1)} %bitcast.207), calls=%async_computation.1 | async-start | bytes 8388608 | tf_op jit(solution)/shard_map/all_to_all | solution.py:28
  71.5 11.8 %collective-permute-start.11 = (bf16[320,256]{1,0:T(8,128)(2,1)S(1)}, bf16[320,256]{1,0:T(8,128)(2,1)S(1)}, u32[]{:S(2)}, u32[]{:S(2)}) collective-permute-start(bf16[320,256]{1,0:T(8,128)(2,1)S(1)} %constant_dynamic-update-slice_fusion), channel_id=1, source_target_pairs={{192,0},{208,16},{224,32},{240,48},{0,64},{16,80},{32,96},{48,112}... | collective-permute-start | bytes 491528 | tf_op jit(solution)/shard_map/ppermute | solution.py:41
  75.8 14.5 %collective-permute-start.9 = (bf16[320,256]{1,0:T(8,128)(2,1)S(1)}, bf16[320,256]{1,0:T(8,128)(2,1)S(1)}, u32[]{:S(2)}, u32[]{:S(2)}) collective-permute-start(bf16[320,256]{1,0:T(8,128)(2,1)S(1)} %constant_dynamic-update-slice_fusion), channel_id=1, source_target_pairs={{64,0},{80,16},{96,32},{112,48},{128,64},{144,80},{160,96},{176,11... | collective-permute-start | bytes 491528 | tf_op jit(solution)/shard_map/ppermute | solution.py:41
  83.3 16.7 %collective-permute-start.12 = (bf16[160,256]{1,0:T(8,128)(2,1)S(1)}, bf16[160,256]{1,0:T(8,128)(2,1)S(1)}, u32[]{:S(2)}, u32[]{:S(2)}) collective-permute-start(bf16[160,256]{1,0:T(8,128)(2,1)S(1)} %slice.160), channel_id=1, source_target_pairs={{192,0},{208,16},{224,32},{240,48},{0,64},{16,80},{32,96},{48,112}... | collective-permute-start | bytes 245768 | tf_op jit(solution)/shard_map/ppermute | solution.py:41
  90.3 11.1 %collective-permute-start.10 = (bf16[160,256]{1,0:T(8,128)(2,1)S(1)}, bf16[160,256]{1,0:T(8,128)(2,1)S(1)}, u32[]{:S(2)}, u32[]{:S(2)}) collective-permute-start(bf16[160,256]{1,0:T(8,128)(2,1)S(1)} %slice.159), channel_id=1, source_target_pairs={{64,0},{80,16},{96,32},{112,48},{128,64},{144,80},{160,96},{176,11... | collective-permute-start | bytes 245768 | tf_op jit(solution)/shard_map/ppermute | solution.py:41
  93.5 44.4 %collective-permute-start.7 = (bf16[2048,256]{1,0:T(8,128)(2,1)S(1)}, bf16[2048,256]{1,0:T(8,128)(2,1)}, u32[]{:S(2)}, u32[]{:S(2)}) collective-permute-start(bf16[2048,256]{1,0:T(8,128)(2,1)S(1)} %bitcast.221), channel_id=1, source_target_pairs={{0,1},{1,0},{2,3},{3,2},{4,5},{5,4},{6,7},{7,6},{8,9},{9,8},{10,11... | collective-permute-start | bytes 3145736 | tf_op jit(solution)/shard_map/ppermute | solution.py:32
  101.6 27.6 %collective-permute-start.13 = (bf16[4,320,256]{2,1,0:T(8,128)(2,1)S(1)}, bf16[4,320,256]{2,1,0:T(8,128)(2,1)S(1)}, u32[]{:S(2)}, u32[]{:S(2)}) collective-permute-start(bf16[4,320,256]{2,1,0:T(8,128)(2,1)S(1)} %get-tuple-element.54), channel_id=1, source_target_pairs={{16,0},{32,16},{48,32},{64,48},{80,64},{96,80},{112,96},{128,112},... | collective-permute-start | bytes 1966088 | tf_op jit(solution)/shard_map/ppermute | solution.py:41
  115.4 19.8 %collective-permute-start.15 = (bf16[4,320,256]{2,1,0:T(8,128)(2,1)S(1)}, bf16[4,320,256]{2,1,0:T(8,128)(2,1)S(1)}, u32[]{:S(2)}, u32[]{:S(2)}) collective-permute-start(bf16[4,320,256]{2,1,0:T(8,128)(2,1)S(1)} %get-tuple-element.54), channel_id=1, source_target_pairs={{240,0},{0,16},{16,32},{32,48},{48,64},{64,80},{80,96},{96,112},{1... | collective-permute-start | bytes 1966088 | tf_op jit(solution)/shard_map/ppermute | solution.py:41
  129.9 15.6 %collective-permute-start.14 = (bf16[2,320,256]{2,1,0:T(8,128)(2,1)}, bf16[2,320,256]{2,1,0:T(8,128)(2,1)}, u32[]{:S(2)}, u32[]{:S(2)}) collective-permute-start(bf16[2,320,256]{2,1,0:T(8,128)(2,1)} %slice.161), channel_id=1, source_target_pairs={{16,0},{32,16},{48,32},{64,48},{80,64},{96,80},{112,96},{128,112},... | collective-permute-start | bytes 983048 | tf_op jit(solution)/shard_map/ppermute | solution.py:41
  136.0 11.1 %collective-permute-start.16 = (bf16[2,320,256]{2,1,0:T(8,128)(2,1)}, bf16[2,320,256]{2,1,0:T(8,128)(2,1)}, u32[]{:S(2)}, u32[]{:S(2)}) collective-permute-start(bf16[2,320,256]{2,1,0:T(8,128)(2,1)} %pad_maximum_fusion.4), channel_id=1, source_target_pairs={{240,0},{0,16},{16,32},{32,48},{48,64},{64,80},{80,96},{96,112},{1... | collective-permute-start | bytes 983048 | tf_op jit(solution)/shard_map/ppermute | solution.py:41
  141.7 10.5 %collective-permute-start.8 = (f32[1024,256]{1,0:T(8,128)S(1)}, f32[1024,256]{1,0:T(8,128)S(1)}, u32[]{:S(2)}, u32[]{:S(2)}) collective-permute-start(f32[1024,256]{1,0:T(8,128)S(1)} %fusion.49), channel_id=1, source_target_pairs={{0,1},{1,0},{2,3},{3,2},{4,5},{5,4},{6,7},{7,6},{8,9},{9,8},{10,11... | collective-permute-start | bytes 3145736 | tf_op jit(solution)/shard_map/ppermute | solution.py:32
  155.5 28.9 %all-to-all-start.2 = ((bf16[16,64,256]{2,1,0:T(8,128)(2,1)}), bf16[16,64,256]{2,1,0:T(8,128)(2,1)}, u32[]{:S(2)}, u32[]{:S(2)}) async-start(bf16[16,64,256]{2,1,0:T(8,128)(2,1)} %copy.337), calls=%async_computation.2 | async-start | bytes 1048576 | tf_op jit(solution)/shard_map/all_to_all | solution.py:28
  162.8 14.4 %collective-permute-start.17 = (bf16[1024,256]{1,0:T(8,128)(2,1)}, bf16[1024,256]{1,0:T(8,128)(2,1)}, u32[]{:S(2)}, u32[]{:S(2)}) collective-permute-start(bf16[1024,256]{1,0:T(8,128)(2,1)} %reshape.257), channel_id=1, source_target_pairs={{0,1},{1,0},{2,3},{3,2},{4,5},{5,4},{6,7},{7,6},{8,9},{9,8},{10,11... | collective-permute-start | bytes 1572872 | tf_op jit(solution)/shard_map/ppermute | solution.py:32
  168.7 15.7 %collective-permute-start.18 = (bf16[1024,256]{1,0:T(8,128)(2,1)S(1)}, bf16[1024,256]{1,0:T(8,128)(2,1)}, u32[]{:S(2)}, u32[]{:S(2)}) collective-permute-start(bf16[1024,256]{1,0:T(8,128)(2,1)S(1)} %pad_maximum_fusion.3), channel_id=1, source_target_pairs={{0,1},{1,0},{2,3},{3,2},{4,5},{5,4},{6,7},{7,6},{8,9},{9,8},{10,11... | collective-permute-start | bytes 1572872 | tf_op jit(solution)/shard_map/ppermute | solution.py:32
  184.4 28.0 %collective-permute-start.19 = (bf16[896,512]{1,0:T(8,128)(2,1)}, bf16[896,512]{1,0:T(8,128)(2,1)}, u32[]{:S(2)}, u32[]{:S(2)}) collective-permute-start(bf16[896,512]{1,0:T(8,128)(2,1)} %fusion.15), channel_id=1, source_target_pairs={{0,256},{256,0},{1,257},{257,1},{2,258},{258,2},{3,259},{259,3},{4... | collective-permute-start | bytes 2752520 | tf_op jit(solution)/shard_map/ppermute | solution.py:36
  187.8 17.7 %collective-permute-start.20 = (f32[1,256]{1,0:T(1,128)S(1)}, f32[1,256]{1,0:T(1,128)S(1)}, u32[]{:S(2)}, u32[]{:S(2)}) collective-permute-start(f32[1,256]{1,0:T(1,128)S(1)} %bitcast.254), channel_id=1, source_target_pairs={{0,256},{256,0},{1,257},{257,1},{2,258},{258,2},{3,259},{259,3},{4... | collective-permute-start | bytes 3080 | tf_op jit(solution)/shard_map/ppermute | solution.py:36
  193.5 18.9 %all-to-all-start.3 = ((f32[16,1,64]{2,1,0:T(1,128)}), f32[16,1,64]{2,1,0:T(1,128)S(1)}, u32[]{:S(2)}, u32[]{:S(2)}) async-start(f32[16,1,64]{2,1,0:T(1,128)} %broadcast_in_dim.17), calls=%async_computation.3 | async-start | bytes 16384 | tf_op jit(solution)/shard_map/all_to_all | solution.py:28
  213.8 30.4 %collective-permute-start.27 = (bf16[64,256]{1,0:T(8,128)(2,1)S(1)}, bf16[64,256]{1,0:T(8,128)(2,1)S(1)}, u32[]{:S(2)}, u32[]{:S(2)}) collective-permute-start(bf16[64,256]{1,0:T(8,128)(2,1)S(1)} %add_convert_fusion.2), channel_id=1, source_target_pairs={{0,256},{256,0},{1,257},{257,1},{2,258},{258,2},{3,259},{259,3},{4... | collective-permute-start | bytes 98312 | tf_op jit(solution)/shard_map/ppermute | solution.py:36
  217.5 35.9 %collective-permute-start.23 = (bf16[72,256]{1,0:T(8,128)(2,1)S(1)}, bf16[72,256]{1,0:T(8,128)(2,1)S(1)}, u32[]{:S(2)}, u32[]{:S(2)}) collective-permute-start(bf16[72,256]{1,0:T(8,128)(2,1)S(1)} %concatenate.65), channel_id=1, source_target_pairs={{192,0},{208,16},{224,32},{240,48},{0,64},{16,80},{32,96},{48,112}... | collective-permute-start | bytes 110600 | tf_op jit(solution)/shard_map/ppermute | solution.py:41
  223.7 29.8 %collective-permute-start.22 = (bf16[72,256]{1,0:T(8,128)(2,1)S(1)}, bf16[72,256]{1,0:T(8,128)(2,1)}, u32[]{:S(2)}, u32[]{:S(2)}) collective-permute-start(bf16[72,256]{1,0:T(8,128)(2,1)S(1)} %concatenate.65), channel_id=1, source_target_pairs={{128,0},{144,16},{160,32},{176,48},{192,64},{208,80},{224,96},{240... | collective-permute-start | bytes 110600 | tf_op jit(solution)/shard_map/ppermute | solution.py:41
  231.1 22.4 %collective-permute-start.21 = (bf16[72,256]{1,0:T(8,128)(2,1)S(1)}, bf16[72,256]{1,0:T(8,128)(2,1)}, u32[]{:S(2)}, u32[]{:S(2)}) collective-permute-start(bf16[72,256]{1,0:T(8,128)(2,1)S(1)} %concatenate.65), channel_id=1, source_target_pairs={{64,0},{80,16},{96,32},{112,48},{128,64},{144,80},{160,96},{176,11... | collective-permute-start | bytes 110600 | tf_op jit(solution)/shard_map/ppermute | solution.py:41
  240.8 33.3 %collective-permute-start.29 = (f32[896,256]{1,0:T(8,128)}, f32[896,256]{1,0:T(8,128)}, u32[]{:S(2)}, u32[]{:S(2)}) collective-permute-start(f32[896,256]{1,0:T(8,128)} %slice.173), channel_id=1, source_target_pairs={{0,1},{1,0},{2,3},{3,2},{4,5},{5,4},{6,7},{7,6},{8,9},{9,8},{10,11... | collective-permute-start | bytes 2752520 | tf_op jit(solution)/shard_map/ppermute | solution.py:32
  247.0 29.6 %all-to-all-start.4 = ((bf16[16,8,4096]{2,1,0:T(8,128)(2,1)}), bf16[16,8,4096]{2,1,0:T(8,128)(2,1)S(1)}, u32[]{:S(2)}, u32[]{:S(2)}) async-start(bf16[16,8,4096]{2,1,0:T(8,128)(2,1)} %reshape.260), calls=%async_computation.4 | async-start | bytes 2097152 | tf_op jit(solution)/shard_map/all_to_all | solution.py:28
  254.9 11.9 %collective-permute-start.26 = (bf16[4,72,256]{2,1,0:T(8,128)(2,1)}, bf16[4,72,256]{2,1,0:T(8,128)(2,1)}, u32[]{:S(2)}, u32[]{:S(2)}) collective-permute-start(bf16[4,72,256]{2,1,0:T(8,128)(2,1)} %get-tuple-element.62), channel_id=1, source_target_pairs={{240,0},{0,16},{16,32},{32,48},{48,64},{64,80},{80,96},{96,112},{1... | collective-permute-start | bytes 442376 | tf_op jit(solution)/shard_map/ppermute | solution.py:41
  257.1 11.9 %collective-permute-start.25 = (bf16[4,72,256]{2,1,0:T(8,128)(2,1)}, bf16[4,72,256]{2,1,0:T(8,128)(2,1)S(1)}, u32[]{:S(2)}, u32[]{:S(2)}) collective-permute-start(bf16[4,72,256]{2,1,0:T(8,128)(2,1)} %get-tuple-element.62), channel_id=1, source_target_pairs={{32,0},{48,16},{64,32},{80,48},{96,64},{112,80},{128,96},{144,112}... | collective-permute-start | bytes 442376 | tf_op jit(solution)/shard_map/ppermute | solution.py:41
  260.9 11.9 %collective-permute-start.24 = (bf16[4,72,256]{2,1,0:T(8,128)(2,1)}, bf16[4,72,256]{2,1,0:T(8,128)(2,1)}, u32[]{:S(2)}, u32[]{:S(2)}) collective-permute-start(bf16[4,72,256]{2,1,0:T(8,128)(2,1)} %get-tuple-element.62), channel_id=1, source_target_pairs={{16,0},{32,16},{48,32},{64,48},{80,64},{96,80},{112,96},{128,112},... | collective-permute-start | bytes 442376 | tf_op jit(solution)/shard_map/ppermute | solution.py:41
  278.3 15.3 %all-to-all-start.5 = ((f32[16,1,256]{2,1,0:T(1,128)}), f32[16,1,256]{2,1,0:T(1,128)S(1)}, u32[]{:S(2)}, u32[]{:S(2)}) async-start(f32[16,1,256]{2,1,0:T(1,128)} %broadcast_in_dim.38), calls=%async_computation.5 | async-start | bytes 32768 | tf_op jit(solution)/shard_map/all_to_all | solution.py:28
  (17 other events, 139.0 us)

commit v9 on v8

--- a/solution.py
+++ b/solution.py
@@ -7,6 +7,7 @@
 epsilon = 1e-05
 narrow = jnp.bfloat16
 wide = jnp.float32
+z_axes = ("z_hi", "z_lo")
 
 
 def swiglu_back(gate_act, up_act, product_grad):
@@ -36,13 +37,13 @@
     return lax.ppermute(value, "y_lo", [(0, 1), (1, 0)])
 
 
-def from_above(value, distance):
-    count = lax.axis_size("z")
-    return lax.ppermute(value, "z", [((i + distance) % count, i) for i in range(count)])
+def from_above(value, distance, axes=z_axes):
+    count = lax.axis_size(axes)
+    return lax.ppermute(value, axes, [((i + distance) % count, i) for i in range(count)])
 
 
 def gather_z(block):
-    z_count = lax.axis_size("z")
+    z_count = lax.axis_size(z_axes)
     quarter = z_count // 4
     strided = jnp.stack([block] + [from_above(block, 4 * step) for step in range(1, quarter)])
     below = from_above(strided, z_count - 1)
@@ -50,32 +51,18 @@
     all_blocks = jnp.stack(
         [strided, from_above(strided, 1), from_above(strided, 2), below], axis=1
     ).reshape(z_count, *block.shape)
-    return from_first(all_blocks)
-
-
-def gather_z_relay(block):
-    z_count = lax.axis_size("z")
-    half = block.shape[0] // 2
-    above, below = from_above(block, 4), from_above(block, z_count - 4)
-    far = jnp.concatenate(
-        [from_above(above[:half], 4), from_above(below[half:], z_count - 4)]
-    )
-    strided = jnp.stack([block, above, far, below])
-    above, below = from_above(strided, 1), from_above(strided, z_count - 1)
-    far = jnp.concatenate(
-        [
-            from_above(above[:2], 1),
-            from_above(jnp.concatenate([below[3:], below[:1]]), z_count - 1),
-        ]
-    )
-    below = jnp.concatenate([below[1:], below[:1]])
-    return jnp.stack([strided, above, far, below], axis=1).reshape(z_count, *block.shape)
-
-
-def from_first(blocks):
+    return from_first(all_blocks, z_axes)
+
+
+def gather_ring(block, axis):
+    count = lax.axis_size(axis)
+    return jnp.stack([block] + [from_above(block, step, axis) for step in range(1, count)])
+
+
+def from_first(blocks, axes):
     twice = jnp.concatenate([blocks, blocks])
     count = blocks.shape[0]
-    return lax.dynamic_slice_in_dim(twice, count - lax.axis_index("z"), count, 0)
+    return lax.dynamic_slice_in_dim(twice, count - lax.axis_index(axes), count, 0)
 
 
 def trade_pair(blocks, axis_name):
@@ -118,7 +105,8 @@
     join_weight,
 ):
     dp_axes = ("x", "y_hi", "core")
-    z_count = lax.axis_size("z")
+    quarter = lax.axis_size("z_lo")
+    z_count = lax.axis_size("z_hi") * quarter
     core_count = lax.axis_size("core")
     dp_count = lax.axis_size("x") * lax.axis_size("y_hi") * core_count
     row_count, width = hidden.shape
@@ -150,7 +138,7 @@
     unit_rows = jnp.stack([gate_rows, up_rows]).transpose(3, 0, 1, 2, 4)
     unit_rows = unit_rows.reshape(z_count, 2 * row_count, 2 * part_width)
     unit_rows, hidden, resid_grad = lax.optimization_barrier((unit_rows, hidden, resid_grad))
-    unit_group = exchange(unit_rows, "z")
+    unit_group = exchange(unit_rows, z_axes)
 
     hidden_wide = hidden.astype(wide)
     row_scale = lax.rsqrt(jnp.mean(hidden_wide * hidden_wide, axis=1, keepdims=True) + epsilon)
@@ -167,9 +155,10 @@
         lax.axis_size("x"), 2, 2, 3 * row_count, features
     )
     norm_block = trade_pair(norm_sent.transpose(2, 0, 1, 3, 4), "core")
-    norm_block, near_gate, near_up = lax.optimization_barrier(
-        (norm_block, swap_near(gate_weight), swap_near(up_weight))
-    )
+    norm_block, near_weights = lax.optimization_barrier(
+        (norm_block, swap_near(jnp.stack([gate_weight, up_weight])))
+    )
+    near_gate, near_up = near_weights[0], near_weights[1]
     norm_block = trade_pair(norm_block.transpose(2, 0, 1, 3, 4), "y_hi")
     norm_block = trade_x(norm_block.transpose(2, 0, 1, 3, 4)).reshape(
         dp_count, 3, row_count, features
@@ -185,7 +174,7 @@
     mlp_block = (normed * gain_block).astype(narrow)
 
     unit_group, mlp_block = lax.optimization_barrier((unit_group, mlp_block))
-    shared_z = gather_z_relay(jnp.concatenate([mlp_block, join_weight]))
+    mlp_z = gather_z(mlp_block)
     unit_halves = (
         unit_group.reshape(z_count, 2, row_count, 2 * part_width)
         .transpose(1, 0, 2, 3)
@@ -195,6 +184,8 @@
         unit_halves[None], (dp_count // core_count, core_count, plane_rows, 2 * part_width)
     ).reshape(dp_count, plane_rows, 2 * part_width)
     half_all = exchange(unit_halves, dp_axes).reshape(tokens, 2 * part_width)
+    join_quad = gather_ring(join_weight, "z_lo")
+    half_all, mlp_z, join_quad = lax.optimization_barrier((half_all, mlp_z, join_quad))
 
     def both_near(own, near):
         both = jnp.pad(by_near(own, near), ((0, 0), (0, half_inputs), (0, 0)))
@@ -217,12 +208,9 @@
         .transpose(1, 0, 2, 3)
         .reshape(z_count, block_rows, features)
     )
-    partial_value, shared_z = lax.optimization_barrier((partial_value, shared_z))
-    join_z = shared_z[:, block_rows:]
 
     mlp_own = (
-        from_first(shared_z[:, :block_rows])
-        .reshape(z_count, dp_count, row_count, features)
+        mlp_z.reshape(z_count, dp_count, row_count, features)
         .transpose(1, 0, 2, 3)
         .reshape(tokens, features)
     )
@@ -233,12 +221,13 @@
     joined_half = jnp.concatenate(
         [half_all[:, units:part_width], half_all[:, part_width + units :]], axis=1
     )
-    partial_far, unit_sent, joined_half, joined_other = lax.optimization_barrier(
+    partial_far, unit_sent, joined_half, joined_other, near_quad = lax.optimization_barrier(
         (
-            exchange(partial_value, "z"),
+            exchange(partial_value, z_axes),
             unit_sent.astype(narrow),
             joined_half,
             swap_cores(joined_half),
+            swap_near(join_quad),
         )
     )
     unit_near = swap_near(unit_sent)
@@ -246,56 +235,74 @@
 
     lifted = input_grad * gain_block
     mean_part = jnp.sum(lifted * normed, axis=1)
-    mean_all = exchange(
-        jnp.broadcast_to(mean_part[None, None], (dp_count, 1, block_rows)), dp_axes
-    )
-    mean_all, unit_near = lax.optimization_barrier((mean_all, unit_near))
-    inner_mean = (jnp.sum(mean_all, axis=(0, 1)) / width)[:, None]
+    gain_part = jnp.sum(input_grad * normed, axis=0)
+    row_parts = jnp.concatenate([mean_part, gain_part])
+    row_parts = exchange(
+        jnp.broadcast_to(row_parts[None, None], (dp_count, 1, block_rows + features)), dp_axes
+    )[:, 0]
+    inner_mean = (jnp.sum(row_parts[:, :block_rows], axis=0) / width)[:, None]
+    gain_part = row_parts[:, block_rows:]
     hidden_grad = (resid_block + scale_block * (lifted - normed * inner_mean)).astype(narrow)
 
-    grad_rows = jnp.stack(
-        [
-            rows.reshape(dp_count, row_count, features)
-            for rows in (hidden_grad, swap_near(hidden_grad))
-        ],
-        axis=1,
-    ).reshape(2 * block_rows, features)
+    grad_sent = jnp.concatenate([hidden_grad, *split_three(gain_part)])
+    sent_rows = block_rows + 3 * dp_count
+    high_count = z_count // quarter
+    grad_high = exchange(
+        jnp.broadcast_to(grad_sent[None], (high_count, sent_rows, features)), "z_hi"
+    )
+
+    join_pair = by_near(join_quad, near_quad).reshape(2 * quarter * inputs, features)
+    joined_half, joined_other = joined_half.T, joined_other.T
+    grad_high, unit_near, join_pair, joined_half, joined_other = lax.optimization_barrier(
+        (grad_high, unit_near, join_pair, joined_half, joined_other)
+    )
+
+    grad_rows = (
+        grad_high[:, :block_rows]
+        .reshape(high_count, dp_count, row_count, features)
+        .transpose(1, 0, 2, 3)
+        .reshape(dp_count * high_count * row_count, features)
+    )
     joined_part = lax.dot_general(
-        grad_rows, join_z, (((1,), (2,)), ((), ())), preferred_element_type=wide
+        grad_rows, join_pair, (((1,), (1,)), ((), ())), preferred_element_type=wide
     ).astype(narrow)
     joined_blocks = exchange(
-        joined_part.reshape(dp_count, 2 * row_count, z_count * inputs), dp_axes
-    )
-    gain_part = jnp.sum(input_grad * normed, axis=0, keepdims=True)
-    gain_part = gain_part + swap_near(gain_part)
-    grad_sent = jnp.concatenate(
-        [hidden_grad] + list(split_three(gain_part)) + [jnp.zeros((5, features), narrow)], axis=0
-    )
-    grad_z = gather_z(grad_sent)
+        joined_part.reshape(dp_count, high_count * row_count, 2 * quarter * inputs), dp_axes
+    )
+    unit_grad = unit_kept + unit_near.astype(wide)
+    other_grad = swap_cores(unit_grad[:, features:])
+
+    def sum_parts(blocks):
+        parts = jnp.sum(blocks.astype(wide).reshape(-1, 3, dp_count, features), axis=0)
+        return (parts[0] + parts[1]) + parts[2]
+
+    gain_high = sum_parts(grad_high[:, block_rows:])
+    gain_high = gain_high + swap_near(gain_high)
+    grad_quad = jnp.concatenate(
+        [grad_high[:, :block_rows].reshape(-1, features), *split_three(gain_high)]
+    )
+    grad_z = from_first(gather_ring(grad_quad, "z_lo"), "z_lo")
     grad_z, joined_blocks = lax.optimization_barrier((grad_z, joined_blocks))
     joined_total = jnp.sum(joined_blocks.astype(wide), axis=0).astype(narrow)
-    joined_total = joined_total.reshape(2, row_count, z_count, inputs).transpose(0, 2, 1, 3)
-    joined_total = by_near(joined_total[0], swap_near(joined_total[1]))
+    joined_high = exchange(
+        joined_total.reshape(high_count, row_count, 2 * quarter * inputs), "z_hi"
+    ).reshape(high_count, row_count, 2, quarter, inputs)
     joined_grad = (
-        from_first(joined_total.transpose(1, 0, 2, 3))
-        .transpose(2, 1, 0, 3)
+        from_first(joined_high.transpose(3, 0, 1, 2, 4), "z_lo")
+        .transpose(2, 3, 1, 0, 4)
         .reshape(row_count, 2 * z_count * inputs)
     )
 
-    gain_sum = jnp.sum(grad_z[:, block_rows : block_rows + 3].astype(wide), axis=(0, 1))
-    gain_grad = exchange(
-        jnp.broadcast_to(gain_sum[None, None], (dp_count, 1, features)), dp_axes
-    ).reshape(width)
+    high_rows = high_count * block_rows
+    gain_grad = sum_parts(grad_z[:, high_rows:]).reshape(width)
     grad_all = (
-        grad_z[:, :block_rows]
-        .reshape(z_count, dp_count, row_count, features)
-        .transpose(1, 0, 2, 3)
+        grad_z[:, :high_rows]
+        .reshape(quarter, high_count, dp_count, row_count, features)
+        .transpose(2, 1, 0, 3, 4)
         .reshape(tokens, features)
     )
 
-    unit_grad = unit_kept + unit_near.astype(wide)
     own_grad = unit_grad[:, :features]
-    other_grad = swap_cores(unit_grad[:, features:])
     gate_weight_grad = jnp.where(on_first, own_grad, other_grad)
     up_weight_grad = jnp.where(on_first, other_grad, own_grad)
 
@@ -305,8 +312,8 @@
         return kept + swap_near(sent)
 
     join_sums = by_core(
-        token_sum(joined_half, grad_all).reshape(2, half_inputs, features),
-        token_sum(joined_other, grad_all).reshape(2, half_inputs, features),
+        jnp.dot(joined_half, grad_all, preferred_element_type=wide).reshape(2, half_inputs, features),
+        jnp.dot(joined_other, grad_all, preferred_element_type=wide).reshape(2, half_inputs, features),
     )
     join_weight_grad = add_near(join_sums.transpose(1, 0, 2, 3)).reshape(inputs, features)
     return (joined_grad, gate_weight_grad, up_weight_grad, join_weight_grad, gain_grad)
@@ -315,10 +322,10 @@
 def solution(mesh):
     tensor_count, dp_count = mesh.shape["tensor"], mesh.shape["dp"]
     fine = Mesh(
-        mesh.devices.reshape(2, tensor_count // 2, dp_count // 4, 2, 2),
-        ("y_lo", "z", "x", "y_hi", "core"),
-    )
-    tensor_axes = ("y_lo", "z")
+        mesh.devices.reshape(2, tensor_count // 8, 4, dp_count // 4, 2, 2),
+        ("y_lo", "z_hi", "z_lo", "x", "y_hi", "core"),
+    )
+    tensor_axes = ("y_lo",) + z_axes
     dp_axes = ("x", "y_hi", "core")
     rows = P(dp_axes + tensor_axes, None)
     blocks = P(tensor_axes, dp_axes)

time: 302 us -> 280 us (0.927)
  starting transfers between devices: 184 us -> 161 us
  waiting for transfers between devices: 40.7 us -> 57.8 us
  local copies, waits for them, and re-layouts: 40.8 us -> 26.8 us
  other arithmetic: 19.3 us -> 16.1 us
    all_to_all x6 -> x7, waiting for transfers between devices: 8.55 us -> 33.3 us  [exchange(): return lax.all_to_all(blocks, axes, split_axis=0, concat_axis=0, tiled=True)]
    ppermute x14 -> x12, starting transfers between devices: 68 us -> 43.6 us  [from_above(): lax.ppermute(value, axes, [((i + distance) % count, i) for i in range(cou...]
    all_to_all x6 -> x7, starting transfers between devices: 53.9 us -> 71.3 us  [exchange(): return lax.all_to_all(blocks, axes, split_axis=0, concat_axis=0, tiled=True)]
    ppermute x5, starting transfers between devices: 20.2 us -> 11.2 us  [swap_cores(): return lax.ppermute(value, 'core', [(0, 1), (1, 0)])]
    ppermute x14 -> x12, waiting for transfers between devices: 23.3 us -> 15.2 us  [from_above(): lax.ppermute(value, axes, [((i + distance) % count, i) for i in range(cou...]
    dot_general x3 -> x2, local copies, waits for them, and re-layouts: 9.65 us -> 3.09 us  [the longest x1 2.06 us: shards(): jnp.dot(joined_other, grad_all, preferred_element_type=wide)]
    ppermute x7 -> x5, starting transfers between devices: 19.4 us -> 14 us  [swap_near(): return lax.ppermute(value, 'y_lo', [(0, 1), (1, 0)])]
  transfers between devices with their start and end apart: 37 -> 34, of which waited for: 14 -> 14; matrix products, arithmetic and copies ran while one was open for 20% -> 15% of each run, Pallas kernels for 0% -> 0%
where the time goes in v9:
time: 280 us; the launch traced here: 277 us
  starting transfers between devices  161 us (58%)
  waiting for transfers between devices  57.8 us (21%)
  local copies, waits for them, and re-layouts  26.8 us (10%)
  other arithmetic  16.1 us (6%)
  matrix products  14 us (5%)
    all_to_all x7, starting transfers between devices, exchange(): return lax.all_to_all(blocks, axes, split_axis=0, concat_axis=0, tiled=True)  71.3 us
    ppermute x12, starting transfers between devices, from_above(): lax.ppermute(value, axes, [((i + distance) % count, i) for i in range(cou...  43.6 us
    all_to_all x7, waiting for transfers between devices, exchange(): return lax.all_to_all(blocks, axes, split_axis=0, concat_axis=0, tiled=True)  33.3 us
    ppermute x12, waiting for transfers between devices, from_above(): lax.ppermute(value, axes, [((i + distance) % count, i) for i in range(cou...  15.2 us
    ppermute x5, starting transfers between devices, swap_near(): return lax.ppermute(value, 'y_lo', [(0, 1), (1, 0)])  14 us
    ppermute x2, starting transfers between devices, trade_pair(): other = lax.ppermute(sent, axis_name, [(0, 1), (1, 0)])  11.2 us
    ppermute x5, starting transfers between devices, swap_cores(): return lax.ppermute(value, 'core', [(0, 1), (1, 0)])  11.2 us
    ppermute x3, starting transfers between devices, trade_x(): lax.ppermute(turned[step], 'x', [(i, (i + step) % count) for i in range(c...  9.33 us
  transfers between devices with their start and end apart: 34, of which 14 were waited for; matrix products, arithmetic and copies ran while one was open for 15% of the time, Pallas kernels for 0%

profile of v9, /device:TPU:1, one launch (start us, length us, event | category | flops | bytes accessed | tf_op | source)
XLA Modules:
  0.0 277.3 jit_solution(5869888491256693524)
XLA Ops:
  2.0 4.0 %collective-permute-start.1 = (bf16[2,896,256]{2,1,0:T(8,128)(2,1)S(1)}, bf16[2,896,256]{2,1,0:T(8,128)(2,1)S(1)}, u32[]{:S(2)}, u32[]{:S(2)}) collective-permute-start(bf16[2,896,256]{2,1,0:T(8,128)(2,1)S(1)} %pad_maximum_fusion.1), channel_id=1, source_target_pairs={{0,256},{256,0},{1,257},{257,1},{2,258},{258,2},{3,259},{259,3},{4... | collective-permute-start | bytes 2752520 | tf_op jit(solution)/shard_map/ppermute | solution.py:37
  11.4 6.7 %collective-permute-start = (bf16[4,2,12,256]{3,1,2,0:T(2,128)(2,1)S(1)}, bf16[4,2,12,256]{3,1,2,0:T(2,128)(2,1)S(1)}, u32[]{:S(2)}, u32[]{:S(2)}) collective-permute-start(bf16[4,2,12,256]{3,1,2,0:T(2,128)(2,1)S(1)} %bitcast.255), channel_id=1, source_target_pairs={{0,1},{1,0},{2,3},{3,2},{4,5},{5,4},{6,7},{7,6},{8,9},{9,8},{10,11... | collective-permute-start | bytes 147464 | tf_op jit(solution)/shard_map/ppermute | solution.py:72
  18.0 11.1 %all-to-all-start = ((bf16[16,8,2048]{2,1,0:T(8,128)(2,1)}), bf16[16,8,2048]{2,1,0:T(8,128)(2,1)S(1)}, u32[]{:S(2)}, u32[]{:S(2)}) async-start(bf16[16,8,2048]{2,1,0:T(8,128)(2,1)} %reshape.246), calls=%async_computation | async-start | bytes 1048576 | tf_op jit(solution)/shard_map/all_to_all | solution.py:29
  29.7 4.5 %collective-permute-start.2 = (bf16[2,4,12,256]{3,1,2,0:T(4,128)(2,1)S(1)}, bf16[2,4,12,256]{3,1,2,0:T(4,128)(2,1)S(1)}, u32[]{:S(2)}, u32[]{:S(2)}) collective-permute-start(bf16[2,4,12,256]{3,1,2,0:T(4,128)(2,1)S(1)} %bitcast.254), channel_id=1, source_target_pairs={{0,2},{2,0},{1,3},{3,1},{4,6},{6,4},{5,7},{7,5},{8,10},{10,8},{9,1... | collective-permute-start | bytes 147464 | tf_op jit(solution)/shard_map/ppermute | solution.py:72
  36.6 4.4 %collective-permute-start.3 = (bf16[2,2,12,256]{3,1,2,0:T(2,128)(2,1)S(1)}, bf16[2,2,12,256]{3,1,2,0:T(2,128)(2,1)S(1)}, u32[]{:S(2)}, u32[]{:S(2)}) collective-permute-start(bf16[2,2,12,256]{3,1,2,0:T(2,128)(2,1)S(1)} %bitcast.260), channel_id=1, source_target_pairs={{0,12},{4,0},{8,4},{12,8},{1,13},{5,1},{9,5},{13,9},{2,14},{6,2},{... | collective-permute-start | bytes 73736 | tf_op jit(solution)/shard_map/ppermute | solution.py:80
  56.9 12.1 %all-to-all-start.1 = ((bf16[16,64,2048]{2,1,0:T(8,128)(2,1)}), bf16[16,64,2048]{2,1,0:T(8,128)(2,1)}, u32[]{:S(2)}, u32[]{:S(2)}) async-start(bf16[16,64,2048]{2,1,0:T(8,128)(2,1)} %bitcast.215), calls=%async_computation.1 | async-start | bytes 8388608 | tf_op jit(solution)/shard_map/all_to_all | solution.py:29
  71.4 4.3 %collective-permute-start.8 = (bf16[64,256]{1,0:T(8,128)(2,1)S(1)}, bf16[64,256]{1,0:T(8,128)(2,1)S(1)}, u32[]{:S(2)}, u32[]{:S(2)}) collective-permute-start(bf16[64,256]{1,0:T(8,128)(2,1)S(1)} %multiply_convert_fusion), channel_id=1, source_target_pairs={{192,0},{208,16},{224,32},{240,48},{0,64},{16,80},{32,96},{48,112}... | collective-permute-start | bytes 98312 | tf_op jit(solution)/shard_map/ppermute | solution.py:42
  75.7 8.7 %collective-permute-start.7 = (bf16[64,256]{1,0:T(8,128)(2,1)S(1)}, bf16[64,256]{1,0:T(8,128)(2,1)S(1)}, u32[]{:S(2)}, u32[]{:S(2)}) collective-permute-start(bf16[64,256]{1,0:T(8,128)(2,1)S(1)} %multiply_convert_fusion), channel_id=1, source_target_pairs={{128,0},{144,16},{160,32},{176,48},{192,64},{208,80},{224,96},{240... | collective-permute-start | bytes 98312 | tf_op jit(solution)/shard_map/ppermute | solution.py:42
  84.3 5.2 %collective-permute-start.6 = (bf16[64,256]{1,0:T(8,128)(2,1)S(1)}, bf16[64,256]{1,0:T(8,128)(2,1)S(1)}, u32[]{:S(2)}, u32[]{:S(2)}) collective-permute-start(bf16[64,256]{1,0:T(8,128)(2,1)S(1)} %multiply_convert_fusion), channel_id=1, source_target_pairs={{64,0},{80,16},{96,32},{112,48},{128,64},{144,80},{160,96},{176,11... | collective-permute-start | bytes 98312 | tf_op jit(solution)/shard_map/ppermute | solution.py:42
  92.2 3.1 %collective-permute-start.13 = (bf16[256,256]{1,0:T(8,128)(2,1)S(1)}, bf16[256,256]{1,0:T(8,128)(2,1)S(1)}, u32[]{:S(2)}, u32[]{:S(2)}) collective-permute-start(bf16[256,256]{1,0:T(8,128)(2,1)S(1)} %copy-done.16), channel_id=1, source_target_pairs={{32,0},{48,16},{0,32},{16,48},{33,1},{49,17},{1,33},{17,49},{34,2}... | collective-permute-start | bytes 393224 | tf_op jit(solution)/shard_map/ppermute | solution.py:42
  95.3 3.5 %collective-permute-start.12 = (bf16[256,256]{1,0:T(8,128)(2,1)S(1)}, bf16[256,256]{1,0:T(8,128)(2,1)S(1)}, u32[]{:S(2)}, u32[]{:S(2)}) collective-permute-start(bf16[256,256]{1,0:T(8,128)(2,1)S(1)} %copy-done.16), channel_id=1, source_target_pairs={{16,0},{32,16},{48,32},{0,48},{17,1},{33,17},{49,33},{1,49},{18,2}... | collective-permute-start | bytes 393224 | tf_op jit(solution)/shard_map/ppermute | solution.py:42
  100.9 2.7 collective-permute-start.10
  109.1 3.0 %collective-permute-done.10 = bf16[4,64,256]{2,1,0:T(8,128)(2,1)S(1)} collective-permute-done((bf16[4,64,256]{2,1,0:T(8,128)(2,1)S(1)}, bf16[4,64,256]{2,1,0:T(8,128)(2,1)S(1)}, u32[]{:S(2)}, u32[]{:S(2)}) %collective-permute-start.10) | collective-permute-done | bytes 131104 | tf_op jit(solution)/shard_map/ppermute | solution.py:42
  112.1 2.8 %collective-permute-done.9 = bf16[4,64,256]{2,1,0:T(8,128)(2,1)S(1)} collective-permute-done((bf16[4,64,256]{2,1,0:T(8,128)(2,1)S(1)}, bf16[4,64,256]{2,1,0:T(8,128)(2,1)S(1)}, u32[]{:S(2)}, u32[]{:S(2)}) %collective-permute-start.9) | collective-permute-done | bytes 131104 | tf_op jit(solution)/shard_map/ppermute | solution.py:42
  115.2 6.5 %all-to-all-done.1 = bf16[16,64,2048]{2,1,0:T(8,128)(2,1)} async-done(((bf16[16,64,2048]{2,1,0:T(8,128)(2,1)}), bf16[16,64,2048]{2,1,0:T(8,128)(2,1)}, u32[]{:S(2)}, u32[]{:S(2)}) %all-to-all-start.1) | async-done | bytes 4194336 | tf_op jit(solution)/shard_map/all_to_all | solution.py:29
  121.7 3.7 %fusion.49 = f32[1024,256]{1,0:T(8,128)S(1)} fusion(bf16[1024,2048]{1,0:T(8,128)(2,1)} %bitcast.31, bf16[2048,256]{1,0:T(8,128)(2,1)} %collective-permute-done.15), kind=kOutput, calls=%fused_computation.155 | convolution fusion | flops 1073741824 | bytes 6291456 | tf_op jit(solution)/shard_map/dot_general | solution.py:202
  127.7 3.4 %fusion.48 = f32[1024,256]{1,0:T(8,128)S(1)} fusion(bf16[1024,2048]{1,0:T(8,128)(2,1)} %bitcast.31, bf16[2048,256]{1,0:T(8,128)(2,1)S(1)} %bitcast.233), kind=kOutput, calls=%fused_computation.154 | convolution fusion | flops 1073741824 | bytes 6291456 | tf_op jit(solution)/shard_map/dot_general | solution.py:203
  132.5 8.4 %all-to-all-start.2 = ((bf16[16,64,256]{2,1,0:T(8,128)(2,1)}), bf16[16,64,256]{2,1,0:T(8,128)(2,1)S(1)}, u32[]{:S(2)}, u32[]{:S(2)}) async-start(bf16[16,64,256]{2,1,0:T(8,128)(2,1)} %copy.269), calls=%async_computation.2 | async-start | bytes 1048576 | tf_op jit(solution)/shard_map/all_to_all | solution.py:29
  141.4 2.7 collective-permute-start.17
  149.7 4.8 %fusion.6 = f32[2048,512]{1,0:T(8,128)S(1)} fusion(bf16[1024,2048]{1,0:T(8,128)(2,1)} %bitcast.31, bf16[1024,256]{1,0:T(8,128)(2,1)} %collective-permute-done.17, bf16[1024,256]{1,0:T(8,128)(2,1)S(1)} %reshape.258), kind=kOutput, calls=%fused_computation.12 | convolution fusion | flops 2149580800 | bytes 9437184 | tf_op jit(solution)/shard_map/dot_general | solution.py:25
  157.7 4.6 %collective-permute-done.19 = bf16[4,256,256]{2,1,0:T(8,128)(2,1)S(1)} collective-permute-done((bf16[4,256,256]{2,1,0:T(8,128)(2,1)S(1)}, bf16[4,256,256]{2,1,0:T(8,128)(2,1)S(1)}, u32[]{:S(2)}, u32[]{:S(2)}) %collective-permute-start.19) | collective-permute-done | bytes 524320 | tf_op jit(solution)/shard_map/ppermute | solution.py:37
  165.7 19.9 %all-to-all-start.3 = ((f32[16,1,320]{2,1,0:T(1,128)}), f32[16,1,320]{2,1,0:T(1,128)S(1)}, u32[]{:S(2)}, u32[]{:S(2)}) async-start(f32[16,1,320]{2,1,0:T(1,128)} %broadcast_in_dim.10), calls=%async_computation.3 | async-start | bytes 49152 | tf_op jit(solution)/shard_map/all_to_all | solution.py:29
  188.0 4.9 %all-to-all-done.3 = f32[16,1,320]{2,1,0:T(1,128)S(1)} async-done(((f32[16,1,320]{2,1,0:T(1,128)}), f32[16,1,320]{2,1,0:T(1,128)S(1)}, u32[]{:S(2)}, u32[]{:S(2)}) %all-to-all-start.3) | async-done | bytes 20512 | tf_op jit(solution)/shard_map/all_to_all | solution.py:29
  193.9 6.1 %all-to-all-start.4 = ((bf16[4,112,256]{2,1,0:T(8,128)(2,1)}), bf16[4,112,256]{2,1,0:T(8,128)(2,1)S(1)}, u32[]{:S(2)}, u32[]{:S(2)}) async-start(bf16[4,112,256]{2,1,0:T(8,128)(2,1)} %broadcast_in_dim.11), calls=%async_computation.4 | async-start | bytes 458752 | tf_op jit(solution)/shard_map/all_to_all | solution.py:29
  200.2 13.3 %all-to-all-done.4 = bf16[4,112,256]{2,1,0:T(8,128)(2,1)S(1)} async-done(((bf16[4,112,256]{2,1,0:T(8,128)(2,1)}), bf16[4,112,256]{2,1,0:T(8,128)(2,1)S(1)}, u32[]{:S(2)}, u32[]{:S(2)}) %all-to-all-start.4) | async-done | bytes 229408 | tf_op jit(solution)/shard_map/all_to_all | solution.py:29
  217.5 9.5 %all-to-all-start.5 = ((bf16[16,16,2048]{2,1,0:T(8,128)(2,1)}), bf16[16,16,2048]{2,1,0:T(8,128)(2,1)S(1)}, u32[]{:S(2)}, u32[]{:S(2)}) async-start(bf16[16,16,2048]{2,1,0:T(8,128)(2,1)} %bitcast.70), calls=%async_computation.5 | async-start | bytes 2097152 | tf_op jit(solution)/shard_map/all_to_all | solution.py:29
  227.8 3.3 %collective-permute-start.22 = (bf16[304,256]{1,0:T(8,128)(2,1)}, bf16[304,256]{1,0:T(8,128)(2,1)}, u32[]{:S(2)}, u32[]{:S(2)}) collective-permute-start(bf16[304,256]{1,0:T(8,128)(2,1)} %pad_maximum_fusion.5), channel_id=1, source_target_pairs={{16,0},{32,16},{48,32},{0,48},{17,1},{33,17},{49,33},{1,49},{18,2}... | collective-permute-start | bytes 466952 | tf_op jit(solution)/shard_map/ppermute | solution.py:42
  239.7 3.8 %collective-permute-start.23 = (bf16[304,256]{1,0:T(8,128)(2,1)}, bf16[304,256]{1,0:T(8,128)(2,1)S(1)}, u32[]{:S(2)}, u32[]{:S(2)}) collective-permute-start(bf16[304,256]{1,0:T(8,128)(2,1)} %pad_maximum_fusion.5), channel_id=1, source_target_pairs={{32,0},{48,16},{0,32},{16,48},{33,1},{49,17},{1,33},{17,49},{34,2}... | collective-permute-start | bytes 466952 | tf_op jit(solution)/shard_map/ppermute | solution.py:42
  247.1 8.1 %collective-permute-done.23 = bf16[304,256]{1,0:T(8,128)(2,1)S(1)} collective-permute-done((bf16[304,256]{1,0:T(8,128)(2,1)}, bf16[304,256]{1,0:T(8,128)(2,1)S(1)}, u32[]{:S(2)}, u32[]{:S(2)}) %collective-permute-start.23) | collective-permute-done | bytes 155680 | tf_op jit(solution)/shard_map/ppermute | solution.py:42
  259.7 4.1 %all-to-all-start.6 = ((bf16[4,4,2048]{2,1,0:T(4,128)(2,1)}), bf16[4,4,2048]{2,1,0:T(4,128)(2,1)S(1)}, u32[]{:S(2)}, u32[]{:S(2)}) async-start(bf16[4,4,2048]{2,1,0:T(4,128)(2,1)} %reshape.265), calls=%async_computation.6 | async-start | bytes 131072 | tf_op jit(solution)/shard_map/all_to_all | solution.py:29
  265.3 3.0 %collective-permute-start.26 = (f32[2,128,256]{2,1,0:T(8,128)S(1)}, f32[2,128,256]{2,1,0:T(8,128)S(1)}, u32[]{:S(2)}, u32[]{:S(2)}) collective-permute-start(f32[2,128,256]{2,1,0:T(8,128)S(1)} %fusion.26), channel_id=1, source_target_pairs={{0,256},{256,0},{1,257},{257,1},{2,258},{258,2},{3,259},{259,3},{4... | collective-permute-start | bytes 786440 | tf_op jit(solution)/shard_map/ppermute | solution.py:37
  268.9 6.8 %all-to-all-done.6 = bf16[4,4,2048]{2,1,0:T(4,128)(2,1)S(1)} async-done(((bf16[4,4,2048]{2,1,0:T(4,128)(2,1)}), bf16[4,4,2048]{2,1,0:T(4,128)(2,1)S(1)}, u32[]{:S(2)}, u32[]{:S(2)}) %all-to-all-start.6) | async-done | bytes 65568 | tf_op jit(solution)/shard_map/all_to_all | solution.py:29
  (217 shorter events, 82.2 us)
Async XLA Ops:
  2.0 27.5 %collective-permute-start.1 = (bf16[2,896,256]{2,1,0:T(8,128)(2,1)S(1)}, bf16[2,896,256]{2,1,0:T(8,128)(2,1)S(1)}, u32[]{:S(2)}, u32[]{:S(2)}) collective-permute-start(bf16[2,896,256]{2,1,0:T(8,128)(2,1)S(1)} %pad_maximum_fusion.1), channel_id=1, source_target_pairs={{0,256},{256,0},{1,257},{257,1},{2,258},{258,2},{3,259},{259,3},{4... | collective-permute-start | bytes 2752520 | tf_op jit(solution)/shard_map/ppermute | solution.py:37
  11.4 17.8 %collective-permute-start = (bf16[4,2,12,256]{3,1,2,0:T(2,128)(2,1)S(1)}, bf16[4,2,12,256]{3,1,2,0:T(2,128)(2,1)S(1)}, u32[]{:S(2)}, u32[]{:S(2)}) collective-permute-start(bf16[4,2,12,256]{3,1,2,0:T(2,128)(2,1)S(1)} %bitcast.255), channel_id=1, source_target_pairs={{0,1},{1,0},{2,3},{3,2},{4,5},{5,4},{6,7},{7,6},{8,9},{9,8},{10,11... | collective-permute-start | bytes 147464 | tf_op jit(solution)/shard_map/ppermute | solution.py:72
  18.0 35.3 %all-to-all-start = ((bf16[16,8,2048]{2,1,0:T(8,128)(2,1)}), bf16[16,8,2048]{2,1,0:T(8,128)(2,1)S(1)}, u32[]{:S(2)}, u32[]{:S(2)}) async-start(bf16[16,8,2048]{2,1,0:T(8,128)(2,1)} %reshape.246), calls=%async_computation | async-start | bytes 1048576 | tf_op jit(solution)/shard_map/all_to_all | solution.py:29
  36.6 10.2 %collective-permute-start.3 = (bf16[2,2,12,256]{3,1,2,0:T(2,128)(2,1)S(1)}, bf16[2,2,12,256]{3,1,2,0:T(2,128)(2,1)S(1)}, u32[]{:S(2)}, u32[]{:S(2)}) collective-permute-start(bf16[2,2,12,256]{3,1,2,0:T(2,128)(2,1)S(1)} %bitcast.260), channel_id=1, source_target_pairs={{0,12},{4,0},{8,4},{12,8},{1,13},{5,1},{9,5},{13,9},{2,14},{6,2},{... | collective-permute-start | bytes 73736 | tf_op jit(solution)/shard_map/ppermute | solution.py:80
  41.0 6.4 %collective-permute-start.4 = (bf16[2,2,12,256]{3,1,2,0:T(2,128)(2,1)S(1)}, bf16[2,2,12,256]{3,1,2,0:T(2,128)(2,1)S(1)}, u32[]{:S(2)}, u32[]{:S(2)}) collective-permute-start(bf16[2,2,12,256]{3,1,2,0:T(2,128)(2,1)S(1)} %bitcast.262), channel_id=1, source_target_pairs={{0,8},{4,12},{8,0},{12,4},{1,9},{5,13},{9,1},{13,5},{2,10},{6,14},... | collective-permute-start | bytes 73736 | tf_op jit(solution)/shard_map/ppermute | solution.py:80
  43.5 6.3 %collective-permute-start.5 = (bf16[2,2,12,256]{3,1,2,0:T(2,128)(2,1)S(1)}, bf16[2,2,12,256]{3,1,2,0:T(2,128)(2,1)S(1)}, u32[]{:S(2)}, u32[]{:S(2)}) collective-permute-start(bf16[2,2,12,256]{3,1,2,0:T(2,128)(2,1)S(1)} %bitcast.264), channel_id=1, source_target_pairs={{0,4},{4,8},{8,12},{12,0},{1,5},{5,9},{9,13},{13,1},{2,6},{6,10},{... | collective-permute-start | bytes 73736 | tf_op jit(solution)/shard_map/ppermute | solution.py:80
  56.9 64.8 %all-to-all-start.1 = ((bf16[16,64,2048]{2,1,0:T(8,128)(2,1)}), bf16[16,64,2048]{2,1,0:T(8,128)(2,1)}, u32[]{:S(2)}, u32[]{:S(2)}) async-start(bf16[16,64,2048]{2,1,0:T(8,128)(2,1)} %bitcast.215), calls=%async_computation.1 | async-start | bytes 8388608 | tf_op jit(solution)/shard_map/all_to_all | solution.py:29
  69.3 52.5 %collective-permute-start.15 = (bf16[2048,256]{1,0:T(8,128)(2,1)S(1)}, bf16[2048,256]{1,0:T(8,128)(2,1)}, u32[]{:S(2)}, u32[]{:S(2)}) collective-permute-start(bf16[2048,256]{1,0:T(8,128)(2,1)S(1)} %bitcast.232), channel_id=1, source_target_pairs={{0,1},{1,0},{2,3},{3,2},{4,5},{5,4},{6,7},{7,6},{8,9},{9,8},{10,11... | collective-permute-start | bytes 3145736 | tf_op jit(solution)/shard_map/ppermute | solution.py:33
  71.4 20.8 %collective-permute-start.8 = (bf16[64,256]{1,0:T(8,128)(2,1)S(1)}, bf16[64,256]{1,0:T(8,128)(2,1)S(1)}, u32[]{:S(2)}, u32[]{:S(2)}) collective-permute-start(bf16[64,256]{1,0:T(8,128)(2,1)S(1)} %multiply_convert_fusion), channel_id=1, source_target_pairs={{192,0},{208,16},{224,32},{240,48},{0,64},{16,80},{32,96},{48,112}... | collective-permute-start | bytes 98312 | tf_op jit(solution)/shard_map/ppermute | solution.py:42
  75.7 19.7 %collective-permute-start.7 = (bf16[64,256]{1,0:T(8,128)(2,1)S(1)}, bf16[64,256]{1,0:T(8,128)(2,1)S(1)}, u32[]{:S(2)}, u32[]{:S(2)}) collective-permute-start(bf16[64,256]{1,0:T(8,128)(2,1)S(1)} %multiply_convert_fusion), channel_id=1, source_target_pairs={{128,0},{144,16},{160,32},{176,48},{192,64},{208,80},{224,96},{240... | collective-permute-start | bytes 98312 | tf_op jit(solution)/shard_map/ppermute | solution.py:42
  84.3 14.5 %collective-permute-start.6 = (bf16[64,256]{1,0:T(8,128)(2,1)S(1)}, bf16[64,256]{1,0:T(8,128)(2,1)S(1)}, u32[]{:S(2)}, u32[]{:S(2)}) collective-permute-start(bf16[64,256]{1,0:T(8,128)(2,1)S(1)} %multiply_convert_fusion), channel_id=1, source_target_pairs={{64,0},{80,16},{96,32},{112,48},{128,64},{144,80},{160,96},{176,11... | collective-permute-start | bytes 98312 | tf_op jit(solution)/shard_map/ppermute | solution.py:42
  89.5 11.3 %collective-permute-start.14 = (bf16[256,256]{1,0:T(8,128)(2,1)S(1)}, bf16[256,256]{1,0:T(8,128)(2,1)S(1)}, u32[]{:S(2)}, u32[]{:S(2)}) collective-permute-start(bf16[256,256]{1,0:T(8,128)(2,1)S(1)} %copy-done.16), channel_id=1, source_target_pairs={{48,0},{0,16},{16,32},{32,48},{49,1},{1,17},{17,33},{33,49},{50,2}... | collective-permute-start | bytes 393224 | tf_op jit(solution)/shard_map/ppermute | solution.py:42
  92.2 12.7 %collective-permute-start.13 = (bf16[256,256]{1,0:T(8,128)(2,1)S(1)}, bf16[256,256]{1,0:T(8,128)(2,1)S(1)}, u32[]{:S(2)}, u32[]{:S(2)}) collective-permute-start(bf16[256,256]{1,0:T(8,128)(2,1)S(1)} %copy-done.16), channel_id=1, source_target_pairs={{32,0},{48,16},{0,32},{16,48},{33,1},{49,17},{1,33},{17,49},{34,2}... | collective-permute-start | bytes 393224 | tf_op jit(solution)/shard_map/ppermute | solution.py:42
  95.3 12.1 %collective-permute-start.12 = (bf16[256,256]{1,0:T(8,128)(2,1)S(1)}, bf16[256,256]{1,0:T(8,128)(2,1)S(1)}, u32[]{:S(2)}, u32[]{:S(2)}) collective-permute-start(bf16[256,256]{1,0:T(8,128)(2,1)S(1)} %copy-done.16), channel_id=1, source_target_pairs={{16,0},{32,16},{48,32},{0,48},{17,1},{33,17},{49,33},{1,49},{18,2}... | collective-permute-start | bytes 393224 | tf_op jit(solution)/shard_map/ppermute | solution.py:42
  98.9 10.1 %collective-permute-start.11 = (bf16[4,64,256]{2,1,0:T(8,128)(2,1)S(1)}, bf16[4,64,256]{2,1,0:T(8,128)(2,1)S(1)}, u32[]{:S(2)}, u32[]{:S(2)}) collective-permute-start(bf16[4,64,256]{2,1,0:T(8,128)(2,1)S(1)} %get-tuple-element.75), channel_id=1, source_target_pairs={{240,0},{0,16},{16,32},{32,48},{48,64},{64,80},{80,96},{96,112},{1... | collective-permute-start | bytes 393224 | tf_op jit(solution)/shard_map/ppermute | solution.py:42
  100.9 11.2 %collective-permute-start.10 = (bf16[4,64,256]{2,1,0:T(8,128)(2,1)S(1)}, bf16[4,64,256]{2,1,0:T(8,128)(2,1)S(1)}, u32[]{:S(2)}, u32[]{:S(2)}) collective-permute-start(bf16[4,64,256]{2,1,0:T(8,128)(2,1)S(1)} %get-tuple-element.75), channel_id=1, source_target_pairs={{32,0},{48,16},{64,32},{80,48},{96,64},{112,80},{128,96},{144,112}... | collective-permute-start | bytes 393224 | tf_op jit(solution)/shard_map/ppermute | solution.py:42
  104.9 10.0 %collective-permute-start.9 = (bf16[4,64,256]{2,1,0:T(8,128)(2,1)S(1)}, bf16[4,64,256]{2,1,0:T(8,128)(2,1)S(1)}, u32[]{:S(2)}, u32[]{:S(2)}) collective-permute-start(bf16[4,64,256]{2,1,0:T(8,128)(2,1)S(1)} %get-tuple-element.75), channel_id=1, source_target_pairs={{16,0},{32,16},{48,32},{64,48},{80,64},{96,80},{112,96},{128,112},... | collective-permute-start | bytes 393224 | tf_op jit(solution)/shard_map/ppermute | solution.py:42
  132.5 31.3 %all-to-all-start.2 = ((bf16[16,64,256]{2,1,0:T(8,128)(2,1)}), bf16[16,64,256]{2,1,0:T(8,128)(2,1)S(1)}, u32[]{:S(2)}, u32[]{:S(2)}) async-start(bf16[16,64,256]{2,1,0:T(8,128)(2,1)} %copy.269), calls=%async_computation.2 | async-start | bytes 1048576 | tf_op jit(solution)/shard_map/all_to_all | solution.py:29
  141.4 8.3 %collective-permute-start.17 = (bf16[1024,256]{1,0:T(8,128)(2,1)S(1)}, bf16[1024,256]{1,0:T(8,128)(2,1)}, u32[]{:S(2)}, u32[]{:S(2)}) collective-permute-start(bf16[1024,256]{1,0:T(8,128)(2,1)S(1)} %reshape.258), channel_id=1, source_target_pairs={{0,1},{1,0},{2,3},{3,2},{4,5},{5,4},{6,7},{7,6},{8,9},{9,8},{10,11... | collective-permute-start | bytes 1572872 | tf_op jit(solution)/shard_map/ppermute | solution.py:33
  145.4 12.2 %collective-permute-start.18 = (bf16[1024,256]{1,0:T(8,128)(2,1)S(1)}, bf16[1024,256]{1,0:T(8,128)(2,1)S(1)}, u32[]{:S(2)}, u32[]{:S(2)}) collective-permute-start(bf16[1024,256]{1,0:T(8,128)(2,1)S(1)} %pad_maximum_fusion.4), channel_id=1, source_target_pairs={{0,1},{1,0},{2,3},{3,2},{4,5},{5,4},{6,7},{7,6},{8,9},{9,8},{10,11... | collective-permute-start | bytes 1572872 | tf_op jit(solution)/shard_map/ppermute | solution.py:33
  147.4 14.9 %collective-permute-start.19 = (bf16[4,256,256]{2,1,0:T(8,128)(2,1)S(1)}, bf16[4,256,256]{2,1,0:T(8,128)(2,1)S(1)}, u32[]{:S(2)}, u32[]{:S(2)}) collective-permute-start(bf16[4,256,256]{2,1,0:T(8,128)(2,1)S(1)} %pad_maximum_fusion.3), channel_id=1, source_target_pairs={{0,256},{256,0},{1,257},{257,1},{2,258},{258,2},{3,259},{259,3},{4... | collective-permute-start | bytes 1572872 | tf_op jit(solution)/shard_map/ppermute | solution.py:37
  165.7 27.2 %all-to-all-start.3 = ((f32[16,1,320]{2,1,0:T(1,128)}), f32[16,1,320]{2,1,0:T(1,128)S(1)}, u32[]{:S(2)}, u32[]{:S(2)}) async-start(f32[16,1,320]{2,1,0:T(1,128)} %broadcast_in_dim.10), calls=%async_computation.3 | async-start | bytes 49152 | tf_op jit(solution)/shard_map/all_to_all | solution.py:29
  185.7 27.8 %collective-permute-start.20 = (bf16[896,512]{1,0:T(8,128)(2,1)}, bf16[896,512]{1,0:T(8,128)(2,1)}, u32[]{:S(2)}, u32[]{:S(2)}) collective-permute-start(bf16[896,512]{1,0:T(8,128)(2,1)} %fusion.10), channel_id=1, source_target_pairs={{0,256},{256,0},{1,257},{257,1},{2,258},{258,2},{3,259},{259,3},{4... | collective-permute-start | bytes 2752520 | tf_op jit(solution)/shard_map/ppermute | solution.py:37
  193.9 19.6 %all-to-all-start.4 = ((bf16[4,112,256]{2,1,0:T(8,128)(2,1)}), bf16[4,112,256]{2,1,0:T(8,128)(2,1)S(1)}, u32[]{:S(2)}, u32[]{:S(2)}) async-start(bf16[4,112,256]{2,1,0:T(8,128)(2,1)} %broadcast_in_dim.11), calls=%async_computation.4 | async-start | bytes 458752 | tf_op jit(solution)/shard_map/all_to_all | solution.py:29
  213.6 13.5 %collective-permute-start.21 = (f32[16,256]{1,0:T(8,128)S(1)}, f32[16,256]{1,0:T(8,128)S(1)}, u32[]{:S(2)}, u32[]{:S(2)}) collective-permute-start(f32[16,256]{1,0:T(8,128)S(1)} %slice_add_fusion.2), channel_id=1, source_target_pairs={{0,256},{256,0},{1,257},{257,1},{2,258},{258,2},{3,259},{259,3},{4... | collective-permute-start | bytes 49160 | tf_op jit(solution)/shard_map/ppermute | solution.py:37
  217.5 41.3 %all-to-all-start.5 = ((bf16[16,16,2048]{2,1,0:T(8,128)(2,1)}), bf16[16,16,2048]{2,1,0:T(8,128)(2,1)S(1)}, u32[]{:S(2)}, u32[]{:S(2)}) async-start(bf16[16,16,2048]{2,1,0:T(8,128)(2,1)} %bitcast.70), calls=%async_computation.5 | async-start | bytes 2097152 | tf_op jit(solution)/shard_map/all_to_all | solution.py:29
  227.8 18.4 %collective-permute-start.22 = (bf16[304,256]{1,0:T(8,128)(2,1)}, bf16[304,256]{1,0:T(8,128)(2,1)}, u32[]{:S(2)}, u32[]{:S(2)}) collective-permute-start(bf16[304,256]{1,0:T(8,128)(2,1)} %pad_maximum_fusion.5), channel_id=1, source_target_pairs={{16,0},{32,16},{48,32},{0,48},{17,1},{33,17},{49,33},{1,49},{18,2}... | collective-permute-start | bytes 466952 | tf_op jit(solution)/shard_map/ppermute | solution.py:42
  234.2 22.1 %collective-permute-start.25 = (f32[896,256]{1,0:T(8,128)}, f32[896,256]{1,0:T(8,128)}, u32[]{:S(2)}, u32[]{:S(2)}) collective-permute-start(f32[896,256]{1,0:T(8,128)} %slice.181), channel_id=1, source_target_pairs={{0,1},{1,0},{2,3},{3,2},{4,5},{5,4},{6,7},{7,6},{8,9},{9,8},{10,11... | collective-permute-start | bytes 2752520 | tf_op jit(solution)/shard_map/ppermute | solution.py:33
  239.7 15.4 %collective-permute-start.23 = (bf16[304,256]{1,0:T(8,128)(2,1)}, bf16[304,256]{1,0:T(8,128)(2,1)S(1)}, u32[]{:S(2)}, u32[]{:S(2)}) collective-permute-start(bf16[304,256]{1,0:T(8,128)(2,1)} %pad_maximum_fusion.5), channel_id=1, source_target_pairs={{32,0},{48,16},{0,32},{16,48},{33,1},{49,17},{1,33},{17,49},{34,2}... | collective-permute-start | bytes 466952 | tf_op jit(solution)/shard_map/ppermute | solution.py:42
  243.5 11.7 %collective-permute-start.24 = (bf16[304,256]{1,0:T(8,128)(2,1)}, bf16[304,256]{1,0:T(8,128)(2,1)S(1)}, u32[]{:S(2)}, u32[]{:S(2)}) collective-permute-start(bf16[304,256]{1,0:T(8,128)(2,1)} %pad_maximum_fusion.5), channel_id=1, source_target_pairs={{48,0},{0,16},{16,32},{32,48},{49,1},{1,17},{17,33},{33,49},{50,2}... | collective-permute-start | bytes 466952 | tf_op jit(solution)/shard_map/ppermute | solution.py:42
  259.7 15.9 %all-to-all-start.6 = ((bf16[4,4,2048]{2,1,0:T(4,128)(2,1)}), bf16[4,4,2048]{2,1,0:T(4,128)(2,1)S(1)}, u32[]{:S(2)}, u32[]{:S(2)}) async-start(bf16[4,4,2048]{2,1,0:T(4,128)(2,1)} %reshape.265), calls=%async_computation.6 | async-start | bytes 131072 | tf_op jit(solution)/shard_map/all_to_all | solution.py:29
  265.3 11.3 %collective-permute-start.26 = (f32[2,128,256]{2,1,0:T(8,128)S(1)}, f32[2,128,256]{2,1,0:T(8,128)S(1)}, u32[]{:S(2)}, u32[]{:S(2)}) collective-permute-start(f32[2,128,256]{2,1,0:T(8,128)S(1)} %fusion.26), channel_id=1, source_target_pairs={{0,256},{256,0},{1,257},{257,1},{2,258},{258,2},{3,259},{259,3},{4... | collective-permute-start | bytes 786440 | tf_op jit(solution)/shard_map/ppermute | solution.py:37
  (21 other events, 228.7 us)

commit v10 on v9

--- a/solution.py
+++ b/solution.py
@@ -90,6 +90,11 @@
     middle = rest.astype(narrow)
     low = (rest - middle.astype(wide)).astype(narrow)
     return (high, middle, low)
+
+
+def split_two(value):
+    high = value.astype(narrow)
+    return (high, (value - high.astype(wide)).astype(narrow))
 
 
 def shards(
@@ -244,8 +249,8 @@
     gain_part = row_parts[:, block_rows:]
     hidden_grad = (resid_block + scale_block * (lifted - normed * inner_mean)).astype(narrow)
 
-    grad_sent = jnp.concatenate([hidden_grad, *split_three(gain_part)])
-    sent_rows = block_rows + 3 * dp_count
+    grad_sent = jnp.concatenate([hidden_grad, *split_two(gain_part)])
+    sent_rows = block_rows + 2 * dp_count
     high_count = z_count // quarter
     grad_high = exchange(
         jnp.broadcast_to(grad_sent[None], (high_count, sent_rows, features)), "z_hi"
@@ -253,8 +258,18 @@
 
     join_pair = by_near(join_quad, near_quad).reshape(2 * quarter * inputs, features)
     joined_half, joined_other = joined_half.T, joined_other.T
-    grad_high, unit_near, join_pair, joined_half, joined_other = lax.optimization_barrier(
-        (grad_high, unit_near, join_pair, joined_half, joined_other)
+    unit_grad = unit_kept + unit_near.astype(wide)
+    grad_high, own_grad, other_sent, join_pair, joined_half, joined_other = (
+        lax.optimization_barrier(
+            (
+                grad_high,
+                unit_grad[:, :features],
+                unit_grad[:, features:],
+                join_pair,
+                joined_half,
+                joined_other,
+            )
+        )
     )
 
     grad_rows = (
@@ -269,17 +284,17 @@
     joined_blocks = exchange(
         joined_part.reshape(dp_count, high_count * row_count, 2 * quarter * inputs), dp_axes
     )
-    unit_grad = unit_kept + unit_near.astype(wide)
-    other_grad = swap_cores(unit_grad[:, features:])
+    grad_high, other_grad = lax.optimization_barrier((grad_high, swap_cores(other_sent)))
+    gate_weight_grad = jnp.where(on_first, own_grad, other_grad)
+    up_weight_grad = jnp.where(on_first, other_grad, own_grad)
 
     def sum_parts(blocks):
-        parts = jnp.sum(blocks.astype(wide).reshape(-1, 3, dp_count, features), axis=0)
-        return (parts[0] + parts[1]) + parts[2]
+        parts = jnp.sum(blocks.astype(wide).reshape(-1, 2, dp_count, features), axis=0)
+        return parts[0] + parts[1]
 
     gain_high = sum_parts(grad_high[:, block_rows:])
-    gain_high = gain_high + swap_near(gain_high)
     grad_quad = jnp.concatenate(
-        [grad_high[:, :block_rows].reshape(-1, features), *split_three(gain_high)]
+        [grad_high[:, :block_rows].reshape(-1, features), *split_two(gain_high)]
     )
     grad_z = from_first(gather_ring(grad_quad, "z_lo"), "z_lo")
     grad_z, joined_blocks = lax.optimization_barrier((grad_z, joined_blocks))
@@ -294,17 +309,14 @@
     )
 
     high_rows = high_count * block_rows
-    gain_grad = sum_parts(grad_z[:, high_rows:]).reshape(width)
+    gain_sum = sum_parts(grad_z[:, high_rows:])
+    gain_grad = (gain_sum + swap_near(gain_sum)).reshape(width)
     grad_all = (
         grad_z[:, :high_rows]
         .reshape(quarter, high_count, dp_count, row_count, features)
         .transpose(2, 1, 0, 3, 4)
         .reshape(tokens, features)
     )
-
-    own_grad = unit_grad[:, :features]
-    gate_weight_grad = jnp.where(on_first, own_grad, other_grad)
-    up_weight_grad = jnp.where(on_first, other_grad, own_grad)
 
     def add_near(sums):
         kept = lax.dynamic_index_in_dim(sums, here, 0, keepdims=False)

time: 280 us -> 268 us (0.957)
  waiting for transfers between devices: 57.8 us -> 50.9 us
    all_to_all x7, waiting for transfers between devices: 33.3 us -> 18.6 us  [exchange(): return lax.all_to_all(blocks, axes, split_axis=0, concat_axis=0, tiled=True)]
    ppermute x5, waiting for transfers between devices: 4.59 us -> 14.2 us  [swap_near(): return lax.ppermute(value, 'y_lo', [(0, 1), (1, 0)])]
    all_to_all x7, starting transfers between devices: 71.3 us -> 66.1 us  [exchange(): return lax.all_to_all(blocks, axes, split_axis=0, concat_axis=0, tiled=True)]
    ppermute x5, starting transfers between devices: 11.2 us -> 16.2 us  [swap_cores(): return lax.ppermute(value, 'core', [(0, 1), (1, 0)])]
  transfers between devices with their start and end apart: 34 -> 34, of which waited for: 14 -> 14; matrix products, arithmetic and copies ran while one was open for 15% -> 14% of each run, Pallas kernels for 0% -> 0%
where the time goes in v10:
time: 268 us; the launch traced here: 266 us
  starting transfers between devices  160 us (60%)
  waiting for transfers between devices  50.9 us (19%)
  local copies, waits for them, and re-layouts  25.1 us (9%)
  other arithmetic  14.2 us (5%)
  matrix products  14.2 us (5%)
    all_to_all x7, starting transfers between devices, exchange(): return lax.all_to_all(blocks, axes, split_axis=0, concat_axis=0, tiled=True)  66.1 us
    ppermute x12, starting transfers between devices, from_above(): lax.ppermute(value, axes, [((i + distance) % count, i) for i in range(cou...  43.2 us
    all_to_all x7, waiting for transfers between devices, exchange(): return lax.all_to_all(blocks, axes, split_axis=0, concat_axis=0, tiled=True)  18.6 us
    ppermute x5, starting transfers between devices, swap_cores(): return lax.ppermute(value, 'core', [(0, 1), (1, 0)])  16.2 us
    ppermute x5, waiting for transfers between devices, swap_near(): return lax.ppermute(value, 'y_lo', [(0, 1), (1, 0)])  14.2 us
    ppermute x5, starting transfers between devices, swap_near(): return lax.ppermute(value, 'y_lo', [(0, 1), (1, 0)])  14 us
    ppermute x12, waiting for transfers between devices, from_above(): lax.ppermute(value, axes, [((i + distance) % count, i) for i in range(cou...  13.3 us
    ppermute x2, starting transfers between devices, trade_pair(): other = lax.ppermute(sent, axis_name, [(0, 1), (1, 0)])  11.2 us
  transfers between devices with their start and end apart: 34, of which 14 were waited for; matrix products, arithmetic and copies ran while one was open for 14% of the time, Pallas kernels for 0%

profile of v10, /device:TPU:1, one launch (start us, length us, event | category | flops | bytes accessed | tf_op | source)
XLA Modules:
  0.0 266.2 jit_solution(6462742319000270914)
XLA Ops:
  2.0 4.0 %collective-permute-start.1 = (bf16[2,896,256]{2,1,0:T(8,128)(2,1)S(1)}, bf16[2,896,256]{2,1,0:T(8,128)(2,1)S(1)}, u32[]{:S(2)}, u32[]{:S(2)}) collective-permute-start(bf16[2,896,256]{2,1,0:T(8,128)(2,1)S(1)} %pad_maximum_fusion.1), channel_id=1, source_target_pairs={{0,256},{256,0},{1,257},{257,1},{2,258},{258,2},{3,259},{259,3},{4... | collective-permute-start | bytes 2752520 | tf_op jit(solution)/shard_map/ppermute | solution.py:37
  11.4 6.7 %collective-permute-start = (bf16[4,2,12,256]{3,1,2,0:T(2,128)(2,1)S(1)}, bf16[4,2,12,256]{3,1,2,0:T(2,128)(2,1)S(1)}, u32[]{:S(2)}, u32[]{:S(2)}) collective-permute-start(bf16[4,2,12,256]{3,1,2,0:T(2,128)(2,1)S(1)} %bitcast.255), channel_id=1, source_target_pairs={{0,1},{1,0},{2,3},{3,2},{4,5},{5,4},{6,7},{7,6},{8,9},{9,8},{10,11... | collective-permute-start | bytes 147464 | tf_op jit(solution)/shard_map/ppermute | solution.py:72
  18.0 11.1 %all-to-all-start = ((bf16[16,8,2048]{2,1,0:T(8,128)(2,1)}), bf16[16,8,2048]{2,1,0:T(8,128)(2,1)S(1)}, u32[]{:S(2)}, u32[]{:S(2)}) async-start(bf16[16,8,2048]{2,1,0:T(8,128)(2,1)} %reshape.239), calls=%async_computation | async-start | bytes 1048576 | tf_op jit(solution)/shard_map/all_to_all | solution.py:29
  29.7 4.5 %collective-permute-start.2 = (bf16[2,4,12,256]{3,1,2,0:T(4,128)(2,1)S(1)}, bf16[2,4,12,256]{3,1,2,0:T(4,128)(2,1)S(1)}, u32[]{:S(2)}, u32[]{:S(2)}) collective-permute-start(bf16[2,4,12,256]{3,1,2,0:T(4,128)(2,1)S(1)} %bitcast.254), channel_id=1, source_target_pairs={{0,2},{2,0},{1,3},{3,1},{4,6},{6,4},{5,7},{7,5},{8,10},{10,8},{9,1... | collective-permute-start | bytes 147464 | tf_op jit(solution)/shard_map/ppermute | solution.py:72
  36.6 4.4 %collective-permute-start.3 = (bf16[2,2,12,256]{3,1,2,0:T(2,128)(2,1)S(1)}, bf16[2,2,12,256]{3,1,2,0:T(2,128)(2,1)S(1)}, u32[]{:S(2)}, u32[]{:S(2)}) collective-permute-start(bf16[2,2,12,256]{3,1,2,0:T(2,128)(2,1)S(1)} %bitcast.260), channel_id=1, source_target_pairs={{0,12},{4,0},{8,4},{12,8},{1,13},{5,1},{9,5},{13,9},{2,14},{6,2},{... | collective-permute-start | bytes 73736 | tf_op jit(solution)/shard_map/ppermute | solution.py:80
  56.9 12.1 %all-to-all-start.1 = ((bf16[16,64,2048]{2,1,0:T(8,128)(2,1)}), bf16[16,64,2048]{2,1,0:T(8,128)(2,1)}, u32[]{:S(2)}, u32[]{:S(2)}) async-start(bf16[16,64,2048]{2,1,0:T(8,128)(2,1)} %bitcast.215), calls=%async_computation.1 | async-start | bytes 8388608 | tf_op jit(solution)/shard_map/all_to_all | solution.py:29
  71.4 4.3 %collective-permute-start.8 = (bf16[64,256]{1,0:T(8,128)(2,1)S(1)}, bf16[64,256]{1,0:T(8,128)(2,1)S(1)}, u32[]{:S(2)}, u32[]{:S(2)}) collective-permute-start(bf16[64,256]{1,0:T(8,128)(2,1)S(1)} %multiply_convert_fusion), channel_id=1, source_target_pairs={{192,0},{208,16},{224,32},{240,48},{0,64},{16,80},{32,96},{48,112}... | collective-permute-start | bytes 98312 | tf_op jit(solution)/shard_map/ppermute | solution.py:42
  75.6 8.0 %collective-permute-start.7 = (bf16[64,256]{1,0:T(8,128)(2,1)S(1)}, bf16[64,256]{1,0:T(8,128)(2,1)S(1)}, u32[]{:S(2)}, u32[]{:S(2)}) collective-permute-start(bf16[64,256]{1,0:T(8,128)(2,1)S(1)} %multiply_convert_fusion), channel_id=1, source_target_pairs={{128,0},{144,16},{160,32},{176,48},{192,64},{208,80},{224,96},{240... | collective-permute-start | bytes 98312 | tf_op jit(solution)/shard_map/ppermute | solution.py:42
  83.7 5.2 %collective-permute-start.6 = (bf16[64,256]{1,0:T(8,128)(2,1)S(1)}, bf16[64,256]{1,0:T(8,128)(2,1)S(1)}, u32[]{:S(2)}, u32[]{:S(2)}) collective-permute-start(bf16[64,256]{1,0:T(8,128)(2,1)S(1)} %multiply_convert_fusion), channel_id=1, source_target_pairs={{64,0},{80,16},{96,32},{112,48},{128,64},{144,80},{160,96},{176,11... | collective-permute-start | bytes 98312 | tf_op jit(solution)/shard_map/ppermute | solution.py:42
  91.5 3.1 %collective-permute-start.13 = (bf16[256,256]{1,0:T(8,128)(2,1)S(1)}, bf16[256,256]{1,0:T(8,128)(2,1)S(1)}, u32[]{:S(2)}, u32[]{:S(2)}) collective-permute-start(bf16[256,256]{1,0:T(8,128)(2,1)S(1)} %copy-done.9), channel_id=1, source_target_pairs={{32,0},{48,16},{0,32},{16,48},{33,1},{49,17},{1,33},{17,49},{34,2}... | collective-permute-start | bytes 393224 | tf_op jit(solution)/shard_map/ppermute | solution.py:42
  94.7 3.5 %collective-permute-start.12 = (bf16[256,256]{1,0:T(8,128)(2,1)S(1)}, bf16[256,256]{1,0:T(8,128)(2,1)S(1)}, u32[]{:S(2)}, u32[]{:S(2)}) collective-permute-start(bf16[256,256]{1,0:T(8,128)(2,1)S(1)} %copy-done.9), channel_id=1, source_target_pairs={{16,0},{32,16},{48,32},{0,48},{17,1},{33,17},{49,33},{1,49},{18,2}... | collective-permute-start | bytes 393224 | tf_op jit(solution)/shard_map/ppermute | solution.py:42
  100.2 3.4 %collective-permute-start.10 = (bf16[4,64,256]{2,1,0:T(8,128)(2,1)S(1)}, bf16[4,64,256]{2,1,0:T(8,128)(2,1)S(1)}, u32[]{:S(2)}, u32[]{:S(2)}) collective-permute-start(bf16[4,64,256]{2,1,0:T(8,128)(2,1)S(1)} %get-tuple-element.84), channel_id=1, source_target_pairs={{32,0},{48,16},{64,32},{80,48},{96,64},{112,80},{128,96},{144,112}... | collective-permute-start | bytes 393224 | tf_op jit(solution)/shard_map/ppermute | solution.py:42
  108.5 3.4 %collective-permute-done.10 = bf16[4,64,256]{2,1,0:T(8,128)(2,1)S(1)} collective-permute-done((bf16[4,64,256]{2,1,0:T(8,128)(2,1)S(1)}, bf16[4,64,256]{2,1,0:T(8,128)(2,1)S(1)}, u32[]{:S(2)}, u32[]{:S(2)}) %collective-permute-start.10) | collective-permute-done | bytes 131104 | tf_op jit(solution)/shard_map/ppermute | solution.py:42
  114.6 7.1 %all-to-all-done.1 = bf16[16,64,2048]{2,1,0:T(8,128)(2,1)} async-done(((bf16[16,64,2048]{2,1,0:T(8,128)(2,1)}), bf16[16,64,2048]{2,1,0:T(8,128)(2,1)}, u32[]{:S(2)}, u32[]{:S(2)}) %all-to-all-start.1) | async-done | bytes 4194336 | tf_op jit(solution)/shard_map/all_to_all | solution.py:29
  121.7 3.7 %fusion.48 = f32[1024,256]{1,0:T(8,128)S(1)} fusion(bf16[1024,2048]{1,0:T(8,128)(2,1)} %bitcast.31, bf16[2048,256]{1,0:T(8,128)(2,1)} %collective-permute-done.15), kind=kOutput, calls=%fused_computation.150 | convolution fusion | flops 1073741824 | bytes 6291456 | tf_op jit(solution)/shard_map/dot_general | solution.py:207
  127.7 3.4 %fusion.47 = f32[1024,256]{1,0:T(8,128)S(1)} fusion(bf16[1024,2048]{1,0:T(8,128)(2,1)} %bitcast.31, bf16[2048,256]{1,0:T(8,128)(2,1)S(1)} %bitcast.233), kind=kOutput, calls=%fused_computation.149 | convolution fusion | flops 1073741824 | bytes 6291456 | tf_op jit(solution)/shard_map/dot_general | solution.py:208
  132.5 7.8 %all-to-all-start.2 = ((bf16[16,64,256]{2,1,0:T(8,128)(2,1)}), bf16[16,64,256]{2,1,0:T(8,128)(2,1)S(1)}, u32[]{:S(2)}, u32[]{:S(2)}) async-start(bf16[16,64,256]{2,1,0:T(8,128)(2,1)} %copy.269), calls=%async_computation.2 | async-start | bytes 1048576 | tf_op jit(solution)/shard_map/all_to_all | solution.py:29
  141.6 2.7 %collective-permute-start.17 = (bf16[1024,256]{1,0:T(8,128)(2,1)}, bf16[1024,256]{1,0:T(8,128)(2,1)}, u32[]{:S(2)}, u32[]{:S(2)}) collective-permute-start(bf16[1024,256]{1,0:T(8,128)(2,1)} %reshape.251), channel_id=1, source_target_pairs={{0,1},{1,0},{2,3},{3,2},{4,5},{5,4},{6,7},{7,6},{8,9},{9,8},{10,11... | collective-permute-start | bytes 1572872 | tf_op jit(solution)/shard_map/ppermute | solution.py:33
  149.9 4.9 %fusion.6 = f32[2048,512]{1,0:T(8,128)S(1)} fusion(bf16[1024,2048]{1,0:T(8,128)(2,1)} %bitcast.31, bf16[1024,256]{1,0:T(8,128)(2,1)} %collective-permute-done.17, bf16[1024,256]{1,0:T(8,128)(2,1)} %reshape.251), kind=kOutput, calls=%fused_computation.12 | convolution fusion | flops 2149580800 | bytes 9437184 | tf_op jit(solution)/shard_map/dot_general | solution.py:25
  158.0 4.4 %collective-permute-done.19 = bf16[4,256,256]{2,1,0:T(8,128)(2,1)S(1)} collective-permute-done((bf16[4,256,256]{2,1,0:T(8,128)(2,1)S(1)}, bf16[4,256,256]{2,1,0:T(8,128)(2,1)S(1)}, u32[]{:S(2)}, u32[]{:S(2)}) %collective-permute-start.19) | collective-permute-done | bytes 524320 | tf_op jit(solution)/shard_map/ppermute | solution.py:37
  164.3 19.9 %all-to-all-start.3 = ((f32[16,1,320]{2,1,0:T(1,128)}), f32[16,1,320]{2,1,0:T(1,128)S(1)}, u32[]{:S(2)}, u32[]{:S(2)}) async-start(f32[16,1,320]{2,1,0:T(1,128)} %broadcast_in_dim.10), calls=%async_computation.3 | async-start | bytes 49152 | tf_op jit(solution)/shard_map/all_to_all | solution.py:29
  186.6 4.9 %all-to-all-done.3 = f32[16,1,320]{2,1,0:T(1,128)S(1)} async-done(((f32[16,1,320]{2,1,0:T(1,128)}), f32[16,1,320]{2,1,0:T(1,128)S(1)}, u32[]{:S(2)}, u32[]{:S(2)}) %all-to-all-start.3) | async-done | bytes 20512 | tf_op jit(solution)/shard_map/all_to_all | solution.py:29
  192.4 6.1 %all-to-all-start.4 = ((bf16[4,96,256]{2,1,0:T(8,128)(2,1)}), bf16[4,96,256]{2,1,0:T(8,128)(2,1)S(1)}, u32[]{:S(2)}, u32[]{:S(2)}) async-start(bf16[4,96,256]{2,1,0:T(8,128)(2,1)} %broadcast_in_dim.11), calls=%async_computation.4 | async-start | bytes 393216 | tf_op jit(solution)/shard_map/all_to_all | solution.py:29
  198.6 9.7 %collective-permute-done.20 = bf16[896,512]{1,0:T(8,128)(2,1)} collective-permute-done((bf16[896,512]{1,0:T(8,128)(2,1)}, bf16[896,512]{1,0:T(8,128)(2,1)}, u32[]{:S(2)}, u32[]{:S(2)}) %collective-permute-start.20) | collective-permute-done | bytes 917536 | tf_op jit(solution)/shard_map/ppermute | solution.py:37
  211.5 7.4 %collective-permute-start.21 = (f32[896,256]{1,0:T(8,128)}, f32[896,256]{1,0:T(8,128)}, u32[]{:S(2)}, u32[]{:S(2)}) collective-permute-start(f32[896,256]{1,0:T(8,128)} %get-tuple-element.46), channel_id=1, source_target_pairs={{0,1},{1,0},{2,3},{3,2},{4,5},{5,4},{6,7},{7,6},{8,9},{9,8},{10,11... | collective-permute-start | bytes 2752520 | tf_op jit(solution)/shard_map/ppermute | solution.py:33
  220.7 3.6 %all-to-all-start.5 = ((bf16[16,16,2048]{2,1,0:T(8,128)(2,1)}), bf16[16,16,2048]{2,1,0:T(8,128)(2,1)S(1)}, u32[]{:S(2)}, u32[]{:S(2)}) async-start(bf16[16,16,2048]{2,1,0:T(8,128)(2,1)} %bitcast.71), calls=%async_computation.5 | async-start | bytes 2097152 | tf_op jit(solution)/shard_map/all_to_all | solution.py:29
  227.5 3.0 %collective-permute-start.22 = (bf16[288,256]{1,0:T(8,128)(2,1)S(1)}, bf16[288,256]{1,0:T(8,128)(2,1)S(1)}, u32[]{:S(2)}, u32[]{:S(2)}) collective-permute-start(bf16[288,256]{1,0:T(8,128)(2,1)S(1)} %pad_maximum_fusion.5), channel_id=1, source_target_pairs={{16,0},{32,16},{48,32},{0,48},{17,1},{33,17},{49,33},{1,49},{18,2}... | collective-permute-start | bytes 442376 | tf_op jit(solution)/shard_map/ppermute | solution.py:42
  230.5 3.7 %collective-permute-start.23 = (bf16[288,256]{1,0:T(8,128)(2,1)S(1)}, bf16[288,256]{1,0:T(8,128)(2,1)S(1)}, u32[]{:S(2)}, u32[]{:S(2)}) collective-permute-start(bf16[288,256]{1,0:T(8,128)(2,1)S(1)} %pad_maximum_fusion.5), channel_id=1, source_target_pairs={{32,0},{48,16},{0,32},{16,48},{33,1},{49,17},{1,33},{17,49},{34,2}... | collective-permute-start | bytes 442376 | tf_op jit(solution)/shard_map/ppermute | solution.py:42
  238.7 6.9 %collective-permute-done.23 = bf16[288,256]{1,0:T(8,128)(2,1)S(1)} collective-permute-done((bf16[288,256]{1,0:T(8,128)(2,1)S(1)}, bf16[288,256]{1,0:T(8,128)(2,1)S(1)}, u32[]{:S(2)}, u32[]{:S(2)}) %collective-permute-start.23) | collective-permute-done | bytes 147488 | tf_op jit(solution)/shard_map/ppermute | solution.py:42
  246.7 5.5 %all-to-all-start.6 = ((bf16[4,4,2048]{2,1,0:T(4,128)(2,1)}), bf16[4,4,2048]{2,1,0:T(4,128)(2,1)S(1)}, u32[]{:S(2)}, u32[]{:S(2)}) async-start(bf16[4,4,2048]{2,1,0:T(4,128)(2,1)} %reshape.258), calls=%async_computation.6 | async-start | bytes 131072 | tf_op jit(solution)/shard_map/all_to_all | solution.py:29
  255.9 3.0 %collective-permute-start.25 = (f32[2,128,256]{2,1,0:T(8,128)S(1)}, f32[2,128,256]{2,1,0:T(8,128)S(1)}, u32[]{:S(2)}, u32[]{:S(2)}) collective-permute-start(f32[2,128,256]{2,1,0:T(8,128)S(1)} %fusion.26), channel_id=1, source_target_pairs={{0,256},{256,0},{1,257},{257,1},{2,258},{258,2},{3,259},{259,3},{4... | collective-permute-start | bytes 786440 | tf_op jit(solution)/shard_map/ppermute | solution.py:37
  259.5 5.0 %all-to-all-done.6 = bf16[4,4,2048]{2,1,0:T(4,128)(2,1)S(1)} async-done(((bf16[4,4,2048]{2,1,0:T(4,128)(2,1)}), bf16[4,4,2048]{2,1,0:T(4,128)(2,1)S(1)}, u32[]{:S(2)}, u32[]{:S(2)}) %all-to-all-start.6) | async-done | bytes 65568 | tf_op jit(solution)/shard_map/all_to_all | solution.py:29
  (206 shorter events, 77.8 us)
Async XLA Ops:
  2.0 27.5 %collective-permute-start.1 = (bf16[2,896,256]{2,1,0:T(8,128)(2,1)S(1)}, bf16[2,896,256]{2,1,0:T(8,128)(2,1)S(1)}, u32[]{:S(2)}, u32[]{:S(2)}) collective-permute-start(bf16[2,896,256]{2,1,0:T(8,128)(2,1)S(1)} %pad_maximum_fusion.1), channel_id=1, source_target_pairs={{0,256},{256,0},{1,257},{257,1},{2,258},{258,2},{3,259},{259,3},{4... | collective-permute-start | bytes 2752520 | tf_op jit(solution)/shard_map/ppermute | solution.py:37
  11.4 17.8 %collective-permute-start = (bf16[4,2,12,256]{3,1,2,0:T(2,128)(2,1)S(1)}, bf16[4,2,12,256]{3,1,2,0:T(2,128)(2,1)S(1)}, u32[]{:S(2)}, u32[]{:S(2)}) collective-permute-start(bf16[4,2,12,256]{3,1,2,0:T(2,128)(2,1)S(1)} %bitcast.255), channel_id=1, source_target_pairs={{0,1},{1,0},{2,3},{3,2},{4,5},{5,4},{6,7},{7,6},{8,9},{9,8},{10,11... | collective-permute-start | bytes 147464 | tf_op jit(solution)/shard_map/ppermute | solution.py:72
  18.0 35.3 %all-to-all-start = ((bf16[16,8,2048]{2,1,0:T(8,128)(2,1)}), bf16[16,8,2048]{2,1,0:T(8,128)(2,1)S(1)}, u32[]{:S(2)}, u32[]{:S(2)}) async-start(bf16[16,8,2048]{2,1,0:T(8,128)(2,1)} %reshape.239), calls=%async_computation | async-start | bytes 1048576 | tf_op jit(solution)/shard_map/all_to_all | solution.py:29
  29.7 6.3 %collective-permute-start.2 = (bf16[2,4,12,256]{3,1,2,0:T(4,128)(2,1)S(1)}, bf16[2,4,12,256]{3,1,2,0:T(4,128)(2,1)S(1)}, u32[]{:S(2)}, u32[]{:S(2)}) collective-permute-start(bf16[2,4,12,256]{3,1,2,0:T(4,128)(2,1)S(1)} %bitcast.254), channel_id=1, source_target_pairs={{0,2},{2,0},{1,3},{3,1},{4,6},{6,4},{5,7},{7,5},{8,10},{10,8},{9,1... | collective-permute-start | bytes 147464 | tf_op jit(solution)/shard_map/ppermute | solution.py:72
  36.6 10.2 %collective-permute-start.3 = (bf16[2,2,12,256]{3,1,2,0:T(2,128)(2,1)S(1)}, bf16[2,2,12,256]{3,1,2,0:T(2,128)(2,1)S(1)}, u32[]{:S(2)}, u32[]{:S(2)}) collective-permute-start(bf16[2,2,12,256]{3,1,2,0:T(2,128)(2,1)S(1)} %bitcast.260), channel_id=1, source_target_pairs={{0,12},{4,0},{8,4},{12,8},{1,13},{5,1},{9,5},{13,9},{2,14},{6,2},{... | collective-permute-start | bytes 73736 | tf_op jit(solution)/shard_map/ppermute | solution.py:80
  41.0 6.4 %collective-permute-start.4 = (bf16[2,2,12,256]{3,1,2,0:T(2,128)(2,1)S(1)}, bf16[2,2,12,256]{3,1,2,0:T(2,128)(2,1)S(1)}, u32[]{:S(2)}, u32[]{:S(2)}) collective-permute-start(bf16[2,2,12,256]{3,1,2,0:T(2,128)(2,1)S(1)} %bitcast.262), channel_id=1, source_target_pairs={{0,8},{4,12},{8,0},{12,4},{1,9},{5,13},{9,1},{13,5},{2,10},{6,14},... | collective-permute-start | bytes 73736 | tf_op jit(solution)/shard_map/ppermute | solution.py:80
  43.5 6.3 %collective-permute-start.5 = (bf16[2,2,12,256]{3,1,2,0:T(2,128)(2,1)S(1)}, bf16[2,2,12,256]{3,1,2,0:T(2,128)(2,1)S(1)}, u32[]{:S(2)}, u32[]{:S(2)}) collective-permute-start(bf16[2,2,12,256]{3,1,2,0:T(2,128)(2,1)S(1)} %bitcast.264), channel_id=1, source_target_pairs={{0,4},{4,8},{8,12},{12,0},{1,5},{5,9},{9,13},{13,1},{2,6},{6,10},{... | collective-permute-start | bytes 73736 | tf_op jit(solution)/shard_map/ppermute | solution.py:80
  56.9 64.8 %all-to-all-start.1 = ((bf16[16,64,2048]{2,1,0:T(8,128)(2,1)}), bf16[16,64,2048]{2,1,0:T(8,128)(2,1)}, u32[]{:S(2)}, u32[]{:S(2)}) async-start(bf16[16,64,2048]{2,1,0:T(8,128)(2,1)} %bitcast.215), calls=%async_computation.1 | async-start | bytes 8388608 | tf_op jit(solution)/shard_map/all_to_all | solution.py:29
  69.3 52.5 %collective-permute-start.15 = (bf16[2048,256]{1,0:T(8,128)(2,1)S(1)}, bf16[2048,256]{1,0:T(8,128)(2,1)}, u32[]{:S(2)}, u32[]{:S(2)}) collective-permute-start(bf16[2048,256]{1,0:T(8,128)(2,1)S(1)} %bitcast.232), channel_id=1, source_target_pairs={{0,1},{1,0},{2,3},{3,2},{4,5},{5,4},{6,7},{7,6},{8,9},{9,8},{10,11... | collective-permute-start | bytes 3145736 | tf_op jit(solution)/shard_map/ppermute | solution.py:33
  71.4 20.2 %collective-permute-start.8 = (bf16[64,256]{1,0:T(8,128)(2,1)S(1)}, bf16[64,256]{1,0:T(8,128)(2,1)S(1)}, u32[]{:S(2)}, u32[]{:S(2)}) collective-permute-start(bf16[64,256]{1,0:T(8,128)(2,1)S(1)} %multiply_convert_fusion), channel_id=1, source_target_pairs={{192,0},{208,16},{224,32},{240,48},{0,64},{16,80},{32,96},{48,112}... | collective-permute-start | bytes 98312 | tf_op jit(solution)/shard_map/ppermute | solution.py:42
  75.6 19.0 %collective-permute-start.7 = (bf16[64,256]{1,0:T(8,128)(2,1)S(1)}, bf16[64,256]{1,0:T(8,128)(2,1)S(1)}, u32[]{:S(2)}, u32[]{:S(2)}) collective-permute-start(bf16[64,256]{1,0:T(8,128)(2,1)S(1)} %multiply_convert_fusion), channel_id=1, source_target_pairs={{128,0},{144,16},{160,32},{176,48},{192,64},{208,80},{224,96},{240... | collective-permute-start | bytes 98312 | tf_op jit(solution)/shard_map/ppermute | solution.py:42
  83.7 14.5 %collective-permute-start.6 = (bf16[64,256]{1,0:T(8,128)(2,1)S(1)}, bf16[64,256]{1,0:T(8,128)(2,1)S(1)}, u32[]{:S(2)}, u32[]{:S(2)}) collective-permute-start(bf16[64,256]{1,0:T(8,128)(2,1)S(1)} %multiply_convert_fusion), channel_id=1, source_target_pairs={{64,0},{80,16},{96,32},{112,48},{128,64},{144,80},{160,96},{176,11... | collective-permute-start | bytes 98312 | tf_op jit(solution)/shard_map/ppermute | solution.py:42
  88.9 11.3 %collective-permute-start.14 = (bf16[256,256]{1,0:T(8,128)(2,1)S(1)}, bf16[256,256]{1,0:T(8,128)(2,1)S(1)}, u32[]{:S(2)}, u32[]{:S(2)}) collective-permute-start(bf16[256,256]{1,0:T(8,128)(2,1)S(1)} %copy-done.9), channel_id=1, source_target_pairs={{48,0},{0,16},{16,32},{32,48},{49,1},{1,17},{17,33},{33,49},{50,2}... | collective-permute-start | bytes 393224 | tf_op jit(solution)/shard_map/ppermute | solution.py:42
  91.5 12.7 %collective-permute-start.13 = (bf16[256,256]{1,0:T(8,128)(2,1)S(1)}, bf16[256,256]{1,0:T(8,128)(2,1)S(1)}, u32[]{:S(2)}, u32[]{:S(2)}) collective-permute-start(bf16[256,256]{1,0:T(8,128)(2,1)S(1)} %copy-done.9), channel_id=1, source_target_pairs={{32,0},{48,16},{0,32},{16,48},{33,1},{49,17},{1,33},{17,49},{34,2}... | collective-permute-start | bytes 393224 | tf_op jit(solution)/shard_map/ppermute | solution.py:42
  94.7 12.1 %collective-permute-start.12 = (bf16[256,256]{1,0:T(8,128)(2,1)S(1)}, bf16[256,256]{1,0:T(8,128)(2,1)S(1)}, u32[]{:S(2)}, u32[]{:S(2)}) collective-permute-start(bf16[256,256]{1,0:T(8,128)(2,1)S(1)} %copy-done.9), channel_id=1, source_target_pairs={{16,0},{32,16},{48,32},{0,48},{17,1},{33,17},{49,33},{1,49},{18,2}... | collective-permute-start | bytes 393224 | tf_op jit(solution)/shard_map/ppermute | solution.py:42
  98.2 10.2 %collective-permute-start.11 = (bf16[4,64,256]{2,1,0:T(8,128)(2,1)S(1)}, bf16[4,64,256]{2,1,0:T(8,128)(2,1)S(1)}, u32[]{:S(2)}, u32[]{:S(2)}) collective-permute-start(bf16[4,64,256]{2,1,0:T(8,128)(2,1)S(1)} %get-tuple-element.84), channel_id=1, source_target_pairs={{240,0},{0,16},{16,32},{32,48},{48,64},{64,80},{80,96},{96,112},{1... | collective-permute-start | bytes 393224 | tf_op jit(solution)/shard_map/ppermute | solution.py:42
  100.2 11.7 %collective-permute-start.10 = (bf16[4,64,256]{2,1,0:T(8,128)(2,1)S(1)}, bf16[4,64,256]{2,1,0:T(8,128)(2,1)S(1)}, u32[]{:S(2)}, u32[]{:S(2)}) collective-permute-start(bf16[4,64,256]{2,1,0:T(8,128)(2,1)S(1)} %get-tuple-element.84), channel_id=1, source_target_pairs={{32,0},{48,16},{64,32},{80,48},{96,64},{112,80},{128,96},{144,112}... | collective-permute-start | bytes 393224 | tf_op jit(solution)/shard_map/ppermute | solution.py:42
  104.2 10.0 %collective-permute-start.9 = (bf16[4,64,256]{2,1,0:T(8,128)(2,1)S(1)}, bf16[4,64,256]{2,1,0:T(8,128)(2,1)S(1)}, u32[]{:S(2)}, u32[]{:S(2)}) collective-permute-start(bf16[4,64,256]{2,1,0:T(8,128)(2,1)S(1)} %get-tuple-element.84), channel_id=1, source_target_pairs={{16,0},{32,16},{48,32},{64,48},{80,64},{96,80},{112,96},{128,112},... | collective-permute-start | bytes 393224 | tf_op jit(solution)/shard_map/ppermute | solution.py:42
  132.5 30.6 %all-to-all-start.2 = ((bf16[16,64,256]{2,1,0:T(8,128)(2,1)}), bf16[16,64,256]{2,1,0:T(8,128)(2,1)S(1)}, u32[]{:S(2)}, u32[]{:S(2)}) async-start(bf16[16,64,256]{2,1,0:T(8,128)(2,1)} %copy.269), calls=%async_computation.2 | async-start | bytes 1048576 | tf_op jit(solution)/shard_map/all_to_all | solution.py:29
  141.6 8.3 %collective-permute-start.17 = (bf16[1024,256]{1,0:T(8,128)(2,1)}, bf16[1024,256]{1,0:T(8,128)(2,1)}, u32[]{:S(2)}, u32[]{:S(2)}) collective-permute-start(bf16[1024,256]{1,0:T(8,128)(2,1)} %reshape.251), channel_id=1, source_target_pairs={{0,1},{1,0},{2,3},{3,2},{4,5},{5,4},{6,7},{7,6},{8,9},{9,8},{10,11... | collective-permute-start | bytes 1572872 | tf_op jit(solution)/shard_map/ppermute | solution.py:33
  145.6 12.4 %collective-permute-start.18 = (bf16[1024,256]{1,0:T(8,128)(2,1)S(1)}, bf16[1024,256]{1,0:T(8,128)(2,1)S(1)}, u32[]{:S(2)}, u32[]{:S(2)}) collective-permute-start(bf16[1024,256]{1,0:T(8,128)(2,1)S(1)} %pad_maximum_fusion.4), channel_id=1, source_target_pairs={{0,1},{1,0},{2,3},{3,2},{4,5},{5,4},{6,7},{7,6},{8,9},{9,8},{10,11... | collective-permute-start | bytes 1572872 | tf_op jit(solution)/shard_map/ppermute | solution.py:33
  147.6 14.9 %collective-permute-start.19 = (bf16[4,256,256]{2,1,0:T(8,128)(2,1)S(1)}, bf16[4,256,256]{2,1,0:T(8,128)(2,1)S(1)}, u32[]{:S(2)}, u32[]{:S(2)}) collective-permute-start(bf16[4,256,256]{2,1,0:T(8,128)(2,1)S(1)} %pad_maximum_fusion.3), channel_id=1, source_target_pairs={{0,256},{256,0},{1,257},{257,1},{2,258},{258,2},{3,259},{259,3},{4... | collective-permute-start | bytes 1572872 | tf_op jit(solution)/shard_map/ppermute | solution.py:37
  164.3 27.2 %all-to-all-start.3 = ((f32[16,1,320]{2,1,0:T(1,128)}), f32[16,1,320]{2,1,0:T(1,128)S(1)}, u32[]{:S(2)}, u32[]{:S(2)}) async-start(f32[16,1,320]{2,1,0:T(1,128)} %broadcast_in_dim.10), calls=%async_computation.3 | async-start | bytes 49152 | tf_op jit(solution)/shard_map/all_to_all | solution.py:29
  184.2 24.2 %collective-permute-start.20 = (bf16[896,512]{1,0:T(8,128)(2,1)}, bf16[896,512]{1,0:T(8,128)(2,1)}, u32[]{:S(2)}, u32[]{:S(2)}) collective-permute-start(bf16[896,512]{1,0:T(8,128)(2,1)} %fusion.10), channel_id=1, source_target_pairs={{0,256},{256,0},{1,257},{257,1},{2,258},{258,2},{3,259},{259,3},{4... | collective-permute-start | bytes 2752520 | tf_op jit(solution)/shard_map/ppermute | solution.py:37
  192.4 19.1 %all-to-all-start.4 = ((bf16[4,96,256]{2,1,0:T(8,128)(2,1)}), bf16[4,96,256]{2,1,0:T(8,128)(2,1)S(1)}, u32[]{:S(2)}, u32[]{:S(2)}) async-start(bf16[4,96,256]{2,1,0:T(8,128)(2,1)} %broadcast_in_dim.11), calls=%async_computation.4 | async-start | bytes 393216 | tf_op jit(solution)/shard_map/all_to_all | solution.py:29
  211.5 14.2 %collective-permute-start.21 = (f32[896,256]{1,0:T(8,128)}, f32[896,256]{1,0:T(8,128)}, u32[]{:S(2)}, u32[]{:S(2)}) collective-permute-start(f32[896,256]{1,0:T(8,128)} %get-tuple-element.46), channel_id=1, source_target_pairs={{0,1},{1,0},{2,3},{3,2},{4,5},{5,4},{6,7},{7,6},{8,9},{9,8},{10,11... | collective-permute-start | bytes 2752520 | tf_op jit(solution)/shard_map/ppermute | solution.py:33
  220.7 25.1 %all-to-all-start.5 = ((bf16[16,16,2048]{2,1,0:T(8,128)(2,1)}), bf16[16,16,2048]{2,1,0:T(8,128)(2,1)S(1)}, u32[]{:S(2)}, u32[]{:S(2)}) async-start(bf16[16,16,2048]{2,1,0:T(8,128)(2,1)} %bitcast.71), calls=%async_computation.5 | async-start | bytes 2097152 | tf_op jit(solution)/shard_map/all_to_all | solution.py:29
  227.5 11.2 %collective-permute-start.22 = (bf16[288,256]{1,0:T(8,128)(2,1)S(1)}, bf16[288,256]{1,0:T(8,128)(2,1)S(1)}, u32[]{:S(2)}, u32[]{:S(2)}) collective-permute-start(bf16[288,256]{1,0:T(8,128)(2,1)S(1)} %pad_maximum_fusion.5), channel_id=1, source_target_pairs={{16,0},{32,16},{48,32},{0,48},{17,1},{33,17},{49,33},{1,49},{18,2}... | collective-permute-start | bytes 442376 | tf_op jit(solution)/shard_map/ppermute | solution.py:42
  230.5 15.1 %collective-permute-start.23 = (bf16[288,256]{1,0:T(8,128)(2,1)S(1)}, bf16[288,256]{1,0:T(8,128)(2,1)S(1)}, u32[]{:S(2)}, u32[]{:S(2)}) collective-permute-start(bf16[288,256]{1,0:T(8,128)(2,1)S(1)} %pad_maximum_fusion.5), channel_id=1, source_target_pairs={{32,0},{48,16},{0,32},{16,48},{33,1},{49,17},{1,33},{17,49},{34,2}... | collective-permute-start | bytes 442376 | tf_op jit(solution)/shard_map/ppermute | solution.py:42
  234.2 11.4 %collective-permute-start.24 = (bf16[288,256]{1,0:T(8,128)(2,1)S(1)}, bf16[288,256]{1,0:T(8,128)(2,1)S(1)}, u32[]{:S(2)}, u32[]{:S(2)}) collective-permute-start(bf16[288,256]{1,0:T(8,128)(2,1)S(1)} %pad_maximum_fusion.5), channel_id=1, source_target_pairs={{48,0},{0,16},{16,32},{32,48},{49,1},{1,17},{17,33},{33,49},{50,2}... | collective-permute-start | bytes 442376 | tf_op jit(solution)/shard_map/ppermute | solution.py:42
  246.7 17.9 %all-to-all-start.6 = ((bf16[4,4,2048]{2,1,0:T(4,128)(2,1)}), bf16[4,4,2048]{2,1,0:T(4,128)(2,1)S(1)}, u32[]{:S(2)}, u32[]{:S(2)}) async-start(bf16[4,4,2048]{2,1,0:T(4,128)(2,1)} %reshape.258), calls=%async_computation.6 | async-start | bytes 131072 | tf_op jit(solution)/shard_map/all_to_all | solution.py:29
  255.9 9.5 %collective-permute-start.25 = (f32[2,128,256]{2,1,0:T(8,128)S(1)}, f32[2,128,256]{2,1,0:T(8,128)S(1)}, u32[]{:S(2)}, u32[]{:S(2)}) collective-permute-start(f32[2,128,256]{2,1,0:T(8,128)S(1)} %fusion.26), channel_id=1, source_target_pairs={{0,256},{256,0},{1,257},{257,1},{2,258},{258,2},{3,259},{259,3},{4... | collective-permute-start | bytes 786440 | tf_op jit(solution)/shard_map/ppermute | solution.py:37
  (15 other events, 121.1 us)

commit v11 on v10

--- a/solution.py
+++ b/solution.py
@@ -7,7 +7,7 @@
 epsilon = 1e-05
 narrow = jnp.bfloat16
 wide = jnp.float32
-z_axes = ("z_hi", "z_lo")
+z_axes = ("z_top", "z_mid", "z_lo")
 
 
 def swiglu_back(gate_act, up_act, product_grad):
@@ -42,15 +42,18 @@
     return lax.ppermute(value, axes, [((i + distance) % count, i) for i in range(count)])
 
 
-def gather_z(block):
+def gather_far(block):
+    quarter = lax.axis_size(z_axes) // 4
+    return jnp.stack([block] + [from_above(block, 4 * step) for step in range(1, quarter)])
+
+
+def gather_near(strided):
     z_count = lax.axis_size(z_axes)
-    quarter = z_count // 4
-    strided = jnp.stack([block] + [from_above(block, 4 * step) for step in range(1, quarter)])
     below = from_above(strided, z_count - 1)
     below = jnp.concatenate([below[1:], below[:1]])
     all_blocks = jnp.stack(
         [strided, from_above(strided, 1), from_above(strided, 2), below], axis=1
-    ).reshape(z_count, *block.shape)
+    ).reshape(z_count, *strided.shape[1:])
     return from_first(all_blocks, z_axes)
 
 
@@ -63,6 +66,12 @@
     twice = jnp.concatenate([blocks, blocks])
     count = blocks.shape[0]
     return lax.dynamic_slice_in_dim(twice, count - lax.axis_index(axes), count, 0)
+
+
+def gather_pair(block, axis):
+    first = lax.axis_index(axis) == 0
+    other = lax.ppermute(block, axis, [(0, 1), (1, 0)])
+    return jnp.stack([jnp.where(first, block, other), jnp.where(first, other, block)])
 
 
 def trade_pair(blocks, axis_name):
@@ -111,7 +120,7 @@
 ):
     dp_axes = ("x", "y_hi", "core")
     quarter = lax.axis_size("z_lo")
-    z_count = lax.axis_size("z_hi") * quarter
+    z_count = 4 * quarter
     core_count = lax.axis_size("core")
     dp_count = lax.axis_size("x") * lax.axis_size("y_hi") * core_count
     row_count, width = hidden.shape
@@ -179,7 +188,10 @@
     mlp_block = (normed * gain_block).astype(narrow)
 
     unit_group, mlp_block = lax.optimization_barrier((unit_group, mlp_block))
-    mlp_z = gather_z(mlp_block)
+    mlp_far, join_pair = lax.optimization_barrier(
+        (gather_far(mlp_block), gather_pair(join_weight, "z_mid"))
+    )
+    mlp_z, join_quad = gather_near(mlp_far), gather_ring(join_pair, "z_lo")
     unit_halves = (
         unit_group.reshape(z_count, 2, row_count, 2 * part_width)
         .transpose(1, 0, 2, 3)
@@ -189,7 +201,6 @@
         unit_halves[None], (dp_count // core_count, core_count, plane_rows, 2 * part_width)
     ).reshape(dp_count, plane_rows, 2 * part_width)
     half_all = exchange(unit_halves, dp_axes).reshape(tokens, 2 * part_width)
-    join_quad = gather_ring(join_weight, "z_lo")
     half_all, mlp_z, join_quad = lax.optimization_barrier((half_all, mlp_z, join_quad))
 
     def both_near(own, near):
@@ -251,25 +262,13 @@
 
     grad_sent = jnp.concatenate([hidden_grad, *split_two(gain_part)])
     sent_rows = block_rows + 2 * dp_count
-    high_count = z_count // quarter
-    grad_high = exchange(
-        jnp.broadcast_to(grad_sent[None], (high_count, sent_rows, features)), "z_hi"
-    )
-
-    join_pair = by_near(join_quad, near_quad).reshape(2 * quarter * inputs, features)
+    high_count = 2
+    grad_high = gather_pair(grad_sent, "z_top")
+
+    join_pair = by_near(join_quad, near_quad).reshape(4 * quarter * inputs, features)
     joined_half, joined_other = joined_half.T, joined_other.T
-    unit_grad = unit_kept + unit_near.astype(wide)
-    grad_high, own_grad, other_sent, join_pair, joined_half, joined_other = (
-        lax.optimization_barrier(
-            (
-                grad_high,
-                unit_grad[:, :features],
-                unit_grad[:, features:],
-                join_pair,
-                joined_half,
-                joined_other,
-            )
-        )
+    grad_high, join_pair, joined_half, joined_other = lax.optimization_barrier(
+        (grad_high, join_pair, joined_half, joined_other)
     )
 
     grad_rows = (
@@ -282,11 +281,10 @@
         grad_rows, join_pair, (((1,), (1,)), ((), ())), preferred_element_type=wide
     ).astype(narrow)
     joined_blocks = exchange(
-        joined_part.reshape(dp_count, high_count * row_count, 2 * quarter * inputs), dp_axes
-    )
-    grad_high, other_grad = lax.optimization_barrier((grad_high, swap_cores(other_sent)))
-    gate_weight_grad = jnp.where(on_first, own_grad, other_grad)
-    up_weight_grad = jnp.where(on_first, other_grad, own_grad)
+        joined_part.reshape(dp_count, high_count * row_count, 4 * quarter * inputs), dp_axes
+    )
+    unit_grad = unit_kept + unit_near.astype(wide)
+    own_grad, other_sent = unit_grad[:, :features], unit_grad[:, features:]
 
     def sum_parts(blocks):
         parts = jnp.sum(blocks.astype(wide).reshape(-1, 2, dp_count, features), axis=0)
@@ -296,27 +294,33 @@
     grad_quad = jnp.concatenate(
         [grad_high[:, :block_rows].reshape(-1, features), *split_two(gain_high)]
     )
-    grad_z = from_first(gather_ring(grad_quad, "z_lo"), "z_lo")
-    grad_z, joined_blocks = lax.optimization_barrier((grad_z, joined_blocks))
+    grad_z = gather_ring(gather_pair(grad_quad, "z_mid"), "z_lo")
+    grad_z, joined_blocks, own_grad, other_sent = lax.optimization_barrier(
+        (grad_z, joined_blocks, own_grad, other_sent)
+    )
+    grad_z = from_first(grad_z, "z_lo")
     joined_total = jnp.sum(joined_blocks.astype(wide), axis=0).astype(narrow)
-    joined_high = exchange(
-        joined_total.reshape(high_count, row_count, 2 * quarter * inputs), "z_hi"
-    ).reshape(high_count, row_count, 2, quarter, inputs)
+    joined_high = trade_pair(
+        joined_total.reshape(high_count, row_count, 4 * quarter * inputs), "z_top"
+    ).reshape(high_count, row_count, 2, quarter, 2, inputs)
     joined_grad = (
-        from_first(joined_high.transpose(3, 0, 1, 2, 4), "z_lo")
-        .transpose(2, 3, 1, 0, 4)
+        from_first(joined_high.transpose(3, 0, 1, 2, 4, 5), "z_lo")
+        .transpose(2, 3, 1, 4, 0, 5)
         .reshape(row_count, 2 * z_count * inputs)
     )
-
     high_rows = high_count * block_rows
-    gain_sum = sum_parts(grad_z[:, high_rows:])
+    gain_sum = sum_parts(grad_z[:, :, high_rows:])
     gain_grad = (gain_sum + swap_near(gain_sum)).reshape(width)
     grad_all = (
-        grad_z[:, :high_rows]
-        .reshape(quarter, high_count, dp_count, row_count, features)
-        .transpose(2, 1, 0, 3, 4)
+        grad_z[:, :, :high_rows]
+        .reshape(quarter, 2, high_count, dp_count, row_count, features)
+        .transpose(3, 2, 1, 0, 4, 5)
         .reshape(tokens, features)
     )
+
+    other_grad = swap_cores(other_sent)
+    gate_weight_grad = jnp.where(on_first, own_grad, other_grad)
+    up_weight_grad = jnp.where(on_first, other_grad, own_grad)
 
     def add_near(sums):
         kept = lax.dynamic_index_in_dim(sums, here, 0, keepdims=False)
@@ -334,8 +338,8 @@
 def solution(mesh):
     tensor_count, dp_count = mesh.shape["tensor"], mesh.shape["dp"]
     fine = Mesh(
-        mesh.devices.reshape(2, tensor_count // 8, 4, dp_count // 4, 2, 2),
-        ("y_lo", "z_hi", "z_lo", "x", "y_hi", "core"),
+        mesh.devices.reshape(2, 2, 2, tensor_count // 8, dp_count // 4, 2, 2),
+        ("y_lo", "z_top", "z_mid", "z_lo", "x", "y_hi", "core"),
     )
     tensor_axes = ("y_lo",) + z_axes
     dp_axes = ("x", "y_hi", "core")

time: 268 us -> 301 us (1.12)
  starting transfers between devices: 160 us -> 179 us
  other arithmetic: 14.2 us -> 23.1 us
  waiting for transfers between devices: 50.9 us -> 58.2 us
  local copies, waits for them, and re-layouts: 25.1 us -> 21.8 us
    ppermute x0 -> x3, starting transfers between devices: none -> 26.3 us  [gather_pair(): other = lax.ppermute(block, axis, [(0, 1), (1, 0)])]
    all_to_all x7 -> x5, starting transfers between devices: 66.1 us -> 46.5 us  [exchange(): return lax.all_to_all(blocks, axes, split_axis=0, concat_axis=0, tiled=True)]
    all_to_all x7 -> x5, waiting for transfers between devices: 18.6 us -> 3.06 us  [exchange(): return lax.all_to_all(blocks, axes, split_axis=0, concat_axis=0, tiled=True)]
    ppermute x0 -> x3, waiting for transfers between devices: none -> 11.5 us  [gather_pair(): other = lax.ppermute(block, axis, [(0, 1), (1, 0)])]
    ppermute x2 -> x3, starting transfers between devices: 11.2 us -> 20.4 us  [trade_pair(): other = lax.ppermute(sent, axis_name, [(0, 1), (1, 0)])]
    ppermute x12, waiting for transfers between devices: 13.3 us -> 21.6 us  [from_above(): lax.ppermute(value, axes, [((i + distance) % count, i) for i in range(cou...]
    ppermute x12, starting transfers between devices: 43.2 us -> 48.8 us  [from_above(): lax.ppermute(value, axes, [((i + distance) % count, i) for i in range(cou...]
    another operation x5, other arithmetic: 0.47 us -> 5.03 us  [by_near(): jnp.stack([jnp.where(near_first, own, near), jnp.where(near_first, near,...]
  transfers between devices with their start and end apart: 34 -> 36, of which waited for: 14 -> 13; matrix products, arithmetic and copies ran while one was open for 14% -> 14% of each run, Pallas kernels for 0% -> 0%
where the time goes in v11:
time: 301 us; the launch traced here: 298 us
  starting transfers between devices  179 us (59%)
  waiting for transfers between devices  58.2 us (19%)
  other arithmetic  23.1 us (8%)
  local copies, waits for them, and re-layouts  21.8 us (7%)
  matrix products  14.4 us (5%)
    ppermute x12, starting transfers between devices, from_above(): lax.ppermute(value, axes, [((i + distance) % count, i) for i in range(cou...  48.8 us
    all_to_all x5, starting transfers between devices, exchange(): return lax.all_to_all(blocks, axes, split_axis=0, concat_axis=0, tiled=True)  46.5 us
    ppermute x3, starting transfers between devices, gather_pair(): other = lax.ppermute(block, axis, [(0, 1), (1, 0)])  26.3 us
    ppermute x12, waiting for transfers between devices, from_above(): lax.ppermute(value, axes, [((i + distance) % count, i) for i in range(cou...  21.6 us
    ppermute x3, starting transfers between devices, trade_pair(): other = lax.ppermute(sent, axis_name, [(0, 1), (1, 0)])  20.4 us
    ppermute x5, waiting for transfers between devices, swap_near(): return lax.ppermute(value, 'y_lo', [(0, 1), (1, 0)])  17.2 us
    ppermute x5, starting transfers between devices, swap_cores(): return lax.ppermute(value, 'core', [(0, 1), (1, 0)])  14.2 us
    ppermute x5, starting transfers between devices, swap_near(): return lax.ppermute(value, 'y_lo', [(0, 1), (1, 0)])  13.1 us
  transfers between devices with their start and end apart: 36, of which 13 were waited for; matrix products, arithmetic and copies ran while one was open for 14% of the time, Pallas kernels for 0%

profile of v11, /device:TPU:1, one launch (start us, length us, event | category | flops | bytes accessed | tf_op | source)
XLA Modules:
  0.0 298.1 jit_solution(5579272234865726204)
XLA Ops:
  2.0 4.0 %collective-permute-start.1 = (bf16[2,896,256]{2,1,0:T(8,128)(2,1)S(1)}, bf16[2,896,256]{2,1,0:T(8,128)(2,1)S(1)}, u32[]{:S(2)}, u32[]{:S(2)}) collective-permute-start(bf16[2,896,256]{2,1,0:T(8,128)(2,1)S(1)} %pad_maximum_fusion.2), channel_id=1, source_target_pairs={{0,256},{256,0},{1,257},{257,1},{2,258},{258,2},{3,259},{259,3},{4... | collective-permute-start | bytes 2752520 | tf_op jit(solution)/shard_map/ppermute | solution.py:37
  11.4 6.7 %collective-permute-start = (bf16[4,2,12,256]{3,1,2,0:T(2,128)(2,1)S(1)}, bf16[4,2,12,256]{3,1,2,0:T(2,128)(2,1)S(1)}, u32[]{:S(2)}, u32[]{:S(2)}) collective-permute-start(bf16[4,2,12,256]{3,1,2,0:T(2,128)(2,1)S(1)} %bitcast.261), channel_id=1, source_target_pairs={{0,1},{1,0},{2,3},{3,2},{4,5},{5,4},{6,7},{7,6},{8,9},{9,8},{10,11... | collective-permute-start | bytes 147464 | tf_op jit(solution)/shard_map/ppermute | solution.py:81
  18.0 11.1 %all-to-all-start = ((bf16[16,8,2048]{2,1,0:T(8,128)(2,1)}), bf16[16,8,2048]{2,1,0:T(8,128)(2,1)S(1)}, u32[]{:S(2)}, u32[]{:S(2)}) async-start(bf16[16,8,2048]{2,1,0:T(8,128)(2,1)} %reshape.242), calls=%async_computation | async-start | bytes 1048576 | tf_op jit(solution)/shard_map/all_to_all | solution.py:29
  29.7 4.5 %collective-permute-start.2 = (bf16[2,4,12,256]{3,1,2,0:T(4,128)(2,1)S(1)}, bf16[2,4,12,256]{3,1,2,0:T(4,128)(2,1)S(1)}, u32[]{:S(2)}, u32[]{:S(2)}) collective-permute-start(bf16[2,4,12,256]{3,1,2,0:T(4,128)(2,1)S(1)} %bitcast.262), channel_id=1, source_target_pairs={{0,2},{2,0},{1,3},{3,1},{4,6},{6,4},{5,7},{7,5},{8,10},{10,8},{9,1... | collective-permute-start | bytes 147464 | tf_op jit(solution)/shard_map/ppermute | solution.py:81
  36.6 4.4 %collective-permute-start.3 = (bf16[2,2,12,256]{3,1,2,0:T(2,128)(2,1)S(1)}, bf16[2,2,12,256]{3,1,2,0:T(2,128)(2,1)S(1)}, u32[]{:S(2)}, u32[]{:S(2)}) collective-permute-start(bf16[2,2,12,256]{3,1,2,0:T(2,128)(2,1)S(1)} %bitcast.267), channel_id=1, source_target_pairs={{0,12},{4,0},{8,4},{12,8},{1,13},{5,1},{9,5},{13,9},{2,14},{6,2},{... | collective-permute-start | bytes 73736 | tf_op jit(solution)/shard_map/ppermute | solution.py:89
  57.2 11.8 %all-to-all-start.1 = ((bf16[16,64,2048]{2,1,0:T(8,128)(2,1)}), bf16[16,64,2048]{2,1,0:T(8,128)(2,1)}, u32[]{:S(2)}, u32[]{:S(2)}) async-start(bf16[16,64,2048]{2,1,0:T(8,128)(2,1)} %bitcast.221), calls=%async_computation.1 | async-start | bytes 8388608 | tf_op jit(solution)/shard_map/all_to_all | solution.py:29
  69.0 4.3 %collective-permute-start.9 = (bf16[256,256]{1,0:T(8,128)(2,1)S(1)}, bf16[256,256]{1,0:T(8,128)(2,1)S(1)}, u32[]{:S(2)}, u32[]{:S(2)}) collective-permute-start(bf16[256,256]{1,0:T(8,128)(2,1)S(1)} %copy-done.16), channel_id=1, source_target_pairs={{0,64},{64,0},{1,65},{65,1},{2,66},{66,2},{3,67},{67,3},{4,68},{68... | collective-permute-start | bytes 393224 | tf_op jit(solution)/shard_map/ppermute | solution.py:73
  76.9 11.4 %collective-permute-done.9 = bf16[256,256]{1,0:T(8,128)(2,1)S(1)} collective-permute-done((bf16[256,256]{1,0:T(8,128)(2,1)S(1)}, bf16[256,256]{1,0:T(8,128)(2,1)S(1)}, u32[]{:S(2)}, u32[]{:S(2)}) %collective-permute-start.9) | collective-permute-done | bytes 131104 | tf_op jit(solution)/shard_map/ppermute | solution.py:73
  90.3 9.6 %collective-permute-start.7 = (bf16[64,256]{1,0:T(8,128)(2,1)S(1)}, bf16[64,256]{1,0:T(8,128)(2,1)S(1)}, u32[]{:S(2)}, u32[]{:S(2)}) collective-permute-start(bf16[64,256]{1,0:T(8,128)(2,1)S(1)} %copy-done.18), channel_id=1, source_target_pairs={{128,0},{144,16},{160,32},{176,48},{192,64},{208,80},{224,96},{240... | collective-permute-start | bytes 98312 | tf_op jit(solution)/shard_map/ppermute | solution.py:42
  99.9 7.3 %collective-permute-start.6 = (bf16[64,256]{1,0:T(8,128)(2,1)S(1)}, bf16[64,256]{1,0:T(8,128)(2,1)S(1)}, u32[]{:S(2)}, u32[]{:S(2)}) collective-permute-start(bf16[64,256]{1,0:T(8,128)(2,1)S(1)} %copy-done.18), channel_id=1, source_target_pairs={{64,0},{80,16},{96,32},{112,48},{128,64},{144,80},{160,96},{176,11... | collective-permute-start | bytes 98312 | tf_op jit(solution)/shard_map/ppermute | solution.py:42
  111.1 4.7 %collective-permute-start.11 = (bf16[4,64,256]{2,1,0:T(8,128)(2,1)S(1)}, bf16[4,64,256]{2,1,0:T(8,128)(2,1)S(1)}, u32[]{:S(2)}, u32[]{:S(2)}) collective-permute-start(bf16[4,64,256]{2,1,0:T(8,128)(2,1)S(1)} %pad_maximum_fusion.8), channel_id=1, source_target_pairs={{32,0},{48,16},{64,32},{80,48},{96,64},{112,80},{128,96},{144,112}... | collective-permute-start | bytes 393224 | tf_op jit(solution)/shard_map/ppermute | solution.py:42
  117.9 3.3 %collective-permute-start.15 = (bf16[2,256,256]{2,1,0:T(8,128)(2,1)S(1)}, bf16[2,256,256]{2,1,0:T(8,128)(2,1)S(1)}, u32[]{:S(2)}, u32[]{:S(2)}) collective-permute-start(bf16[2,256,256]{2,1,0:T(8,128)(2,1)S(1)} %pad_maximum_fusion.6), channel_id=1, source_target_pairs={{48,0},{0,16},{16,32},{32,48},{49,1},{1,17},{17,33},{33,49},{50,2}... | collective-permute-start | bytes 786440 | tf_op jit(solution)/shard_map/ppermute | solution.py:42
  121.2 3.7 %collective-permute-start.14 = (bf16[2,256,256]{2,1,0:T(8,128)(2,1)S(1)}, bf16[2,256,256]{2,1,0:T(8,128)(2,1)S(1)}, u32[]{:S(2)}, u32[]{:S(2)}) collective-permute-start(bf16[2,256,256]{2,1,0:T(8,128)(2,1)S(1)} %pad_maximum_fusion.6), channel_id=1, source_target_pairs={{32,0},{48,16},{0,32},{16,48},{33,1},{49,17},{1,33},{17,49},{34,2}... | collective-permute-start | bytes 786440 | tf_op jit(solution)/shard_map/ppermute | solution.py:42
  128.5 3.5 %collective-permute-done.15 = bf16[2,256,256]{2,1,0:T(8,128)(2,1)S(1)} collective-permute-done((bf16[2,256,256]{2,1,0:T(8,128)(2,1)S(1)}, bf16[2,256,256]{2,1,0:T(8,128)(2,1)S(1)}, u32[]{:S(2)}, u32[]{:S(2)}) %collective-permute-start.15) | collective-permute-done | bytes 262176 | tf_op jit(solution)/shard_map/ppermute | solution.py:42
  132.1 11.2 %collective-permute-done.14 = bf16[2,256,256]{2,1,0:T(8,128)(2,1)S(1)} collective-permute-done((bf16[2,256,256]{2,1,0:T(8,128)(2,1)S(1)}, bf16[2,256,256]{2,1,0:T(8,128)(2,1)S(1)}, u32[]{:S(2)}, u32[]{:S(2)}) %collective-permute-start.14) | collective-permute-done | bytes 262176 | tf_op jit(solution)/shard_map/ppermute | solution.py:42
  143.4 3.7 %fusion.50 = f32[1024,256]{1,0:T(8,128)S(1)} fusion(bf16[1024,2048]{1,0:T(8,128)(2,1)} %bitcast.31, bf16[2048,256]{1,0:T(8,128)(2,1)} %collective-permute-done.16), kind=kOutput, calls=%fused_computation.160 | convolution fusion | flops 1073741824 | bytes 6291456 | tf_op jit(solution)/shard_map/dot_general | solution.py:218
  147.2 3.8 %collective-permute-start.17 = (f32[1024,256]{1,0:T(8,128)S(1)}, f32[1024,256]{1,0:T(8,128)S(1)}, u32[]{:S(2)}, u32[]{:S(2)}) collective-permute-start(f32[1024,256]{1,0:T(8,128)S(1)} %fusion.50), channel_id=1, source_target_pairs={{0,1},{1,0},{2,3},{3,2},{4,5},{5,4},{6,7},{7,6},{8,9},{9,8},{10,11... | collective-permute-start | bytes 3145736 | tf_op jit(solution)/shard_map/ppermute | solution.py:33
  151.1 3.4 %fusion.49 = f32[1024,256]{1,0:T(8,128)S(1)} fusion(bf16[1024,2048]{1,0:T(8,128)(2,1)} %bitcast.31, bf16[2048,256]{1,0:T(8,128)(2,1)S(1)} %bitcast.237), kind=kOutput, calls=%fused_computation.159 | convolution fusion | flops 1073741824 | bytes 6291456 | tf_op jit(solution)/shard_map/dot_general | solution.py:219
  155.9 11.0 %all-to-all-start.2 = ((bf16[16,64,256]{2,1,0:T(8,128)(2,1)}), bf16[16,64,256]{2,1,0:T(8,128)(2,1)S(1)}, u32[]{:S(2)}, u32[]{:S(2)}) async-start(bf16[16,64,256]{2,1,0:T(8,128)(2,1)} %copy.265), calls=%async_computation.2 | async-start | bytes 1048576 | tf_op jit(solution)/shard_map/all_to_all | solution.py:29
  175.2 4.8 %fusion.7 = f32[2048,512]{1,0:T(8,128)S(1)} fusion(bf16[1024,2048]{1,0:T(8,128)(2,1)} %bitcast.31, bf16[1024,256]{1,0:T(8,128)(2,1)} %collective-permute-done.18, bf16[1024,256]{1,0:T(8,128)(2,1)S(1)} %reshape.254), kind=kOutput, calls=%fused_computation.17 | convolution fusion | flops 2149580800 | bytes 9437184 | tf_op jit(solution)/shard_map/dot_general | solution.py:25
  183.2 13.3 %collective-permute-done.20 = bf16[4,2,256,256]{3,2,1,0:T(8,128)(2,1)} collective-permute-done((bf16[4,2,256,256]{3,2,1,0:T(8,128)(2,1)S(1)}, bf16[4,2,256,256]{3,2,1,0:T(8,128)(2,1)}, u32[]{:S(2)}, u32[]{:S(2)}) %collective-permute-start.20) | collective-permute-done | bytes 1048608 | tf_op jit(solution)/shard_map/ppermute | solution.py:37
  198.4 7.5 %all-to-all-start.3 = ((f32[16,1,320]{2,1,0:T(1,128)}), f32[16,1,320]{2,1,0:T(1,128)S(1)}, u32[]{:S(2)}, u32[]{:S(2)}) async-start(f32[16,1,320]{2,1,0:T(1,128)} %broadcast_in_dim.8), calls=%async_computation.3 | async-start | bytes 49152 | tf_op jit(solution)/shard_map/all_to_all | solution.py:29
  213.5 12.3 %collective-permute-start.21 = (bf16[96,256]{1,0:T(8,128)(2,1)S(1)}, bf16[96,256]{1,0:T(8,128)(2,1)S(1)}, u32[]{:S(2)}, u32[]{:S(2)}) collective-permute-start(bf16[96,256]{1,0:T(8,128)(2,1)S(1)} %pad_maximum_fusion.12), channel_id=1, source_target_pairs={{0,128},{128,0},{1,129},{129,1},{2,130},{130,2},{3,131},{131,3},{4... | collective-permute-start | bytes 147464 | tf_op jit(solution)/shard_map/ppermute | solution.py:73
  227.5 9.8 %collective-permute-start.22 = (bf16[160,256]{1,0:T(8,128)(2,1)S(1)}, bf16[160,256]{1,0:T(8,128)(2,1)S(1)}, u32[]{:S(2)}, u32[]{:S(2)}) collective-permute-start(bf16[160,256]{1,0:T(8,128)(2,1)S(1)} %pad_maximum_fusion.11), channel_id=1, source_target_pairs={{0,64},{64,0},{1,65},{65,1},{2,66},{66,2},{3,67},{67,3},{4,68},{68... | collective-permute-start | bytes 245768 | tf_op jit(solution)/shard_map/ppermute | solution.py:73
  239.2 5.0 %all-to-all-start.4 = ((bf16[16,8,4096]{2,1,0:T(8,128)(2,1)}), bf16[16,8,4096]{2,1,0:T(8,128)(2,1)S(1)}, u32[]{:S(2)}, u32[]{:S(2)}) async-start(bf16[16,8,4096]{2,1,0:T(8,128)(2,1)} %fusion), calls=%async_computation.4 | async-start | bytes 2097152 | tf_op jit(solution)/shard_map/all_to_all | solution.py:29
  246.9 5.0 %collective-permute-start.24 = (bf16[2,160,256]{2,1,0:T(8,128)(2,1)}, bf16[2,160,256]{2,1,0:T(8,128)(2,1)S(1)}, u32[]{:S(2)}, u32[]{:S(2)}) collective-permute-start(bf16[2,160,256]{2,1,0:T(8,128)(2,1)} %get-tuple-element.82), channel_id=1, source_target_pairs={{32,0},{48,16},{0,32},{16,48},{33,1},{49,17},{1,33},{17,49},{34,2}... | collective-permute-start | bytes 491528 | tf_op jit(solution)/shard_map/ppermute | solution.py:42
  251.9 4.3 %collective-permute-start.23 = (bf16[2,160,256]{2,1,0:T(8,128)(2,1)}, bf16[2,160,256]{2,1,0:T(8,128)(2,1)S(1)}, u32[]{:S(2)}, u32[]{:S(2)}) collective-permute-start(bf16[2,160,256]{2,1,0:T(8,128)(2,1)} %get-tuple-element.82), channel_id=1, source_target_pairs={{16,0},{32,16},{48,32},{0,48},{17,1},{33,17},{49,33},{1,49},{18,2}... | collective-permute-start | bytes 491528 | tf_op jit(solution)/shard_map/ppermute | solution.py:42
  257.4 4.7 %collective-permute-done.24 = bf16[2,160,256]{2,1,0:T(8,128)(2,1)S(1)} collective-permute-done((bf16[2,160,256]{2,1,0:T(8,128)(2,1)}, bf16[2,160,256]{2,1,0:T(8,128)(2,1)S(1)}, u32[]{:S(2)}, u32[]{:S(2)}) %collective-permute-start.24) | collective-permute-done | bytes 163872 | tf_op jit(solution)/shard_map/ppermute | solution.py:42
  267.8 9.2 %collective-permute-start.27 = (bf16[4,4096]{1,0:T(4,128)(2,1)}, bf16[4,4096]{1,0:T(4,128)(2,1)}, u32[]{:S(2)}, u32[]{:S(2)}) collective-permute-start(bf16[4,4096]{1,0:T(4,128)(2,1)} %broadcast_select_fusion.14), channel_id=1, source_target_pairs={{0,128},{128,0},{1,129},{129,1},{2,130},{130,2},{3,131},{131,3},{4... | collective-permute-start | bytes 98312 | tf_op jit(solution)/shard_map/ppermute | solution.py:81
  277.0 3.7 %collective-permute-start.28 = (f32[896,256]{1,0:T(8,128)}, f32[896,256]{1,0:T(8,128)}, u32[]{:S(2)}, u32[]{:S(2)}) collective-permute-start(f32[896,256]{1,0:T(8,128)} %get-tuple-element.51), channel_id=1, source_target_pairs={{0,1},{1,0},{2,3},{3,2},{4,5},{5,4},{6,7},{7,6},{8,9},{9,8},{10,11... | collective-permute-start | bytes 2752520 | tf_op jit(solution)/shard_map/ppermute | solution.py:33
  285.1 3.4 %collective-permute-start.29 = (f32[2,128,256]{2,1,0:T(8,128)S(1)}, f32[2,128,256]{2,1,0:T(8,128)S(1)}, u32[]{:S(2)}, u32[]{:S(2)}) collective-permute-start(f32[2,128,256]{2,1,0:T(8,128)S(1)} %fusion.28), channel_id=1, source_target_pairs={{0,256},{256,0},{1,257},{257,1},{2,258},{258,2},{3,259},{259,3},{4... | collective-permute-start | bytes 786440 | tf_op jit(solution)/shard_map/ppermute | solution.py:37
  291.0 3.9 %collective-permute-done.29 = f32[2,128,256]{2,1,0:T(8,128)S(1)} collective-permute-done((f32[2,128,256]{2,1,0:T(8,128)S(1)}, f32[2,128,256]{2,1,0:T(8,128)S(1)}, u32[]{:S(2)}, u32[]{:S(2)}) %collective-permute-start.29) | collective-permute-done | bytes 262176 | tf_op jit(solution)/shard_map/ppermute | solution.py:37
  (224 shorter events, 85.7 us)
Async XLA Ops:
  2.0 27.5 %collective-permute-start.1 = (bf16[2,896,256]{2,1,0:T(8,128)(2,1)S(1)}, bf16[2,896,256]{2,1,0:T(8,128)(2,1)S(1)}, u32[]{:S(2)}, u32[]{:S(2)}) collective-permute-start(bf16[2,896,256]{2,1,0:T(8,128)(2,1)S(1)} %pad_maximum_fusion.2), channel_id=1, source_target_pairs={{0,256},{256,0},{1,257},{257,1},{2,258},{258,2},{3,259},{259,3},{4... | collective-permute-start | bytes 2752520 | tf_op jit(solution)/shard_map/ppermute | solution.py:37
  11.4 17.8 %collective-permute-start = (bf16[4,2,12,256]{3,1,2,0:T(2,128)(2,1)S(1)}, bf16[4,2,12,256]{3,1,2,0:T(2,128)(2,1)S(1)}, u32[]{:S(2)}, u32[]{:S(2)}) collective-permute-start(bf16[4,2,12,256]{3,1,2,0:T(2,128)(2,1)S(1)} %bitcast.261), channel_id=1, source_target_pairs={{0,1},{1,0},{2,3},{3,2},{4,5},{5,4},{6,7},{7,6},{8,9},{9,8},{10,11... | collective-permute-start | bytes 147464 | tf_op jit(solution)/shard_map/ppermute | solution.py:81
  18.0 35.6 %all-to-all-start = ((bf16[16,8,2048]{2,1,0:T(8,128)(2,1)}), bf16[16,8,2048]{2,1,0:T(8,128)(2,1)S(1)}, u32[]{:S(2)}, u32[]{:S(2)}) async-start(bf16[16,8,2048]{2,1,0:T(8,128)(2,1)} %reshape.242), calls=%async_computation | async-start | bytes 1048576 | tf_op jit(solution)/shard_map/all_to_all | solution.py:29
  36.6 10.2 %collective-permute-start.3 = (bf16[2,2,12,256]{3,1,2,0:T(2,128)(2,1)S(1)}, bf16[2,2,12,256]{3,1,2,0:T(2,128)(2,1)S(1)}, u32[]{:S(2)}, u32[]{:S(2)}) collective-permute-start(bf16[2,2,12,256]{3,1,2,0:T(2,128)(2,1)S(1)} %bitcast.267), channel_id=1, source_target_pairs={{0,12},{4,0},{8,4},{12,8},{1,13},{5,1},{9,5},{13,9},{2,14},{6,2},{... | collective-permute-start | bytes 73736 | tf_op jit(solution)/shard_map/ppermute | solution.py:89
  57.2 86.2 %all-to-all-start.1 = ((bf16[16,64,2048]{2,1,0:T(8,128)(2,1)}), bf16[16,64,2048]{2,1,0:T(8,128)(2,1)}, u32[]{:S(2)}, u32[]{:S(2)}) async-start(bf16[16,64,2048]{2,1,0:T(8,128)(2,1)} %bitcast.221), calls=%async_computation.1 | async-start | bytes 8388608 | tf_op jit(solution)/shard_map/all_to_all | solution.py:29
  69.0 19.3 %collective-permute-start.9 = (bf16[256,256]{1,0:T(8,128)(2,1)S(1)}, bf16[256,256]{1,0:T(8,128)(2,1)S(1)}, u32[]{:S(2)}, u32[]{:S(2)}) collective-permute-start(bf16[256,256]{1,0:T(8,128)(2,1)S(1)} %copy-done.16), channel_id=1, source_target_pairs={{0,64},{64,0},{1,65},{65,1},{2,66},{66,2},{3,67},{67,3},{4,68},{68... | collective-permute-start | bytes 393224 | tf_op jit(solution)/shard_map/ppermute | solution.py:73
  74.5 68.9 %collective-permute-start.16 = (bf16[2048,256]{1,0:T(8,128)(2,1)}, bf16[2048,256]{1,0:T(8,128)(2,1)}, u32[]{:S(2)}, u32[]{:S(2)}) collective-permute-start(bf16[2048,256]{1,0:T(8,128)(2,1)} %bitcast.54), channel_id=1, source_target_pairs={{0,1},{1,0},{2,3},{3,2},{4,5},{5,4},{6,7},{7,6},{8,9},{9,8},{10,11... | collective-permute-start | bytes 3145736 | tf_op jit(solution)/shard_map/ppermute | solution.py:33
  88.3 18.9 %collective-permute-start.8 = (bf16[64,256]{1,0:T(8,128)(2,1)S(1)}, bf16[64,256]{1,0:T(8,128)(2,1)S(1)}, u32[]{:S(2)}, u32[]{:S(2)}) collective-permute-start(bf16[64,256]{1,0:T(8,128)(2,1)S(1)} %copy-done.18), channel_id=1, source_target_pairs={{192,0},{208,16},{224,32},{240,48},{0,64},{16,80},{32,96},{48,112}... | collective-permute-start | bytes 98312 | tf_op jit(solution)/shard_map/ppermute | solution.py:42
  90.3 16.9 %collective-permute-start.7 = (bf16[64,256]{1,0:T(8,128)(2,1)S(1)}, bf16[64,256]{1,0:T(8,128)(2,1)S(1)}, u32[]{:S(2)}, u32[]{:S(2)}) collective-permute-start(bf16[64,256]{1,0:T(8,128)(2,1)S(1)} %copy-done.18), channel_id=1, source_target_pairs={{128,0},{144,16},{160,32},{176,48},{192,64},{208,80},{224,96},{240... | collective-permute-start | bytes 98312 | tf_op jit(solution)/shard_map/ppermute | solution.py:42
  99.9 9.3 %collective-permute-start.6 = (bf16[64,256]{1,0:T(8,128)(2,1)S(1)}, bf16[64,256]{1,0:T(8,128)(2,1)S(1)}, u32[]{:S(2)}, u32[]{:S(2)}) collective-permute-start(bf16[64,256]{1,0:T(8,128)(2,1)S(1)} %copy-done.18), channel_id=1, source_target_pairs={{64,0},{80,16},{96,32},{112,48},{128,64},{144,80},{160,96},{176,11... | collective-permute-start | bytes 98312 | tf_op jit(solution)/shard_map/ppermute | solution.py:42
  109.2 12.0 %collective-permute-start.12 = (bf16[4,64,256]{2,1,0:T(8,128)(2,1)S(1)}, bf16[4,64,256]{2,1,0:T(8,128)(2,1)S(1)}, u32[]{:S(2)}, u32[]{:S(2)}) collective-permute-start(bf16[4,64,256]{2,1,0:T(8,128)(2,1)S(1)} %pad_maximum_fusion.8), channel_id=1, source_target_pairs={{240,0},{0,16},{16,32},{32,48},{48,64},{64,80},{80,96},{96,112},{1... | collective-permute-start | bytes 393224 | tf_op jit(solution)/shard_map/ppermute | solution.py:42
  111.1 13.8 %collective-permute-start.11 = (bf16[4,64,256]{2,1,0:T(8,128)(2,1)S(1)}, bf16[4,64,256]{2,1,0:T(8,128)(2,1)S(1)}, u32[]{:S(2)}, u32[]{:S(2)}) collective-permute-start(bf16[4,64,256]{2,1,0:T(8,128)(2,1)S(1)} %pad_maximum_fusion.8), channel_id=1, source_target_pairs={{32,0},{48,16},{64,32},{80,48},{96,64},{112,80},{128,96},{144,112}... | collective-permute-start | bytes 393224 | tf_op jit(solution)/shard_map/ppermute | solution.py:42
  115.9 12.3 %collective-permute-start.10 = (bf16[4,64,256]{2,1,0:T(8,128)(2,1)S(1)}, bf16[4,64,256]{2,1,0:T(8,128)(2,1)S(1)}, u32[]{:S(2)}, u32[]{:S(2)}) collective-permute-start(bf16[4,64,256]{2,1,0:T(8,128)(2,1)S(1)} %pad_maximum_fusion.8), channel_id=1, source_target_pairs={{16,0},{32,16},{48,32},{64,48},{80,64},{96,80},{112,96},{128,112},... | collective-permute-start | bytes 393224 | tf_op jit(solution)/shard_map/ppermute | solution.py:42
  117.9 14.1 %collective-permute-start.15 = (bf16[2,256,256]{2,1,0:T(8,128)(2,1)S(1)}, bf16[2,256,256]{2,1,0:T(8,128)(2,1)S(1)}, u32[]{:S(2)}, u32[]{:S(2)}) collective-permute-start(bf16[2,256,256]{2,1,0:T(8,128)(2,1)S(1)} %pad_maximum_fusion.6), channel_id=1, source_target_pairs={{48,0},{0,16},{16,32},{32,48},{49,1},{1,17},{17,33},{33,49},{50,2}... | collective-permute-start | bytes 786440 | tf_op jit(solution)/shard_map/ppermute | solution.py:42
  121.2 22.1 %collective-permute-start.14 = (bf16[2,256,256]{2,1,0:T(8,128)(2,1)S(1)}, bf16[2,256,256]{2,1,0:T(8,128)(2,1)S(1)}, u32[]{:S(2)}, u32[]{:S(2)}) collective-permute-start(bf16[2,256,256]{2,1,0:T(8,128)(2,1)S(1)} %pad_maximum_fusion.6), channel_id=1, source_target_pairs={{32,0},{48,16},{0,32},{16,48},{33,1},{49,17},{1,33},{17,49},{34,2}... | collective-permute-start | bytes 786440 | tf_op jit(solution)/shard_map/ppermute | solution.py:42
  125.0 18.3 %collective-permute-start.13 = (bf16[2,256,256]{2,1,0:T(8,128)(2,1)S(1)}, bf16[2,256,256]{2,1,0:T(8,128)(2,1)S(1)}, u32[]{:S(2)}, u32[]{:S(2)}) collective-permute-start(bf16[2,256,256]{2,1,0:T(8,128)(2,1)S(1)} %pad_maximum_fusion.6), channel_id=1, source_target_pairs={{16,0},{32,16},{48,32},{0,48},{17,1},{33,17},{49,33},{1,49},{18,2}... | collective-permute-start | bytes 786440 | tf_op jit(solution)/shard_map/ppermute | solution.py:42
  147.2 7.4 %collective-permute-start.17 = (f32[1024,256]{1,0:T(8,128)S(1)}, f32[1024,256]{1,0:T(8,128)S(1)}, u32[]{:S(2)}, u32[]{:S(2)}) collective-permute-start(f32[1024,256]{1,0:T(8,128)S(1)} %fusion.50), channel_id=1, source_target_pairs={{0,1},{1,0},{2,3},{3,2},{4,5},{5,4},{6,7},{7,6},{8,9},{9,8},{10,11... | collective-permute-start | bytes 3145736 | tf_op jit(solution)/shard_map/ppermute | solution.py:33
  155.9 40.6 %all-to-all-start.2 = ((bf16[16,64,256]{2,1,0:T(8,128)(2,1)}), bf16[16,64,256]{2,1,0:T(8,128)(2,1)S(1)}, u32[]{:S(2)}, u32[]{:S(2)}) async-start(bf16[16,64,256]{2,1,0:T(8,128)(2,1)} %copy.265), calls=%async_computation.2 | async-start | bytes 1048576 | tf_op jit(solution)/shard_map/all_to_all | solution.py:29
  167.5 7.7 %collective-permute-start.18 = (bf16[1024,256]{1,0:T(8,128)(2,1)S(1)}, bf16[1024,256]{1,0:T(8,128)(2,1)}, u32[]{:S(2)}, u32[]{:S(2)}) collective-permute-start(bf16[1024,256]{1,0:T(8,128)(2,1)S(1)} %reshape.254), channel_id=1, source_target_pairs={{0,1},{1,0},{2,3},{3,2},{4,5},{5,4},{6,7},{7,6},{8,9},{9,8},{10,11... | collective-permute-start | bytes 1572872 | tf_op jit(solution)/shard_map/ppermute | solution.py:33
  170.0 26.5 %collective-permute-start.20 = (bf16[4,2,256,256]{3,2,1,0:T(8,128)(2,1)S(1)}, bf16[4,2,256,256]{3,2,1,0:T(8,128)(2,1)}, u32[]{:S(2)}, u32[]{:S(2)}) collective-permute-start(bf16[4,2,256,256]{3,2,1,0:T(8,128)(2,1)S(1)} %pad_maximum_fusion.1), channel_id=1, source_target_pairs={{0,256},{256,0},{1,257},{257,1},{2,258},{258,2},{3,259},{259,3},{4... | collective-permute-start | bytes 3145736 | tf_op jit(solution)/shard_map/ppermute | solution.py:37
  173.1 10.1 %collective-permute-start.19 = (bf16[1024,256]{1,0:T(8,128)(2,1)S(1)}, bf16[1024,256]{1,0:T(8,128)(2,1)S(1)}, u32[]{:S(2)}, u32[]{:S(2)}) collective-permute-start(bf16[1024,256]{1,0:T(8,128)(2,1)S(1)} %pad_maximum_fusion.5), channel_id=1, source_target_pairs={{0,1},{1,0},{2,3},{3,2},{4,5},{5,4},{6,7},{7,6},{8,9},{9,8},{10,11... | collective-permute-start | bytes 1572872 | tf_op jit(solution)/shard_map/ppermute | solution.py:33
  198.4 14.9 %all-to-all-start.3 = ((f32[16,1,320]{2,1,0:T(1,128)}), f32[16,1,320]{2,1,0:T(1,128)S(1)}, u32[]{:S(2)}, u32[]{:S(2)}) async-start(f32[16,1,320]{2,1,0:T(1,128)} %broadcast_in_dim.8), calls=%async_computation.3 | async-start | bytes 49152 | tf_op jit(solution)/shard_map/all_to_all | solution.py:29
  208.3 54.0 %collective-permute-start.26 = (bf16[896,512]{1,0:T(8,128)(2,1)}, bf16[896,512]{1,0:T(8,128)(2,1)}, u32[]{:S(2)}, u32[]{:S(2)}) collective-permute-start(bf16[896,512]{1,0:T(8,128)(2,1)} %fusion.11), channel_id=1, source_target_pairs={{0,256},{256,0},{1,257},{257,1},{2,258},{258,2},{3,259},{259,3},{4... | collective-permute-start | bytes 2752520 | tf_op jit(solution)/shard_map/ppermute | solution.py:37
  213.5 13.8 %collective-permute-start.21 = (bf16[96,256]{1,0:T(8,128)(2,1)S(1)}, bf16[96,256]{1,0:T(8,128)(2,1)S(1)}, u32[]{:S(2)}, u32[]{:S(2)}) collective-permute-start(bf16[96,256]{1,0:T(8,128)(2,1)S(1)} %pad_maximum_fusion.12), channel_id=1, source_target_pairs={{0,128},{128,0},{1,129},{129,1},{2,130},{130,2},{3,131},{131,3},{4... | collective-permute-start | bytes 147464 | tf_op jit(solution)/shard_map/ppermute | solution.py:73
  227.5 16.7 %collective-permute-start.22 = (bf16[160,256]{1,0:T(8,128)(2,1)S(1)}, bf16[160,256]{1,0:T(8,128)(2,1)S(1)}, u32[]{:S(2)}, u32[]{:S(2)}) collective-permute-start(bf16[160,256]{1,0:T(8,128)(2,1)S(1)} %pad_maximum_fusion.11), channel_id=1, source_target_pairs={{0,64},{64,0},{1,65},{65,1},{2,66},{66,2},{3,67},{67,3},{4,68},{68... | collective-permute-start | bytes 245768 | tf_op jit(solution)/shard_map/ppermute | solution.py:73
  239.2 26.3 %all-to-all-start.4 = ((bf16[16,8,4096]{2,1,0:T(8,128)(2,1)}), bf16[16,8,4096]{2,1,0:T(8,128)(2,1)S(1)}, u32[]{:S(2)}, u32[]{:S(2)}) async-start(bf16[16,8,4096]{2,1,0:T(8,128)(2,1)} %fusion), calls=%async_computation.4 | async-start | bytes 2097152 | tf_op jit(solution)/shard_map/all_to_all | solution.py:29
  245.0 12.4 %collective-permute-start.25 = (bf16[2,160,256]{2,1,0:T(8,128)(2,1)}, bf16[2,160,256]{2,1,0:T(8,128)(2,1)S(1)}, u32[]{:S(2)}, u32[]{:S(2)}) collective-permute-start(bf16[2,160,256]{2,1,0:T(8,128)(2,1)} %get-tuple-element.82), channel_id=1, source_target_pairs={{48,0},{0,16},{16,32},{32,48},{49,1},{1,17},{17,33},{33,49},{50,2}... | collective-permute-start | bytes 491528 | tf_op jit(solution)/shard_map/ppermute | solution.py:42
  246.9 15.2 %collective-permute-start.24 = (bf16[2,160,256]{2,1,0:T(8,128)(2,1)}, bf16[2,160,256]{2,1,0:T(8,128)(2,1)S(1)}, u32[]{:S(2)}, u32[]{:S(2)}) collective-permute-start(bf16[2,160,256]{2,1,0:T(8,128)(2,1)} %get-tuple-element.82), channel_id=1, source_target_pairs={{32,0},{48,16},{0,32},{16,48},{33,1},{49,17},{1,33},{17,49},{34,2}... | collective-permute-start | bytes 491528 | tf_op jit(solution)/shard_map/ppermute | solution.py:42
  251.9 10.4 %collective-permute-start.23 = (bf16[2,160,256]{2,1,0:T(8,128)(2,1)}, bf16[2,160,256]{2,1,0:T(8,128)(2,1)S(1)}, u32[]{:S(2)}, u32[]{:S(2)}) collective-permute-start(bf16[2,160,256]{2,1,0:T(8,128)(2,1)} %get-tuple-element.82), channel_id=1, source_target_pairs={{16,0},{32,16},{48,32},{0,48},{17,1},{33,17},{49,33},{1,49},{18,2}... | collective-permute-start | bytes 491528 | tf_op jit(solution)/shard_map/ppermute | solution.py:42
  267.8 21.3 %collective-permute-start.27 = (bf16[4,4096]{1,0:T(4,128)(2,1)}, bf16[4,4096]{1,0:T(4,128)(2,1)}, u32[]{:S(2)}, u32[]{:S(2)}) collective-permute-start(bf16[4,4096]{1,0:T(4,128)(2,1)} %broadcast_select_fusion.14), channel_id=1, source_target_pairs={{0,128},{128,0},{1,129},{129,1},{2,130},{130,2},{3,131},{131,3},{4... | collective-permute-start | bytes 98312 | tf_op jit(solution)/shard_map/ppermute | solution.py:81
  277.0 18.5 %collective-permute-start.28 = (f32[896,256]{1,0:T(8,128)}, f32[896,256]{1,0:T(8,128)}, u32[]{:S(2)}, u32[]{:S(2)}) collective-permute-start(f32[896,256]{1,0:T(8,128)} %get-tuple-element.51), channel_id=1, source_target_pairs={{0,1},{1,0},{2,3},{3,2},{4,5},{5,4},{6,7},{7,6},{8,9},{9,8},{10,11... | collective-permute-start | bytes 2752520 | tf_op jit(solution)/shard_map/ppermute | solution.py:33
  285.1 9.8 %collective-permute-start.29 = (f32[2,128,256]{2,1,0:T(8,128)S(1)}, f32[2,128,256]{2,1,0:T(8,128)S(1)}, u32[]{:S(2)}, u32[]{:S(2)}) collective-permute-start(f32[2,128,256]{2,1,0:T(8,128)S(1)} %fusion.28), channel_id=1, source_target_pairs={{0,256},{256,0},{1,257},{257,1},{2,258},{258,2},{3,259},{259,3},{4... | collective-permute-start | bytes 786440 | tf_op jit(solution)/shard_map/ppermute | solution.py:37
  (24 other events, 217.3 us)

commit v12 on v10

--- a/solution.py
+++ b/solution.py
@@ -297,7 +297,6 @@
         [grad_high[:, :block_rows].reshape(-1, features), *split_two(gain_high)]
     )
     grad_z = from_first(gather_ring(grad_quad, "z_lo"), "z_lo")
-    grad_z, joined_blocks = lax.optimization_barrier((grad_z, joined_blocks))
     joined_total = jnp.sum(joined_blocks.astype(wide), axis=0).astype(narrow)
     joined_high = exchange(
         joined_total.reshape(high_count, row_count, 2 * quarter * inputs), "z_hi"

time: 268 us -> 271 us (1.011)
  waiting for transfers between devices: 50.9 us -> 44.1 us
  local copies, waits for them, and re-layouts: 25.1 us -> 31.8 us
  other arithmetic: 14.2 us -> 17.1 us
    ppermute x12, waiting for transfers between devices: 13.3 us -> 6.42 us  [from_above(): lax.ppermute(value, axes, [((i + distance) % count, i) for i in range(cou...]
    unnamed x38, local copies, waits for them, and re-layouts: 3.35 us -> 7.52 us
    ppermute x5, waiting for transfers between devices: 14.2 us -> 17.9 us  [swap_near(): return lax.ppermute(value, 'y_lo', [(0, 1), (1, 0)])]
    all_to_all x7, waiting for transfers between devices: 18.6 us -> 15 us  [exchange(): return lax.all_to_all(blocks, axes, split_axis=0, concat_axis=0, tiled=True)]
  transfers between devices with their start and end apart: 34 -> 34, of which waited for: 14 -> 14; matrix products, arithmetic and copies ran while one was open for 14% -> 18% of each run, Pallas kernels for 0% -> 0%
where the time goes in v12:
time: 271 us; the launch traced here: 268 us
  starting transfers between devices  159 us (59%)
  waiting for transfers between devices  44.1 us (16%)
  local copies, waits for them, and re-layouts  31.8 us (12%)
  other arithmetic  17.1 us (6%)
  matrix products  14.1 us (5%)
    all_to_all x7, starting transfers between devices, exchange(): return lax.all_to_all(blocks, axes, split_axis=0, concat_axis=0, tiled=True)  65.4 us
    ppermute x12, starting transfers between devices, from_above(): lax.ppermute(value, axes, [((i + distance) % count, i) for i in range(cou...  43.2 us
    ppermute x5, waiting for transfers between devices, swap_near(): return lax.ppermute(value, 'y_lo', [(0, 1), (1, 0)])  17.9 us
    ppermute x5, starting transfers between devices, swap_cores(): return lax.ppermute(value, 'core', [(0, 1), (1, 0)])  16.2 us
    all_to_all x7, waiting for transfers between devices, exchange(): return lax.all_to_all(blocks, axes, split_axis=0, concat_axis=0, tiled=True)  15 us
    ppermute x5, starting transfers between devices, swap_near(): return lax.ppermute(value, 'y_lo', [(0, 1), (1, 0)])  14 us
    ppermute x2, starting transfers between devices, trade_pair(): other = lax.ppermute(sent, axis_name, [(0, 1), (1, 0)])  11.2 us
    ppermute x3, starting transfers between devices, trade_x(): lax.ppermute(turned[step], 'x', [(i, (i + step) % count) for i in range(c...  9.33 us
  transfers between devices with their start and end apart: 34, of which 14 were waited for; matrix products, arithmetic and copies ran while one was open for 18% of the time, Pallas kernels for 0%

profile of v12, /device:TPU:1, one launch (start us, length us, event | category | flops | bytes accessed | tf_op | source)
XLA Modules:
  0.0 268.3 jit_solution(2753544618414197744)
XLA Ops:
  2.0 4.0 %collective-permute-start.1 = (bf16[2,896,256]{2,1,0:T(8,128)(2,1)S(1)}, bf16[2,896,256]{2,1,0:T(8,128)(2,1)S(1)}, u32[]{:S(2)}, u32[]{:S(2)}) collective-permute-start(bf16[2,896,256]{2,1,0:T(8,128)(2,1)S(1)} %pad_maximum_fusion.1), channel_id=1, source_target_pairs={{0,256},{256,0},{1,257},{257,1},{2,258},{258,2},{3,259},{259,3},{4... | collective-permute-start | bytes 2752520 | tf_op jit(solution)/shard_map/ppermute | solution.py:37
  11.4 6.7 %collective-permute-start = (bf16[4,2,12,256]{3,1,2,0:T(2,128)(2,1)S(1)}, bf16[4,2,12,256]{3,1,2,0:T(2,128)(2,1)S(1)}, u32[]{:S(2)}, u32[]{:S(2)}) collective-permute-start(bf16[4,2,12,256]{3,1,2,0:T(2,128)(2,1)S(1)} %bitcast.255), channel_id=1, source_target_pairs={{0,1},{1,0},{2,3},{3,2},{4,5},{5,4},{6,7},{7,6},{8,9},{9,8},{10,11... | collective-permute-start | bytes 147464 | tf_op jit(solution)/shard_map/ppermute | solution.py:72
  18.0 11.1 %all-to-all-start = ((bf16[16,8,2048]{2,1,0:T(8,128)(2,1)}), bf16[16,8,2048]{2,1,0:T(8,128)(2,1)S(1)}, u32[]{:S(2)}, u32[]{:S(2)}) async-start(bf16[16,8,2048]{2,1,0:T(8,128)(2,1)} %reshape.239), calls=%async_computation | async-start | bytes 1048576 | tf_op jit(solution)/shard_map/all_to_all | solution.py:29
  29.7 4.5 %collective-permute-start.2 = (bf16[2,4,12,256]{3,1,2,0:T(4,128)(2,1)S(1)}, bf16[2,4,12,256]{3,1,2,0:T(4,128)(2,1)S(1)}, u32[]{:S(2)}, u32[]{:S(2)}) collective-permute-start(bf16[2,4,12,256]{3,1,2,0:T(4,128)(2,1)S(1)} %bitcast.254), channel_id=1, source_target_pairs={{0,2},{2,0},{1,3},{3,1},{4,6},{6,4},{5,7},{7,5},{8,10},{10,8},{9,1... | collective-permute-start | bytes 147464 | tf_op jit(solution)/shard_map/ppermute | solution.py:72
  36.6 4.4 %collective-permute-start.3 = (bf16[2,2,12,256]{3,1,2,0:T(2,128)(2,1)S(1)}, bf16[2,2,12,256]{3,1,2,0:T(2,128)(2,1)S(1)}, u32[]{:S(2)}, u32[]{:S(2)}) collective-permute-start(bf16[2,2,12,256]{3,1,2,0:T(2,128)(2,1)S(1)} %bitcast.260), channel_id=1, source_target_pairs={{0,12},{4,0},{8,4},{12,8},{1,13},{5,1},{9,5},{13,9},{2,14},{6,2},{... | collective-permute-start | bytes 73736 | tf_op jit(solution)/shard_map/ppermute | solution.py:80
  56.9 12.1 %all-to-all-start.1 = ((bf16[16,64,2048]{2,1,0:T(8,128)(2,1)}), bf16[16,64,2048]{2,1,0:T(8,128)(2,1)}, u32[]{:S(2)}, u32[]{:S(2)}) async-start(bf16[16,64,2048]{2,1,0:T(8,128)(2,1)} %bitcast.215), calls=%async_computation.1 | async-start | bytes 8388608 | tf_op jit(solution)/shard_map/all_to_all | solution.py:29
  71.4 4.3 %collective-permute-start.8 = (bf16[64,256]{1,0:T(8,128)(2,1)S(1)}, bf16[64,256]{1,0:T(8,128)(2,1)S(1)}, u32[]{:S(2)}, u32[]{:S(2)}) collective-permute-start(bf16[64,256]{1,0:T(8,128)(2,1)S(1)} %multiply_convert_fusion), channel_id=1, source_target_pairs={{192,0},{208,16},{224,32},{240,48},{0,64},{16,80},{32,96},{48,112}... | collective-permute-start | bytes 98312 | tf_op jit(solution)/shard_map/ppermute | solution.py:42
  75.6 8.0 %collective-permute-start.7 = (bf16[64,256]{1,0:T(8,128)(2,1)S(1)}, bf16[64,256]{1,0:T(8,128)(2,1)S(1)}, u32[]{:S(2)}, u32[]{:S(2)}) collective-permute-start(bf16[64,256]{1,0:T(8,128)(2,1)S(1)} %multiply_convert_fusion), channel_id=1, source_target_pairs={{128,0},{144,16},{160,32},{176,48},{192,64},{208,80},{224,96},{240... | collective-permute-start | bytes 98312 | tf_op jit(solution)/shard_map/ppermute | solution.py:42
  83.7 5.2 %collective-permute-start.6 = (bf16[64,256]{1,0:T(8,128)(2,1)S(1)}, bf16[64,256]{1,0:T(8,128)(2,1)S(1)}, u32[]{:S(2)}, u32[]{:S(2)}) collective-permute-start(bf16[64,256]{1,0:T(8,128)(2,1)S(1)} %multiply_convert_fusion), channel_id=1, source_target_pairs={{64,0},{80,16},{96,32},{112,48},{128,64},{144,80},{160,96},{176,11... | collective-permute-start | bytes 98312 | tf_op jit(solution)/shard_map/ppermute | solution.py:42
  88.9 2.6 collective-permute-start.14
  91.5 3.1 %collective-permute-start.13 = (bf16[256,256]{1,0:T(8,128)(2,1)S(1)}, bf16[256,256]{1,0:T(8,128)(2,1)S(1)}, u32[]{:S(2)}, u32[]{:S(2)}) collective-permute-start(bf16[256,256]{1,0:T(8,128)(2,1)S(1)} %copy-done.9), channel_id=1, source_target_pairs={{32,0},{48,16},{0,32},{16,48},{33,1},{49,17},{1,33},{17,49},{34,2}... | collective-permute-start | bytes 393224 | tf_op jit(solution)/shard_map/ppermute | solution.py:42
  94.7 3.5 %collective-permute-start.12 = (bf16[256,256]{1,0:T(8,128)(2,1)S(1)}, bf16[256,256]{1,0:T(8,128)(2,1)S(1)}, u32[]{:S(2)}, u32[]{:S(2)}) collective-permute-start(bf16[256,256]{1,0:T(8,128)(2,1)S(1)} %copy-done.9), channel_id=1, source_target_pairs={{16,0},{32,16},{48,32},{0,48},{17,1},{33,17},{49,33},{1,49},{18,2}... | collective-permute-start | bytes 393224 | tf_op jit(solution)/shard_map/ppermute | solution.py:42
  100.2 3.4 %collective-permute-start.10 = (bf16[4,64,256]{2,1,0:T(8,128)(2,1)S(1)}, bf16[4,64,256]{2,1,0:T(8,128)(2,1)S(1)}, u32[]{:S(2)}, u32[]{:S(2)}) collective-permute-start(bf16[4,64,256]{2,1,0:T(8,128)(2,1)S(1)} %get-tuple-element.80), channel_id=1, source_target_pairs={{32,0},{48,16},{64,32},{80,48},{96,64},{112,80},{128,96},{144,112}... | collective-permute-start | bytes 393224 | tf_op jit(solution)/shard_map/ppermute | solution.py:42
  108.5 3.4 %collective-permute-done.10 = bf16[4,64,256]{2,1,0:T(8,128)(2,1)S(1)} collective-permute-done((bf16[4,64,256]{2,1,0:T(8,128)(2,1)S(1)}, bf16[4,64,256]{2,1,0:T(8,128)(2,1)S(1)}, u32[]{:S(2)}, u32[]{:S(2)}) %collective-permute-start.10) | collective-permute-done | bytes 131104 | tf_op jit(solution)/shard_map/ppermute | solution.py:42
  114.6 7.1 %all-to-all-done.1 = bf16[16,64,2048]{2,1,0:T(8,128)(2,1)} async-done(((bf16[16,64,2048]{2,1,0:T(8,128)(2,1)}), bf16[16,64,2048]{2,1,0:T(8,128)(2,1)}, u32[]{:S(2)}, u32[]{:S(2)}) %all-to-all-start.1) | async-done | bytes 4194336 | tf_op jit(solution)/shard_map/all_to_all | solution.py:29
  121.7 3.7 %fusion.48 = f32[1024,256]{1,0:T(8,128)S(1)} fusion(bf16[1024,2048]{1,0:T(8,128)(2,1)} %bitcast.31, bf16[2048,256]{1,0:T(8,128)(2,1)} %collective-permute-done.15), kind=kOutput, calls=%fused_computation.150 | convolution fusion | flops 1073741824 | bytes 6291456 | tf_op jit(solution)/shard_map/dot_general | solution.py:207
  127.7 3.4 %fusion.47 = f32[1024,256]{1,0:T(8,128)S(1)} fusion(bf16[1024,2048]{1,0:T(8,128)(2,1)} %bitcast.31, bf16[2048,256]{1,0:T(8,128)(2,1)S(1)} %bitcast.233), kind=kOutput, calls=%fused_computation.149 | convolution fusion | flops 1073741824 | bytes 6291456 | tf_op jit(solution)/shard_map/dot_general | solution.py:208
  132.5 7.8 %all-to-all-start.2 = ((bf16[16,64,256]{2,1,0:T(8,128)(2,1)}), bf16[16,64,256]{2,1,0:T(8,128)(2,1)S(1)}, u32[]{:S(2)}, u32[]{:S(2)}) async-start(bf16[16,64,256]{2,1,0:T(8,128)(2,1)} %copy.269), calls=%async_computation.2 | async-start | bytes 1048576 | tf_op jit(solution)/shard_map/all_to_all | solution.py:29
  141.6 2.7 collective-permute-start.17
  149.9 4.9 %fusion.6 = f32[2048,512]{1,0:T(8,128)S(1)} fusion(bf16[1024,2048]{1,0:T(8,128)(2,1)} %bitcast.31, bf16[1024,256]{1,0:T(8,128)(2,1)} %collective-permute-done.17, bf16[1024,256]{1,0:T(8,128)(2,1)} %reshape.251), kind=kOutput, calls=%fused_computation.12 | convolution fusion | flops 2149580800 | bytes 9437184 | tf_op jit(solution)/shard_map/dot_general | solution.py:25
  158.0 4.4 %collective-permute-done.19 = bf16[4,256,256]{2,1,0:T(8,128)(2,1)S(1)} collective-permute-done((bf16[4,256,256]{2,1,0:T(8,128)(2,1)S(1)}, bf16[4,256,256]{2,1,0:T(8,128)(2,1)S(1)}, u32[]{:S(2)}, u32[]{:S(2)}) %collective-permute-start.19) | collective-permute-done | bytes 524320 | tf_op jit(solution)/shard_map/ppermute | solution.py:37
  164.3 19.9 %all-to-all-start.3 = ((f32[16,1,320]{2,1,0:T(1,128)}), f32[16,1,320]{2,1,0:T(1,128)S(1)}, u32[]{:S(2)}, u32[]{:S(2)}) async-start(f32[16,1,320]{2,1,0:T(1,128)} %broadcast_in_dim.10), calls=%async_computation.3 | async-start | bytes 49152 | tf_op jit(solution)/shard_map/all_to_all | solution.py:29
  186.6 4.9 %all-to-all-done.3 = f32[16,1,320]{2,1,0:T(1,128)S(1)} async-done(((f32[16,1,320]{2,1,0:T(1,128)}), f32[16,1,320]{2,1,0:T(1,128)S(1)}, u32[]{:S(2)}, u32[]{:S(2)}) %all-to-all-start.3) | async-done | bytes 20512 | tf_op jit(solution)/shard_map/all_to_all | solution.py:29
  192.4 6.1 %all-to-all-start.4 = ((bf16[4,96,256]{2,1,0:T(8,128)(2,1)}), bf16[4,96,256]{2,1,0:T(8,128)(2,1)S(1)}, u32[]{:S(2)}, u32[]{:S(2)}) async-start(bf16[4,96,256]{2,1,0:T(8,128)(2,1)} %broadcast_in_dim.11), calls=%async_computation.4 | async-start | bytes 393216 | tf_op jit(solution)/shard_map/all_to_all | solution.py:29
  198.6 9.7 %collective-permute-done.20 = bf16[896,512]{1,0:T(8,128)(2,1)} collective-permute-done((bf16[896,512]{1,0:T(8,128)(2,1)}, bf16[896,512]{1,0:T(8,128)(2,1)}, u32[]{:S(2)}, u32[]{:S(2)}) %collective-permute-start.20) | collective-permute-done | bytes 917536 | tf_op jit(solution)/shard_map/ppermute | solution.py:37
  211.5 7.4 %collective-permute-start.21 = (f32[896,256]{1,0:T(8,128)}, f32[896,256]{1,0:T(8,128)}, u32[]{:S(2)}, u32[]{:S(2)}) collective-permute-start(f32[896,256]{1,0:T(8,128)} %get-tuple-element.46), channel_id=1, source_target_pairs={{0,1},{1,0},{2,3},{3,2},{4,5},{5,4},{6,7},{7,6},{8,9},{9,8},{10,11... | collective-permute-start | bytes 2752520 | tf_op jit(solution)/shard_map/ppermute | solution.py:33
  220.6 3.6 %all-to-all-start.5 = ((bf16[16,16,2048]{2,1,0:T(8,128)(2,1)}), bf16[16,16,2048]{2,1,0:T(8,128)(2,1)S(1)}, u32[]{:S(2)}, u32[]{:S(2)}) async-start(bf16[16,16,2048]{2,1,0:T(8,128)(2,1)} %bitcast.66), calls=%async_computation.5 | async-start | bytes 2097152 | tf_op jit(solution)/shard_map/all_to_all | solution.py:29
  228.1 3.0 %collective-permute-start.22 = (bf16[288,256]{1,0:T(8,128)(2,1)}, bf16[288,256]{1,0:T(8,128)(2,1)S(1)}, u32[]{:S(2)}, u32[]{:S(2)}) collective-permute-start(bf16[288,256]{1,0:T(8,128)(2,1)} %pad_maximum_fusion.5), channel_id=1, source_target_pairs={{16,0},{32,16},{48,32},{0,48},{17,1},{33,17},{49,33},{1,49},{18,2}... | collective-permute-start | bytes 442376 | tf_op jit(solution)/shard_map/ppermute | solution.py:42
  231.2 3.7 %collective-permute-start.23 = (bf16[288,256]{1,0:T(8,128)(2,1)}, bf16[288,256]{1,0:T(8,128)(2,1)S(1)}, u32[]{:S(2)}, u32[]{:S(2)}) collective-permute-start(bf16[288,256]{1,0:T(8,128)(2,1)} %pad_maximum_fusion.5), channel_id=1, source_target_pairs={{32,0},{48,16},{0,32},{16,48},{33,1},{49,17},{1,33},{17,49},{34,2}... | collective-permute-start | bytes 442376 | tf_op jit(solution)/shard_map/ppermute | solution.py:42
  242.2 4.8 %all-to-all-start.6 = ((bf16[4,4,2048]{2,1,0:T(4,128)(2,1)}), bf16[4,4,2048]{2,1,0:T(4,128)(2,1)S(1)}, u32[]{:S(2)}, u32[]{:S(2)}) async-start(bf16[4,4,2048]{2,1,0:T(4,128)(2,1)} %reshape.257), calls=%async_computation.6 | async-start | bytes 131072 | tf_op jit(solution)/shard_map/all_to_all | solution.py:29
  259.3 3.0 %collective-permute-start.25 = (f32[2,128,256]{2,1,0:T(8,128)S(1)}, f32[2,128,256]{2,1,0:T(8,128)S(1)}, u32[]{:S(2)}, u32[]{:S(2)}) collective-permute-start(f32[2,128,256]{2,1,0:T(8,128)S(1)} %fusion.26), channel_id=1, source_target_pairs={{0,256},{256,0},{1,257},{257,1},{2,258},{258,2},{3,259},{259,3},{4... | collective-permute-start | bytes 786440 | tf_op jit(solution)/shard_map/ppermute | solution.py:37
  263.8 3.7 %collective-permute-done.25 = f32[2,128,256]{2,1,0:T(8,128)S(1)} collective-permute-done((f32[2,128,256]{2,1,0:T(8,128)S(1)}, f32[2,128,256]{2,1,0:T(8,128)S(1)}, u32[]{:S(2)}, u32[]{:S(2)}) %collective-permute-start.25) | collective-permute-done | bytes 262176 | tf_op jit(solution)/shard_map/ppermute | solution.py:37
  (205 shorter events, 86.1 us)
Async XLA Ops:
  2.0 27.5 %collective-permute-start.1 = (bf16[2,896,256]{2,1,0:T(8,128)(2,1)S(1)}, bf16[2,896,256]{2,1,0:T(8,128)(2,1)S(1)}, u32[]{:S(2)}, u32[]{:S(2)}) collective-permute-start(bf16[2,896,256]{2,1,0:T(8,128)(2,1)S(1)} %pad_maximum_fusion.1), channel_id=1, source_target_pairs={{0,256},{256,0},{1,257},{257,1},{2,258},{258,2},{3,259},{259,3},{4... | collective-permute-start | bytes 2752520 | tf_op jit(solution)/shard_map/ppermute | solution.py:37
  11.4 17.8 %collective-permute-start = (bf16[4,2,12,256]{3,1,2,0:T(2,128)(2,1)S(1)}, bf16[4,2,12,256]{3,1,2,0:T(2,128)(2,1)S(1)}, u32[]{:S(2)}, u32[]{:S(2)}) collective-permute-start(bf16[4,2,12,256]{3,1,2,0:T(2,128)(2,1)S(1)} %bitcast.255), channel_id=1, source_target_pairs={{0,1},{1,0},{2,3},{3,2},{4,5},{5,4},{6,7},{7,6},{8,9},{9,8},{10,11... | collective-permute-start | bytes 147464 | tf_op jit(solution)/shard_map/ppermute | solution.py:72
  18.0 35.3 %all-to-all-start = ((bf16[16,8,2048]{2,1,0:T(8,128)(2,1)}), bf16[16,8,2048]{2,1,0:T(8,128)(2,1)S(1)}, u32[]{:S(2)}, u32[]{:S(2)}) async-start(bf16[16,8,2048]{2,1,0:T(8,128)(2,1)} %reshape.239), calls=%async_computation | async-start | bytes 1048576 | tf_op jit(solution)/shard_map/all_to_all | solution.py:29
  29.7 6.3 %collective-permute-start.2 = (bf16[2,4,12,256]{3,1,2,0:T(4,128)(2,1)S(1)}, bf16[2,4,12,256]{3,1,2,0:T(4,128)(2,1)S(1)}, u32[]{:S(2)}, u32[]{:S(2)}) collective-permute-start(bf16[2,4,12,256]{3,1,2,0:T(4,128)(2,1)S(1)} %bitcast.254), channel_id=1, source_target_pairs={{0,2},{2,0},{1,3},{3,1},{4,6},{6,4},{5,7},{7,5},{8,10},{10,8},{9,1... | collective-permute-start | bytes 147464 | tf_op jit(solution)/shard_map/ppermute | solution.py:72
  36.6 10.2 %collective-permute-start.3 = (bf16[2,2,12,256]{3,1,2,0:T(2,128)(2,1)S(1)}, bf16[2,2,12,256]{3,1,2,0:T(2,128)(2,1)S(1)}, u32[]{:S(2)}, u32[]{:S(2)}) collective-permute-start(bf16[2,2,12,256]{3,1,2,0:T(2,128)(2,1)S(1)} %bitcast.260), channel_id=1, source_target_pairs={{0,12},{4,0},{8,4},{12,8},{1,13},{5,1},{9,5},{13,9},{2,14},{6,2},{... | collective-permute-start | bytes 73736 | tf_op jit(solution)/shard_map/ppermute | solution.py:80
  41.0 6.4 %collective-permute-start.4 = (bf16[2,2,12,256]{3,1,2,0:T(2,128)(2,1)S(1)}, bf16[2,2,12,256]{3,1,2,0:T(2,128)(2,1)S(1)}, u32[]{:S(2)}, u32[]{:S(2)}) collective-permute-start(bf16[2,2,12,256]{3,1,2,0:T(2,128)(2,1)S(1)} %bitcast.262), channel_id=1, source_target_pairs={{0,8},{4,12},{8,0},{12,4},{1,9},{5,13},{9,1},{13,5},{2,10},{6,14},... | collective-permute-start | bytes 73736 | tf_op jit(solution)/shard_map/ppermute | solution.py:80
  43.5 6.3 %collective-permute-start.5 = (bf16[2,2,12,256]{3,1,2,0:T(2,128)(2,1)S(1)}, bf16[2,2,12,256]{3,1,2,0:T(2,128)(2,1)S(1)}, u32[]{:S(2)}, u32[]{:S(2)}) collective-permute-start(bf16[2,2,12,256]{3,1,2,0:T(2,128)(2,1)S(1)} %bitcast.264), channel_id=1, source_target_pairs={{0,4},{4,8},{8,12},{12,0},{1,5},{5,9},{9,13},{13,1},{2,6},{6,10},{... | collective-permute-start | bytes 73736 | tf_op jit(solution)/shard_map/ppermute | solution.py:80
  56.9 64.8 %all-to-all-start.1 = ((bf16[16,64,2048]{2,1,0:T(8,128)(2,1)}), bf16[16,64,2048]{2,1,0:T(8,128)(2,1)}, u32[]{:S(2)}, u32[]{:S(2)}) async-start(bf16[16,64,2048]{2,1,0:T(8,128)(2,1)} %bitcast.215), calls=%async_computation.1 | async-start | bytes 8388608 | tf_op jit(solution)/shard_map/all_to_all | solution.py:29
  69.3 52.5 %collective-permute-start.15 = (bf16[2048,256]{1,0:T(8,128)(2,1)S(1)}, bf16[2048,256]{1,0:T(8,128)(2,1)}, u32[]{:S(2)}, u32[]{:S(2)}) collective-permute-start(bf16[2048,256]{1,0:T(8,128)(2,1)S(1)} %bitcast.232), channel_id=1, source_target_pairs={{0,1},{1,0},{2,3},{3,2},{4,5},{5,4},{6,7},{7,6},{8,9},{9,8},{10,11... | collective-permute-start | bytes 3145736 | tf_op jit(solution)/shard_map/ppermute | solution.py:33
  71.4 20.2 %collective-permute-start.8 = (bf16[64,256]{1,0:T(8,128)(2,1)S(1)}, bf16[64,256]{1,0:T(8,128)(2,1)S(1)}, u32[]{:S(2)}, u32[]{:S(2)}) collective-permute-start(bf16[64,256]{1,0:T(8,128)(2,1)S(1)} %multiply_convert_fusion), channel_id=1, source_target_pairs={{192,0},{208,16},{224,32},{240,48},{0,64},{16,80},{32,96},{48,112}... | collective-permute-start | bytes 98312 | tf_op jit(solution)/shard_map/ppermute | solution.py:42
  75.6 19.0 %collective-permute-start.7 = (bf16[64,256]{1,0:T(8,128)(2,1)S(1)}, bf16[64,256]{1,0:T(8,128)(2,1)S(1)}, u32[]{:S(2)}, u32[]{:S(2)}) collective-permute-start(bf16[64,256]{1,0:T(8,128)(2,1)S(1)} %multiply_convert_fusion), channel_id=1, source_target_pairs={{128,0},{144,16},{160,32},{176,48},{192,64},{208,80},{224,96},{240... | collective-permute-start | bytes 98312 | tf_op jit(solution)/shard_map/ppermute | solution.py:42
  83.7 14.5 %collective-permute-start.6 = (bf16[64,256]{1,0:T(8,128)(2,1)S(1)}, bf16[64,256]{1,0:T(8,128)(2,1)S(1)}, u32[]{:S(2)}, u32[]{:S(2)}) collective-permute-start(bf16[64,256]{1,0:T(8,128)(2,1)S(1)} %multiply_convert_fusion), channel_id=1, source_target_pairs={{64,0},{80,16},{96,32},{112,48},{128,64},{144,80},{160,96},{176,11... | collective-permute-start | bytes 98312 | tf_op jit(solution)/shard_map/ppermute | solution.py:42
  88.9 11.3 %collective-permute-start.14 = (bf16[256,256]{1,0:T(8,128)(2,1)S(1)}, bf16[256,256]{1,0:T(8,128)(2,1)S(1)}, u32[]{:S(2)}, u32[]{:S(2)}) collective-permute-start(bf16[256,256]{1,0:T(8,128)(2,1)S(1)} %copy-done.9), channel_id=1, source_target_pairs={{48,0},{0,16},{16,32},{32,48},{49,1},{1,17},{17,33},{33,49},{50,2}... | collective-permute-start | bytes 393224 | tf_op jit(solution)/shard_map/ppermute | solution.py:42
  91.5 12.7 %collective-permute-start.13 = (bf16[256,256]{1,0:T(8,128)(2,1)S(1)}, bf16[256,256]{1,0:T(8,128)(2,1)S(1)}, u32[]{:S(2)}, u32[]{:S(2)}) collective-permute-start(bf16[256,256]{1,0:T(8,128)(2,1)S(1)} %copy-done.9), channel_id=1, source_target_pairs={{32,0},{48,16},{0,32},{16,48},{33,1},{49,17},{1,33},{17,49},{34,2}... | collective-permute-start | bytes 393224 | tf_op jit(solution)/shard_map/ppermute | solution.py:42
  94.7 12.1 %collective-permute-start.12 = (bf16[256,256]{1,0:T(8,128)(2,1)S(1)}, bf16[256,256]{1,0:T(8,128)(2,1)S(1)}, u32[]{:S(2)}, u32[]{:S(2)}) collective-permute-start(bf16[256,256]{1,0:T(8,128)(2,1)S(1)} %copy-done.9), channel_id=1, source_target_pairs={{16,0},{32,16},{48,32},{0,48},{17,1},{33,17},{49,33},{1,49},{18,2}... | collective-permute-start | bytes 393224 | tf_op jit(solution)/shard_map/ppermute | solution.py:42
  98.2 10.2 %collective-permute-start.11 = (bf16[4,64,256]{2,1,0:T(8,128)(2,1)S(1)}, bf16[4,64,256]{2,1,0:T(8,128)(2,1)S(1)}, u32[]{:S(2)}, u32[]{:S(2)}) collective-permute-start(bf16[4,64,256]{2,1,0:T(8,128)(2,1)S(1)} %get-tuple-element.80), channel_id=1, source_target_pairs={{240,0},{0,16},{16,32},{32,48},{48,64},{64,80},{80,96},{96,112},{1... | collective-permute-start | bytes 393224 | tf_op jit(solution)/shard_map/ppermute | solution.py:42
  100.2 11.7 %collective-permute-start.10 = (bf16[4,64,256]{2,1,0:T(8,128)(2,1)S(1)}, bf16[4,64,256]{2,1,0:T(8,128)(2,1)S(1)}, u32[]{:S(2)}, u32[]{:S(2)}) collective-permute-start(bf16[4,64,256]{2,1,0:T(8,128)(2,1)S(1)} %get-tuple-element.80), channel_id=1, source_target_pairs={{32,0},{48,16},{64,32},{80,48},{96,64},{112,80},{128,96},{144,112}... | collective-permute-start | bytes 393224 | tf_op jit(solution)/shard_map/ppermute | solution.py:42
  104.2 10.0 %collective-permute-start.9 = (bf16[4,64,256]{2,1,0:T(8,128)(2,1)S(1)}, bf16[4,64,256]{2,1,0:T(8,128)(2,1)S(1)}, u32[]{:S(2)}, u32[]{:S(2)}) collective-permute-start(bf16[4,64,256]{2,1,0:T(8,128)(2,1)S(1)} %get-tuple-element.80), channel_id=1, source_target_pairs={{16,0},{32,16},{48,32},{64,48},{80,64},{96,80},{112,96},{128,112},... | collective-permute-start | bytes 393224 | tf_op jit(solution)/shard_map/ppermute | solution.py:42
  132.5 30.6 %all-to-all-start.2 = ((bf16[16,64,256]{2,1,0:T(8,128)(2,1)}), bf16[16,64,256]{2,1,0:T(8,128)(2,1)S(1)}, u32[]{:S(2)}, u32[]{:S(2)}) async-start(bf16[16,64,256]{2,1,0:T(8,128)(2,1)} %copy.269), calls=%async_computation.2 | async-start | bytes 1048576 | tf_op jit(solution)/shard_map/all_to_all | solution.py:29
  141.6 8.3 %collective-permute-start.17 = (bf16[1024,256]{1,0:T(8,128)(2,1)}, bf16[1024,256]{1,0:T(8,128)(2,1)}, u32[]{:S(2)}, u32[]{:S(2)}) collective-permute-start(bf16[1024,256]{1,0:T(8,128)(2,1)} %reshape.251), channel_id=1, source_target_pairs={{0,1},{1,0},{2,3},{3,2},{4,5},{5,4},{6,7},{7,6},{8,9},{9,8},{10,11... | collective-permute-start | bytes 1572872 | tf_op jit(solution)/shard_map/ppermute | solution.py:33
  145.6 12.4 %collective-permute-start.18 = (bf16[1024,256]{1,0:T(8,128)(2,1)S(1)}, bf16[1024,256]{1,0:T(8,128)(2,1)S(1)}, u32[]{:S(2)}, u32[]{:S(2)}) collective-permute-start(bf16[1024,256]{1,0:T(8,128)(2,1)S(1)} %pad_maximum_fusion.4), channel_id=1, source_target_pairs={{0,1},{1,0},{2,3},{3,2},{4,5},{5,4},{6,7},{7,6},{8,9},{9,8},{10,11... | collective-permute-start | bytes 1572872 | tf_op jit(solution)/shard_map/ppermute | solution.py:33
  147.6 14.9 %collective-permute-start.19 = (bf16[4,256,256]{2,1,0:T(8,128)(2,1)S(1)}, bf16[4,256,256]{2,1,0:T(8,128)(2,1)S(1)}, u32[]{:S(2)}, u32[]{:S(2)}) collective-permute-start(bf16[4,256,256]{2,1,0:T(8,128)(2,1)S(1)} %pad_maximum_fusion.3), channel_id=1, source_target_pairs={{0,256},{256,0},{1,257},{257,1},{2,258},{258,2},{3,259},{259,3},{4... | collective-permute-start | bytes 1572872 | tf_op jit(solution)/shard_map/ppermute | solution.py:37
  164.3 27.2 %all-to-all-start.3 = ((f32[16,1,320]{2,1,0:T(1,128)}), f32[16,1,320]{2,1,0:T(1,128)S(1)}, u32[]{:S(2)}, u32[]{:S(2)}) async-start(f32[16,1,320]{2,1,0:T(1,128)} %broadcast_in_dim.10), calls=%async_computation.3 | async-start | bytes 49152 | tf_op jit(solution)/shard_map/all_to_all | solution.py:29
  184.2 24.2 %collective-permute-start.20 = (bf16[896,512]{1,0:T(8,128)(2,1)}, bf16[896,512]{1,0:T(8,128)(2,1)}, u32[]{:S(2)}, u32[]{:S(2)}) collective-permute-start(bf16[896,512]{1,0:T(8,128)(2,1)} %fusion.10), channel_id=1, source_target_pairs={{0,256},{256,0},{1,257},{257,1},{2,258},{258,2},{3,259},{259,3},{4... | collective-permute-start | bytes 2752520 | tf_op jit(solution)/shard_map/ppermute | solution.py:37
  192.4 19.1 %all-to-all-start.4 = ((bf16[4,96,256]{2,1,0:T(8,128)(2,1)}), bf16[4,96,256]{2,1,0:T(8,128)(2,1)S(1)}, u32[]{:S(2)}, u32[]{:S(2)}) async-start(bf16[4,96,256]{2,1,0:T(8,128)(2,1)} %broadcast_in_dim.11), calls=%async_computation.4 | async-start | bytes 393216 | tf_op jit(solution)/shard_map/all_to_all | solution.py:29
  211.5 14.1 %collective-permute-start.21 = (f32[896,256]{1,0:T(8,128)}, f32[896,256]{1,0:T(8,128)}, u32[]{:S(2)}, u32[]{:S(2)}) collective-permute-start(f32[896,256]{1,0:T(8,128)} %get-tuple-element.46), channel_id=1, source_target_pairs={{0,1},{1,0},{2,3},{3,2},{4,5},{5,4},{6,7},{7,6},{8,9},{9,8},{10,11... | collective-permute-start | bytes 2752520 | tf_op jit(solution)/shard_map/ppermute | solution.py:33
  220.6 20.7 %all-to-all-start.5 = ((bf16[16,16,2048]{2,1,0:T(8,128)(2,1)}), bf16[16,16,2048]{2,1,0:T(8,128)(2,1)S(1)}, u32[]{:S(2)}, u32[]{:S(2)}) async-start(bf16[16,16,2048]{2,1,0:T(8,128)(2,1)} %bitcast.66), calls=%async_computation.5 | async-start | bytes 2097152 | tf_op jit(solution)/shard_map/all_to_all | solution.py:29
  228.1 18.9 %collective-permute-start.22 = (bf16[288,256]{1,0:T(8,128)(2,1)}, bf16[288,256]{1,0:T(8,128)(2,1)S(1)}, u32[]{:S(2)}, u32[]{:S(2)}) collective-permute-start(bf16[288,256]{1,0:T(8,128)(2,1)} %pad_maximum_fusion.5), channel_id=1, source_target_pairs={{16,0},{32,16},{48,32},{0,48},{17,1},{33,17},{49,33},{1,49},{18,2}... | collective-permute-start | bytes 442376 | tf_op jit(solution)/shard_map/ppermute | solution.py:42
  231.2 16.5 %collective-permute-start.23 = (bf16[288,256]{1,0:T(8,128)(2,1)}, bf16[288,256]{1,0:T(8,128)(2,1)S(1)}, u32[]{:S(2)}, u32[]{:S(2)}) collective-permute-start(bf16[288,256]{1,0:T(8,128)(2,1)} %pad_maximum_fusion.5), channel_id=1, source_target_pairs={{32,0},{48,16},{0,32},{16,48},{33,1},{49,17},{1,33},{17,49},{34,2}... | collective-permute-start | bytes 442376 | tf_op jit(solution)/shard_map/ppermute | solution.py:42
  234.8 13.5 %collective-permute-start.24 = (bf16[288,256]{1,0:T(8,128)(2,1)}, bf16[288,256]{1,0:T(8,128)(2,1)}, u32[]{:S(2)}, u32[]{:S(2)}) collective-permute-start(bf16[288,256]{1,0:T(8,128)(2,1)} %pad_maximum_fusion.5), channel_id=1, source_target_pairs={{48,0},{0,16},{16,32},{32,48},{49,1},{1,17},{17,33},{33,49},{50,2}... | collective-permute-start | bytes 442376 | tf_op jit(solution)/shard_map/ppermute | solution.py:42
  242.2 20.7 %all-to-all-start.6 = ((bf16[4,4,2048]{2,1,0:T(4,128)(2,1)}), bf16[4,4,2048]{2,1,0:T(4,128)(2,1)S(1)}, u32[]{:S(2)}, u32[]{:S(2)}) async-start(bf16[4,4,2048]{2,1,0:T(4,128)(2,1)} %reshape.257), calls=%async_computation.6 | async-start | bytes 131072 | tf_op jit(solution)/shard_map/all_to_all | solution.py:29
  259.3 8.3 %collective-permute-start.25 = (f32[2,128,256]{2,1,0:T(8,128)S(1)}, f32[2,128,256]{2,1,0:T(8,128)S(1)}, u32[]{:S(2)}, u32[]{:S(2)}) collective-permute-start(f32[2,128,256]{2,1,0:T(8,128)S(1)} %fusion.26), channel_id=1, source_target_pairs={{0,256},{256,0},{1,257},{257,1},{2,258},{258,2},{3,259},{259,3},{4... | collective-permute-start | bytes 786440 | tf_op jit(solution)/shard_map/ppermute | solution.py:37
  (15 other events, 121.1 us)

commit v13 on v12

--- a/solution.py
+++ b/solution.py
@@ -226,6 +226,10 @@
     joined_half = jnp.concatenate(
         [half_all[:, units:part_width], half_all[:, part_width + units :]], axis=1
     )
+    joined_half = joined_half.reshape(-1, quarter, row_count, inputs)
+    joined_half = lax.dynamic_slice_in_dim(
+        jnp.concatenate([joined_half, joined_half], axis=1), lax.axis_index("z_lo"), quarter, 1
+    ).reshape(tokens, inputs)
     partial_far, unit_sent, joined_half, joined_other, near_quad = lax.optimization_barrier(
         (
             exchange(partial_value, z_axes),
@@ -296,7 +300,7 @@
     grad_quad = jnp.concatenate(
         [grad_high[:, :block_rows].reshape(-1, features), *split_two(gain_high)]
     )
-    grad_z = from_first(gather_ring(grad_quad, "z_lo"), "z_lo")
+    grad_z = gather_ring(grad_quad, "z_lo")
     joined_total = jnp.sum(joined_blocks.astype(wide), axis=0).astype(narrow)
     joined_high = exchange(
         joined_total.reshape(high_count, row_count, 2 * quarter * inputs), "z_hi"
@@ -308,7 +312,7 @@
     )
 
     high_rows = high_count * block_rows
-    gain_sum = sum_parts(grad_z[:, high_rows:])
+    gain_sum = sum_parts(from_first(grad_z[:, high_rows:], "z_lo"))
     gain_grad = (gain_sum + swap_near(gain_sum)).reshape(width)
     grad_all = (
         grad_z[:, :high_rows]

time: 271 us -> 266 us (0.982)
  local copies, waits for them, and re-layouts: 31.8 us -> 24.9 us
  starting transfers between devices: 159 us -> 162 us
    unnamed x38 -> x39, local copies, waits for them, and re-layouts: 7.52 us -> 3.29 us
    ppermute x5, waiting for transfers between devices: 17.9 us -> 14.8 us  [swap_near(): return lax.ppermute(value, 'y_lo', [(0, 1), (1, 0)])]
  transfers between devices with their start and end apart: 34 -> 34, of which waited for: 14 -> 15; matrix products, arithmetic and copies ran while one was open for 18% -> 16% of each run, Pallas kernels for 0% -> 0%
where the time goes in v13:
time: 266 us; the launch traced here: 264 us
  starting transfers between devices  162 us (61%)
  waiting for transfers between devices  43.3 us (16%)
  local copies, waits for them, and re-layouts  24.9 us (9%)
  other arithmetic  17.8 us (7%)
  matrix products  14.2 us (5%)
    all_to_all x7, starting transfers between devices, exchange(): return lax.all_to_all(blocks, axes, split_axis=0, concat_axis=0, tiled=True)  66.7 us
    ppermute x12, starting transfers between devices, from_above(): lax.ppermute(value, axes, [((i + distance) % count, i) for i in range(cou...  45.7 us
    all_to_all x7, waiting for transfers between devices, exchange(): return lax.all_to_all(blocks, axes, split_axis=0, concat_axis=0, tiled=True)  16.6 us
    ppermute x5, starting transfers between devices, swap_cores(): return lax.ppermute(value, 'core', [(0, 1), (1, 0)])  14.9 us
    ppermute x5, waiting for transfers between devices, swap_near(): return lax.ppermute(value, 'y_lo', [(0, 1), (1, 0)])  14.8 us
    ppermute x5, starting transfers between devices, swap_near(): return lax.ppermute(value, 'y_lo', [(0, 1), (1, 0)])  14 us
    ppermute x2, starting transfers between devices, trade_pair(): other = lax.ppermute(sent, axis_name, [(0, 1), (1, 0)])  11.2 us
    ppermute x3, starting transfers between devices, trade_x(): lax.ppermute(turned[step], 'x', [(i, (i + step) % count) for i in range(c...  9.33 us
  transfers between devices with their start and end apart: 34, of which 15 were waited for; matrix products, arithmetic and copies ran while one was open for 16% of the time, Pallas kernels for 0%

profile of v13, /device:TPU:1, one launch (start us, length us, event | category | flops | bytes accessed | tf_op | source)
XLA Modules:
  0.0 263.8 jit_solution(7206974498360795730)
XLA Ops:
  2.0 4.0 %collective-permute-start.1 = (bf16[2,896,256]{2,1,0:T(8,128)(2,1)S(1)}, bf16[2,896,256]{2,1,0:T(8,128)(2,1)S(1)}, u32[]{:S(2)}, u32[]{:S(2)}) collective-permute-start(bf16[2,896,256]{2,1,0:T(8,128)(2,1)S(1)} %pad_maximum_fusion.1), channel_id=1, source_target_pairs={{0,256},{256,0},{1,257},{257,1},{2,258},{258,2},{3,259},{259,3},{4... | collective-permute-start | bytes 2752520 | tf_op jit(solution)/shard_map/ppermute | solution.py:37
  11.4 6.7 %collective-permute-start = (bf16[4,2,12,256]{3,1,2,0:T(2,128)(2,1)S(1)}, bf16[4,2,12,256]{3,1,2,0:T(2,128)(2,1)S(1)}, u32[]{:S(2)}, u32[]{:S(2)}) collective-permute-start(bf16[4,2,12,256]{3,1,2,0:T(2,128)(2,1)S(1)} %bitcast.249), channel_id=1, source_target_pairs={{0,1},{1,0},{2,3},{3,2},{4,5},{5,4},{6,7},{7,6},{8,9},{9,8},{10,11... | collective-permute-start | bytes 147464 | tf_op jit(solution)/shard_map/ppermute | solution.py:72
  18.0 11.1 %all-to-all-start = ((bf16[16,8,2048]{2,1,0:T(8,128)(2,1)}), bf16[16,8,2048]{2,1,0:T(8,128)(2,1)S(1)}, u32[]{:S(2)}, u32[]{:S(2)}) async-start(bf16[16,8,2048]{2,1,0:T(8,128)(2,1)} %reshape.245), calls=%async_computation | async-start | bytes 1048576 | tf_op jit(solution)/shard_map/all_to_all | solution.py:29
  29.7 4.5 %collective-permute-start.2 = (bf16[2,4,12,256]{3,1,2,0:T(4,128)(2,1)S(1)}, bf16[2,4,12,256]{3,1,2,0:T(4,128)(2,1)S(1)}, u32[]{:S(2)}, u32[]{:S(2)}) collective-permute-start(bf16[2,4,12,256]{3,1,2,0:T(4,128)(2,1)S(1)} %bitcast.250), channel_id=1, source_target_pairs={{0,2},{2,0},{1,3},{3,1},{4,6},{6,4},{5,7},{7,5},{8,10},{10,8},{9,1... | collective-permute-start | bytes 147464 | tf_op jit(solution)/shard_map/ppermute | solution.py:72
  36.6 4.4 %collective-permute-start.3 = (bf16[2,2,12,256]{3,1,2,0:T(2,128)(2,1)S(1)}, bf16[2,2,12,256]{3,1,2,0:T(2,128)(2,1)S(1)}, u32[]{:S(2)}, u32[]{:S(2)}) collective-permute-start(bf16[2,2,12,256]{3,1,2,0:T(2,128)(2,1)S(1)} %bitcast.255), channel_id=1, source_target_pairs={{0,12},{4,0},{8,4},{12,8},{1,13},{5,1},{9,5},{13,9},{2,14},{6,2},{... | collective-permute-start | bytes 73736 | tf_op jit(solution)/shard_map/ppermute | solution.py:80
  56.9 12.1 %all-to-all-start.1 = ((bf16[16,64,2048]{2,1,0:T(8,128)(2,1)}), bf16[16,64,2048]{2,1,0:T(8,128)(2,1)}, u32[]{:S(2)}, u32[]{:S(2)}) async-start(bf16[16,64,2048]{2,1,0:T(8,128)(2,1)} %bitcast.208), calls=%async_computation.1 | async-start | bytes 8388608 | tf_op jit(solution)/shard_map/all_to_all | solution.py:29
  71.4 4.3 %collective-permute-start.8 = (bf16[64,256]{1,0:T(8,128)(2,1)S(1)}, bf16[64,256]{1,0:T(8,128)(2,1)S(1)}, u32[]{:S(2)}, u32[]{:S(2)}) collective-permute-start(bf16[64,256]{1,0:T(8,128)(2,1)S(1)} %multiply_convert_fusion), channel_id=1, source_target_pairs={{192,0},{208,16},{224,32},{240,48},{0,64},{16,80},{32,96},{48,112}... | collective-permute-start | bytes 98312 | tf_op jit(solution)/shard_map/ppermute | solution.py:42
  75.7 8.7 %collective-permute-start.7 = (bf16[64,256]{1,0:T(8,128)(2,1)S(1)}, bf16[64,256]{1,0:T(8,128)(2,1)S(1)}, u32[]{:S(2)}, u32[]{:S(2)}) collective-permute-start(bf16[64,256]{1,0:T(8,128)(2,1)S(1)} %multiply_convert_fusion), channel_id=1, source_target_pairs={{128,0},{144,16},{160,32},{176,48},{192,64},{208,80},{224,96},{240... | collective-permute-start | bytes 98312 | tf_op jit(solution)/shard_map/ppermute | solution.py:42
  84.3 5.2 %collective-permute-start.6 = (bf16[64,256]{1,0:T(8,128)(2,1)S(1)}, bf16[64,256]{1,0:T(8,128)(2,1)S(1)}, u32[]{:S(2)}, u32[]{:S(2)}) collective-permute-start(bf16[64,256]{1,0:T(8,128)(2,1)S(1)} %multiply_convert_fusion), channel_id=1, source_target_pairs={{64,0},{80,16},{96,32},{112,48},{128,64},{144,80},{160,96},{176,11... | collective-permute-start | bytes 98312 | tf_op jit(solution)/shard_map/ppermute | solution.py:42
  92.2 3.1 %collective-permute-start.13 = (bf16[256,256]{1,0:T(8,128)(2,1)S(1)}, bf16[256,256]{1,0:T(8,128)(2,1)S(1)}, u32[]{:S(2)}, u32[]{:S(2)}) collective-permute-start(bf16[256,256]{1,0:T(8,128)(2,1)S(1)} %copy-done.13), channel_id=1, source_target_pairs={{32,0},{48,16},{0,32},{16,48},{33,1},{49,17},{1,33},{17,49},{34,2}... | collective-permute-start | bytes 393224 | tf_op jit(solution)/shard_map/ppermute | solution.py:42
  95.3 3.5 %collective-permute-start.12 = (bf16[256,256]{1,0:T(8,128)(2,1)S(1)}, bf16[256,256]{1,0:T(8,128)(2,1)S(1)}, u32[]{:S(2)}, u32[]{:S(2)}) collective-permute-start(bf16[256,256]{1,0:T(8,128)(2,1)S(1)} %copy-done.13), channel_id=1, source_target_pairs={{16,0},{32,16},{48,32},{0,48},{17,1},{33,17},{49,33},{1,49},{18,2}... | collective-permute-start | bytes 393224 | tf_op jit(solution)/shard_map/ppermute | solution.py:42
  100.9 2.7 %collective-permute-start.10 = (bf16[4,64,256]{2,1,0:T(8,128)(2,1)S(1)}, bf16[4,64,256]{2,1,0:T(8,128)(2,1)S(1)}, u32[]{:S(2)}, u32[]{:S(2)}) collective-permute-start(bf16[4,64,256]{2,1,0:T(8,128)(2,1)S(1)} %get-tuple-element.82), channel_id=1, source_target_pairs={{32,0},{48,16},{64,32},{80,48},{96,64},{112,80},{128,96},{144,112}... | collective-permute-start | bytes 393224 | tf_op jit(solution)/shard_map/ppermute | solution.py:42
  109.1 3.0 %collective-permute-done.10 = bf16[4,64,256]{2,1,0:T(8,128)(2,1)S(1)} collective-permute-done((bf16[4,64,256]{2,1,0:T(8,128)(2,1)S(1)}, bf16[4,64,256]{2,1,0:T(8,128)(2,1)S(1)}, u32[]{:S(2)}, u32[]{:S(2)}) %collective-permute-start.10) | collective-permute-done | bytes 131104 | tf_op jit(solution)/shard_map/ppermute | solution.py:42
  112.1 2.8 %collective-permute-done.9 = bf16[4,64,256]{2,1,0:T(8,128)(2,1)S(1)} collective-permute-done((bf16[4,64,256]{2,1,0:T(8,128)(2,1)S(1)}, bf16[4,64,256]{2,1,0:T(8,128)(2,1)S(1)}, u32[]{:S(2)}, u32[]{:S(2)}) %collective-permute-start.9) | collective-permute-done | bytes 131104 | tf_op jit(solution)/shard_map/ppermute | solution.py:42
  115.2 6.5 %all-to-all-done.1 = bf16[16,64,2048]{2,1,0:T(8,128)(2,1)} async-done(((bf16[16,64,2048]{2,1,0:T(8,128)(2,1)}), bf16[16,64,2048]{2,1,0:T(8,128)(2,1)}, u32[]{:S(2)}, u32[]{:S(2)}) %all-to-all-start.1) | async-done | bytes 4194336 | tf_op jit(solution)/shard_map/all_to_all | solution.py:29
  121.8 3.7 %fusion.51 = f32[1024,256]{1,0:T(8,128)S(1)} fusion(bf16[1024,2048]{1,0:T(8,128)(2,1)} %bitcast.31, bf16[2048,256]{1,0:T(8,128)(2,1)} %collective-permute-done.15), kind=kOutput, calls=%fused_computation.150 | convolution fusion | flops 1073741824 | bytes 6291456 | tf_op jit(solution)/shard_map/dot_general | solution.py:207
  127.7 3.4 %fusion.50 = f32[1024,256]{1,0:T(8,128)S(1)} fusion(bf16[1024,2048]{1,0:T(8,128)(2,1)} %bitcast.31, bf16[2048,256]{1,0:T(8,128)(2,1)S(1)} %bitcast.223), kind=kOutput, calls=%fused_computation.149 | convolution fusion | flops 1073741824 | bytes 6291456 | tf_op jit(solution)/shard_map/dot_general | solution.py:208
  132.5 8.5 %all-to-all-start.2 = ((bf16[16,64,256]{2,1,0:T(8,128)(2,1)}), bf16[16,64,256]{2,1,0:T(8,128)(2,1)S(1)}, u32[]{:S(2)}, u32[]{:S(2)}) async-start(bf16[16,64,256]{2,1,0:T(8,128)(2,1)} %copy.266), calls=%async_computation.2 | async-start | bytes 1048576 | tf_op jit(solution)/shard_map/all_to_all | solution.py:29
  142.4 2.7 %collective-permute-start.17 = (bf16[1024,256]{1,0:T(8,128)(2,1)}, bf16[1024,256]{1,0:T(8,128)(2,1)}, u32[]{:S(2)}, u32[]{:S(2)}) collective-permute-start(bf16[1024,256]{1,0:T(8,128)(2,1)} %reshape.257), channel_id=1, source_target_pairs={{0,1},{1,0},{2,3},{3,2},{4,5},{5,4},{6,7},{7,6},{8,9},{9,8},{10,11... | collective-permute-start | bytes 1572872 | tf_op jit(solution)/shard_map/ppermute | solution.py:33
  152.2 4.9 %fusion.6 = f32[2048,512]{1,0:T(8,128)S(1)} fusion(bf16[1024,2048]{1,0:T(8,128)(2,1)} %bitcast.31, bf16[1024,256]{1,0:T(8,128)(2,1)} %collective-permute-done.17, bf16[1024,256]{1,0:T(8,128)(2,1)} %reshape.257), kind=kOutput, calls=%fused_computation.12 | convolution fusion | flops 2149580800 | bytes 9437184 | tf_op jit(solution)/shard_map/dot_general | solution.py:25
  160.4 4.4 %collective-permute-done.19 = bf16[4,256,256]{2,1,0:T(8,128)(2,1)S(1)} collective-permute-done((bf16[4,256,256]{2,1,0:T(8,128)(2,1)S(1)}, bf16[4,256,256]{2,1,0:T(8,128)(2,1)S(1)}, u32[]{:S(2)}, u32[]{:S(2)}) %collective-permute-start.19) | collective-permute-done | bytes 524320 | tf_op jit(solution)/shard_map/ppermute | solution.py:37
  166.7 19.0 %all-to-all-start.3 = ((f32[16,1,320]{2,1,0:T(1,128)}), f32[16,1,320]{2,1,0:T(1,128)S(1)}, u32[]{:S(2)}, u32[]{:S(2)}) async-start(f32[16,1,320]{2,1,0:T(1,128)} %broadcast_in_dim.10), calls=%async_computation.3 | async-start | bytes 49152 | tf_op jit(solution)/shard_map/all_to_all | solution.py:29
  188.2 4.9 %all-to-all-done.3 = f32[16,1,320]{2,1,0:T(1,128)S(1)} async-done(((f32[16,1,320]{2,1,0:T(1,128)}), f32[16,1,320]{2,1,0:T(1,128)S(1)}, u32[]{:S(2)}, u32[]{:S(2)}) %all-to-all-start.3) | async-done | bytes 20512 | tf_op jit(solution)/shard_map/all_to_all | solution.py:29
  194.0 6.7 %all-to-all-start.4 = ((bf16[4,96,256]{2,1,0:T(8,128)(2,1)}), bf16[4,96,256]{2,1,0:T(8,128)(2,1)S(1)}, u32[]{:S(2)}, u32[]{:S(2)}) async-start(bf16[4,96,256]{2,1,0:T(8,128)(2,1)} %broadcast_in_dim.11), calls=%async_computation.4 | async-start | bytes 393216 | tf_op jit(solution)/shard_map/all_to_all | solution.py:29
  200.8 9.1 %collective-permute-done.20 = bf16[896,512]{1,0:T(8,128)(2,1)} collective-permute-done((bf16[896,512]{1,0:T(8,128)(2,1)}, bf16[896,512]{1,0:T(8,128)(2,1)}, u32[]{:S(2)}, u32[]{:S(2)}) %collective-permute-start.20) | collective-permute-done | bytes 917536 | tf_op jit(solution)/shard_map/ppermute | solution.py:37
  214.2 6.1 %collective-permute-start.21 = (f32[896,256]{1,0:T(8,128)}, f32[896,256]{1,0:T(8,128)}, u32[]{:S(2)}, u32[]{:S(2)}) collective-permute-start(f32[896,256]{1,0:T(8,128)} %get-tuple-element.46), channel_id=1, source_target_pairs={{0,1},{1,0},{2,3},{3,2},{4,5},{5,4},{6,7},{7,6},{8,9},{9,8},{10,11... | collective-permute-start | bytes 2752520 | tf_op jit(solution)/shard_map/ppermute | solution.py:33
  222.0 3.5 %all-to-all-start.5 = ((bf16[16,16,2048]{2,1,0:T(8,128)(2,1)}), bf16[16,16,2048]{2,1,0:T(8,128)(2,1)S(1)}, u32[]{:S(2)}, u32[]{:S(2)}) async-start(bf16[16,16,2048]{2,1,0:T(8,128)(2,1)} %bitcast.66), calls=%async_computation.5 | async-start | bytes 2097152 | tf_op jit(solution)/shard_map/all_to_all | solution.py:29
  227.8 2.8 %collective-permute-start.24 = (bf16[288,256]{1,0:T(8,128)(2,1)}, bf16[288,256]{1,0:T(8,128)(2,1)S(1)}, u32[]{:S(2)}, u32[]{:S(2)}) collective-permute-start(bf16[288,256]{1,0:T(8,128)(2,1)} %get-tuple-element.76), channel_id=1, source_target_pairs={{48,0},{0,16},{16,32},{32,48},{49,1},{1,17},{17,33},{33,49},{50,2}... | collective-permute-start | bytes 442376 | tf_op jit(solution)/shard_map/ppermute | solution.py:42
  230.6 4.1 %collective-permute-start.23 = (bf16[288,256]{1,0:T(8,128)(2,1)}, bf16[288,256]{1,0:T(8,128)(2,1)S(1)}, u32[]{:S(2)}, u32[]{:S(2)}) collective-permute-start(bf16[288,256]{1,0:T(8,128)(2,1)} %get-tuple-element.76), channel_id=1, source_target_pairs={{32,0},{48,16},{0,32},{16,48},{33,1},{49,17},{1,33},{17,49},{34,2}... | collective-permute-start | bytes 442376 | tf_op jit(solution)/shard_map/ppermute | solution.py:42
  234.7 4.3 %collective-permute-start.22 = (bf16[288,256]{1,0:T(8,128)(2,1)}, bf16[288,256]{1,0:T(8,128)(2,1)}, u32[]{:S(2)}, u32[]{:S(2)}) collective-permute-start(bf16[288,256]{1,0:T(8,128)(2,1)} %get-tuple-element.76), channel_id=1, source_target_pairs={{16,0},{32,16},{48,32},{0,48},{17,1},{33,17},{49,33},{1,49},{18,2}... | collective-permute-start | bytes 442376 | tf_op jit(solution)/shard_map/ppermute | solution.py:42
  243.6 5.6 %all-to-all-start.6 = ((bf16[4,4,2048]{2,1,0:T(4,128)(2,1)}), bf16[4,4,2048]{2,1,0:T(4,128)(2,1)S(1)}, u32[]{:S(2)}, u32[]{:S(2)}) async-start(bf16[4,4,2048]{2,1,0:T(4,128)(2,1)} %reshape.265), calls=%async_computation.6 | async-start | bytes 131072 | tf_op jit(solution)/shard_map/all_to_all | solution.py:29
  254.8 3.0 %collective-permute-start.25 = (f32[2,128,256]{2,1,0:T(8,128)S(1)}, f32[2,128,256]{2,1,0:T(8,128)S(1)}, u32[]{:S(2)}, u32[]{:S(2)}) collective-permute-start(f32[2,128,256]{2,1,0:T(8,128)S(1)} %fusion.27), channel_id=1, source_target_pairs={{0,256},{256,0},{1,257},{257,1},{2,258},{258,2},{3,259},{259,3},{4... | collective-permute-start | bytes 786440 | tf_op jit(solution)/shard_map/ppermute | solution.py:37
  (208 shorter events, 82.4 us)
Async XLA Ops:
  2.0 27.5 %collective-permute-start.1 = (bf16[2,896,256]{2,1,0:T(8,128)(2,1)S(1)}, bf16[2,896,256]{2,1,0:T(8,128)(2,1)S(1)}, u32[]{:S(2)}, u32[]{:S(2)}) collective-permute-start(bf16[2,896,256]{2,1,0:T(8,128)(2,1)S(1)} %pad_maximum_fusion.1), channel_id=1, source_target_pairs={{0,256},{256,0},{1,257},{257,1},{2,258},{258,2},{3,259},{259,3},{4... | collective-permute-start | bytes 2752520 | tf_op jit(solution)/shard_map/ppermute | solution.py:37
  11.4 17.8 %collective-permute-start = (bf16[4,2,12,256]{3,1,2,0:T(2,128)(2,1)S(1)}, bf16[4,2,12,256]{3,1,2,0:T(2,128)(2,1)S(1)}, u32[]{:S(2)}, u32[]{:S(2)}) collective-permute-start(bf16[4,2,12,256]{3,1,2,0:T(2,128)(2,1)S(1)} %bitcast.249), channel_id=1, source_target_pairs={{0,1},{1,0},{2,3},{3,2},{4,5},{5,4},{6,7},{7,6},{8,9},{9,8},{10,11... | collective-permute-start | bytes 147464 | tf_op jit(solution)/shard_map/ppermute | solution.py:72
  18.0 35.3 %all-to-all-start = ((bf16[16,8,2048]{2,1,0:T(8,128)(2,1)}), bf16[16,8,2048]{2,1,0:T(8,128)(2,1)S(1)}, u32[]{:S(2)}, u32[]{:S(2)}) async-start(bf16[16,8,2048]{2,1,0:T(8,128)(2,1)} %reshape.245), calls=%async_computation | async-start | bytes 1048576 | tf_op jit(solution)/shard_map/all_to_all | solution.py:29
  29.7 6.3 %collective-permute-start.2 = (bf16[2,4,12,256]{3,1,2,0:T(4,128)(2,1)S(1)}, bf16[2,4,12,256]{3,1,2,0:T(4,128)(2,1)S(1)}, u32[]{:S(2)}, u32[]{:S(2)}) collective-permute-start(bf16[2,4,12,256]{3,1,2,0:T(4,128)(2,1)S(1)} %bitcast.250), channel_id=1, source_target_pairs={{0,2},{2,0},{1,3},{3,1},{4,6},{6,4},{5,7},{7,5},{8,10},{10,8},{9,1... | collective-permute-start | bytes 147464 | tf_op jit(solution)/shard_map/ppermute | solution.py:72
  36.6 10.2 %collective-permute-start.3 = (bf16[2,2,12,256]{3,1,2,0:T(2,128)(2,1)S(1)}, bf16[2,2,12,256]{3,1,2,0:T(2,128)(2,1)S(1)}, u32[]{:S(2)}, u32[]{:S(2)}) collective-permute-start(bf16[2,2,12,256]{3,1,2,0:T(2,128)(2,1)S(1)} %bitcast.255), channel_id=1, source_target_pairs={{0,12},{4,0},{8,4},{12,8},{1,13},{5,1},{9,5},{13,9},{2,14},{6,2},{... | collective-permute-start | bytes 73736 | tf_op jit(solution)/shard_map/ppermute | solution.py:80
  41.0 6.4 %collective-permute-start.4 = (bf16[2,2,12,256]{3,1,2,0:T(2,128)(2,1)S(1)}, bf16[2,2,12,256]{3,1,2,0:T(2,128)(2,1)S(1)}, u32[]{:S(2)}, u32[]{:S(2)}) collective-permute-start(bf16[2,2,12,256]{3,1,2,0:T(2,128)(2,1)S(1)} %bitcast.257), channel_id=1, source_target_pairs={{0,8},{4,12},{8,0},{12,4},{1,9},{5,13},{9,1},{13,5},{2,10},{6,14},... | collective-permute-start | bytes 73736 | tf_op jit(solution)/shard_map/ppermute | solution.py:80
  43.5 6.3 %collective-permute-start.5 = (bf16[2,2,12,256]{3,1,2,0:T(2,128)(2,1)S(1)}, bf16[2,2,12,256]{3,1,2,0:T(2,128)(2,1)S(1)}, u32[]{:S(2)}, u32[]{:S(2)}) collective-permute-start(bf16[2,2,12,256]{3,1,2,0:T(2,128)(2,1)S(1)} %bitcast.259), channel_id=1, source_target_pairs={{0,4},{4,8},{8,12},{12,0},{1,5},{5,9},{9,13},{13,1},{2,6},{6,10},{... | collective-permute-start | bytes 73736 | tf_op jit(solution)/shard_map/ppermute | solution.py:80
  56.9 64.8 %all-to-all-start.1 = ((bf16[16,64,2048]{2,1,0:T(8,128)(2,1)}), bf16[16,64,2048]{2,1,0:T(8,128)(2,1)}, u32[]{:S(2)}, u32[]{:S(2)}) async-start(bf16[16,64,2048]{2,1,0:T(8,128)(2,1)} %bitcast.208), calls=%async_computation.1 | async-start | bytes 8388608 | tf_op jit(solution)/shard_map/all_to_all | solution.py:29
  69.3 52.5 %collective-permute-start.15 = (bf16[2048,256]{1,0:T(8,128)(2,1)S(1)}, bf16[2048,256]{1,0:T(8,128)(2,1)}, u32[]{:S(2)}, u32[]{:S(2)}) collective-permute-start(bf16[2048,256]{1,0:T(8,128)(2,1)S(1)} %bitcast.222), channel_id=1, source_target_pairs={{0,1},{1,0},{2,3},{3,2},{4,5},{5,4},{6,7},{7,6},{8,9},{9,8},{10,11... | collective-permute-start | bytes 3145736 | tf_op jit(solution)/shard_map/ppermute | solution.py:33
  71.4 20.8 %collective-permute-start.8 = (bf16[64,256]{1,0:T(8,128)(2,1)S(1)}, bf16[64,256]{1,0:T(8,128)(2,1)S(1)}, u32[]{:S(2)}, u32[]{:S(2)}) collective-permute-start(bf16[64,256]{1,0:T(8,128)(2,1)S(1)} %multiply_convert_fusion), channel_id=1, source_target_pairs={{192,0},{208,16},{224,32},{240,48},{0,64},{16,80},{32,96},{48,112}... | collective-permute-start | bytes 98312 | tf_op jit(solution)/shard_map/ppermute | solution.py:42
  75.7 19.7 %collective-permute-start.7 = (bf16[64,256]{1,0:T(8,128)(2,1)S(1)}, bf16[64,256]{1,0:T(8,128)(2,1)S(1)}, u32[]{:S(2)}, u32[]{:S(2)}) collective-permute-start(bf16[64,256]{1,0:T(8,128)(2,1)S(1)} %multiply_convert_fusion), channel_id=1, source_target_pairs={{128,0},{144,16},{160,32},{176,48},{192,64},{208,80},{224,96},{240... | collective-permute-start | bytes 98312 | tf_op jit(solution)/shard_map/ppermute | solution.py:42
  84.3 14.5 %collective-permute-start.6 = (bf16[64,256]{1,0:T(8,128)(2,1)S(1)}, bf16[64,256]{1,0:T(8,128)(2,1)S(1)}, u32[]{:S(2)}, u32[]{:S(2)}) collective-permute-start(bf16[64,256]{1,0:T(8,128)(2,1)S(1)} %multiply_convert_fusion), channel_id=1, source_target_pairs={{64,0},{80,16},{96,32},{112,48},{128,64},{144,80},{160,96},{176,11... | collective-permute-start | bytes 98312 | tf_op jit(solution)/shard_map/ppermute | solution.py:42
  89.5 11.3 %collective-permute-start.14 = (bf16[256,256]{1,0:T(8,128)(2,1)S(1)}, bf16[256,256]{1,0:T(8,128)(2,1)S(1)}, u32[]{:S(2)}, u32[]{:S(2)}) collective-permute-start(bf16[256,256]{1,0:T(8,128)(2,1)S(1)} %copy-done.13), channel_id=1, source_target_pairs={{48,0},{0,16},{16,32},{32,48},{49,1},{1,17},{17,33},{33,49},{50,2}... | collective-permute-start | bytes 393224 | tf_op jit(solution)/shard_map/ppermute | solution.py:42
  92.2 12.7 %collective-permute-start.13 = (bf16[256,256]{1,0:T(8,128)(2,1)S(1)}, bf16[256,256]{1,0:T(8,128)(2,1)S(1)}, u32[]{:S(2)}, u32[]{:S(2)}) collective-permute-start(bf16[256,256]{1,0:T(8,128)(2,1)S(1)} %copy-done.13), channel_id=1, source_target_pairs={{32,0},{48,16},{0,32},{16,48},{33,1},{49,17},{1,33},{17,49},{34,2}... | collective-permute-start | bytes 393224 | tf_op jit(solution)/shard_map/ppermute | solution.py:42
  95.3 12.1 %collective-permute-start.12 = (bf16[256,256]{1,0:T(8,128)(2,1)S(1)}, bf16[256,256]{1,0:T(8,128)(2,1)S(1)}, u32[]{:S(2)}, u32[]{:S(2)}) collective-permute-start(bf16[256,256]{1,0:T(8,128)(2,1)S(1)} %copy-done.13), channel_id=1, source_target_pairs={{16,0},{32,16},{48,32},{0,48},{17,1},{33,17},{49,33},{1,49},{18,2}... | collective-permute-start | bytes 393224 | tf_op jit(solution)/shard_map/ppermute | solution.py:42
  98.9 10.1 %collective-permute-start.11 = (bf16[4,64,256]{2,1,0:T(8,128)(2,1)S(1)}, bf16[4,64,256]{2,1,0:T(8,128)(2,1)S(1)}, u32[]{:S(2)}, u32[]{:S(2)}) collective-permute-start(bf16[4,64,256]{2,1,0:T(8,128)(2,1)S(1)} %get-tuple-element.82), channel_id=1, source_target_pairs={{240,0},{0,16},{16,32},{32,48},{48,64},{64,80},{80,96},{96,112},{1... | collective-permute-start | bytes 393224 | tf_op jit(solution)/shard_map/ppermute | solution.py:42
  100.9 11.2 %collective-permute-start.10 = (bf16[4,64,256]{2,1,0:T(8,128)(2,1)S(1)}, bf16[4,64,256]{2,1,0:T(8,128)(2,1)S(1)}, u32[]{:S(2)}, u32[]{:S(2)}) collective-permute-start(bf16[4,64,256]{2,1,0:T(8,128)(2,1)S(1)} %get-tuple-element.82), channel_id=1, source_target_pairs={{32,0},{48,16},{64,32},{80,48},{96,64},{112,80},{128,96},{144,112}... | collective-permute-start | bytes 393224 | tf_op jit(solution)/shard_map/ppermute | solution.py:42
  104.9 10.0 %collective-permute-start.9 = (bf16[4,64,256]{2,1,0:T(8,128)(2,1)S(1)}, bf16[4,64,256]{2,1,0:T(8,128)(2,1)S(1)}, u32[]{:S(2)}, u32[]{:S(2)}) collective-permute-start(bf16[4,64,256]{2,1,0:T(8,128)(2,1)S(1)} %get-tuple-element.82), channel_id=1, source_target_pairs={{16,0},{32,16},{48,32},{64,48},{80,64},{96,80},{112,96},{128,112},... | collective-permute-start | bytes 393224 | tf_op jit(solution)/shard_map/ppermute | solution.py:42
  132.5 32.3 %all-to-all-start.2 = ((bf16[16,64,256]{2,1,0:T(8,128)(2,1)}), bf16[16,64,256]{2,1,0:T(8,128)(2,1)S(1)}, u32[]{:S(2)}, u32[]{:S(2)}) async-start(bf16[16,64,256]{2,1,0:T(8,128)(2,1)} %copy.266), calls=%async_computation.2 | async-start | bytes 1048576 | tf_op jit(solution)/shard_map/all_to_all | solution.py:29
  142.4 9.9 %collective-permute-start.17 = (bf16[1024,256]{1,0:T(8,128)(2,1)}, bf16[1024,256]{1,0:T(8,128)(2,1)}, u32[]{:S(2)}, u32[]{:S(2)}) collective-permute-start(bf16[1024,256]{1,0:T(8,128)(2,1)} %reshape.257), channel_id=1, source_target_pairs={{0,1},{1,0},{2,3},{3,2},{4,5},{5,4},{6,7},{7,6},{8,9},{9,8},{10,11... | collective-permute-start | bytes 1572872 | tf_op jit(solution)/shard_map/ppermute | solution.py:33
  148.0 12.4 %collective-permute-start.18 = (bf16[1024,256]{1,0:T(8,128)(2,1)S(1)}, bf16[1024,256]{1,0:T(8,128)(2,1)S(1)}, u32[]{:S(2)}, u32[]{:S(2)}) collective-permute-start(bf16[1024,256]{1,0:T(8,128)(2,1)S(1)} %reshape.260), channel_id=1, source_target_pairs={{0,1},{1,0},{2,3},{3,2},{4,5},{5,4},{6,7},{7,6},{8,9},{9,8},{10,11... | collective-permute-start | bytes 1572872 | tf_op jit(solution)/shard_map/ppermute | solution.py:33
  149.9 14.9 %collective-permute-start.19 = (bf16[4,256,256]{2,1,0:T(8,128)(2,1)S(1)}, bf16[4,256,256]{2,1,0:T(8,128)(2,1)S(1)}, u32[]{:S(2)}, u32[]{:S(2)}) collective-permute-start(bf16[4,256,256]{2,1,0:T(8,128)(2,1)S(1)} %pad_maximum_fusion.4), channel_id=1, source_target_pairs={{0,256},{256,0},{1,257},{257,1},{2,258},{258,2},{3,259},{259,3},{4... | collective-permute-start | bytes 1572872 | tf_op jit(solution)/shard_map/ppermute | solution.py:37
  166.7 26.3 %all-to-all-start.3 = ((f32[16,1,320]{2,1,0:T(1,128)}), f32[16,1,320]{2,1,0:T(1,128)S(1)}, u32[]{:S(2)}, u32[]{:S(2)}) async-start(f32[16,1,320]{2,1,0:T(1,128)} %broadcast_in_dim.10), calls=%async_computation.3 | async-start | bytes 49152 | tf_op jit(solution)/shard_map/all_to_all | solution.py:29
  185.7 24.2 %collective-permute-start.20 = (bf16[896,512]{1,0:T(8,128)(2,1)}, bf16[896,512]{1,0:T(8,128)(2,1)}, u32[]{:S(2)}, u32[]{:S(2)}) collective-permute-start(bf16[896,512]{1,0:T(8,128)(2,1)} %fusion.10), channel_id=1, source_target_pairs={{0,256},{256,0},{1,257},{257,1},{2,258},{258,2},{3,259},{259,3},{4... | collective-permute-start | bytes 2752520 | tf_op jit(solution)/shard_map/ppermute | solution.py:37
  194.0 20.2 %all-to-all-start.4 = ((bf16[4,96,256]{2,1,0:T(8,128)(2,1)}), bf16[4,96,256]{2,1,0:T(8,128)(2,1)S(1)}, u32[]{:S(2)}, u32[]{:S(2)}) async-start(bf16[4,96,256]{2,1,0:T(8,128)(2,1)} %broadcast_in_dim.11), calls=%async_computation.4 | async-start | bytes 393216 | tf_op jit(solution)/shard_map/all_to_all | solution.py:29
  214.2 12.8 %collective-permute-start.21 = (f32[896,256]{1,0:T(8,128)}, f32[896,256]{1,0:T(8,128)}, u32[]{:S(2)}, u32[]{:S(2)}) collective-permute-start(f32[896,256]{1,0:T(8,128)} %get-tuple-element.46), channel_id=1, source_target_pairs={{0,1},{1,0},{2,3},{3,2},{4,5},{5,4},{6,7},{7,6},{8,9},{9,8},{10,11... | collective-permute-start | bytes 2752520 | tf_op jit(solution)/shard_map/ppermute | solution.py:33
  222.0 20.7 %all-to-all-start.5 = ((bf16[16,16,2048]{2,1,0:T(8,128)(2,1)}), bf16[16,16,2048]{2,1,0:T(8,128)(2,1)S(1)}, u32[]{:S(2)}, u32[]{:S(2)}) async-start(bf16[16,16,2048]{2,1,0:T(8,128)(2,1)} %bitcast.66), calls=%async_computation.5 | async-start | bytes 2097152 | tf_op jit(solution)/shard_map/all_to_all | solution.py:29
  227.8 21.4 %collective-permute-start.24 = (bf16[288,256]{1,0:T(8,128)(2,1)}, bf16[288,256]{1,0:T(8,128)(2,1)S(1)}, u32[]{:S(2)}, u32[]{:S(2)}) collective-permute-start(bf16[288,256]{1,0:T(8,128)(2,1)} %get-tuple-element.76), channel_id=1, source_target_pairs={{48,0},{0,16},{16,32},{32,48},{49,1},{1,17},{17,33},{33,49},{50,2}... | collective-permute-start | bytes 442376 | tf_op jit(solution)/shard_map/ppermute | solution.py:42
  230.6 18.6 %collective-permute-start.23 = (bf16[288,256]{1,0:T(8,128)(2,1)}, bf16[288,256]{1,0:T(8,128)(2,1)S(1)}, u32[]{:S(2)}, u32[]{:S(2)}) collective-permute-start(bf16[288,256]{1,0:T(8,128)(2,1)} %get-tuple-element.76), channel_id=1, source_target_pairs={{32,0},{48,16},{0,32},{16,48},{33,1},{49,17},{1,33},{17,49},{34,2}... | collective-permute-start | bytes 442376 | tf_op jit(solution)/shard_map/ppermute | solution.py:42
  234.7 14.5 %collective-permute-start.22 = (bf16[288,256]{1,0:T(8,128)(2,1)}, bf16[288,256]{1,0:T(8,128)(2,1)}, u32[]{:S(2)}, u32[]{:S(2)}) collective-permute-start(bf16[288,256]{1,0:T(8,128)(2,1)} %get-tuple-element.76), channel_id=1, source_target_pairs={{16,0},{32,16},{48,32},{0,48},{17,1},{33,17},{49,33},{1,49},{18,2}... | collective-permute-start | bytes 442376 | tf_op jit(solution)/shard_map/ppermute | solution.py:42
  243.6 17.4 %all-to-all-start.6 = ((bf16[4,4,2048]{2,1,0:T(4,128)(2,1)}), bf16[4,4,2048]{2,1,0:T(4,128)(2,1)S(1)}, u32[]{:S(2)}, u32[]{:S(2)}) async-start(bf16[4,4,2048]{2,1,0:T(4,128)(2,1)} %reshape.265), calls=%async_computation.6 | async-start | bytes 131072 | tf_op jit(solution)/shard_map/all_to_all | solution.py:29
  254.8 8.3 %collective-permute-start.25 = (f32[2,128,256]{2,1,0:T(8,128)S(1)}, f32[2,128,256]{2,1,0:T(8,128)S(1)}, u32[]{:S(2)}, u32[]{:S(2)}) collective-permute-start(f32[2,128,256]{2,1,0:T(8,128)S(1)} %fusion.27), channel_id=1, source_target_pairs={{0,256},{256,0},{1,257},{257,1},{2,258},{258,2},{3,259},{259,3},{4... | collective-permute-start | bytes 786440 | tf_op jit(solution)/shard_map/ppermute | solution.py:37
  (18 other events, 201.3 us)
